TPU v7x, 32 devices: a whole 2x2x4 slice. The times are simulated.
32 devices in a mesh: uly: 8 (over y, x, core), blk: 4 (over z).
Axes of the slice: x: 2, y: 2, z: 4, core: 2. Of those that a mesh axis runs over, the one named last changes fastest.
Arguments:
- hidden_in: bfloat16 [4096, 2048], P(('uly', 'blk')), may hold values from -6 to 6
- out_grad: bfloat16 [4096, 2048], P(('uly', 'blk')), may hold values from -6 to 6
- attn_gain: bfloat16 [2048], P(('uly', 'blk')), may hold values from 0.5 to 1.5
- query_weight: bfloat16 [2048, 2048], P(('uly', 'blk')), may hold values from -0.125 to 0.125
- key_weight: bfloat16 [2048, 2048], P(('uly', 'blk')), may hold values from -0.125 to 0.125
- value_weight: bfloat16 [2048, 2048], P(('uly', 'blk')), may hold values from -0.125 to 0.125
- out_weight: bfloat16 [2048, 2048], P(('uly', 'blk')), may hold values from -1.5 to 1.5
- query_gain: bfloat16 [2048], P(('uly', 'blk')), may hold values from 0.5 to 1.5
- key_gain: bfloat16 [2048], P(('uly', 'blk')), may hold values from 0.5 to 1.5
- ffn_gain: bfloat16 [2048], P(('uly', 'blk')), may hold values from 0.5 to 1.5
- router_weight: bfloat16 [2048, 64], P(('uly', 'blk')), may hold values from -0.0625 to 0.0625
- expert_weights: bfloat16 [64, 3, 2048, 1024], P('uly', None, None, 'blk'), may hold values from -4 to 4
- routes: int32 [4096, 8], P(('uly', 'blk')), may hold values from 0 to 63, all different within a row; in each aligned block of 128 rows (0 to 127, 128 to 255, ...) at most 17 rows name the same one
- doc_starts: int32 [5], replicated, may hold values from 0 to 3378, as said below
Outputs:
- output: bfloat16 [4096, 2048], P(('uly', 'blk'))
- hidden_grad: float32 [4096, 2048], P(('uly', 'blk'))
- attn_gain_grad: float32 [2048], P(('uly', 'blk'))
- query_weight_grad: float32 [2048, 2048], P(('uly', 'blk'))
- key_weight_grad: float32 [2048, 2048], P(('uly', 'blk'))
- value_weight_grad: float32 [2048, 2048], P(('uly', 'blk'))
- out_weight_grad: float32 [2048, 2048], P(('uly', 'blk'))
- query_gain_grad: float32 [2048], P(('uly', 'blk'))
- key_gain_grad: float32 [2048], P(('uly', 'blk'))
- ffn_gain_grad: float32 [2048], P(('uly', 'blk'))
- router_weight_grad: float32 [2048, 64], P(('uly', 'blk'))
- expert_weights_grad: float32 [64, 3, 2048, 1024], P('uly', None, None, 'blk')
Inputs may be any that keep to these rules, and one draw needn't show every extreme that they name: `routes`: each row names 8 different experts; at most 17 of the rows of one device name the same expert. `doc_starts`: increasing, the first 0.
All inputs are finite; a program needn't handle non-finite values.
Results may differ from a plain program's by a relative error of at most 0.02.
Values may be sent and summed in bfloat16 or wider, within the bound.
A program may use at most 512 MiB of HBM per device.

v0:
```python
import jax
import jax.numpy as jnp
from jax import lax
from jax.sharding import PartitionSpec as P

HEADS = 16
HEAD_DIM = 128
EXPERTS = 64
CAP = 17


EPS = 1e-05
THETA = 10000.0
NEG = -1e30
FIRST_DIM = (((0,), (0,)), ((), ()))
LAST_DIM = (((1,), (1,)), ((), ()))


def norm_forward(values, gain_row):
    scaling = lax.rsqrt(jnp.mean(values * values, axis=-1, keepdims=True) + EPS)
    return (values * scaling * gain_row, scaling)


def norm_backward(values, scaling, gain_row, upstream):
    weighted = upstream * gain_row
    inner_mean = jnp.mean(weighted * values, axis=-1, keepdims=True)
    result = scaling * weighted - values * (scaling * scaling * scaling) * inner_mean
    return (result, jnp.sum(upstream * values * scaling, axis=0))


def rotary_tables(position, head_dim):
    halfway = head_dim // 2
    frequency = THETA ** (-(jnp.arange(halfway).astype(jnp.float32) * 2.0 / head_dim))
    angles = position.astype(jnp.float32)[:, None] * frequency[None, :]
    cosine = jnp.concatenate([jnp.cos(angles), jnp.cos(angles)], axis=1)[:, None, :]
    sine_table = jnp.concatenate([jnp.sin(angles), jnp.sin(angles)], axis=1)[:, None, :]
    return (cosine, sine_table)


def rotate_forward(values, cosine, sine_table):
    halfway = values.shape[-1] // 2
    turned = jnp.concatenate([-values[..., halfway:], values[..., :halfway]], axis=-1)
    return values * cosine + turned * sine_table


def rotate_backward(upstream, cosine, sine_table):
    halfway = upstream.shape[-1] // 2
    moved = upstream * sine_table
    turned = jnp.concatenate([moved[..., halfway:], -moved[..., :halfway]], axis=-1)
    return upstream * cosine + turned


def to_heads(stacked):
    return lax.all_to_all(stacked, "uly", split_axis=2, concat_axis=1, tiled=True)


def to_tokens(stacked):
    return lax.all_to_all(stacked, "uly", split_axis=1, concat_axis=2, tiled=True)


def dispatch(buffer):
    return lax.all_to_all(buffer, "uly", split_axis=0, concat_axis=1, tiled=True)


def combine(buffer):
    return lax.all_to_all(buffer, "uly", split_axis=1, concat_axis=0, tiled=True)


def gather_rows(row_block):
    return lax.all_gather(row_block, "blk", axis=0, tiled=True)


def sum_rows(partial_value):
    return lax.psum_scatter(
        partial_value.astype(jnp.bfloat16), "blk", scatter_dimension=0, tiled=True
    ).astype(jnp.float32)


def expert_forward(entry_rows, weights):
    gate_pre = jnp.dot(entry_rows, weights[0], preferred_element_type=jnp.float32)
    up_value = jnp.dot(entry_rows, weights[1], preferred_element_type=jnp.float32)
    inner_low = (jax.nn.silu(gate_pre) * up_value).astype(jnp.bfloat16)
    result = lax.dot_general(inner_low, weights[2], LAST_DIM, preferred_element_type=jnp.float32)
    return (gate_pre, up_value, inner_low, result)


def activation_grads(gate_pre, up_value, inner_grad):
    sigmoid_gate = jax.nn.sigmoid(gate_pre)
    gate_grad = (
        inner_grad * up_value * sigmoid_gate * (1.0 + gate_pre * (1.0 - sigmoid_gate))
    ).astype(jnp.bfloat16)
    up_grad = (inner_grad * gate_pre * sigmoid_gate).astype(jnp.bfloat16)
    return (gate_grad, up_grad)


def weight_grads(entry_rows, upstream, inner_low, gate_grad, up_grad):
    grad_gate = lax.dot_general(
        entry_rows, gate_grad, FIRST_DIM, preferred_element_type=jnp.float32
    )
    grad_up = lax.dot_general(entry_rows, up_grad, FIRST_DIM, preferred_element_type=jnp.float32)
    grad_down = lax.dot_general(upstream, inner_low, FIRST_DIM, preferred_element_type=jnp.float32)
    return jnp.stack([grad_gate, grad_up, grad_down])


def entry_grads_of(weights, gate_grad, up_grad):
    entry_grad = lax.dot_general(
        gate_grad, weights[0], LAST_DIM, preferred_element_type=jnp.float32
    )
    return entry_grad + lax.dot_general(
        up_grad, weights[1], LAST_DIM, preferred_element_type=jnp.float32
    )


def expert_backward(entry_rows, weights, gate_pre, up_value, inner_low, upstream):
    inner_grad = jnp.dot(upstream, weights[2], preferred_element_type=jnp.float32)
    gate_grad, up_grad = activation_grads(gate_pre, up_value, inner_grad)
    return (
        weight_grads(entry_rows, upstream, inner_low, gate_grad, up_grad),
        entry_grads_of(weights, gate_grad, up_grad),
    )


def body(
    hidden_in,
    out_grad,
    attn_gain,
    query_weight,
    key_weight,
    value_weight,
    out_weight,
    query_gain,
    key_gain,
    ffn_gain,
    router_weight,
    expert_weights,
    routes,
    doc_starts,
):
    ulysses_size = lax.axis_size("uly")
    cycle_size = lax.axis_size("blk")
    tok_rows = hidden_in.shape[0]
    width = hidden_in.shape[1]
    all_tokens = tok_rows * ulysses_size * cycle_size
    top_count = routes.shape[1]
    gathered = (
        lax.all_gather(attn_gain, ("uly", "blk"), axis=0, tiled=True),
        lax.all_gather(query_weight, ("uly", "blk"), axis=0, tiled=True),
        lax.all_gather(key_weight, ("uly", "blk"), axis=0, tiled=True),
        lax.all_gather(value_weight, ("uly", "blk"), axis=0, tiled=True),
        lax.all_gather(out_weight, ("uly", "blk"), axis=0, tiled=True),
        lax.all_gather(query_gain, ("uly", "blk"), axis=0, tiled=True),
        lax.all_gather(key_gain, ("uly", "blk"), axis=0, tiled=True),
        lax.all_gather(ffn_gain, ("uly", "blk"), axis=0, tiled=True),
        lax.all_gather(router_weight, ("uly", "blk"), axis=0, tiled=True),
    )
    (
        gain_attn,
        weight_query,
        weight_key,
        weight_value,
        weight_out,
        gain_query,
        gain_key,
        gain_ffn,
        weight_router,
    ) = gathered
    cycle_index = lax.axis_index("blk")
    row_anchor = (lax.axis_index("uly") * cycle_size + cycle_index) * tok_rows
    my_position = row_anchor + jnp.arange(tok_rows, dtype=jnp.int32)
    cosine, sine_table = rotary_tables(my_position, HEAD_DIM)
    hidden = hidden_in.astype(jnp.float32)
    first_normed, first_scale = norm_forward(hidden, gain_attn)
    first_low = first_normed.astype(jnp.bfloat16)
    query_pre = jnp.dot(first_low, weight_query, preferred_element_type=jnp.float32)
    key_pre = jnp.dot(first_low, weight_key, preferred_element_type=jnp.float32)
    value_pre = jnp.dot(first_low, weight_value, preferred_element_type=jnp.float32)
    query_normed, query_scale = norm_forward(query_pre, gain_query)
    key_normed, key_scale = norm_forward(key_pre, gain_key)
    query_rot = rotate_forward(
        query_normed.reshape(tok_rows, HEADS, HEAD_DIM), cosine, sine_table
    ).reshape(tok_rows, width)
    key_rot = rotate_forward(
        key_normed.reshape(tok_rows, HEADS, HEAD_DIM), cosine, sine_table
    ).reshape(tok_rows, width)
    head_stack = to_heads(jnp.stack([query_rot, key_rot, value_pre]).astype(jnp.bfloat16))
    local_rows = head_stack.shape[1]
    head_count = head_stack.shape[2] // HEAD_DIM
    query_heads = head_stack[0].reshape(local_rows, head_count, HEAD_DIM)
    key_values = lax.all_gather(head_stack[1:], "blk", axis=1, tiled=True)
    key_all = key_values[0].reshape(all_tokens, head_count, HEAD_DIM)
    value_all = key_values[1].reshape(all_tokens, head_count, HEAD_DIM)
    local_iota = jnp.arange(local_rows, dtype=jnp.int32)
    query_position = (
        local_iota // tok_rows * cycle_size + cycle_index
    ) * tok_rows + local_iota % tok_rows
    key_iota = jnp.arange(all_tokens, dtype=jnp.int32)
    key_position = (
        key_iota % local_rows // tok_rows * cycle_size + key_iota // local_rows
    ) * tok_rows + key_iota % tok_rows
    query_doc = jnp.sum((doc_starts[None, :] <= query_position[:, None]).astype(jnp.int32), axis=1)
    key_doc = jnp.sum((doc_starts[None, :] <= key_position[:, None]).astype(jnp.int32), axis=1)
    query_block = 512
    block_count = local_rows // query_block
    scaling = HEAD_DIM ** (-0.5)

    def block_scores(query_part, qpos_part, qdoc_part, key_index):
        key_part = lax.dynamic_slice_in_dim(key_all, key_index * local_rows, local_rows, 0)
        kpos_part = lax.dynamic_slice_in_dim(key_position, key_index * local_rows, local_rows, 0)
        kdoc_part = lax.dynamic_slice_in_dim(key_doc, key_index * local_rows, local_rows, 0)
        raw_scores = (
            jnp.einsum("qhd,khd->hqk", query_part, key_part, preferred_element_type=jnp.float32)
            * scaling
        )
        allowed = (kpos_part[None, :] <= qpos_part[:, None]) & (
            kdoc_part[None, :] == qdoc_part[:, None]
        )
        return jnp.where(allowed[None], raw_scores, NEG)

    def query_slices(block_index):
        row_first = block_index * query_block
        return (
            lax.dynamic_slice_in_dim(query_heads, row_first, query_block, 0),
            lax.dynamic_slice_in_dim(query_position, row_first, query_block, 0),
            lax.dynamic_slice_in_dim(query_doc, row_first, query_block, 0),
        )

    def forward_block(block_index):
        query_part, qpos_part, qdoc_part = query_slices(block_index)

        def stats_step(loop_state, key_index):
            running_max, running_sum = loop_state
            scores = block_scores(query_part, qpos_part, qdoc_part, key_index)
            new_max = jnp.maximum(running_max, jnp.max(scores, axis=2))
            running_sum = running_sum * jnp.exp(running_max - new_max) + jnp.sum(
                jnp.exp(scores - new_max[:, :, None]), axis=2
            )
            return ((new_max, running_sum), None)

        start_max = jnp.full((head_count, query_block), NEG, jnp.float32)
        (final_max, final_sum), unused = lax.scan(
            stats_step, (start_max, jnp.zeros_like(start_max)), jnp.arange(cycle_size)
        )
        log_total = final_max + jnp.log(final_sum)

        def value_step(accum, key_index):
            scores = block_scores(query_part, qpos_part, qdoc_part, key_index)
            weights_low = jnp.exp(scores - log_total[:, :, None]).astype(jnp.bfloat16)
            value_part = lax.dynamic_slice_in_dim(value_all, key_index * local_rows, local_rows, 0)
            return (
                accum
                + jnp.einsum(
                    "hqk,khd->qhd", weights_low, value_part, preferred_element_type=jnp.float32
                ),
                None,
            )

        attended_part, unused = lax.scan(
            value_step,
            jnp.zeros((query_block, head_count, HEAD_DIM), jnp.float32),
            jnp.arange(cycle_size),
        )
        return (attended_part, log_total)

    attended_blocks, log_totals = lax.map(forward_block, jnp.arange(block_count))
    attended_heads = attended_blocks.reshape(local_rows, head_count, HEAD_DIM)
    attended_low = attended_heads.reshape(local_rows, head_count * HEAD_DIM).astype(jnp.bfloat16)
    mixed = to_tokens(attended_low[None])[0]
    residual = hidden + jnp.dot(mixed, weight_out, preferred_element_type=jnp.float32)
    second_normed, second_scale = norm_forward(residual, gain_ffn)
    second_low = second_normed.astype(jnp.bfloat16)
    logits = jnp.dot(second_low, weight_router, preferred_element_type=jnp.float32)
    probabilities = jax.nn.softmax(logits, axis=-1)
    expert_iota = jnp.arange(EXPERTS, dtype=jnp.int32)
    picked = (routes[:, :, None] == expert_iota[None, None, :]).astype(jnp.float32)
    gate_value = jnp.sum(picked * probabilities[:, None, :], axis=2)
    flat_routes = routes.reshape(-1)
    route_hits = (flat_routes[:, None] == expert_iota[None, :]).astype(jnp.int32)
    slot_index = jnp.sum((jnp.cumsum(route_hits, axis=0) - 1) * route_hits, axis=1)
    capacity = CAP
    target = flat_routes * capacity + slot_index
    source_row = jnp.arange(flat_routes.shape[0], dtype=jnp.int32) // top_count

    def to_buffer(route_rows):
        empty = jnp.zeros((EXPERTS * capacity, width), jnp.bfloat16)
        return empty.at[target].set(route_rows).reshape(EXPERTS, capacity, width)

    received = dispatch(to_buffer(second_low[source_row]))
    local_experts = expert_weights.shape[0]
    kept_state = []
    outputs = []
    for expert_local in range(local_experts):
        entry_rows = received[expert_local]
        entry_all = gather_rows(entry_rows)
        gate_pre, up_value, inner_low, result = expert_forward(
            entry_all, expert_weights[expert_local]
        )
        outputs.append(sum_rows(result).astype(jnp.bfloat16))
        kept_state.append((entry_all, gate_pre, up_value, inner_low))
    returned = combine(jnp.stack(outputs)).reshape(EXPERTS * capacity, width)
    per_route = returned[target].reshape(tok_rows, top_count, width)
    moe_sum = jnp.sum(gate_value[:, :, None] * per_route, axis=1)
    output = (residual + moe_sum).astype(jnp.bfloat16)
    upstream = out_grad.astype(jnp.float32)
    gate_grad = jnp.sum(per_route * upstream[:, None, :], axis=2)
    route_grad = (
        (gate_value[:, :, None] * upstream[:, None, :])
        .astype(jnp.bfloat16)
        .reshape(tok_rows * top_count, width)
    )
    back_in = dispatch(to_buffer(route_grad))
    grads_expert = []
    entry_grads = []
    for expert_local in range(local_experts):
        upstream_rows = back_in[expert_local]
        entry_rows, gate_pre, up_value, inner_low = kept_state[expert_local]
        upstream_all = gather_rows(upstream_rows)
        weight_grad, entry_grad = expert_backward(
            entry_rows, expert_weights[expert_local], gate_pre, up_value, inner_low, upstream_all
        )
        grads_expert.append(weight_grad)
        entry_grads.append(sum_rows(entry_grad).astype(jnp.bfloat16))
    expert_grad_out = jnp.stack(grads_expert)
    returned_grad = combine(jnp.stack(entry_grads)).reshape(EXPERTS * capacity, width)[target]
    second_grad = jnp.sum(
        returned_grad.reshape(tok_rows, top_count, width), axis=1, dtype=jnp.float32
    )
    prob_grad = jnp.sum(picked * gate_grad[:, :, None], axis=1)
    logit_grad = (
        probabilities * (prob_grad - jnp.sum(probabilities * prob_grad, axis=1, keepdims=True))
    ).astype(jnp.bfloat16)
    router_grad = lax.dot_general(
        second_low, logit_grad, FIRST_DIM, preferred_element_type=jnp.float32
    )
    second_grad = second_grad + lax.dot_general(
        logit_grad, weight_router, LAST_DIM, preferred_element_type=jnp.float32
    )
    residual_part, ffn_gain_grad = norm_backward(residual, second_scale, gain_ffn, second_grad)
    residual_grad = upstream + residual_part
    residual_low = residual_grad.astype(jnp.bfloat16)
    out_weight_grad = lax.dot_general(
        mixed, residual_low, FIRST_DIM, preferred_element_type=jnp.float32
    )
    mixed_grad = lax.dot_general(
        residual_low, weight_out, LAST_DIM, preferred_element_type=jnp.float32
    ).astype(jnp.bfloat16)
    mixed_heads = to_heads(mixed_grad[None])[0].reshape(local_rows, head_count, HEAD_DIM)
    row_delta = jnp.sum(mixed_heads * attended_heads, axis=2).T

    def backward_block(loop_state, block_index):
        key_grad_all, value_grad_all = loop_state
        query_part, qpos_part, qdoc_part = query_slices(block_index)
        row_first = block_index * query_block
        grad_part = lax.dynamic_slice_in_dim(mixed_heads, row_first, query_block, 0)
        delta_part = lax.dynamic_slice_in_dim(row_delta, row_first, query_block, 1)
        log_part = log_totals[block_index]

        def key_step(inner_state, key_index):
            query_grad, key_grad_acc, value_grad_acc = inner_state
            scores = block_scores(query_part, qpos_part, qdoc_part, key_index)
            weights = jnp.exp(scores - log_part[:, :, None])
            key_first = key_index * local_rows
            key_part = lax.dynamic_slice_in_dim(key_all, key_first, local_rows, 0)
            value_part = lax.dynamic_slice_in_dim(value_all, key_first, local_rows, 0)
            weight_grad = jnp.einsum(
                "qhd,khd->hqk", grad_part, value_part, preferred_element_type=jnp.float32
            )
            score_grad = (weights * (weight_grad - delta_part[:, :, None])).astype(jnp.bfloat16)
            value_grad = jnp.einsum(
                "hqk,qhd->khd",
                weights.astype(jnp.bfloat16),
                grad_part,
                preferred_element_type=jnp.float32,
            )
            key_grad = (
                jnp.einsum(
                    "hqk,qhd->khd", score_grad, query_part, preferred_element_type=jnp.float32
                )
                * scaling
            )
            query_grad = (
                query_grad
                + jnp.einsum(
                    "hqk,khd->qhd", score_grad, key_part, preferred_element_type=jnp.float32
                )
                * scaling
            )
            key_grad_acc = lax.dynamic_update_slice_in_dim(
                key_grad_acc,
                lax.dynamic_slice_in_dim(key_grad_acc, key_first, local_rows, 0) + key_grad,
                key_first,
                0,
            )
            value_grad_acc = lax.dynamic_update_slice_in_dim(
                value_grad_acc,
                lax.dynamic_slice_in_dim(value_grad_acc, key_first, local_rows, 0) + value_grad,
                key_first,
                0,
            )
            return ((query_grad, key_grad_acc, value_grad_acc), None)

        start_grad = jnp.zeros((query_block, head_count, HEAD_DIM), jnp.float32)
        (query_grad, key_grad_all, value_grad_all), unused = lax.scan(
            key_step, (start_grad, key_grad_all, value_grad_all), jnp.arange(cycle_size)
        )
        return ((key_grad_all, value_grad_all), query_grad)

    zero_keys = jnp.zeros((all_tokens, head_count, HEAD_DIM), jnp.float32)
    (key_grad_all, value_grad_all), query_grads = lax.scan(
        backward_block, (zero_keys, zero_keys), jnp.arange(block_count)
    )
    kv_grads = lax.psum_scatter(
        jnp.stack([key_grad_all, value_grad_all])
        .reshape(2, all_tokens, head_count * HEAD_DIM)
        .astype(jnp.bfloat16),
        "blk",
        scatter_dimension=1,
        tiled=True,
    ).astype(jnp.float32)
    back_stack = jnp.stack(
        [query_grads.reshape(local_rows, head_count * HEAD_DIM), kv_grads[0], kv_grads[1]]
    ).astype(jnp.bfloat16)
    token_grads = to_tokens(back_stack)
    query_rot_grad = token_grads[0].astype(jnp.float32).reshape(tok_rows, HEADS, HEAD_DIM)
    key_rot_grad = token_grads[1].astype(jnp.float32).reshape(tok_rows, HEADS, HEAD_DIM)
    query_normed_grad = rotate_backward(query_rot_grad, cosine, sine_table).reshape(tok_rows, width)
    key_normed_grad = rotate_backward(key_rot_grad, cosine, sine_table).reshape(tok_rows, width)
    query_pre_grad, query_gain_grad = norm_backward(
        query_pre, query_scale, gain_query, query_normed_grad
    )
    key_pre_grad, key_gain_grad = norm_backward(key_pre, key_scale, gain_key, key_normed_grad)
    query_low = query_pre_grad.astype(jnp.bfloat16)
    key_low = key_pre_grad.astype(jnp.bfloat16)
    value_low = token_grads[2]
    query_weight_grad = lax.dot_general(
        first_low, query_low, FIRST_DIM, preferred_element_type=jnp.float32
    )
    key_weight_grad = lax.dot_general(
        first_low, key_low, FIRST_DIM, preferred_element_type=jnp.float32
    )
    value_weight_grad = lax.dot_general(
        first_low, value_low, FIRST_DIM, preferred_element_type=jnp.float32
    )
    first_grad = lax.dot_general(
        query_low, weight_query, LAST_DIM, preferred_element_type=jnp.float32
    )
    first_grad = first_grad + lax.dot_general(
        key_low, weight_key, LAST_DIM, preferred_element_type=jnp.float32
    )
    first_grad = first_grad + lax.dot_general(
        value_low, weight_value, LAST_DIM, preferred_element_type=jnp.float32
    )
    hidden_part, attn_gain_grad = norm_backward(hidden, first_scale, gain_attn, first_grad)
    hidden_grad = residual_grad + hidden_part
    dense_grads = (
        lax.psum_scatter(attn_gain_grad, ("uly", "blk"), scatter_dimension=0, tiled=True),
        lax.psum_scatter(query_weight_grad, ("uly", "blk"), scatter_dimension=0, tiled=True),
        lax.psum_scatter(key_weight_grad, ("uly", "blk"), scatter_dimension=0, tiled=True),
        lax.psum_scatter(value_weight_grad, ("uly", "blk"), scatter_dimension=0, tiled=True),
        lax.psum_scatter(out_weight_grad, ("uly", "blk"), scatter_dimension=0, tiled=True),
        lax.psum_scatter(query_gain_grad, ("uly", "blk"), scatter_dimension=0, tiled=True),
        lax.psum_scatter(key_gain_grad, ("uly", "blk"), scatter_dimension=0, tiled=True),
        lax.psum_scatter(ffn_gain_grad, ("uly", "blk"), scatter_dimension=0, tiled=True),
        lax.psum_scatter(router_grad, ("uly", "blk"), scatter_dimension=0, tiled=True),
    )
    return (
        output,
        hidden_grad,
        dense_grads[0],
        dense_grads[1],
        dense_grads[2],
        dense_grads[3],
        dense_grads[4],
        dense_grads[5],
        dense_grads[6],
        dense_grads[7],
        dense_grads[8],
        expert_grad_out,
    )


def solution(mesh):
    return jax.shard_map(
        body,
        mesh=mesh,
        in_specs=(
            P(("uly", "blk"), None),
            P(("uly", "blk"), None),
            P(("uly", "blk")),
            P(("uly", "blk"), None),
            P(("uly", "blk"), None),
            P(("uly", "blk"), None),
            P(("uly", "blk"), None),
            P(("uly", "blk")),
            P(("uly", "blk")),
            P(("uly", "blk")),
            P(("uly", "blk"), None),
            P("uly", None, None, "blk"),
            P(("uly", "blk"), None),
            P(),
        ),
        out_specs=(
            P(("uly", "blk"), None),
            P(("uly", "blk"), None),
            P(("uly", "blk")),
            P(("uly", "blk"), None),
            P(("uly", "blk"), None),
            P(("uly", "blk"), None),
            P(("uly", "blk"), None),
            P(("uly", "blk")),
            P(("uly", "blk")),
            P(("uly", "blk")),
            P(("uly", "blk"), None),
            P("uly", None, None, "blk"),
        ),
        check_vma=False,
    )
```

profile of v0, /device:TPU:13, one launch (start us, length us, event | category | flops | bytes accessed | tf_op | source)
XLA Modules:
  0.0 4213.3 jit_solution(9988433151941567331)
XLA Ops:
  12.8 40.5 all-reduce.9
  55.5 34.9 all-gather.24.cloned.1.call-done
  97.4 72.0 %all-gather.22.cloned.1.call-done = bf16[2048,2048]{1,0:T(8,128)(2,1)} async-done(((bf16[64,2048]{1,0:T(8,128)(2,1)}), bf16[2048,2048]{1,0:T(8,128)(2,1)}) %all-gather.22.cloned.1.call-update) | async-done | bytes 8388624 | tf_op jit(solution)/shard_map/all_gather | solution.py:147
  191.2 57.2 %all-gather.26.cloned.1.call-done = bf16[2048,2048]{1,0:T(8,128)(2,1)} async-done(((bf16[64,2048]{1,0:T(8,128)(2,1)}), bf16[2048,2048]{1,0:T(8,128)(2,1)}) %all-gather.26.cloned.1.call-update) | async-done | bytes 8388624 | tf_op jit(solution)/shard_map/all_gather | solution.py:149
  257.4 27.2 all_to_all.120
  288.0 18.0 reduce-window.6
  308.9 55.1 %all-gather.28.cloned.1.call-done = bf16[2,4096,256]{2,1,0:T(8,128)(2,1)} async-done(((bf16[2,1024,256]{2,1,0:T(8,128)(2,1)}), bf16[2,4096,256]{2,1,0:T(8,128)(2,1)}) %all-gather.28.cloned.1.call-update) | async-done | bytes 4194320 | tf_op jit(solution)/shard_map/all_gather | solution.py:189
  381.9 112.6 %while.85 = (s32[]{:T(128)}, f32[2,512,2,128]{1,3,2,0:T(8,128)}, f32[2,2,512]{2,1,0:T(2,128)S(1)}, s32[2]{0:T(128)S(1)}, bf16[1024,2,128]{2,0,1:T(8,128)(2,1)}, ...) while((s32[]{:T(128)}, f32[2,512,2,128]{1,3,2,0:T(8,128)}, ...), condition=%wide.region_12.13_spmd.clone.clone.clone, body=%wide.region_5.12_spmd.clone.clone.sunk.clone | while | flops 820406272 | bytes 15886785 | solution.py:264
  384.4 33.8 while.83
  418.2 19.4 while.84
  440.9 33.3 while.83
  474.3 19.4 while.84
  525.3 23.2 scatter_custom_fusion
  556.1 8.8 all-to-all-start.2
  564.9 66.5 %all_gather.87 = bf16[2048,64]{1,0:T(8,128)(2,1)S(1)} all-gather(bf16[64,64]{1,0:T(8,128)(2,1)S(1)} %copy-done.124), channel_id=1, replica_groups=mesh['uly'=8,'blk'=4] {'uly','blk'}, dimensions={0}, use_global_device_ids=true | all-gather | bytes 270336 | tf_op jit(solution)/shard_map/all_gather | solution.py:154
  633.2 9.6 scatter_custom_fusion.1
  650.4 10.7 all-to-all-start.4
  667.5 61.4 %all-to-all-done.4 = bf16[64,17,2048]{2,1,0:T(8,128)(2,1)} async-done(((bf16[64,17,2048]{2,1,0:T(8,128)(2,1)}), bf16[64,17,2048]{2,1,0:T(8,128)(2,1)}, u32[]{:S(2)}, u32[]{:S(2)}) %all-to-all-start.4) | async-done | bytes 4456480 | tf_op jit(solution)/shard_map/all_to_all | solution.py:62
  768.5 16.6 all-gather.48.cloned.1.call-done
  793.7 40.2 all-gather.34.cloned.1.call-done
  838.7 44.0 %all-gather.50.cloned.1.call-done = bf16[544,2048]{1,0:T(8,128)(2,1)} async-done(((bf16[136,2048]{1,0:T(8,128)(2,1)}), bf16[544,2048]{1,0:T(8,128)(2,1)}) %all-gather.50.cloned.1.call-update) | async-done | bytes 2228240 | tf_op jit(solution)/shard_map/all_gather | solution.py:70
  891.8 39.5 all-gather.36.cloned.1.call-done
  936.1 44.0 %all-gather.52.cloned.1.call-done = bf16[544,2048]{1,0:T(8,128)(2,1)} async-done(((bf16[136,2048]{1,0:T(8,128)(2,1)}), bf16[544,2048]{1,0:T(8,128)(2,1)}) %all-gather.52.cloned.1.call-update) | async-done | bytes 2228240 | tf_op jit(solution)/shard_map/all_gather | solution.py:70
  988.6 40.0 all-gather.38.cloned.1.call-done
  1033.4 44.0 %all-gather.54.cloned.1.call-done = bf16[544,2048]{1,0:T(8,128)(2,1)} async-done(((bf16[136,2048]{1,0:T(8,128)(2,1)}), bf16[544,2048]{1,0:T(8,128)(2,1)}) %all-gather.54.cloned.1.call-update) | async-done | bytes 2228240 | tf_op jit(solution)/shard_map/all_gather | solution.py:70
  1086.0 40.0 all-gather.40.cloned.1.call-done
  1130.8 43.8 %all-gather.56.cloned.1.call-done = bf16[544,2048]{1,0:T(8,128)(2,1)} async-done(((bf16[136,2048]{1,0:T(8,128)(2,1)}), bf16[544,2048]{1,0:T(8,128)(2,1)}) %all-gather.56.cloned.1.call-update) | async-done | bytes 2228240 | tf_op jit(solution)/shard_map/all_gather | solution.py:70
  1183.3 39.9 all-gather.42.cloned.1.call-done
  1228.0 43.8 %all-gather.58.cloned.1.call-done = bf16[544,2048]{1,0:T(8,128)(2,1)} async-done(((bf16[136,2048]{1,0:T(8,128)(2,1)}), bf16[544,2048]{1,0:T(8,128)(2,1)}) %all-gather.58.cloned.1.call-update) | async-done | bytes 2228240 | tf_op jit(solution)/shard_map/all_gather | solution.py:70
  1280.4 40.0 all-gather.44.cloned.1.call-done
  1325.2 44.0 %all-gather.60.cloned.1.call-done = bf16[544,2048]{1,0:T(8,128)(2,1)} async-done(((bf16[136,2048]{1,0:T(8,128)(2,1)}), bf16[544,2048]{1,0:T(8,128)(2,1)}) %all-gather.60.cloned.1.call-update) | async-done | bytes 2228240 | tf_op jit(solution)/shard_map/all_gather | solution.py:70
  1377.7 40.0 all-gather.46.cloned.1.call-done
  1422.5 44.0 %all-gather.62.cloned.1.call-done = bf16[544,2048]{1,0:T(8,128)(2,1)} async-done(((bf16[136,2048]{1,0:T(8,128)(2,1)}), bf16[544,2048]{1,0:T(8,128)(2,1)}) %all-gather.62.cloned.1.call-update) | async-done | bytes 2228240 | tf_op jit(solution)/shard_map/all_gather | solution.py:70
  1503.0 10.5 reduce-scatter.39.cloned.1.call-done
  1515.4 45.9 %reduce-scatter.41.cloned.1.call-done = bf16[136,2048]{1,0:T(8,128)(2,1)} async-done(((bf16[544,2048]{1,0:T(8,128)(2,1)}), bf16[136,2048]{1,0:T(8,128)(2,1)}) %reduce-scatter.41.cloned.1.call-update) | async-done | bytes 557072 | tf_op jit(solution)/shard_map/reduce_scatter | solution.py:74
  1563.2 45.7 %reduce-scatter.43.cloned.1.call-done = bf16[136,2048]{1,0:T(8,128)(2,1)} async-done(((bf16[544,2048]{1,0:T(8,128)(2,1)}), bf16[136,2048]{1,0:T(8,128)(2,1)}) %reduce-scatter.43.cloned.1.call-update) | async-done | bytes 557072 | tf_op jit(solution)/shard_map/reduce_scatter | solution.py:74
  1610.8 45.9 %reduce-scatter.45.cloned.1.call-done = bf16[136,2048]{1,0:T(8,128)(2,1)} async-done(((bf16[544,2048]{1,0:T(8,128)(2,1)}), bf16[136,2048]{1,0:T(8,128)(2,1)}) %reduce-scatter.45.cloned.1.call-update) | async-done | bytes 557072 | tf_op jit(solution)/shard_map/reduce_scatter | solution.py:74
  1658.6 45.7 %reduce-scatter.47.cloned.1.call-done = bf16[136,2048]{1,0:T(8,128)(2,1)} async-done(((bf16[544,2048]{1,0:T(8,128)(2,1)}), bf16[136,2048]{1,0:T(8,128)(2,1)}) %reduce-scatter.47.cloned.1.call-update) | async-done | bytes 557072 | tf_op jit(solution)/shard_map/reduce_scatter | solution.py:74
  1706.2 45.7 %reduce-scatter.49.cloned.1.call-done = bf16[136,2048]{1,0:T(8,128)(2,1)} async-done(((bf16[544,2048]{1,0:T(8,128)(2,1)}), bf16[136,2048]{1,0:T(8,128)(2,1)}) %reduce-scatter.49.cloned.1.call-update) | async-done | bytes 557072 | tf_op jit(solution)/shard_map/reduce_scatter | solution.py:74
  1753.8 45.9 %reduce-scatter.51.cloned.1.call-done = bf16[136,2048]{1,0:T(8,128)(2,1)} async-done(((bf16[544,2048]{1,0:T(8,128)(2,1)}), bf16[136,2048]{1,0:T(8,128)(2,1)}) %reduce-scatter.51.cloned.1.call-update) | async-done | bytes 557072 | tf_op jit(solution)/shard_map/reduce_scatter | solution.py:74
  1801.6 45.9 %reduce-scatter.53.cloned.1.call-done = bf16[136,2048]{1,0:T(8,128)(2,1)} async-done(((bf16[544,2048]{1,0:T(8,128)(2,1)}), bf16[136,2048]{1,0:T(8,128)(2,1)}) %reduce-scatter.53.cloned.1.call-update) | async-done | bytes 557072 | tf_op jit(solution)/shard_map/reduce_scatter | solution.py:74
  1861.5 33.6 reduce-scatter.23.cloned.1.call-done
  1896.9 45.9 %reduce-scatter.25.cloned.1.call-done = bf16[136,2048]{1,0:T(8,128)(2,1)} async-done(((bf16[544,2048]{1,0:T(8,128)(2,1)}), bf16[136,2048]{1,0:T(8,128)(2,1)}) %reduce-scatter.25.cloned.1.call-update) | async-done | bytes 557072 | tf_op jit(solution)/shard_map/reduce_scatter | solution.py:74
  1944.7 45.9 %reduce-scatter.27.cloned.1.call-done = bf16[136,2048]{1,0:T(8,128)(2,1)} async-done(((bf16[544,2048]{1,0:T(8,128)(2,1)}), bf16[136,2048]{1,0:T(8,128)(2,1)}) %reduce-scatter.27.cloned.1.call-update) | async-done | bytes 557072 | tf_op jit(solution)/shard_map/reduce_scatter | solution.py:74
  1992.5 45.7 %reduce-scatter.29.cloned.1.call-done = bf16[136,2048]{1,0:T(8,128)(2,1)} async-done(((bf16[544,2048]{1,0:T(8,128)(2,1)}), bf16[136,2048]{1,0:T(8,128)(2,1)}) %reduce-scatter.29.cloned.1.call-update) | async-done | bytes 557072 | tf_op jit(solution)/shard_map/reduce_scatter | solution.py:74
  2040.1 45.9 %reduce-scatter.31.cloned.1.call-done = bf16[136,2048]{1,0:T(8,128)(2,1)} async-done(((bf16[544,2048]{1,0:T(8,128)(2,1)}), bf16[136,2048]{1,0:T(8,128)(2,1)}) %reduce-scatter.31.cloned.1.call-update) | async-done | bytes 557072 | tf_op jit(solution)/shard_map/reduce_scatter | solution.py:74
  2087.8 45.9 %reduce-scatter.33.cloned.1.call-done = bf16[136,2048]{1,0:T(8,128)(2,1)} async-done(((bf16[544,2048]{1,0:T(8,128)(2,1)}), bf16[136,2048]{1,0:T(8,128)(2,1)}) %reduce-scatter.33.cloned.1.call-update) | async-done | bytes 557072 | tf_op jit(solution)/shard_map/reduce_scatter | solution.py:74
  2135.6 45.7 %reduce-scatter.35.cloned.1.call-done = bf16[136,2048]{1,0:T(8,128)(2,1)} async-done(((bf16[544,2048]{1,0:T(8,128)(2,1)}), bf16[136,2048]{1,0:T(8,128)(2,1)}) %reduce-scatter.35.cloned.1.call-update) | async-done | bytes 557072 | tf_op jit(solution)/shard_map/reduce_scatter | solution.py:74
  2183.2 45.7 %reduce-scatter.37.cloned.1.call-done = bf16[136,2048]{1,0:T(8,128)(2,1)} async-done(((bf16[544,2048]{1,0:T(8,128)(2,1)}), bf16[136,2048]{1,0:T(8,128)(2,1)}) %reduce-scatter.37.cloned.1.call-update) | async-done | bytes 557072 | tf_op jit(solution)/shard_map/reduce_scatter | solution.py:74
  2259.4 11.6 gather_fusion.1
  2277.0 14.6 all-to-all-done.3
  2307.5 11.9 gather_fusion
  2341.3 13.4 reduce.6
  2383.0 136.6 %while.82 = (s32[]{:T(128)}, f32[4096,2,128]{2,0,1:T(8,128)}, f32[4096,2,128]{2,0,1:T(8,128)}, bf16[2,512,2,128]{1,3,2,0:T(8,128)(2,1)}, s32[2]{0:T(128)S(1)}, /...) while((s32[]{:T(128)}, f32[4096,2,128]{2,0,1:T(8,128)}, ...), condition=%wide.region_48.49_spmd.clone.clone, body=%wide.region_45.48_spmd.clone.sunk.clone | while | flops 1355567104 | bytes 66667376 | solution.py:408
  2389.2 61.4 %while.81 = (s32[]{:T(128)}, f32[512,2,128]{0,2,1:T(8,128)S(1)}, f32[4096,2,128]{2,0,1:T(8,128)}, f32[4096,2,128]{2,0,1:T(8,128)}, s32[4]{0:T(128)S(1)}, /*index...) while((s32[]{:T(128)}, f32[512,2,128]{0,2,1:T(8,128)S(1)}, ...), condition=%wide.region_47.47_spmd.clone, body=%wide.region_46.46_spmd.clone.sunk | while | flops 1355415552 | bytes 64004484 | solution.py:402
  2457.5 61.4 %while.81 = (s32[]{:T(128)}, f32[512,2,128]{0,2,1:T(8,128)S(1)}, f32[4096,2,128]{2,0,1:T(8,128)}, f32[4096,2,128]{2,0,1:T(8,128)}, s32[4]{0:T(128)S(1)}, /*index...) while((s32[]{:T(128)}, f32[512,2,128]{0,2,1:T(8,128)S(1)}, ...), condition=%wide.region_47.47_spmd.clone, body=%wide.region_46.46_spmd.clone.sunk | while | flops 1355415552 | bytes 64004484 | solution.py:402
  2534.6 8.7 fusion.266
  2545.2 66.5 %reduce-scatter.55.cloned.1.call-done = bf16[2,1024,256]{1,2,0:T(8,128)(2,1)} async-done(((bf16[2,4096,256]{1,2,0:T(8,128)(2,1)}), bf16[2,1024,256]{1,2,0:T(8,128)(2,1)}) %reduce-scatter.55.cloned.1.call-update) | async-done | bytes 1048592 | tf_op jit(solution)/shard_map/reduce_scatter | solution.py:411
  2617.2 28.4 all_to_all.121
  2784.7 44.7 %all-reduce.8 = (f32[2048]{0:T(1024)S(1)}, f32[2048]{0:T(1024)S(1)}, f32[2048]{0:T(1024)S(1)}, f32[2048]{0:T(1024)S(1)}) all-reduce(f32[2048]{0:T(1024)S(1)} %get-tuple-element.796, f32[2048]{0:T(1024)S(1)} %get-tuple-element.978, f32[2048]{0:T(1024)S(1)} %get-tuple-element.792, ...), channel_id=19, replica_groups=mesh['uly'=8,'blk'=4] {'uly','blk'}, use_global_device_ids=true, to_apply=%region_54.55.clone | all-reduce | flops 8192 | bytes 65536
  2833.1 278.2 %reduce-scatter.63.cloned.1.call-done = f32[64,2048]{1,0:T(8,128)} async-done(((f32[2048,2048]{1,0:T(8,128)}), f32[64,2048]{1,0:T(8,128)}) %reduce-scatter.63.cloned.1.call-update) | async-done | bytes 524304 | tf_op jit(solution)/shard_map/reduce_scatter | solution.py:459
  3111.3 365.1 %reduce-scatter.57.cloned.1.call-done = f32[64,2048]{1,0:T(8,128)} async-done(((f32[2048,2048]{1,0:T(8,128)}), f32[64,2048]{1,0:T(8,128)}) %reduce-scatter.57.cloned.1.call-update) | async-done | bytes 524304 | tf_op jit(solution)/shard_map/reduce_scatter | solution.py:456
  3476.4 365.1 %reduce-scatter.59.cloned.1.call-done = f32[64,2048]{1,0:T(8,128)} async-done(((f32[2048,2048]{1,0:T(8,128)}), f32[64,2048]{1,0:T(8,128)}) %reduce-scatter.59.cloned.1.call-update) | async-done | bytes 524304 | tf_op jit(solution)/shard_map/reduce_scatter | solution.py:457
  3841.4 364.9 %reduce-scatter.61.cloned.1.call-done = f32[64,2048]{1,0:T(8,128)} async-done(((f32[2048,2048]{1,0:T(8,128)}), f32[64,2048]{1,0:T(8,128)}) %reduce-scatter.61.cloned.1.call-update) | async-done | bytes 524304 | tf_op jit(solution)/shard_map/reduce_scatter | solution.py:458
  (1015 shorter events, 825.6 us)
Async XLA Ops:
  7.2 83.2 %all-gather.24.cloned.1.call-start = ((), (), s32[]{:S(2)}) async-start(), calls=%async_computation.31 | async-start | bytes 8650752 | tf_op jit(solution)/shard_map/all_gather | solution.py:148
  7.9 161.4 %all-gather.22.cloned.1.call-start = ((), (), s32[]{:S(2)}) async-start(), calls=%async_computation.30 | async-start | bytes 8650752 | tf_op jit(solution)/shard_map/all_gather | solution.py:147
  8.7 239.7 %all-gather.26.cloned.1.call-start = ((), (), s32[]{:S(2)}) async-start(), calls=%async_computation.32 | async-start | bytes 8650752 | tf_op jit(solution)/shard_map/all_gather | solution.py:149
  9.4 354.6 %all-gather.28.cloned.1.call-start = ((), (), s32[]{:S(2)}) async-start(), calls=%async_computation.33 | async-start | bytes 5242880 | tf_op jit(solution)/shard_map/all_gather | solution.py:189
  53.4 195.0 %copy-start.32 = (f32[2048]{0:T(1024)}, f32[2048]{0:T(1024)S(1)}, u32[]{:S(2)}) copy-start(f32[2048]{0:T(1024)S(1)} %convert_element_type.305) | copy-start | bytes 24580
  53.4 133.5 %copy-start.103 = (f32[2048]{0:T(1024)}, f32[2048]{0:T(1024)S(1)}, u32[]{:S(2)}) copy-start(f32[2048]{0:T(1024)S(1)} %convert_element_type.310) | copy-start | bytes 24580
  53.4 133.5 %copy-start.105 = (f32[2048]{0:T(1024)}, f32[2048]{0:T(1024)S(1)}, u32[]{:S(2)}) copy-start(f32[2048]{0:T(1024)S(1)} %convert_element_type.307) | copy-start | bytes 24580
  53.6 126.6 %copy-start.67 = (f32[128,128]{0,1:T(8,128)}, f32[128,128]{0,1:T(8,128)S(1)}, u32[]{:S(2)}) copy-start(f32[128,128]{0,1:T(8,128)S(1)} %get-tuple-element.1017) | copy-start | bytes 196612
  55.5 192.8 %copy-start.115 = (f32[128]{0:T(128)}, f32[128]{0:T(128)S(1)}, u32[]{:S(2)}) copy-start(f32[128]{0:T(128)S(1)} %get-tuple-element.999) | copy-start | bytes 1540
  95.4 91.5 %copy-start.6 = (f32[128,2048]{1,0:T(8,128)}, f32[128,2048]{1,0:T(8,128)S(1)}, u32[]{:S(2)}) copy-start(f32[128,2048]{1,0:T(8,128)S(1)} %get-tuple-element.1009) | copy-start | bytes 3145732
  286.3 232.9 %all-gather.30.cloned.1.call-start = ((), (), s32[]{:S(2)}) async-start(), calls=%async_computation.34 | async-start | bytes 8650752 | tf_op jit(solution)/shard_map/all_gather | solution.py:150
  504.9 10.8 all-to-all-start.1
  510.1 123.1 %copy-start.125 = (s32[1024,1]{0,1:T(1,128)}, s32[1024,1]{0,1:T(1,128)S(1)}, u32[]{:S(2)}) copy-start(s32[1024,1]{0,1:T(1,128)S(1)} %compare_select_fusion.1) | copy-start | bytes 12292
  525.3 106.2 %copy-start.25 = (bf16[128,2048]{1,0:T(8,128)(2,1)}, bf16[128,2048]{1,0:T(8,128)(2,1)S(1)}, u32[]{:S(2)}) copy-start(bf16[128,2048]{1,0:T(8,128)(2,1)S(1)} %multiply_convert_fusion) | copy-start | bytes 1572868
  556.1 94.3 %all-to-all-start.2 = ((bf16[64,17,2048]{2,1,0:T(8,128)(2,1)}), bf16[64,17,2048]{2,1,0:T(8,128)(2,1)}, u32[]{:S(2)}, u32[]{:S(2)}) async-start(bf16[64,17,2048]{2,1,0:T(8,128)(2,1)} %reshape.668), calls=%async_computation.2 | async-start | bytes 12582912 | tf_op jit(solution)/shard_map/all_to_all | solution.py:62
  650.4 78.5 %all-to-all-start.4 = ((bf16[64,17,2048]{2,1,0:T(8,128)(2,1)}), bf16[64,17,2048]{2,1,0:T(8,128)(2,1)}, u32[]{:S(2)}, u32[]{:S(2)}) async-start(bf16[64,17,2048]{2,1,0:T(8,128)(2,1)} %reshape.670), calls=%async_computation.12 | async-start | bytes 12582912 | tf_op jit(solution)/shard_map/all_to_all | solution.py:62
  661.1 102.6 %all-gather.32.cloned.1.call-start = ((), (), s32[]{:S(2)}) async-start(), calls=%async_computation.35 | async-start | bytes 2785280 | tf_op jit(solution)/shard_map/all_gather | solution.py:70
  667.5 117.7 %all-gather.48.cloned.1.call-start = ((), (), s32[]{:S(2)}) async-start(), calls=%async_computation.51 | async-start | bytes 2785280 | tf_op jit(solution)/shard_map/all_gather | solution.py:70
  736.7 97.3 %all-gather.34.cloned.1.call-start = ((), (), s32[]{:S(2)}) async-start(), calls=%async_computation.37 | async-start | bytes 2785280 | tf_op jit(solution)/shard_map/all_gather | solution.py:70
  738.9 143.8 %all-gather.50.cloned.1.call-start = ((), (), s32[]{:S(2)}) async-start(), calls=%async_computation.53 | async-start | bytes 2785280 | tf_op jit(solution)/shard_map/all_gather | solution.py:70
  741.1 190.2 %all-gather.36.cloned.1.call-start = ((), (), s32[]{:S(2)}) async-start(), calls=%async_computation.39 | async-start | bytes 2785280 | tf_op jit(solution)/shard_map/all_gather | solution.py:70
  743.3 236.7 %all-gather.52.cloned.1.call-start = ((), (), s32[]{:S(2)}) async-start(), calls=%async_computation.55 | async-start | bytes 2785280 | tf_op jit(solution)/shard_map/all_gather | solution.py:70
  745.6 283.1 %all-gather.38.cloned.1.call-start = ((), (), s32[]{:S(2)}) async-start(), calls=%async_computation.41 | async-start | bytes 2785280 | tf_op jit(solution)/shard_map/all_gather | solution.py:70
  747.8 329.5 %all-gather.54.cloned.1.call-start = ((), (), s32[]{:S(2)}) async-start(), calls=%async_computation.57 | async-start | bytes 2785280 | tf_op jit(solution)/shard_map/all_gather | solution.py:70
  750.1 375.9 %all-gather.40.cloned.1.call-start = ((), (), s32[]{:S(2)}) async-start(), calls=%async_computation.43 | async-start | bytes 2785280 | tf_op jit(solution)/shard_map/all_gather | solution.py:70
  752.3 422.3 %all-gather.56.cloned.1.call-start = ((), (), s32[]{:S(2)}) async-start(), calls=%async_computation.59 | async-start | bytes 2785280 | tf_op jit(solution)/shard_map/all_gather | solution.py:70
  754.5 468.7 %all-gather.42.cloned.1.call-start = ((), (), s32[]{:S(2)}) async-start(), calls=%async_computation.45 | async-start | bytes 2785280 | tf_op jit(solution)/shard_map/all_gather | solution.py:70
  757.0 514.8 %all-gather.58.cloned.1.call-start = ((), (), s32[]{:S(2)}) async-start(), calls=%async_computation.61 | async-start | bytes 2785280 | tf_op jit(solution)/shard_map/all_gather | solution.py:70
  759.3 561.2 %all-gather.44.cloned.1.call-start = ((), (), s32[]{:S(2)}) async-start(), calls=%async_computation.47 | async-start | bytes 2785280 | tf_op jit(solution)/shard_map/all_gather | solution.py:70
  760.3 608.8 %all-gather.60.cloned.1.call-start = ((), (), s32[]{:S(2)}) async-start(), calls=%async_computation.63 | async-start | bytes 2785280 | tf_op jit(solution)/shard_map/all_gather | solution.py:70
  761.5 656.3 %all-gather.46.cloned.1.call-start = ((), (), s32[]{:S(2)}) async-start(), calls=%async_computation.49 | async-start | bytes 2785280 | tf_op jit(solution)/shard_map/all_gather | solution.py:70
  762.6 704.0 %all-gather.62.cloned.1.call-start = ((), (), s32[]{:S(2)}) async-start(), calls=%async_computation.65 | async-start | bytes 2785280 | tf_op jit(solution)/shard_map/all_gather | solution.py:70
  763.6 749.9 %reduce-scatter.39.cloned.1.call-start = ((), (), s32[]{:S(2)}) async-start(), calls=%async_computation.52 | async-start | bytes 2785280 | tf_op jit(solution)/shard_map/reduce_scatter | solution.py:74
  788.0 687.2 %copy-start.73 = (bf16[544,256]{1,0:T(8,128)(2,1)}, bf16[544,256]{1,0:T(8,128)(2,1)S(1)}, u32[]{:S(2)}) copy-start(bf16[544,256]{1,0:T(8,128)(2,1)S(1)} %get-tuple-element.976) | copy-start | bytes 835588
  793.7 767.6 %reduce-scatter.41.cloned.1.call-start = ((), (), s32[]{:S(2)}) async-start(), calls=%async_computation.54 | async-start | bytes 2785280 | tf_op jit(solution)/shard_map/reduce_scatter | solution.py:74
  885.5 593.4 %copy-start.77 = (bf16[544,256]{1,0:T(8,128)(2,1)}, bf16[544,256]{1,0:T(8,128)(2,1)S(1)}, u32[]{:S(2)}) copy-start(bf16[544,256]{1,0:T(8,128)(2,1)S(1)} %get-tuple-element.973) | copy-start | bytes 835588
  891.3 717.6 %reduce-scatter.43.cloned.1.call-start = ((), (), s32[]{:S(2)}) async-start(), calls=%async_computation.56 | async-start | bytes 2785280 | tf_op jit(solution)/shard_map/reduce_scatter | solution.py:74
  982.8 499.5 %copy-start.81 = (bf16[544,256]{1,0:T(8,128)(2,1)}, bf16[544,256]{1,0:T(8,128)(2,1)S(1)}, u32[]{:S(2)}) copy-start(bf16[544,256]{1,0:T(8,128)(2,1)S(1)} %get-tuple-element.970) | copy-start | bytes 835588
  988.6 668.1 %reduce-scatter.45.cloned.1.call-start = ((), (), s32[]{:S(2)}) async-start(), calls=%async_computation.58 | async-start | bytes 2785280 | tf_op jit(solution)/shard_map/reduce_scatter | solution.py:74
  1080.2 405.6 %copy-start.85 = (bf16[544,256]{1,0:T(8,128)(2,1)}, bf16[544,256]{1,0:T(8,128)(2,1)S(1)}, u32[]{:S(2)}) copy-start(bf16[544,256]{1,0:T(8,128)(2,1)S(1)} %get-tuple-element.967) | copy-start | bytes 835588
  1085.9 618.3 %reduce-scatter.47.cloned.1.call-start = ((), (), s32[]{:S(2)}) async-start(), calls=%async_computation.60 | async-start | bytes 2785280 | tf_op jit(solution)/shard_map/reduce_scatter | solution.py:74
  1177.4 311.8 %copy-start.89 = (bf16[544,256]{1,0:T(8,128)(2,1)}, bf16[544,256]{1,0:T(8,128)(2,1)S(1)}, u32[]{:S(2)}) copy-start(bf16[544,256]{1,0:T(8,128)(2,1)S(1)} %get-tuple-element.964) | copy-start | bytes 835588
  1183.1 568.8 %reduce-scatter.49.cloned.1.call-start = ((), (), s32[]{:S(2)}) async-start(), calls=%async_computation.62 | async-start | bytes 2785280 | tf_op jit(solution)/shard_map/reduce_scatter | solution.py:74
  1274.6 218.0 %copy-start.93 = (bf16[544,256]{1,0:T(8,128)(2,1)}, bf16[544,256]{1,0:T(8,128)(2,1)S(1)}, u32[]{:S(2)}) copy-start(bf16[544,256]{1,0:T(8,128)(2,1)S(1)} %get-tuple-element.961) | copy-start | bytes 835588
  1280.3 519.3 %reduce-scatter.51.cloned.1.call-start = ((), (), s32[]{:S(2)}) async-start(), calls=%async_computation.64 | async-start | bytes 2785280 | tf_op jit(solution)/shard_map/reduce_scatter | solution.py:74
  1372.0 124.1 %copy-start.97 = (bf16[544,256]{1,0:T(8,128)(2,1)}, bf16[544,256]{1,0:T(8,128)(2,1)S(1)}, u32[]{:S(2)}) copy-start(bf16[544,256]{1,0:T(8,128)(2,1)S(1)} %get-tuple-element.958) | copy-start | bytes 835588
  1377.7 469.7 %reduce-scatter.53.cloned.1.call-start = ((), (), s32[]{:S(2)}) async-start(), calls=%async_computation.66 | async-start | bytes 2785280 | tf_op jit(solution)/shard_map/reduce_scatter | solution.py:74
  1475.1 419.9 %reduce-scatter.23.cloned.1.call-start = ((), (), s32[]{:S(2)}) async-start(), calls=%async_computation.36 | async-start | bytes 2785280 | tf_op jit(solution)/shard_map/reduce_scatter | solution.py:74
  1478.6 464.2 %reduce-scatter.25.cloned.1.call-start = ((), (), s32[]{:S(2)}) async-start(), calls=%async_computation.38 | async-start | bytes 2785280 | tf_op jit(solution)/shard_map/reduce_scatter | solution.py:74
  1482.3 508.3 %reduce-scatter.27.cloned.1.call-start = ((), (), s32[]{:S(2)}) async-start(), calls=%async_computation.40 | async-start | bytes 2785280 | tf_op jit(solution)/shard_map/reduce_scatter | solution.py:74
  1485.7 552.5 %reduce-scatter.29.cloned.1.call-start = ((), (), s32[]{:S(2)}) async-start(), calls=%async_computation.42 | async-start | bytes 2785280 | tf_op jit(solution)/shard_map/reduce_scatter | solution.py:74
  1489.2 596.8 %reduce-scatter.31.cloned.1.call-start = ((), (), s32[]{:S(2)}) async-start(), calls=%async_computation.44 | async-start | bytes 2785280 | tf_op jit(solution)/shard_map/reduce_scatter | solution.py:74
  1492.6 641.2 %reduce-scatter.33.cloned.1.call-start = ((), (), s32[]{:S(2)}) async-start(), calls=%async_computation.46 | async-start | bytes 2785280 | tf_op jit(solution)/shard_map/reduce_scatter | solution.py:74
  1496.0 685.3 %reduce-scatter.35.cloned.1.call-start = ((), (), s32[]{:S(2)}) async-start(), calls=%async_computation.48 | async-start | bytes 2785280 | tf_op jit(solution)/shard_map/reduce_scatter | solution.py:74
  1499.5 729.5 %reduce-scatter.37.cloned.1.call-start = ((), (), s32[]{:S(2)}) async-start(), calls=%async_computation.50 | async-start | bytes 2785280 | tf_op jit(solution)/shard_map/reduce_scatter | solution.py:74
  1856.0 381.5 %all-to-all-start.5 = ((bf16[8,136,2048]{2,0,1:T(8,128)(2,1)}), bf16[8,136,2048]{2,0,1:T(8,128)(2,1)}, u32[]{:S(2)}, u32[]{:S(2)}) async-start(bf16[8,136,2048]{2,0,1:T(8,128)(2,1)} %copy.366), calls=%async_computation.21 | async-start | bytes 8912896 | tf_op jit(solution)/shard_map/all_to_all | solution.py:66
  2237.6 54.0 %all-to-all-start.3 = ((bf16[8,136,2048]{2,0,1:T(8,128)(2,1)}), bf16[8,136,2048]{2,0,1:T(8,128)(2,1)}, u32[]{:S(2)}, u32[]{:S(2)}) async-start(bf16[8,136,2048]{2,0,1:T(8,128)(2,1)} %copy.362), calls=%async_computation.11 | async-start | bytes 8912896 | tf_op jit(solution)/shard_map/all_to_all | solution.py:66
  2356.6 13.8 all-to-all-start.6
  2364.5 247.3 %reduce-scatter.55.cloned.1.call-start = ((), (), s32[]{:S(2)}) async-start(), calls=%async_computation.67 | async-start | bytes 5242880 | tf_op jit(solution)/shard_map/reduce_scatter | solution.py:411
  2531.7 301.4 %reduce-scatter.65.cloned.1.call-start = ((), (), s32[]{:S(2)}) async-start(), calls=%async_computation.72 | async-start | bytes 1081344 | tf_op jit(solution)/shard_map/reduce_scatter | solution.py:463
  2534.1 577.2 %reduce-scatter.63.cloned.1.call-start = ((), (), s32[]{:S(2)}) async-start(), calls=%async_computation.71 | async-start | bytes 17301504 | tf_op jit(solution)/shard_map/reduce_scatter | solution.py:459
  2543.3 933.1 %reduce-scatter.57.cloned.1.call-start = ((), (), s32[]{:S(2)}) async-start(), calls=%async_computation.68 | async-start | bytes 17301504 | tf_op jit(solution)/shard_map/reduce_scatter | solution.py:456
  2672.5 1168.9 %reduce-scatter.59.cloned.1.call-start = ((), (), s32[]{:S(2)}) async-start(), calls=%async_computation.69 | async-start | bytes 17301504 | tf_op jit(solution)/shard_map/reduce_scatter | solution.py:457
  2683.0 1523.4 %reduce-scatter.61.cloned.1.call-start = ((), (), s32[]{:S(2)}) async-start(), calls=%async_computation.70 | async-start | bytes 17301504 | tf_op jit(solution)/shard_map/reduce_scatter | solution.py:458
  (186 other events, 1472.0 us)
Sparse Core Ops, SparseCore 0:
  10.9 79.4 all-gather.23
  93.3 75.9 all-gather.21
  172.3 75.9 all-gather.25
  286.4 77.5 all-gather.27
  366.8 78.9 all-gather.29
  667.6 46.8 all-gather.31
  736.8 48.3 all-gather.47
  786.7 47.1 all-gather.33
  835.5 47.1 all-gather.49
  884.1 47.1 all-gather.35
  932.8 47.1 all-gather.51
  981.5 47.1 all-gather.37
  1030.2 47.1 all-gather.53
  1078.8 47.1 all-gather.39
  1127.4 47.1 all-gather.55
  1176.0 47.1 all-gather.41
  1224.6 47.1 all-gather.57
  1273.2 47.1 all-gather.43
  1322.0 47.1 all-gather.59
  1370.6 47.1 all-gather.45
  1419.3 47.1 all-gather.61
  1469.4 44.0 reduce-scatter.38
  1515.8 45.4 reduce-scatter.40
  1563.5 45.4 reduce-scatter.42
  1611.2 45.4 reduce-scatter.44
  1658.8 45.4 reduce-scatter.46
  1706.4 45.4 reduce-scatter.48
  1754.2 45.4 reduce-scatter.50
  1802.0 45.4 reduce-scatter.52
  1849.6 45.4 reduce-scatter.22
  1897.3 45.4 reduce-scatter.24
  1945.1 45.4 reduce-scatter.26
  1992.7 45.4 reduce-scatter.28
  2040.5 45.4 reduce-scatter.30
  2088.3 45.4 reduce-scatter.32
  2135.9 45.4 reduce-scatter.34
  2183.5 45.4 reduce-scatter.36
  2531.9 79.8 reduce-scatter.54
  2614.5 127.4 reduce-scatter.64
  2744.9 366.3 reduce-scatter.62
  3114.2 362.1 reduce-scatter.56
  3479.2 362.1 reduce-scatter.58
  3844.1 362.1 reduce-scatter.60
where the time goes:
time: 4230 us; the launch traced here: 4210 us
  waiting for transfers between devices  3030 us (72%)
  matrix products  394 us (9%)
  local copies, waits for them, and re-layouts  315 us (7%)
  blocking collectives  207 us (5%)
  other arithmetic  175 us (4%)
  starting transfers between devices  46.9 us (1%)
    reduce_scatter x16, waiting for transfers between devices, sum_rows(): lax.psum_scatter(partial_value.astype(jnp.bfloat16), 'blk', scatter_dimen...  685 us
    all_gather x16, waiting for transfers between devices, gather_rows(): return lax.all_gather(row_block, 'blk', axis=0, tiled=True)  604 us
    reduce_scatter x1, waiting for transfers between devices, body(): lax.psum_scatter(key_weight_grad, ('uly', 'blk'), scatter_dimension=0, ti...  365 us
    reduce_scatter x1, waiting for transfers between devices, body(): lax.psum_scatter(query_weight_grad, ('uly', 'blk'), scatter_dimension=0,...  365 us
    reduce_scatter x1, waiting for transfers between devices, body(): lax.psum_scatter(value_weight_grad, ('uly', 'blk'), scatter_dimension=0,...  365 us
    reduce_scatter x1, waiting for transfers between devices, body(): lax.psum_scatter(out_weight_grad, ('uly', 'blk'), scatter_dimension=0, ti...  278 us
    unnamed x2, blocking collectives  85.2 us
  transfers between devices with their start and end apart: 49, of which 44 were waited for; matrix products, arithmetic and copies ran while one was open for 14% of the time, Pallas kernels for 0%

commit v1 on v0

v1 whole, which is shorter than its diff:
```python
import functools

import jax
import jax.numpy as jnp
from jax import lax
from jax.experimental import pallas as pl
from jax.experimental.pallas import tpu as pltpu
from jax.sharding import PartitionSpec as P

HEADS = 16
HEAD_DIM = 128
EXPERTS = 64
CAP = 17

EPS = 1e-05
THETA = 10000.0
NEG = -1e30
FIRST_DIM = (((0,), (0,)), ((), ()))
LAST_DIM = (((1,), (1,)), ((), ()))
ALL = ("uly", "blk")
F32 = jnp.float32
BF16 = jnp.bfloat16
VMEM_BYTES = 56 * 1024 * 1024


def dot(a, b, dims=(((1,), (0,)), ((), ()))):
    return lax.dot_general(a, b, dims, preferred_element_type=F32)


def rotary_tables(position):
    halfway = HEAD_DIM // 2
    frequency = THETA ** (-(jnp.arange(halfway).astype(F32) * 2.0 / HEAD_DIM))
    angles = position.astype(F32)[:, None] * frequency[None, :]
    cosine = jnp.concatenate([jnp.cos(angles), jnp.cos(angles)], axis=1)
    sine = jnp.concatenate([jnp.sin(angles), jnp.sin(angles)], axis=1)
    return cosine, sine


def rotate_forward(values, cosine, sine):
    halfway = values.shape[-1] // 2
    turned = jnp.concatenate([-values[..., halfway:], values[..., :halfway]], axis=-1)
    return values * cosine + turned * sine


def rotate_backward(upstream, cosine, sine):
    halfway = upstream.shape[-1] // 2
    moved = upstream * sine
    turned = jnp.concatenate([moved[..., halfway:], -moved[..., :halfway]], axis=-1)
    return upstream * cosine + turned


def norm_scale(values):
    return lax.rsqrt(jnp.mean(values * values, axis=-1, keepdims=True) + EPS)


MESH = pl.DeviceIdType.MESH


def _send(src, dst, send_sem, recv_sem, to):
    copy = pltpu.make_async_remote_copy(
        src_ref=src, dst_ref=dst, send_sem=send_sem, recv_sem=recv_sem, device_id=to, device_id_type=MESH
    )
    copy.start()
    return copy


def _expect(ref, sem, here):
    pltpu.make_async_remote_copy(
        src_ref=ref, dst_ref=ref, send_sem=sem, recv_sem=sem, device_id=here, device_id_type=MESH
    ).wait_recv()


def _sent(ref, sem, here):
    pltpu.make_async_remote_copy(
        src_ref=ref, dst_ref=ref, send_sem=sem, recv_sem=sem, device_id=here, device_id_type=MESH
    ).wait_send()


def _greet(u, z, planes, line, depth):
    barrier = pltpu.get_barrier_semaphore()
    for bit in planes:
        pl.semaphore_signal(barrier, inc=1, device_id=(u ^ bit, z), device_id_type=MESH)
    if line:

        @pl.when(z > 0)
        def _():
            pl.semaphore_signal(barrier, inc=1, device_id=(u, z - 1), device_id_type=MESH)

        @pl.when(z < depth - 1)
        def _():
            pl.semaphore_signal(barrier, inc=1, device_id=(u, z + 1), device_id_type=MESH)

    ends = jnp.where((z == 0) | (z == depth - 1), 1, 2) if line else 0
    pl.semaphore_wait(barrier, len(planes) + ends)


def _line_order(z):
    second = jnp.where(z == 0, 1, z - 1)
    third = jnp.where(z == 0, 2, jnp.where(z == 3, 1, z + 1))
    fourth = jnp.where(z < 2, 3, 0)
    return (z, second, third, fourth)


def _gather_all_kernel(x_ref, o_ref, own_sem, z_send, z_recv, p_send, p_recv, c_send, c_recv):
    u, z = lax.axis_index("uly"), lax.axis_index("blk")
    depth = 4
    half = x_ref.shape[0] // 2
    halves = (pl.ds(0, half), pl.ds(half, half))
    here = (u, z)
    _greet(u, z, (1, 2, 4), True, depth)
    own = pltpu.make_async_copy(x_ref, o_ref.at[u * depth + z], own_sem)
    own.start()
    order = _line_order(z)

    def block(who, level):
        return o_ref.at[who * depth + level]

    def part(who, level, h):
        return o_ref.at[who * depth + level, halves[h]]

    first, then = (2, 4), (4, 2)

    def along(level, source, step):
        @pl.when((z > 0) & (level >= z))
        def _():
            step(source, 0, level, (u, z - 1))

        @pl.when((z < depth - 1) & (level <= z))
        def _():
            step(source, 1, level, (u, z + 1))

    def go(source, way, level, to):
        _send(source, block(u, level), z_send.at[way, level], z_recv.at[level], to)

    def gone(source, way, level, to):
        _sent(source, z_send.at[way, level], here)

    def across(level, source):
        for h in range(2):
            _send(
                source.at[halves[h]], part(u, level, h), p_send.at[level, h, 0], p_recv.at[level, h, 0], (u ^ first[h], z)
            )
        _send(source, block(u, level), c_send.at[level, 0], c_recv.at[level, 0], (u ^ 1, z))

    def onward(level, source):
        for h in range(2):
            _expect(part(u ^ first[h], level, h), p_recv.at[level, h, 0], here)
            to = (u ^ then[h], z)
            _send(source.at[halves[h]], part(u, level, h), p_send.at[level, h, 1], p_recv.at[level, h, 1], to)
            _send(
                part(u ^ first[h], level, h),
                part(u ^ first[h], level, h),
                p_send.at[level, h, 2],
                p_recv.at[level, h, 2],
                to,
            )

    def share(level):
        for h in range(2):
            _expect(part(u ^ then[h], level, h), p_recv.at[level, h, 1], here)
            _expect(part(u ^ 6, level, h), p_recv.at[level, h, 2], here)
        for i, bit in enumerate((2, 4, 6)):
            _send(block(u ^ bit, level), block(u ^ bit, level), c_send.at[level, i + 1], c_recv.at[level, i + 1], (u ^ 1, z))

    sources = [x_ref] + [block(u, order[i]) for i in range(1, 4)]
    along(z, x_ref, go)
    across(z, x_ref)
    for i in range(1, 4):
        _expect(block(u, order[i]), z_recv.at[order[i]], here)
        along(order[i], sources[i], go)
        across(order[i], sources[i])
        onward(order[i - 1], sources[i - 1])
        if i >= 2:
            share(order[i - 2])
    onward(order[3], sources[3])
    share(order[2])
    share(order[3])
    for i in range(4):
        level = order[i]
        along(level, sources[i], gone)
        for h in range(2):
            for k in range(3):
                _sent(part(u, level, h), p_send.at[level, h, k], here)
        for k, bit in enumerate((0, 2, 4, 6)):
            _sent(block(u, level), c_send.at[level, k], here)
            _expect(block(u ^ 1 ^ bit, level), c_recv.at[level, k], here)
    own.wait()


def gather_all(x, collective_id):
    U, Z = lax.axis_size("uly"), lax.axis_size("blk")
    if (U, Z) != (8, 4):
        return lax.all_gather(x, ALL, axis=0, tiled=True)
    T, D = x.shape
    dma = pltpu.SemaphoreType.DMA
    any_space = pl.BlockSpec(memory_space=pl.ANY)
    out = pl.pallas_call(
        _gather_all_kernel,
        out_shape=jax.ShapeDtypeStruct((U * Z, T, D), x.dtype),
        in_specs=[any_space],
        out_specs=any_space,
        scratch_shapes=[
            dma,
            dma((2, 4)),
            dma((4,)),
            dma((4, 2, 3)),
            dma((4, 2, 3)),
            dma((4, 4)),
            dma((4, 4)),
        ],
        compiler_params=pltpu.CompilerParams(collective_id=collective_id, has_side_effects=True),
        cost_estimate=pl.CostEstimate(flops=0, bytes_accessed=2 * U * Z * T * D * 2, transcendentals=0),
    )(x)
    return out.reshape(U * Z * T, D)


def _accumulate(target, source, rows):
    strip = 16

    def step(i, _):
        at = pl.ds(pl.multiple_of(i * strip, strip), strip)
        target[at, :] = target[at, :] + source[at, :]
        return 0

    lax.fori_loop(0, rows // strip, step, 0)


def _scatter_all_kernel(
    x_ref, o_ref, work, c_buf, p_buf, q_buf, z_buf, load_sem, c_send, c_recv, p_send, p_recv, q_send, q_recv, z_send, z_recv
):
    u, z = lax.axis_index("uly"), lax.axis_index("blk")
    depth = 4
    T = x_ref.shape[1]
    half = T // 2
    halves = (pl.ds(0, half), pl.ds(half, half))
    here = (u, z)
    order = tuple(reversed(_line_order(z)))
    _greet(u, z, (1, 2, 4), True, depth)
    chips = (0, 2, 4, 6)

    def sibling(i, bit):
        return x_ref.at[(u ^ bit ^ 1) * depth + order[i]]

    def load(i, k, bit):
        return pltpu.make_async_copy(x_ref.at[(u ^ bit) * depth + order[i]], work.at[i, k], load_sem.at[i, k])

    def core(i):
        for k, bit in enumerate(chips):
            _send(sibling(i, bit), c_buf.at[i, k], c_send.at[i, k], c_recv.at[i, k], (u ^ 1, z))
            load(i, k, bit).start()

    first, then = (4, 2), (2, 4)

    def add_core(i):
        for k in (3, 2, 1, 0):
            load(i, k, chips[k]).wait()
            _expect(c_buf.at[i, k], c_recv.at[i, k], here)
            _accumulate(work.at[i, k], c_buf.at[i, k], T)
        for h in range(2):
            to = (u ^ first[h], z)
            for j, bit in enumerate((first[h], 6)):
                k = chips.index(bit)
                _send(work.at[i, k, halves[h]], p_buf.at[i, h, j], p_send.at[i, h, j], p_recv.at[i, h, j], to)

    def add_first(i):
        for h in range(2):
            k = chips.index(then[h])
            _expect(p_buf.at[i, h, 1], p_recv.at[i, h, 1], here)
            _accumulate(work.at[i, k, halves[h]], p_buf.at[i, h, 1], half)
            _send(work.at[i, k, halves[h]], q_buf.at[i, h], q_send.at[i, h], q_recv.at[i, h], (u ^ then[h], z))
            _expect(p_buf.at[i, h, 0], p_recv.at[i, h, 0], here)
            _accumulate(work.at[i, 0, halves[h]], p_buf.at[i, h, 0], half)

    def add_then(i):
        for h in range(2):
            _expect(q_buf.at[i, h], q_recv.at[i, h], here)
            _accumulate(work.at[i, 0, halves[h]], q_buf.at[i, h], half)

    def line(i):
        level = order[i]

        @pl.when((level > z) & (z > 0))
        def _():
            _expect(z_buf.at[0, level], z_recv.at[0, level], here)
            _accumulate(work.at[i, 0], z_buf.at[0, level], T)

        @pl.when((level < z) & (z < depth - 1))
        def _():
            _expect(z_buf.at[1, level], z_recv.at[1, level], here)
            _accumulate(work.at[i, 0], z_buf.at[1, level], T)

        @pl.when(level > z)
        def _():
            _send(work.at[i, 0], z_buf.at[0, level], z_send.at[i], z_recv.at[0, level], (u, z + 1))

        @pl.when(level < z)
        def _():
            _send(work.at[i, 0], z_buf.at[1, level], z_send.at[i], z_recv.at[1, level], (u, z - 1))

    for i in range(4):
        core(i)
    for i in range(4):
        add_core(i)
        if i >= 1:
            add_first(i - 1)
        if i >= 2:
            add_then(i - 2)
            line(i - 2)
    add_first(3)
    add_then(2)
    line(2)
    add_then(3)

    @pl.when(z > 0)
    def _():
        _expect(z_buf.at[0, z], z_recv.at[0, z], here)
        _accumulate(work.at[3, 0], z_buf.at[0, z], T)

    @pl.when(z < depth - 1)
    def _():
        _expect(z_buf.at[1, z], z_recv.at[1, z], here)
        _accumulate(work.at[3, 0], z_buf.at[1, z], T)

    o_ref[...] = work[3, 0]
    for i in range(4):
        for k in range(4):
            _sent(c_buf.at[i, k], c_send.at[i, k], here)
        for h in range(2):
            for j in range(2):
                _sent(p_buf.at[i, h, j], p_send.at[i, h, j], here)
            _sent(q_buf.at[i, h], q_send.at[i, h], here)
        if i < 3:
            _sent(work.at[i, 0], z_send.at[i], here)


def scatter_all(x, collective_id):
    U, Z = lax.axis_size("uly"), lax.axis_size("blk")
    if (U, Z) != (8, 4):
        return lax.psum_scatter(x, ALL, scatter_dimension=0, tiled=True)
    N, D = x.shape
    T = N // (U * Z)
    half = T // 2
    dma = pltpu.SemaphoreType.DMA
    return pl.pallas_call(
        _scatter_all_kernel,
        out_shape=jax.ShapeDtypeStruct((T, D), x.dtype),
        in_specs=[pl.BlockSpec(memory_space=pl.ANY)],
        out_specs=pl.BlockSpec(memory_space=pltpu.VMEM),
        scratch_shapes=[
            pltpu.VMEM((4, 4, T, D), BF16),
            pltpu.VMEM((4, 4, T, D), BF16),
            pltpu.VMEM((4, 2, 2, half, D), BF16),
            pltpu.VMEM((4, 2, half, D), BF16),
            pltpu.VMEM((2, 4, T, D), BF16),
            dma((4, 4)),
            dma((4, 4)),
            dma((4, 4)),
            dma((4, 2, 2)),
            dma((4, 2, 2)),
            dma((4, 2)),
            dma((4, 2)),
            dma((4,)),
            dma((2, 4)),
        ],
        compiler_params=pltpu.CompilerParams(
            collective_id=collective_id, has_side_effects=True, vmem_limit_bytes=VMEM_BYTES
        ),
        cost_estimate=pl.CostEstimate(flops=N * D * 2, bytes_accessed=2 * N * D * 2, transcendentals=0),
    )(x.reshape(U * Z, T, D))


def _gather_small_kernel(*refs, count):
    xs, outs = refs[:count], refs[count : 2 * count]
    own_sem, z_send, z_recv, u_send, u_recv = refs[2 * count :]
    u, z = lax.axis_index("uly"), lax.axis_index("blk")
    here = (u, z)
    barrier = pltpu.get_barrier_semaphore()
    for k in range(1, 4):
        pl.semaphore_signal(barrier, inc=1, device_id=(u, z ^ k), device_id_type=MESH)
    for k in range(1, 8):
        pl.semaphore_signal(barrier, inc=1, device_id=(u ^ k, z), device_id_type=MESH)
    pl.semaphore_wait(barrier, 10)
    for a, (x, o) in enumerate(zip(xs, outs)):
        pltpu.make_async_copy(x, o.at[u, z], own_sem.at[a]).start()
        for k in range(1, 4):
            _send(x, o.at[u, z], z_send.at[a, k], z_recv.at[a, k], (u, z ^ k))
    for a, (x, o) in enumerate(zip(xs, outs)):
        pltpu.make_async_copy(x, o.at[u, z], own_sem.at[a]).wait()
        for k in range(1, 4):
            _expect(o.at[u, z ^ k], z_recv.at[a, k], here)
        for k in range(1, 8):
            _send(o.at[u], o.at[u], u_send.at[a, k], u_recv.at[a, k], (u ^ k, z))
    for a, (x, o) in enumerate(zip(xs, outs)):
        for k in range(1, 4):
            _sent(x, z_send.at[a, k], here)
        for k in range(1, 8):
            _sent(o.at[u], u_send.at[a, k], here)
            _expect(o.at[u ^ k], u_recv.at[a, k], here)


def gather_small(xs, collective_id):
    U, Z = lax.axis_size("uly"), lax.axis_size("blk")
    if (U, Z) != (8, 4):
        return [lax.all_gather(x, ALL).reshape((U, Z) + x.shape) for x in xs]
    dma = pltpu.SemaphoreType.DMA
    space = pl.BlockSpec(memory_space=pl.ANY)
    n = len(xs)
    return pl.pallas_call(
        functools.partial(_gather_small_kernel, count=n),
        out_shape=[jax.ShapeDtypeStruct((U, Z) + x.shape, x.dtype) for x in xs],
        in_specs=[space] * n,
        out_specs=[space] * n,
        scratch_shapes=[dma((n,)), dma((n, 4)), dma((n, 4)), dma((n, 8)), dma((n, 8))],
        compiler_params=pltpu.CompilerParams(collective_id=collective_id, has_side_effects=True),
    )(*xs)


def gather_uly(x):
    return lax.all_gather(x, "uly", axis=0, tiled=True)


def scatter_uly(x):
    return lax.psum_scatter(x, "uly", scatter_dimension=0, tiled=True)


def gather_blk(x):
    return lax.all_gather(x, "blk", axis=0, tiled=True)


def _row_limits(doc_ref, first, rows):
    position = first + lax.broadcasted_iota(jnp.int32, (rows, 1), 0)
    start = jnp.zeros_like(position)
    lowest = jnp.int32(0)
    for d in range(doc_ref.shape[0]):
        begin = doc_ref[d]
        start = jnp.where(begin <= position, jnp.maximum(start, begin), start)
        lowest = jnp.where(begin <= first, jnp.maximum(lowest, begin), lowest)
    return position, start, lowest


def _scores(query, key, position, start, key_first, scaling):
    raw = dot(query, key, LAST_DIM) * scaling
    key_position = key_first + lax.broadcasted_iota(jnp.int32, raw.shape, 1)
    return jnp.where((key_position <= position) & (key_position >= start), raw, NEG)


def _attend_kernel(index_ref, doc_ref, q_ref, k_ref, v_ref, o_ref, log_ref, *, chunk, scaling):
    rows = q_ref.shape[0]
    heads = q_ref.shape[1] // HEAD_DIM
    first = (pl.program_id(0) * index_ref[1] + index_ref[0]) * rows
    position, start, lowest = _row_limits(doc_ref, first, rows)

    def step(i, state):
        at = pl.multiple_of(i * chunk, chunk)
        new = []
        for h in range(heads):
            cols = pl.ds(h * HEAD_DIM, HEAD_DIM)
            top, total, out = state[h]
            scores = _scores(q_ref[:, cols], k_ref[pl.ds(at, chunk), cols], position, start, at, scaling)
            now = jnp.maximum(top, jnp.max(scores, axis=1, keepdims=True))
            weights = jnp.exp(scores - now)
            fade = jnp.exp(top - now)
            total = total * fade + jnp.sum(weights, axis=1, keepdims=True)
            out = out * fade + dot(weights.astype(BF16), v_ref[pl.ds(at, chunk), cols])
            new.append((now, total, out))
        return tuple(new)

    zero = (
        jnp.full((rows, 1), NEG, F32),
        jnp.zeros((rows, 1), F32),
        jnp.zeros((rows, HEAD_DIM), F32),
    )
    last = first + rows
    state = lax.fori_loop(lowest // chunk, (last + chunk - 1) // chunk, step, (zero,) * heads)
    for h in range(heads):
        cols = pl.ds(h * HEAD_DIM, HEAD_DIM)
        top, total, out = state[h]
        o_ref[:, cols] = out / total
        log_ref[:, cols] = jnp.broadcast_to(top + jnp.log(total), (rows, HEAD_DIM))


def _attend_back_kernel(
    index_ref, doc_ref, q_ref, g_ref, o_ref, log_ref, k_ref, v_ref, dq_ref, dk_ref, dv_ref, dk_sum, dv_sum, *, chunk, scaling
):
    rows = q_ref.shape[0]
    heads = q_ref.shape[1] // HEAD_DIM
    first = (pl.program_id(0) * index_ref[1] + index_ref[0]) * rows
    position, start, lowest = _row_limits(doc_ref, first, rows)

    @pl.when(pl.program_id(0) == 0)
    def _():
        dk_sum[...] = jnp.zeros_like(dk_sum)
        dv_sum[...] = jnp.zeros_like(dv_sum)

    deltas, logs = [], []
    for h in range(heads):
        cols = pl.ds(h * HEAD_DIM, HEAD_DIM)
        deltas.append(jnp.sum(g_ref[:, cols].astype(F32) * o_ref[:, cols], axis=1, keepdims=True))
        logs.append(log_ref[:, cols][:, :1])

    def step(i, state):
        at = pl.multiple_of(i * chunk, chunk)
        new = []
        for h in range(heads):
            cols = pl.ds(h * HEAD_DIM, HEAD_DIM)
            query, grad = q_ref[:, cols], g_ref[:, cols]
            key = k_ref[pl.ds(at, chunk), cols]
            scores = _scores(query, key, position, start, at, scaling)
            weights = jnp.exp(scores - logs[h])
            weight_grad = dot(grad, v_ref[pl.ds(at, chunk), cols], LAST_DIM)
            score_grad = (weights * (weight_grad - deltas[h])).astype(BF16)
            dv_sum[pl.ds(at, chunk), cols] += dot(weights.astype(BF16), grad, FIRST_DIM)
            dk_sum[pl.ds(at, chunk), cols] += dot(score_grad, query, FIRST_DIM)
            new.append(state[h] + dot(score_grad, key))
        return tuple(new)

    last = first + rows
    state = lax.fori_loop(
        lowest // chunk, (last + chunk - 1) // chunk, step, (jnp.zeros((rows, HEAD_DIM), F32),) * heads
    )
    for h in range(heads):
        dq_ref[:, pl.ds(h * HEAD_DIM, HEAD_DIM)] = (state[h] * scaling).astype(BF16)

    @pl.when(pl.program_id(0) == pl.num_programs(0) - 1)
    def _():
        dk_ref[...] = (dk_sum[...] * scaling).astype(BF16)
        dv_ref[...] = dv_sum[...].astype(BF16)


def _attention_specs(L, N, C, rows):
    block = pl.BlockSpec((rows, C), lambda i, *_: (i, 0))
    whole = pl.BlockSpec((N, C), lambda i, *_: (0, 0), pipeline_mode=pl.Buffered(1))
    return block, whole


def attention_forward(index, docs, query, key_all, value_all, rows, chunk):
    (L, C), N = query.shape, key_all.shape[0]
    block, whole = _attention_specs(L, N, C, rows)
    return pl.pallas_call(
        functools.partial(_attend_kernel, chunk=chunk, scaling=HEAD_DIM ** (-0.5)),
        out_shape=[jax.ShapeDtypeStruct((L, C), F32)] * 2,
        grid_spec=pltpu.PrefetchScalarGridSpec(
            num_scalar_prefetch=2, grid=(L // rows,), in_specs=[block, whole, whole], out_specs=[block, block]
        ),
        compiler_params=pltpu.CompilerParams(vmem_limit_bytes=VMEM_BYTES),
        cost_estimate=pl.CostEstimate(flops=4 * L * C * 1024, bytes_accessed=4 * N * C, transcendentals=L * 1024),
    )(index, docs, query, key_all, value_all)


def attention_backward(index, docs, query, grad, attended, logs, key_all, value_all, rows, chunk):
    (L, C), N = query.shape, key_all.shape[0]
    block, whole = _attention_specs(L, N, C, rows)
    return pl.pallas_call(
        functools.partial(_attend_back_kernel, chunk=chunk, scaling=HEAD_DIM ** (-0.5)),
        out_shape=[jax.ShapeDtypeStruct((L, C), BF16)] + [jax.ShapeDtypeStruct((N, C), BF16)] * 2,
        grid_spec=pltpu.PrefetchScalarGridSpec(
            num_scalar_prefetch=2,
            grid=(L // rows,),
            in_specs=[block, block, block, block, whole, whole],
            out_specs=[block, whole, whole],
            scratch_shapes=[pltpu.VMEM((N, C), F32)] * 2,
        ),
        compiler_params=pltpu.CompilerParams(vmem_limit_bytes=VMEM_BYTES),
        cost_estimate=pl.CostEstimate(flops=10 * L * C * 1024, bytes_accessed=8 * N * C, transcendentals=L * 1024),
    )(index, docs, query, grad, attended, logs, key_all, value_all)


def body(
    hidden_in,
    out_grad,
    attn_gain,
    query_weight,
    key_weight,
    value_weight,
    out_weight,
    query_gain,
    key_gain,
    ffn_gain,
    router_weight,
    expert_weights,
    routes,
    doc_starts,
):
    U = lax.axis_size("uly")
    Z = lax.axis_size("blk")
    u = lax.axis_index("uly")
    z = lax.axis_index("blk")
    T, D = hidden_in.shape
    EL = expert_weights.shape[0]
    C = D // U
    L = U * T
    N = U * Z * T
    RW = query_weight.shape[0]

    gain_rows = attn_gain.astype(F32)[:, None]
    own_weights = jnp.stack([query_weight, key_weight, value_weight], axis=1).astype(F32)
    scaled_rows = (own_weights * gain_rows[:, :, None]).astype(BF16).reshape(RW, 3, U, C)
    swapped = lax.all_to_all(scaled_rows, "uly", split_axis=2, concat_axis=0, tiled=True)
    swapped = swapped.reshape(U, RW, 3 * C)
    qkv_weight = lax.all_gather(swapped, "blk", axis=1, tiled=True).reshape(D, 3 * C)
    out_rows = gather_blk(out_weight)
    head_gains = gather_blk(jnp.stack([query_gain, key_gain], axis=1)).astype(F32)
    gain_query, gain_key = head_gains[:, 0], head_gains[:, 1]
    router_pack = jnp.pad(jnp.concatenate([router_weight, ffn_gain[:, None]], axis=1), ((0, 0), (0, 127 - EXPERTS)))
    packed, routes_all = gather_small([router_pack, routes.T], 3)
    packed = packed.reshape(D, 128)
    weight_router = packed[:, :EXPERTS]
    gain_ffn = packed[:, EXPERTS].astype(F32)
    upstream_all = lax.all_gather(out_grad, ALL, axis=0, tiled=True)
    routes_all = routes_all.transpose(0, 1, 3, 2).reshape(N, -1)

    hidden = hidden_in.astype(F32)
    first_scale = norm_scale(hidden)
    first_rows = gather_uly((hidden * first_scale).astype(BF16))
    qkv_pre = dot(first_rows, qkv_weight)
    query_pre, key_pre, value_pre = qkv_pre[:, :C], qkv_pre[:, C : 2 * C], qkv_pre[:, 2 * C :]
    squares = jnp.stack([jnp.sum(query_pre * query_pre, axis=1), jnp.sum(key_pre * key_pre, axis=1)])
    scales = lax.rsqrt(lax.psum(squares, "uly") / D + EPS)
    query_scale, key_scale = scales[0][:, None], scales[1][:, None]
    local = jnp.arange(L, dtype=jnp.int32)
    qpos = (local // T * Z + z) * T + local % T
    cosine, sine = rotary_tables(qpos)
    cosine, sine = cosine[:, None, :], sine[:, None, :]

    def rotated(pre, scale, gain):
        return rotate_forward((pre * scale * gain).reshape(L, C // HEAD_DIM, HEAD_DIM), cosine, sine).reshape(L, C).astype(BF16)

    query_rot = rotated(query_pre, query_scale, gain_query)
    key_rot = rotated(key_pre, key_scale, gain_key)
    key_values = lax.all_gather(jnp.stack([key_rot, value_pre.astype(BF16)]).reshape(2, U, T, C), "blk", axis=2, tiled=False)
    key_all, value_all = key_values[0].reshape(N, C), key_values[1].reshape(N, C)
    index = jnp.stack([z, jnp.int32(Z)]).astype(jnp.int32)
    chunk = min(512, N)
    attended, logs = attention_forward(index, doc_starts, query_rot, key_all, value_all, T, chunk)
    attended_low = attended.astype(BF16)
    residual = hidden + scatter_uly(dot(attended_low, out_rows).astype(BF16)).astype(F32)

    second_scale = norm_scale(residual)
    second_low = (residual * second_scale * gain_ffn).astype(BF16)
    probabilities = jax.nn.softmax(dot(second_low, weight_router), axis=-1)
    second_all = gather_all(second_low, 1)

    group = min(512, N)
    groups = N // group
    slots = -(-(group // T * CAP) // 8) * 8
    own_experts = u * EL + jnp.arange(EL, dtype=jnp.int32)
    chosen = jnp.any(routes_all[:, :, None] == own_experts[None, None, :], axis=1)
    logits_all = dot(second_all, weight_router)
    probs_all = jax.nn.softmax(logits_all, axis=-1)
    gate_all = jnp.where(chosen, lax.dynamic_slice_in_dim(probs_all, u * EL, EL, 1), 0.0)
    chosen_groups = chosen.reshape(groups, group, EL).astype(jnp.int32)
    slot = jnp.cumsum(chosen_groups, axis=1) - 1
    slot = jnp.where(chosen_groups > 0, slot, -1).transpose(0, 2, 1)
    pick = (slot[:, :, None, :] == jnp.arange(slots, dtype=jnp.int32)[None, None, :, None]).astype(BF16)
    second_groups = second_all.reshape(groups, group, D)
    upstream_groups = upstream_all.reshape(groups, group, D)
    rows = groups * slots

    def picked(x):
        r = jnp.einsum("gert,gtd->egrd", pick, x, preferred_element_type=F32)
        return r.astype(BF16).reshape(EL, rows, D)

    entry_rows = picked(second_groups)
    upstream_rows = picked(upstream_groups)
    gate_rows = jnp.einsum(
        "gert,gte->egr", pick.astype(F32), gate_all.reshape(groups, group, EL), precision=lax.Precision.HIGHEST
    ).reshape(EL, rows, 1)
    gate_pre = jnp.einsum("erd,edf->erf", entry_rows, expert_weights[:, 0], preferred_element_type=F32)
    up_value = jnp.einsum("erd,edf->erf", entry_rows, expert_weights[:, 1], preferred_element_type=F32)
    back = jnp.einsum("erd,edf->erf", upstream_rows, expert_weights[:, 2], preferred_element_type=F32)
    sigmoid_gate = jax.nn.sigmoid(gate_pre)
    inner = gate_pre * sigmoid_gate * up_value
    gate_grad_rows = jnp.sum(inner * back, axis=2)
    inner_grad = back * gate_rows
    gate_pre_grad = (inner_grad * up_value * sigmoid_gate * (1.0 + gate_pre * (1.0 - sigmoid_gate))).astype(BF16)
    up_grad = (inner_grad * gate_pre * sigmoid_gate).astype(BF16)
    inner_gated = (inner * gate_rows).astype(BF16)
    out_rows_e = jnp.einsum("erf,edf->erd", inner_gated, expert_weights[:, 2], preferred_element_type=F32)
    entry_grad_rows = jnp.einsum("erf,edf->erd", gate_pre_grad, expert_weights[:, 0], preferred_element_type=F32)
    entry_grad_rows += jnp.einsum("erf,edf->erd", up_grad, expert_weights[:, 1], preferred_element_type=F32)

    def spread(x):
        return jnp.einsum(
            "gert,egrd->gtd", pick, x.astype(BF16).reshape(EL, groups, slots, D), preferred_element_type=F32
        ).reshape(N, D)

    gate_grad_all = jnp.einsum(
        "gert,egr->gte", pick.astype(F32), gate_grad_rows.reshape(EL, groups, slots), precision=lax.Precision.HIGHEST
    ).reshape(N, EL)
    expert_iota = jnp.arange(EXPERTS, dtype=jnp.int32)
    place = (own_experts[:, None] == expert_iota[None, :]).astype(F32)
    gate_grad_wide = jnp.dot(gate_grad_all, place, precision=lax.Precision.HIGHEST)
    gate_grad_wide = jnp.pad(gate_grad_wide, ((0, 0), (0, 128 - EXPERTS)))
    entry_part = jnp.concatenate([spread(entry_grad_rows), gate_grad_wide], axis=1).astype(BF16)
    entry_sum = scatter_all(entry_part, 2).astype(F32)
    out_sum = scatter_all(spread(out_rows_e).astype(BF16), 5).astype(F32)
    output = (residual + out_sum).astype(BF16)
    expert_grads = jnp.stack(
        [
            jnp.einsum("erd,erf->edf", entry_rows, gate_pre_grad, preferred_element_type=F32),
            jnp.einsum("erd,erf->edf", entry_rows, up_grad, preferred_element_type=F32),
            jnp.einsum("erd,erf->edf", upstream_rows, inner_gated, preferred_element_type=F32),
        ],
        axis=1,
    )

    second_grad, prob_grad = entry_sum[:, :D], entry_sum[:, D : D + EXPERTS]
    logit_grad = (
        probabilities * (prob_grad - jnp.sum(probabilities * prob_grad, axis=1, keepdims=True))
    ).astype(BF16)
    logit_grad_all = gather_small([jnp.pad(logit_grad, ((0, 0), (0, 128 - EXPERTS)))], 4)[0].reshape(N, 128)[:, :EXPERTS]
    own_columns = lax.dynamic_slice_in_dim(second_all, (u * Z + z) * RW, RW, 1)
    router_grad = dot(own_columns, logit_grad_all, FIRST_DIM)
    second_grad = second_grad + dot(logit_grad, weight_router, LAST_DIM)
    upstream = out_grad.astype(F32)
    weighted = second_grad * gain_ffn
    inner_mean = jnp.mean(weighted * residual, axis=-1, keepdims=True)
    residual_grad = upstream + second_scale * weighted - residual * (second_scale**3) * inner_mean
    ffn_gain_part = jnp.sum(second_grad * residual * second_scale, axis=0)
    ffn_gain_grad = lax.psum_scatter(ffn_gain_part, ALL, scatter_dimension=0, tiled=True)

    residual_rows = gather_uly(residual_grad.astype(BF16))
    out_part = dot(attended_low, residual_rows, FIRST_DIM).astype(BF16)
    out_weight_grad = lax.psum_scatter(out_part, "blk", scatter_dimension=0, tiled=True).astype(F32)
    attended_grad = dot(residual_rows, out_rows, LAST_DIM).astype(BF16)
    dq, dk, dv = attention_backward(
        index, doc_starts, query_rot, attended_grad, attended, logs, key_all, value_all, T, chunk
    )
    kv_grads = lax.psum_scatter(
        jnp.stack([dk, dv]).reshape(2, U, Z, T, C), "blk", scatter_dimension=2, tiled=True
    ).reshape(2, L, C)

    def rotated_back(grad):
        return rotate_backward(grad.astype(F32).reshape(L, C // HEAD_DIM, HEAD_DIM), cosine, sine).reshape(L, C)

    query_up = rotated_back(dq.astype(BF16))
    key_up = rotated_back(kv_grads[0])
    inner_sums = lax.psum(
        jnp.stack([jnp.sum(query_up * gain_query * query_pre, axis=1), jnp.sum(key_up * gain_key * key_pre, axis=1)]),
        "uly",
    ) / D

    def pre_grad(up, gain, pre, scale, mean):
        return (scale * (up * gain) - pre * (scale**3) * mean[:, None]).astype(BF16)

    pre_grads = jnp.concatenate(
        [
            pre_grad(query_up, gain_query, query_pre, query_scale, inner_sums[0]),
            pre_grad(key_up, gain_key, key_pre, key_scale, inner_sums[1]),
            kv_grads[1],
        ],
        axis=1,
    )
    gain_parts = jnp.stack(
        [jnp.sum(query_up * query_pre * query_scale, axis=0), jnp.sum(key_up * key_pre * key_scale, axis=0)], axis=1
    )
    head_gain_grads = lax.psum_scatter(gain_parts, "blk", scatter_dimension=0, tiled=True)
    weight_part = dot(first_rows, pre_grads, FIRST_DIM).astype(BF16).reshape(U, Z * RW, 3 * C)
    weight_part = lax.psum_scatter(weight_part, "blk", scatter_dimension=1, tiled=True)
    weight_sum = lax.all_to_all(weight_part, "uly", split_axis=0, concat_axis=0, tiled=True)
    weight_sum = weight_sum.reshape(U, RW, 3, C).transpose(1, 2, 0, 3).reshape(RW, 3, D).astype(F32)
    attn_gain_grad = jnp.sum(own_weights * weight_sum, axis=(1, 2))
    weight_grads = weight_sum * gain_rows[:, :, None]
    first_part = dot(pre_grads, qkv_weight, LAST_DIM).astype(BF16)
    first_weighted = scatter_uly(first_part).astype(F32)
    first_mean = jnp.mean(first_weighted * hidden, axis=-1, keepdims=True)
    hidden_grad = residual_grad + first_scale * first_weighted - hidden * (first_scale**3) * first_mean
    return (
        output,
        hidden_grad,
        attn_gain_grad,
        weight_grads[:, 0],
        weight_grads[:, 1],
        weight_grads[:, 2],
        out_weight_grad,
        head_gain_grads[:, 0],
        head_gain_grads[:, 1],
        ffn_gain_grad,
        router_grad,
        expert_grads,
    )


def solution(mesh):
    rows = P(ALL, None)
    flat = P(ALL)
    experts = P("uly", None, None, "blk")
    return jax.shard_map(
        body,
        mesh=mesh,
        in_specs=(rows, rows, flat, rows, rows, rows, rows, flat, flat, flat, rows, experts, rows, P()),
        out_specs=(rows, rows, flat, rows, rows, rows, rows, flat, flat, flat, rows, experts),
        check_vma=False,
    )
```

time: 4230 us -> 1400 us (0.33)
  waiting for transfers between devices: 3030 us -> 395 us
  Pallas kernels: 0 us -> 368 us
  local copies, waits for them, and re-layouts: 315 us -> 108 us
  blocking collectives: 207 us -> 84.5 us
  matrix products: 394 us -> 294 us
  other arithmetic: 175 us -> 116 us
    reduce_scatter x22 -> x4, waiting for transfers between devices: 2120 us -> 25.4 us  [the longest x2 25.4 us: scatter_uly(): return lax.psum_scatter(x, 'uly', scatter_dimension=0, tiled=True)]
    all_gather x21 -> x6, waiting for transfers between devices: 823 us -> 217 us  [the longest x1 78.7 us: body(): lax.all_gather(jnp.stack([key_rot, value_pre.astype(BF16)]).reshape(2, U,...]
    pallas_call x0 -> x7, Pallas kernels: none -> 368 us  [the longest x2 186 us: scatter_all(): pl.pallas_call(_scatter_all_kernel, out_shape=jax.ShapeDtypeStruct((T, D)...]
    unnamed x43 -> x14, waiting for transfers between devices: 3.01 us -> 147 us
    dot_general x143 -> x26, matrix products: 394 us -> 294 us  [the longest x2 45.6 us: spread(): jnp.einsum('gert,egrd->gtd', pick, x.astype(BF16).reshape(EL, groups, slo...]
    all_to_all x6 -> x1, waiting for transfers between devices: 83.6 us -> 5.61 us  [body(): lax.all_to_all(weight_part, 'uly', split_axis=0, concat_axis=0, tiled=True)]
    all_gather x1, blocking collectives: 66.5 us -> 6.15 us  [gather_blk(): return lax.all_gather(x, 'blk', axis=0, tiled=True)]
    unnamed x2 -> x1, blocking collectives: 85.2 us -> 39.7 us
  transfers between devices with their start and end apart: 49 -> 13, of which waited for: 44 -> 8; matrix products, arithmetic and copies ran while one was open for 14% -> 22% of each run, Pallas kernels for 0% -> 18%
where the time goes in v1:
time: 1400 us; the launch traced here: 1390 us
  waiting for transfers between devices  395 us (28%)
  Pallas kernels  368 us (26%)
  matrix products  294 us (21%)
  other arithmetic  116 us (8%)
  local copies, waits for them, and re-layouts  108 us (8%)
  blocking collectives  84.5 us (6%)
  between operations  16.8 us (1%)
    pallas_call x2, Pallas kernels, scatter_all(): pl.pallas_call(_scatter_all_kernel, out_shape=jax.ShapeDtypeStruct((T, D)...  186 us
    unnamed x14, waiting for transfers between devices  147 us
    pallas_call x1, Pallas kernels, gather_all(): pl.pallas_call(_gather_all_kernel, out_shape=jax.ShapeDtypeStruct((U * Z,...  105 us
    all_gather x1, waiting for transfers between devices, body(): lax.all_gather(jnp.stack([key_rot, value_pre.astype(BF16)]).reshape(2, U,...  78.7 us
    all_gather x2, waiting for transfers between devices, gather_uly(): return lax.all_gather(x, 'uly', axis=0, tiled=True)  77.5 us
    all_gather x1, waiting for transfers between devices, body(): lax.all_gather(swapped, 'blk', axis=1, tiled=True).reshape(D, 3 * C)  50.5 us
    unnamed x161, local copies, waits for them, and re-layouts  46.4 us
    dot_general x2, matrix products, spread(): jnp.einsum('gert,egrd->gtd', pick, x.astype(BF16).reshape(EL, groups, slo...  45.6 us
  transfers between devices with their start and end apart: 13, of which 8 were waited for; matrix products, arithmetic and copies ran while one was open for 22% of the time, Pallas kernels for 18%

profile of v1, /device:TPU:13, one launch (start us, length us, event | category | flops | bytes accessed | tf_op | source)
XLA Modules:
  0.0 1387.5 jit_solution(5768031544733215664)
XLA Ops:
  12.4 14.5 %all_to_all.20 = bf16[64,3,8,256]{3,0,1,2:T(8,128)(2,1)S(1)} all-to-all(bf16[64,3,8,256]{3,0,1,2:T(8,128)(2,1)S(1)} %copy.137), channel_id=1, replica_groups=mesh['uly'=8,'blk'=4] {'uly'}, dimensions={2} | all-to-all | bytes 1572864 | tf_op jit(solution)/shard_map/all_to_all | solution.py:598
  31.6 6.2 all-gather
  37.8 1.9 multiply_cosine_fusion
  40.9 50.5 %all-gather.10.cloned.1.call-done = bf16[8,256,768]{2,1,0:T(8,128)(2,1)} async-done(((bf16[8,64,768]{2,1,0:T(8,128)(2,1)}), bf16[8,256,768]{2,1,0:T(8,128)(2,1)}) %all-gather.10.cloned.1.call-update) | async-done | bytes 3145744 | tf_op jit(solution)/shard_map/all_gather | solution.py:600
  91.4 40.5 %all-gather.8.cloned.1.call-done = bf16[1024,2048]{1,0:T(8,128)(2,1)} async-done(((bf16[128,2048]{1,0:T(8,128)(2,1)}), bf16[1024,2048]{1,0:T(8,128)(2,1)}) %all-gather.8.cloned.1.call-update) | async-done | bytes 4194320 | tf_op jit(solution)/shard_map/all_gather | solution.py:419
  131.8 6.2 fusion.91
  142.6 12.1 psum.14
  155.9 2.7 reshape.292
  159.8 2.7 reshape.291
  162.5 2.0 copy.170
  164.6 4.5 slice_negate_fusion.2
  169.1 2.4 maximum_multiply_fusion.1
  175.5 78.7 %all-gather.12.cloned.1.call-done = bf16[2,8,4,128,256]{4,3,2,1,0:T(8,128)(2,1)} async-done(((bf16[2,8,1,128,256]{4,3,2,1,0:T(8,128)(2,1)}), bf16[2,8,4,128,256]{4,3,2,1,0:T(8,128)(2,1)}) %all-gather.12.cloned.1.call-update) | async-done | bytes 4194320 | tf_op jit(solution)/shard_map/all_gather | solution.py:630
  254.2 4.7 fusion.81
  258.9 15.5 %shard_map.229 = (f32[1024,256]{1,0:T(8,128)}, f32[1024,256]{1,0:T(8,128)}) custom-call(s32[2]{0:T(128)} %pad_add_fusion.index_ref, s32[5]{0:T(128)} %doc_ref.3, bf16[1024,256]{1,0:T(8,128)(2,1)} %get-tuple-element.132.q_ref, bf16[4096,256]{1,0:T(8,128)(2,1)} %bitcast.244, bf16[4096,256]{1,0:T(8,128)(2,1)} %bitcast.242), custom_call_target="tpu_custom_call" | custom-call | flops 1073741824 | bytes 4194304 | tf_op jit(solution)/shard_map/pallas_call | solution.py:539
  274.5 10.0 all-gather.14.cloned.1.call-done
  284.5 4.8 convolution_convert_fusion.2
  290.8 17.9 %shard_map.230 = (bf16[8,4,64,128]{3,2,1,0:T(8,128)(2,1)}, s32[8,4,8,128]{3,2,1,0:T(8,128)}) custom-call(bf16[64,128]{1,0:T(8,128)(2,1)} %fusion.60.refs_0_, s32[8,128]{1,0:T(8,128)} %bitcast.309), custom_call_target="tpu_custom_call" | custom-call | tf_op jit(solution)/shard_map/pallas_call | solution.py:408
  311.5 9.0 reduce-window.6
  321.1 25.4 %reduce-scatter.11.cloned.1.call-done = bf16[128,2048]{1,0:T(8,128)(2,1)} async-done(((bf16[1024,2048]{1,0:T(8,128)(2,1)}), bf16[128,2048]{1,0:T(8,128)(2,1)}) %reduce-scatter.11.cloned.1.call-update) | async-done | bytes 524304 | tf_op jit(solution)/shard_map/reduce_scatter | solution.py:423
  348.3 2.0 multiply_convert_fusion.3.x_ref
  350.3 105.1 %shard_map.231 = bf16[32,128,2048]{2,1,0:T(8,128)(2,1)} custom-call(bf16[128,2048]{1,0:T(8,128)(2,1)} %multiply_convert_fusion.3.x_ref), custom_call_target="tpu_custom_call" | custom-call | bytes 33554432 | tf_op jit(solution)/shard_map/pallas_call | solution.py:197
  455.5 20.2 %convert_bitcast_fusion.1 = bf16[8,8,72,2048]{3,2,0,1:T(8,128)(2,1)} fusion(bf16[8,512,2048,1]{2,1,3,0:T(8,128)(2,1)} %bitcast.232, s32[8,8,512]{2,1,0:T(8,128)S(1)} %fusion.53), kind=kOutput, calls=%fused_computation.9 | convolution fusion | flops 9675472896 | bytes 35782656 | tf_op jit(solution)/shard_map/gert,gtd->egrd/dot_general | solution.py:660
  475.7 17.0 %copy.148 = bf16[8,8,72,2048]{3,2,1,0:T(8,128)(2,1)} copy(bf16[8,8,72,2048]{3,2,0,1:T(8,128)(2,1)} %convert_bitcast_fusion.1) | data formatting | bytes 37748736 | tf_op jit(solution)/shard_map/convert_element_type | solution.py:661
  492.7 11.0 fusion.89
  503.9 4.4 fusion.9
  509.5 13.0 fusion.16
  522.6 18.8 %convert_bitcast_fusion = bf16[8,8,72,2048]{3,2,0,1:T(8,128)(2,1)} fusion(bf16[8,512,2048,1]{2,1,3,0:T(8,128)(2,1)} %bitcast.313, s32[8,8,512]{2,1,0:T(8,128)S(1)} %fusion.53), kind=kOutput, calls=%fused_computation.8 | convolution fusion | flops 9675472896 | bytes 35782656 | tf_op jit(solution)/shard_map/gert,gtd->egrd/dot_general | solution.py:660
  541.4 16.9 %copy.153 = bf16[8,8,72,2048]{3,2,1,0:T(8,128)(2,1)} copy(bf16[8,8,72,2048]{3,2,0,1:T(8,128)(2,1)} %convert_bitcast_fusion) | data formatting | bytes 37748736 | tf_op jit(solution)/shard_map/convert_element_type | solution.py:661
  558.3 12.8 fusion.18
  571.1 18.5 %multiply_convert_fusion.1 = (bf16[8,576,256]{2,1,0:T(8,128)(2,1)}, f32[8,576]{1,0:T(8,128)S(1)}, bf16[8,576,256]{2,1,0:T(8,128)(2,1)S(1)}, f32[8,576,256]{2,1,0:T(8,128)}) fusion(f32[8,576,256]{2,1,0:T(8,128)} %fusion.16, f32[8,576,256]{2,1,0:T(8,128)} %fusion.18, f32[8,576]{1,0:T(8,128)S(1)} %mul.455, bf16[8,576,2048]{2,1,0:T(8,128)(2,1)} %bitcast.229, ...), kind=kOutput, calls=%fused_computation.37 | convolution fusion | flops 4853067264 | bytes 46174208 | tf_op jit(solution)/shard_map/erd,edf->erf/dot_general | solution.py:668
  589.7 3.1 fusion.8
  595.8 18.6 %fusion.11 = f32[8,576,2048]{2,1,0:T(8,128)} fusion(bf16[8,576,256]{2,1,0:T(8,128)(2,1)} %get-tuple-element.110, bf16[8,3,2048,256]{3,2,1,0:T(8,128)(2,1)} %param.25), kind=kOutput, calls=%fused_computation.16 | convolution fusion | flops 4831838208 | bytes 48496640 | tf_op jit(solution)/shard_map/erf,edf->erd/dot_general | solution.py:679
  614.4 21.4 %add_convert_fusion = bf16[8,576,2048]{2,1,0:T(8,128)(2,1)} fusion(f32[8,576,2048]{2,1,0:T(8,128)} %fusion.11, bf16[8,576,256]{2,1,0:T(8,128)(2,1)S(1)} %get-tuple-element.112, bf16[8,3,2048,256]{3,2,1,0:T(8,128)(2,1)} %param.25), kind=kOutput, calls=%fused_computation.1 | convolution fusion | flops 4850712576 | bytes 67371008 | tf_op jit(solution)/shard_map/erf,edf->erd/dot_general | solution.py:680
  635.9 22.7 %bitcast_convert_fusion = bf16[8,512,2048]{2,1,0:T(8,128)(2,1)} fusion(bf16[8,8,72,2048]{3,2,1,0:T(8,128)(2,1)} %bitcast.235, s32[8,8,512]{2,1,0:T(8,128)S(1)} %fusion.53), kind=kOutput, calls=%fused_computation.2 | convolution fusion | flops 9674424320 | bytes 35782656 | tf_op jit(solution)/shard_map/gert,egrd->gtd/dot_general | solution.py:683
  658.8 14.2 %pad_maximum_fusion.1.x_ref = bf16[32,128,2176]{2,1,0:T(8,128)(2,1)} fusion(bf16[32,128,128]{2,1,0:T(8,128)(2,1)S(1)} %bitcast.250, bf16[32,128,2048]{2,1,0:T(8,128)(2,1)} %bitcast.238), kind=kLoop, calls=%fused_computation.10 | loop fusion | flops 35651584 | bytes 35651584 | tf_op jit(solution)/shard_map/concatenate | solution.py:694
  673.1 100.0 %shard_map.233 = bf16[128,2176]{1,0:T(8,128)(2,1)} custom-call(bf16[32,128,2176]{2,1,0:T(8,128)(2,1)} %pad_maximum_fusion.1.x_ref), custom_call_target="tpu_custom_call" | custom-call | flops 17825792 | bytes 35651584 | tf_op jit(solution)/shard_map/pallas_call | solution.py:344
  777.7 37.0 %all-gather.18.cloned.1.call-done = bf16[1024,2048]{1,0:T(8,128)(2,1)} async-done(((bf16[128,2048]{1,0:T(8,128)(2,1)}), bf16[1024,2048]{1,0:T(8,128)(2,1)}) %all-gather.18.cloned.1.call-update) | async-done | bytes 4194320 | tf_op jit(solution)/shard_map/all_gather | solution.py:419
  814.7 4.3 convolution_convert_fusion.6.g_ref
  819.0 20.8 %shard_map.234 = (bf16[1024,256]{1,0:T(8,128)(2,1)}, bf16[4096,256]{1,0:T(8,128)(2,1)}, bf16[4096,256]{1,0:T(8,128)(2,1)}) custom-call(s32[2]{0:T(128)} %pad_add_fusion.index_ref, s32[5]{0:T(128)} %doc_ref.3, bf16[1024,256]{1,0:T(8,128)(2,1)} %get-tuple-element.132.q_ref, bf16[1024,256]{1,0:T(8,128)(2,1)} %convolution_convert_fusion.6.g_ref, ...), custom_call_target="tpu_custom_call" | custom-call | flops 2684354560 | bytes 8388608 | tf_op jit(solution)/shard_map/pallas_call | solution.py:553
  839.7 2.6 pad_maximum_fusion.2
  842.4 2.3 copy.171
  845.9 4.5 convolution_convert_fusion.5
  850.8 146.0 %all-reduce.7.cloned.1.call-done = bf16[2,8,4,128,256]{4,3,1,2,0:T(8,128)(2,1)} async-done(((bf16[2,8,4,128,256]{4,3,1,2,0:T(8,128)(2,1)}), bf16[2,8,4,128,256]{4,3,1,2,0:T(8,128)(2,1)}) %all-reduce.7.cloned.1.call-update) | async-done | bytes 4194320
  996.8 2.8 dynamic-slice_convert_fusion
  1001.1 2.1 broadcast_multiply_fusion.2
  1011.4 12.0 psum.15
  1027.9 5.1 convolution_convert_fusion.3
  1034.2 22.7 %shard_map.235 = bf16[8,4,128,128]{3,2,1,0:T(8,128)(2,1)} custom-call(bf16[128,128]{1,0:T(8,128)(2,1)} %pad.15.refs_0_), custom_call_target="tpu_custom_call" | custom-call | tf_op jit(solution)/shard_map/pallas_call | solution.py:408
  1056.9 16.7 %convolution_bitcast_fusion.1 = f32[8,1,2048,256]{3,2,0,1:T(8,128)} fusion(bf16[8,576,2048]{2,1,0:T(8,128)(2,1)} %bitcast.230, bf16[8,576,256]{2,1,0:T(8,128)(2,1)S(1)} %copy-done.10), kind=kOutput, calls=%fused_computation.33 | convolution fusion | flops 4831838208 | bytes 38010880 | tf_op jit(solution)/shard_map/erd,erf->edf/dot_general | solution.py:701
  1073.6 15.3 %convolution_bitcast_fusion.2 = f32[8,1,2048,256]{3,2,0,1:T(8,128)} fusion(bf16[8,576,2048]{2,1,0:T(8,128)(2,1)} %bitcast.231, bf16[8,576,256]{2,1,0:T(8,128)(2,1)} %get-tuple-element.110), kind=kOutput, calls=%fused_computation.34 | convolution fusion | flops 4831838208 | bytes 38010880 | tf_op jit(solution)/shard_map/erd,erf->edf/dot_general | solution.py:700
  1088.9 22.0 %convolution_bitcast_fusion = f32[8,1,2048,256]{3,2,0,1:T(8,128)} fusion(bf16[8,576,2048]{2,1,0:T(8,128)(2,1)} %bitcast.237, f32[8,576]{1,0:T(8,128)S(1)} %copy-done.51, f32[8,576,256]{2,1,0:T(8,128)} %fusion.16, f32[8,576,256]{2,1,0:T(8,128)} %get-tuple-element.157), kind=kOutput, calls=%fused_computation.32 | convolution fusion | flops 4840095744 | bytes 45107200 | tf_op jit(solution)/shard_map/erd,erf->edf/dot_general | solution.py:702
  1110.9 5.0 convolution_convert_fusion.4
  1115.9 35.1 %pad_maximum_fusion = f32[8,3,2048,256]{3,2,0,1:T(8,128)} fusion(f32[8,1,2048,256]{3,2,0,1:T(8,128)} %convolution_bitcast_fusion, f32[8,1,2048,256]{3,2,0,1:T(8,128)} %convolution_bitcast_fusion.1, f32[8,1,2048,256]{3,2,0,1:T(8,128)} %convolution_bitcast_fusion.2), kind=kLoop, calls=%fused_computation | loop fusion | flops 25165824 | bytes 100663296 | tf_op jit(solution)/shard_map/stack | solution.py:698
  1151.1 33.7 %copy.160 = f32[8,3,2048,256]{3,2,1,0:T(8,128)} copy(f32[8,3,2048,256]{3,2,0,1:T(8,128)} %pad_maximum_fusion) | data formatting | bytes 100663296
  1184.7 39.7 %all-reduce.4 = f32[2048]{0:T(1024)S(1)} all-reduce(f32[2048]{0:T(1024)S(1)} %get-tuple-element.98), channel_id=8, replica_groups=mesh['uly'=8,'blk'=4] {'uly','blk'}, use_global_device_ids=true, to_apply=%region_29.30.clone | all-reduce | flops 2048 | bytes 16384
  1225.0 17.3 %convolution_convert_fusion = bf16[8,576,2048]{2,1,0:T(8,128)(2,1)} fusion(bf16[8,3,2048,256]{3,2,1,0:T(8,128)(2,1)} %param.25, f32[8,576]{1,0:T(8,128)S(1)} %copy-done.51, f32[8,576,256]{2,1,0:T(8,128)} %fusion.16, f32[8,576,256]{2,1,0:T(8,128)} %get-tuple-element.157), kind=kOutput, calls=%fused_computation.11 | convolution fusion | flops 4849532928 | bytes 36718592 | tf_op jit(solution)/shard_map/erf,edf->erd/dot_general | solution.py:678
  1242.3 22.9 %bitcast_convert_fusion.1 = bf16[8,512,2048]{2,1,0:T(8,128)(2,1)} fusion(bf16[8,8,72,2048]{3,2,1,0:T(8,128)(2,1)} %bitcast.318, s32[8,8,512]{2,1,0:T(8,128)S(1)} %copy-done.45), kind=kOutput, calls=%fused_computation.3 | convolution fusion | flops 9674424320 | bytes 35782656 | tf_op jit(solution)/shard_map/gert,egrd->gtd/dot_general | solution.py:683
  1265.2 86.3 %shard_map.232 = bf16[128,2048]{1,0:T(8,128)(2,1)} custom-call(bf16[32,128,2048]{2,1,0:T(8,128)(2,1)} %bitcast.239), custom_call_target="tpu_custom_call" | custom-call | flops 16777216 | bytes 33554432 | tf_op jit(solution)/shard_map/pallas_call | solution.py:344
  1351.6 2.7 fusion.42
  1359.5 4.4 all-to-all-start.1
  1363.9 3.1 fusion.35
  1367.1 5.6 all-to-all-done.1
  1373.5 3.7 fusion.33
  (271 shorter events, 62.8 us)
Async XLA Ops:
  8.0 83.4 %all-gather.10.cloned.1.call-start = ((), (), s32[]{:S(2)}) async-start(), calls=%async_computation.8 | async-start | bytes 3932160 | tf_op jit(solution)/shard_map/all_gather | solution.py:600
  8.7 18.1 %copy-start.59 = (f32[64]{0:T(128)}, f32[64]{0:T(128)S(1)}, u32[]{:S(2)}) copy-start(f32[64]{0:T(128)S(1)} %convert_element_type.194) | copy-start | bytes 772
  9.7 17.1 %copy-start.23 = (bf16[8,8,8,256]{3,2,1,0:T(8,128)(2,1)}, bf16[8,8,8,256]{3,2,1,0:T(8,128)(2,1)S(1)}, u32[]{:S(2)}) copy-start(bf16[8,8,8,256]{3,2,1,0:T(8,128)(2,1)S(1)} %copy.187) | copy-start | bytes 786436
  10.8 16.0 %copy-start.24 = (bf16[8,8,8,256]{3,2,1,0:T(8,128)(2,1)}, bf16[8,8,8,256]{3,2,1,0:T(8,128)(2,1)S(1)}, u32[]{:S(2)}) copy-start(bf16[8,8,8,256]{3,2,1,0:T(8,128)(2,1)S(1)} %copy.186) | copy-start | bytes 786436
  11.9 14.9 %copy-start.25 = (bf16[8,8,8,256]{3,2,1,0:T(8,128)(2,1)}, bf16[8,8,8,256]{3,2,1,0:T(8,128)(2,1)S(1)}, u32[]{:S(2)}) copy-start(bf16[8,8,8,256]{3,2,1,0:T(8,128)(2,1)S(1)} %copy.185) | copy-start | bytes 786436
  12.0 17.3 %copy-start.4 = (bf16[128,2048]{1,0:T(8,128)(2,1)S(1)}, bf16[128,2048]{1,0:T(8,128)(2,1)}, u32[]{:S(2)}) copy-start(bf16[128,2048]{1,0:T(8,128)(2,1)} %param.14) | copy-start | bytes 1572868
  12.2 19.4 %copy-start.71 = (bf16[64]{0:T(256)(128)(2,1)S(1)}, bf16[64]{0:T(256)(128)(2,1)}, u32[]{:S(2)}) copy-start(bf16[64]{0:T(256)(128)(2,1)} %param.22) | copy-start | bytes 388
  12.2 19.4 %copy-start.72 = (bf16[64]{0:T(256)(128)(2,1)S(1)}, bf16[64]{0:T(256)(128)(2,1)}, u32[]{:S(2)}) copy-start(bf16[64]{0:T(256)(128)(2,1)} %param.21) | copy-start | bytes 388
  29.2 102.6 %all-gather.8.cloned.1.call-start = ((), (), s32[]{:S(2)}) async-start(), calls=%async_computation.7 | async-start | bytes 4718592 | tf_op jit(solution)/shard_map/all_gather | solution.py:419
  31.5 222.8 %all-gather.12.cloned.1.call-start = ((), (), s32[]{:S(2)}) async-start(), calls=%async_computation.9 | async-start | bytes 5242880 | tf_op jit(solution)/shard_map/all_gather | solution.py:630
  40.9 128.2 %copy-start.20 = (f32[1024,128]{1,0:T(8,128)}, f32[1024,128]{1,0:T(8,128)S(1)}, u32[]{:S(2)}) copy-start(f32[1024,128]{1,0:T(8,128)S(1)} %get-tuple-element.162) | copy-start | bytes 1572868
  40.9 131.0 %copy-start.46 = (f32[256,1]{0,1:T(1,128)}, f32[256,1]{0,1:T(1,128)S(1)}, u32[]{:S(2)}) copy-start(f32[256,1]{0,1:T(1,128)S(1)} %get-tuple-element.150) | copy-start | bytes 3076
  40.9 131.0 %copy-start.48 = (f32[256,1]{0,1:T(1,128)}, f32[256,1]{0,1:T(1,128)S(1)}, u32[]{:S(2)}) copy-start(f32[256,1]{0,1:T(1,128)S(1)} %get-tuple-element.149) | copy-start | bytes 3076
  140.4 31.5 %copy-start.2 = (f32[1024,256]{1,0:T(8,128)}, f32[1024,256]{1,0:T(8,128)S(1)}, u32[]{:S(2)}) copy-start(f32[1024,256]{1,0:T(8,128)S(1)} %copy.177) | copy-start | bytes 3145732
  142.3 29.6 %copy-start = (f32[1024,256]{1,0:T(8,128)}, f32[1024,256]{1,0:T(8,128)S(1)}, u32[]{:S(2)}) copy-start(f32[1024,256]{1,0:T(8,128)S(1)} %copy.176) | copy-start | bytes 3145732
  154.7 17.2 %copy-start.40 = (f32[1,1024]{1,0:T(1,128)}, f32[1,1024]{1,0:T(1,128)S(1)}, u32[]{:S(2)}) copy-start(f32[1,1024]{1,0:T(1,128)S(1)} %get-tuple-element.146) | copy-start | bytes 12292
  154.7 17.2 %copy-start.42 = (f32[1,1024]{1,0:T(1,128)}, f32[1,1024]{1,0:T(1,128)S(1)}, u32[]{:S(2)}) copy-start(f32[1,1024]{1,0:T(1,128)S(1)} %get-tuple-element.145) | copy-start | bytes 12292
  174.3 110.2 %all-gather.14.cloned.1.call-start = ((), (), s32[]{:S(2)}) async-start(), calls=%async_computation.10 | async-start | bytes 1310720 | tf_op jit(solution)/shard_map/all_gather | solution.py:427
  174.9 171.6 %reduce-scatter.11.cloned.1.call-start = ((), (), s32[]{:S(2)}) async-start(), calls=%async_computation.11 | async-start | bytes 4718592 | tf_op jit(solution)/shard_map/reduce_scatter | solution.py:423
  289.3 233.2 %all-gather.16.cloned.1.call-start = ((), (), s32[]{:S(2)}) async-start(), calls=%async_computation.12 | async-start | bytes 17301504 | tf_op jit(solution)/shard_map/all_gather | solution.py:609
  289.9 524.8 %all-gather.18.cloned.1.call-start = ((), (), s32[]{:S(2)}) async-start(), calls=%async_computation.13 | async-start | bytes 4718592 | tf_op jit(solution)/shard_map/all_gather | solution.py:419
  310.3 145.1 %copy-start.37 = (f32[2048,1]{0,1:T(1,128)}, f32[2048,1]{0,1:T(1,128)S(1)}, u32[]{:S(2)}) copy-start(f32[2048,1]{0,1:T(1,128)S(1)} %copy.193) | copy-start | bytes 24580
  321.1 314.8 %copy-start.44 = (s32[8,8,512]{2,1,0:T(8,128)}, s32[8,8,512]{2,1,0:T(8,128)S(1)}, u32[]{:S(2)}) copy-start(s32[8,8,512]{2,1,0:T(8,128)S(1)} %fusion.53) | copy-start | bytes 393220
  348.3 107.1 %copy-start.55 = (f32[128]{0:T(128)}, f32[128]{0:T(128)S(1)}, u32[]{:S(2)}) copy-start(f32[128]{0:T(128)S(1)} %get-tuple-element.154) | copy-start | bytes 1540
  475.7 17.0 %copy-start.15 = (bf16[8,4,64,128]{3,2,1,0:T(8,128)(2,1)S(1)}, bf16[8,4,64,128]{3,2,1,0:T(8,128)(2,1)}, u32[]{:S(2)}) copy-start(bf16[8,4,64,128]{3,2,1,0:T(8,128)(2,1)} %get-tuple-element.21) | copy-start | bytes 1572868
  508.3 62.8 %copy-start.50 = (f32[8,576]{1,0:T(8,128)}, f32[8,576]{1,0:T(8,128)S(1)}, u32[]{:S(2)}) copy-start(f32[8,576]{1,0:T(8,128)S(1)} %mul.455) | copy-start | bytes 55300
  508.7 13.9 copy-start.53
  508.8 13.8 copy-start.32
  589.6 24.8 %copy-start.9 = (bf16[8,576,256]{2,1,0:T(8,128)(2,1)}, bf16[8,576,256]{2,1,0:T(8,128)(2,1)S(1)}, u32[]{:S(2)}) copy-start(bf16[8,576,256]{2,1,0:T(8,128)(2,1)S(1)} %get-tuple-element.112) | copy-start | bytes 7077892
  673.1 101.4 %copy-start.33 = (f32[128,64]{1,0:T(8,128)S(1)}, f32[128,64]{1,0:T(8,128)}, u32[]{:S(2)}) copy-start(f32[128,64]{1,0:T(8,128)} %copy-done.32) | copy-start | bytes 98308
  673.1 101.4 %copy-start.54 = (f32[128]{0:T(128)S(1)}, f32[128]{0:T(128)}, u32[]{:S(2)}) copy-start(f32[128]{0:T(128)} %copy-done.53) | copy-start | bytes 1540
  673.1 101.4 %copy-start.58 = (f32[128]{0:T(128)S(1)}, f32[128]{0:T(128)}, u32[]{:S(2)}) copy-start(f32[128]{0:T(128)} %fusion.56) | copy-start | bytes 1540
  673.1 101.7 %copy-start.5 = (bf16[128,2048]{1,0:T(8,128)(2,1)S(1)}, bf16[128,2048]{1,0:T(8,128)(2,1)}, u32[]{:S(2)}) copy-start(bf16[128,2048]{1,0:T(8,128)(2,1)} %param.14) | copy-start | bytes 1572868
  673.1 101.7 %copy-start.7 = (bf16[128,2048]{1,0:T(8,128)(2,1)S(1)}, bf16[128,2048]{1,0:T(8,128)(2,1)}, u32[]{:S(2)}) copy-start(bf16[128,2048]{1,0:T(8,128)(2,1)} %reduce-scatter.11.cloned.1.call-done) | copy-start | bytes 1572868
  673.1 101.7 %copy-start.16 = (bf16[8,4,64,128]{3,2,1,0:T(8,128)(2,1)S(1)}, bf16[8,4,64,128]{3,2,1,0:T(8,128)(2,1)}, u32[]{:S(2)}) copy-start(bf16[8,4,64,128]{3,2,1,0:T(8,128)(2,1)} %get-tuple-element.21) | copy-start | bytes 1572868
  673.1 101.7 %copy-start.38 = (f32[2048,1]{0,1:T(1,128)S(1)}, f32[2048,1]{0,1:T(1,128)}, u32[]{:S(2)}) copy-start(f32[2048,1]{0,1:T(1,128)} %copy-done.37) | copy-start | bytes 24580
  673.1 101.7 %copy-start.56 = (f32[128]{0:T(128)S(1)}, f32[128]{0:T(128)}, u32[]{:S(2)}) copy-start(f32[128]{0:T(128)} %copy-done.55) | copy-start | bytes 1540
  773.2 41.5 %copy-start.31 = (bf16[256,2048]{1,0:T(8,128)(2,1)S(1)}, bf16[256,2048]{1,0:T(8,128)(2,1)}, u32[]{:S(2)}) copy-start(bf16[256,2048]{1,0:T(8,128)(2,1)} %all-gather.14.cloned.1.call-done) | copy-start | bytes 3145732
  775.4 43.6 %copy-start.65 = (f32[128]{0:T(128)}, f32[128]{0:T(128)S(1)}, u32[]{:S(2)}) copy-start(f32[128]{0:T(128)S(1)} %broadcast_multiply_fusion.5) | copy-start | bytes 1540
  777.7 219.1 %all-reduce.7.cloned.1.call-start = ((), (), s32[]{:S(2)}) async-start(), calls=%async_computation.18 | async-start | bytes 8388608
  844.7 509.6 %reduce-scatter.17.cloned.1.call-start = ((), (), s32[]{:S(2)}) async-start(), calls=%async_computation.16 | async-start | bytes 1310720 | tf_op jit(solution)/shard_map/reduce_scatter | solution.py:724
  845.9 155.1 %copy-start.21 = (f32[1024,128]{1,0:T(8,128)S(1)}, f32[1024,128]{1,0:T(8,128)}, u32[]{:S(2)}) copy-start(f32[1024,128]{1,0:T(8,128)} %copy-done.20) | copy-start | bytes 1572868
  850.5 505.6 %reduce-scatter.19.cloned.1.call-start = ((), (), s32[]{:S(2)}) async-start(), calls=%async_computation.17 | async-start | bytes 163840
  1010.6 17.4 %copy-start.34 = (bf16[1,8,1,128,256]{4,3,1,2,0:T(8,128)(2,1)S(1)}, bf16[1,8,1,128,256]{4,3,1,2,0:T(8,128)(2,1)}, u32[]{:S(2)}) copy-start(bf16[1,8,1,128,256]{4,3,1,2,0:T(8,128)(2,1)} %get-tuple-element.114) | copy-start | bytes 1572868
  1023.5 334.7 %reduce-scatter.13.cloned.1.call-start = ((), (), s32[]{:S(2)}) async-start(), calls=%async_computation.14 | async-start | bytes 4718592 | tf_op jit(solution)/shard_map/reduce_scatter | solution.py:423
  1033.0 23.9 %copy-start.10 = (bf16[8,576,256]{2,1,0:T(8,128)(2,1)S(1)}, bf16[8,576,256]{2,1,0:T(8,128)(2,1)}, u32[]{:S(2)}) copy-start(bf16[8,576,256]{2,1,0:T(8,128)(2,1)} %copy-done.9) | copy-start | bytes 7077892
  1033.0 326.4 %reduce-scatter.15.cloned.1.call-start = ((), (), s32[]{:S(2)}) async-start(), calls=%async_computation.15 | async-start | bytes 3932160 | tf_op jit(solution)/shard_map/reduce_scatter | solution.py:759
  1073.6 15.3 %copy-start.51 = (f32[8,576]{1,0:T(8,128)S(1)}, f32[8,576]{1,0:T(8,128)}, u32[]{:S(2)}) copy-start(f32[8,576]{1,0:T(8,128)} %copy-done.50) | copy-start | bytes 55300
  1088.9 22.0 %copy-start.36 = (bf16[1024,256]{1,0:T(8,128)(2,1)S(1)}, bf16[1024,256]{1,0:T(8,128)(2,1)}, u32[]{:S(2)}) copy-start(bf16[1024,256]{1,0:T(8,128)(2,1)} %copy-done.35) | copy-start | bytes 1572868
  1088.9 22.0 %copy-start.69 = (bf16[1024,2048]{1,0:T(8,128)(2,1)S(1)}, bf16[1024,2048]{1,0:T(8,128)(2,1)}, u32[]{:S(2)}) copy-start(bf16[1024,2048]{1,0:T(8,128)(2,1)} %all-gather.8.cloned.1.call-done) | copy-start | bytes 12582916
  1225.0 17.3 %copy-start.45 = (s32[8,8,512]{2,1,0:T(8,128)S(1)}, s32[8,8,512]{2,1,0:T(8,128)}, u32[]{:S(2)}) copy-start(s32[8,8,512]{2,1,0:T(8,128)} %copy-done.44) | copy-start | bytes 393220
  1265.2 86.4 %copy-start.22 = (bf16[8,4,128,128]{3,2,1,0:T(8,128)(2,1)S(1)}, bf16[8,4,128,128]{3,2,1,0:T(8,128)(2,1)}, u32[]{:S(2)}) copy-start(bf16[8,4,128,128]{3,2,1,0:T(8,128)(2,1)} %shard_map.235) | copy-start | bytes 3145732
  1265.2 93.0 %copy-start.6 = (bf16[128,2048]{1,0:T(8,128)(2,1)S(1)}, bf16[128,2048]{1,0:T(8,128)(2,1)}, u32[]{:S(2)}) copy-start(bf16[128,2048]{1,0:T(8,128)(2,1)} %param.14) | copy-start | bytes 1572868
  1351.5 12.3 copy-start.8
  1351.5 12.3 copy-start.12
  1351.5 12.3 copy-start.19
  1351.5 12.3 copy-start.39
  1351.5 12.3 copy-start.57
  1351.6 12.3 copy-start.62
  1351.6 12.3 copy-start.64
  1351.6 12.3 copy-start.66
  1351.6 12.3 copy-start.68
  1359.5 13.2 all-to-all-start.1
  1367.1 11.7 copy-start.60
  (23 other events, 70.4 us)
Sparse Core Ops, SparseCore 0:
  29.4 61.9 all-gather.9
  93.8 37.9 all-gather.7
  174.4 79.7 all-gather.11
  255.7 28.7 all-gather.13
  289.4 56.9 reduce-scatter.10
  777.8 36.8 all-gather.17
  844.8 151.9 all-reduce.6
  999.1 26.0 reduce-scatter.16
  1028.1 15.4 reduce-scatter.18
  1046.8 54.2 reduce-scatter.12
  1116.1 60.5 reduce-scatter.14
Sparse Core Ops, SparseCore 1:
  293.2 126.5 all-gather.15

commit v2 on v1

v2 whole, which is shorter than its diff:
```python
import functools

import jax
import jax.numpy as jnp
from jax import lax
from jax.experimental import pallas as pl
from jax.experimental.pallas import tpu as pltpu
from jax.sharding import PartitionSpec as P

HEADS = 16
HEAD_DIM = 128
EXPERTS = 64
CAP = 17

EPS = 1e-05
THETA = 10000.0
NEG = -1e30
FIRST_DIM = (((0,), (0,)), ((), ()))
LAST_DIM = (((1,), (1,)), ((), ()))
ALL = ("uly", "blk")
F32 = jnp.float32
BF16 = jnp.bfloat16
VMEM_BYTES = 56 * 1024 * 1024


def dot(a, b, dims=(((1,), (0,)), ((), ()))):
    return lax.dot_general(a, b, dims, preferred_element_type=F32)


def rotary_tables(position):
    halfway = HEAD_DIM // 2
    frequency = THETA ** (-(jnp.arange(halfway).astype(F32) * 2.0 / HEAD_DIM))
    angles = position.astype(F32)[:, None] * frequency[None, :]
    cosine = jnp.concatenate([jnp.cos(angles), jnp.cos(angles)], axis=1)
    sine = jnp.concatenate([jnp.sin(angles), jnp.sin(angles)], axis=1)
    return cosine, sine


def rotate_forward(values, cosine, sine):
    halfway = values.shape[-1] // 2
    turned = jnp.concatenate([-values[..., halfway:], values[..., :halfway]], axis=-1)
    return values * cosine + turned * sine


def rotate_backward(upstream, cosine, sine):
    halfway = upstream.shape[-1] // 2
    moved = upstream * sine
    turned = jnp.concatenate([moved[..., halfway:], -moved[..., :halfway]], axis=-1)
    return upstream * cosine + turned


def norm_scale(values):
    return lax.rsqrt(jnp.mean(values * values, axis=-1, keepdims=True) + EPS)


MESH = pl.DeviceIdType.MESH
DMA = pltpu.SemaphoreType.DMA
ANY_SPACE = pl.BlockSpec(memory_space=pl.ANY)
IN_VMEM = pl.BlockSpec(memory_space=pltpu.VMEM)
DEPTH = 4
CHIPS = (0, 2, 4, 6)
FIRST, THEN = (2, 4), (4, 2)


def _send(src, dst, send_sem, recv_sem, to):
    pltpu.make_async_remote_copy(
        src_ref=src, dst_ref=dst, send_sem=send_sem, recv_sem=recv_sem, device_id=to, device_id_type=MESH
    ).start()


def _expect(ref, sem, here):
    pltpu.make_async_remote_copy(
        src_ref=ref, dst_ref=ref, send_sem=sem, recv_sem=sem, device_id=here, device_id_type=MESH
    ).wait_recv()


def _sent(ref, sem, here):
    pltpu.make_async_remote_copy(
        src_ref=ref, dst_ref=ref, send_sem=sem, recv_sem=sem, device_id=here, device_id_type=MESH
    ).wait_send()


def _greet(u, z, planes, line=False, others=(), maybe=None):
    barrier = pltpu.get_barrier_semaphore()
    for bit in planes:
        pl.semaphore_signal(barrier, inc=1, device_id=(u ^ bit, z), device_id_type=MESH)
    for to in others:
        pl.semaphore_signal(barrier, inc=1, device_id=to, device_id_type=MESH)
    count = len(planes) + len(others)
    if line:

        @pl.when(z > 0)
        def _():
            pl.semaphore_signal(barrier, inc=1, device_id=(u, z - 1), device_id_type=MESH)

        @pl.when(z < DEPTH - 1)
        def _():
            pl.semaphore_signal(barrier, inc=1, device_id=(u, z + 1), device_id_type=MESH)

        count = count + jnp.where((z == 0) | (z == DEPTH - 1), 1, 2)
    if maybe is not None:
        to, real = maybe

        @pl.when(real)
        def _():
            pl.semaphore_signal(barrier, inc=1, device_id=to, device_id_type=MESH)

        count = count + jnp.where(real, 1, 0)
    pl.semaphore_wait(barrier, count)


def _line_order(z):
    second = jnp.where(z == 0, 1, z - 1)
    third = jnp.where(z == 0, 2, jnp.where(z == 3, 1, z + 1))
    fourth = jnp.where(z < 2, 3, 0)
    return (z, second, third, fourth)


def _accumulate(target, source, rows):
    strip = 16

    def step(i, _):
        at = pl.ds(pl.multiple_of(i * strip, strip), strip)
        target[at, :] = target[at, :] + source[at, :]
        return 0

    lax.fori_loop(0, rows // strip, step, 0)


def _run(*parts):
    live = list(parts)
    while live:
        for part in list(live):
            try:
                next(part)
            except StopIteration:
                live.remove(part)


def _line_part(u, z, source, block, sems, share=True):
    z_send, z_recv, c_send, c_recv, own_sem = sems
    here, core = (u, z), u % 2
    own = pltpu.make_async_copy(source, block(core, z), own_sem)
    own.start()
    order = _line_order(z)

    def along(level, ref, step):
        @pl.when((z > 0) & (level >= z))
        def _():
            step(ref, 0, level, (u, z - 1))

        @pl.when((z < DEPTH - 1) & (level <= z))
        def _():
            step(ref, 1, level, (u, z + 1))

    def go(ref, way, level, to):
        _send(ref, block(core, level), z_send.at[way, level], z_recv.at[level], to)

    def gone(ref, way, level, to):
        _sent(ref, z_send.at[way, level], here)

    for i in range(4):
        level = order[i]
        ref = source if i == 0 else block(core, level)
        if i > 0:
            yield
            _expect(ref, z_recv.at[level], here)
        along(level, ref, go)
        if share:
            _send(ref, block(core, level), c_send.at[level], c_recv.at[level], (u ^ 1, z))
    yield
    if share:
        for i in range(4):
            _expect(block(1 - core, order[i]), c_recv.at[order[i]], here)
    yield
    for i in range(4):
        along(order[i], block(core, order[i]), gone)
        if share:
            _sent(block(core, order[i]), c_send.at[order[i]], here)
    own.wait()


def _plane_part(u, z, own, block, sems):
    p_send, p_recv, o_sem = sems
    here = (u, z)
    for h in range(2):
        _send(own(h), block(h, u), p_send.at[h, 0], p_recv.at[h, 0], (u ^ FIRST[h], z))
    for h in range(2):
        pltpu.make_async_copy(own(h), block(h, u), o_sem.at[h]).start()
    for h in range(2):
        yield
        _expect(block(h, u ^ FIRST[h]), p_recv.at[h, 0], here)
        to = (u ^ THEN[h], z)
        _send(own(h), block(h, u), p_send.at[h, 1], p_recv.at[h, 1], to)
        near = block(h, u ^ FIRST[h])
        _send(near, near, p_send.at[h, 2], p_recv.at[h, 2], to)
    yield
    for h in range(2):
        _expect(block(h, u ^ THEN[h]), p_recv.at[h, 1], here)
        _expect(block(h, u ^ 6), p_recv.at[h, 2], here)
    yield
    for h in range(2):
        for k in range(3):
            _sent(block(h, u), p_send.at[h, k], here)
        pltpu.make_async_copy(own(h), block(h, u), o_sem.at[h]).wait()


def _plane_share_part(u, z, block, half, sems):
    p_send, p_recv, c_send, c_recv = sems
    here = (u, z)
    halves = (pl.ds(0, half), pl.ds(half, half))

    def source(i):
        return block(u, i)

    for i in range(4):
        for h in range(2):
            at = halves[h]
            _send(source(i).at[at], block(u, i).at[at], p_send.at[i, h, 0], p_recv.at[i, h, 0], (u ^ FIRST[h], z))
        _send(source(i), block(u, i), c_send.at[i, 0], c_recv.at[i, 0], (u ^ 1, z))

    def share(i):
        for h in range(2):
            _expect(block(u ^ THEN[h], i).at[halves[h]], p_recv.at[i, h, 1], here)
            _expect(block(u ^ 6, i).at[halves[h]], p_recv.at[i, h, 2], here)
        for k, bit in enumerate((2, 4, 6)):
            ref = block(u ^ bit, i)
            _send(ref, ref, c_send.at[i, k + 1], c_recv.at[i, k + 1], (u ^ 1, z))

    for i in range(4):
        yield
        for h in range(2):
            at = halves[h]
            near = block(u ^ FIRST[h], i).at[at]
            _expect(near, p_recv.at[i, h, 0], here)
            to = (u ^ THEN[h], z)
            _send(source(i).at[at], block(u, i).at[at], p_send.at[i, h, 1], p_recv.at[i, h, 1], to)
            _send(near, near, p_send.at[i, h, 2], p_recv.at[i, h, 2], to)
        if i > 0:
            share(i - 1)
    yield
    share(3)
    yield
    for i in range(4):
        for h in range(2):
            for k in range(3):
                _sent(block(u, i).at[halves[h]], p_send.at[i, h, k], here)
        for k, bit in enumerate((0, 2, 4, 6)):
            _sent(block(u, i), c_send.at[i, k], here)
            _expect(block(u ^ 1 ^ bit, i), c_recv.at[i, k], here)


PLANE_SHARE_SEMS = [DMA((4, 2, 3)), DMA((4, 2, 3)), DMA((4, 4)), DMA((4, 4))]


def _plane_sum_part(u, z, source, work, bufs, sems, rows, then_do):
    p_buf, q_buf = bufs
    load, p_send, p_recv, q_send, q_recv = sems
    here = (u, z)
    for h in range(2):
        for j, bit in enumerate((THEN[h], 6)):
            _send(source(h, u ^ bit), p_buf.at[h, j], p_send.at[h, j], p_recv.at[h, j], (u ^ THEN[h], z))
        for j, bit in enumerate((0, FIRST[h])):
            pltpu.make_async_copy(source(h, u ^ bit), work.at[h, j], load.at[h, j]).start()
    for h in range(2):
        yield
        for j, bit in enumerate((0, FIRST[h])):
            pltpu.make_async_copy(source(h, u ^ bit), work.at[h, j], load.at[h, j]).wait()
        _expect(p_buf.at[h, 1], p_recv.at[h, 1], here)
        _accumulate(work.at[h, 1], p_buf.at[h, 1], rows)
        _send(work.at[h, 1], q_buf.at[h], q_send.at[h], q_recv.at[h], (u ^ FIRST[h], z))
        _expect(p_buf.at[h, 0], p_recv.at[h, 0], here)
        _accumulate(work.at[h, 0], p_buf.at[h, 0], rows)
    yield
    for h in range(2):
        _expect(q_buf.at[h], q_recv.at[h], here)
        _accumulate(work.at[h, 0], q_buf.at[h], rows)
    then_do()
    yield
    for h in range(2):
        for j in range(2):
            _sent(p_buf.at[h, j], p_send.at[h, j], here)
        _sent(q_buf.at[h], q_send.at[h], here)


def _line_sum_part(u, z, source, work, bufs, sems, rows, then_do):
    c_buf, z_buf = bufs
    load, c_send, c_recv, z_send, z_recv = sems
    here, core = (u, z), u % 2
    order = tuple(reversed(_line_order(z)))
    for i in range(4):
        _send(source(1 - core, order[i]), c_buf.at[i], c_send.at[i], c_recv.at[i], (u ^ 1, z))
        pltpu.make_async_copy(source(core, order[i]), work.at[i], load.at[i]).start()
    for i in range(4):
        yield
        pltpu.make_async_copy(source(core, order[i]), work.at[i], load.at[i]).wait()
        _expect(c_buf.at[i], c_recv.at[i], here)
        _accumulate(work.at[i], c_buf.at[i], rows)
        if i == 3:
            yield
        _line_end(u, z, order[i], i, work.at[i], z_buf, (z_send, z_recv), rows)
    then_do()
    yield
    for i in range(4):
        _sent(c_buf.at[i], c_send.at[i], here)
        if i < 3:
            _sent(work.at[i], z_send.at[i], here)


def _column_peers(u, z):
    return [((u ^ c, z ^ k), c, k) for c in range(2) for k in range(4) if c or k]


def _comm(kernel, outs, scratch, collective_id, specs, flops=0, moved=100_000_000, aliases={}):
    return pl.pallas_call(
        kernel,
        out_shape=outs,
        in_specs=specs[0],
        out_specs=specs[1],
        scratch_shapes=scratch,
        input_output_aliases=aliases,
        compiler_params=pltpu.CompilerParams(
            collective_id=collective_id, has_side_effects=True, vmem_limit_bytes=VMEM_BYTES
        ),
        cost_estimate=pl.CostEstimate(flops=flops, bytes_accessed=moved, transcendentals=0),
    )


LINE_SEMS = [DMA((2, 4)), DMA((4,)), DMA((4,)), DMA((4,)), DMA]
PLANE_SEMS = [DMA((2, 3)), DMA((2, 3)), DMA((2,))]
PLANE_SUM_SEMS = [DMA((2, 2)), DMA((2, 2)), DMA((2, 2)), DMA((2,)), DMA((2,))]
LINE_SUM_SEMS = [DMA((4,)), DMA((4,)), DMA((4,)), DMA((4,)), DMA((2, 4))]


def _small_part(u, z, xs, outs, sems):
    own_sem, z_send, z_recv, u_send, u_recv = sems
    here = (u, z)
    for a, (x, o) in enumerate(zip(xs, outs)):
        pltpu.make_async_copy(x, o.at[u, z], own_sem.at[a]).start()
        for k in range(1, 4):
            _send(x, o.at[u, z], z_send.at[a, k], z_recv.at[a, k], (u, z ^ k))
    yield
    for a, (x, o) in enumerate(zip(xs, outs)):
        pltpu.make_async_copy(x, o.at[u, z], own_sem.at[a]).wait()
        for k in range(1, 4):
            _expect(o.at[u, z ^ k], z_recv.at[a, k], here)
        for k in range(1, 8):
            _send(o.at[u], o.at[u], u_send.at[a, k], u_recv.at[a, k], (u ^ k, z))
    yield
    yield
    for a, (x, o) in enumerate(zip(xs, outs)):
        for k in range(1, 4):
            _sent(x, z_send.at[a, k], here)
        for k in range(1, 8):
            _sent(o.at[u], u_send.at[a, k], here)
            _expect(o.at[u ^ k], u_recv.at[a, k], here)


def _small_sems(n):
    return [DMA((n,)), DMA((n, 4)), DMA((n, 4)), DMA((n, 8)), DMA((n, 8))]


def enter(rows, weights, out_weight, smalls, collective_id):
    n = len(smalls)

    def kernel(*refs):
        x_ref, w_ref, o_ref = refs[:3]
        small_in = refs[3 : 3 + n]
        x_out, w_out, o_out = refs[3 + n : 6 + n]
        small_out = refs[6 + n : 6 + 2 * n]
        w_buf, o_buf = refs[6 + 2 * n : 8 + 2 * n]
        sems = refs[8 + 2 * n :]
        line, plane_w, plane_o, (w_own, w_send, w_recv, o_own, o_send, o_recv) = sems[:5], sems[5:8], sems[8:11], sems[11:17]
        small_sems = sems[17:]
        u, z = lax.axis_index("uly"), lax.axis_index("blk")
        here, core, chip = (u, z), u % 2, u // 2
        turned = (2 * z + core, chip)
        away = chip != z
        column = _column_peers(u, z)
        _greet(u, z, range(1, 8), others=[to for to, c, k in column if k], maybe=(turned, away))

        def weight_part():
            own = pltpu.make_async_copy(w_ref.at[core, z], w_buf.at[core, z], w_own)
            own.start()
            for i, (to, c, k) in enumerate(column):
                _send(w_ref.at[core ^ c, z ^ k], w_buf.at[core, z], w_send.at[i], w_recv.at[i], to)
            yield
            own.wait()
            for i, (to, c, k) in enumerate(column):
                _expect(w_buf.at[core ^ c, z ^ k], w_recv.at[i], here)
            yield from _plane_part(u, z, lambda h: w_buf.at[h], lambda h, v: w_out.at[v // 2, h], plane_w)
            for i, (to, c, k) in enumerate(column):
                _sent(w_ref.at[core ^ c, z ^ k], w_send.at[i], here)

        def out_part():
            @pl.when(away)
            def _():
                _send(o_ref, o_buf, o_send, o_recv, turned)

            @pl.when(jnp.logical_not(away))
            def _():
                pltpu.make_async_copy(o_ref, o_buf, o_own).start()

            yield
            yield

            @pl.when(away)
            def _():
                _expect(o_buf, o_recv, here)

            @pl.when(jnp.logical_not(away))
            def _():
                pltpu.make_async_copy(o_ref, o_buf, o_own).wait()

            half = out_weight.shape[0] // 2
            cut = [pl.ds(h * half, half) for h in range(2)]
            yield from _plane_part(u, z, lambda h: o_buf.at[cut[h]], lambda h, v: o_out.at[v // 2, cut[h]], plane_o)

            @pl.when(away)
            def _():
                _sent(o_ref, o_send, here)

        _run(
            weight_part(),
            _small_part(u, z, small_in, small_out, small_sems),
            _line_part(u, z, x_ref, lambda c, level: x_out.at[c, level], line),
            out_part(),
        )

    outs = [
        jax.ShapeDtypeStruct((2, 4) + rows.shape, rows.dtype),
        jax.ShapeDtypeStruct((4,) + weights.shape, weights.dtype),
        jax.ShapeDtypeStruct((4,) + out_weight.shape, out_weight.dtype),
    ] + [jax.ShapeDtypeStruct((8, 4) + x.shape, x.dtype) for x in smalls]
    scratch = [pltpu.VMEM(weights.shape, BF16), pltpu.VMEM(out_weight.shape, BF16)]
    scratch += LINE_SEMS + PLANE_SEMS * 2 + [DMA, DMA((7,)), DMA((7,)), DMA, DMA, DMA] + _small_sems(n)
    specs = ([IN_VMEM, IN_VMEM, ANY_SPACE] + [IN_VMEM] * n, [ANY_SPACE] * len(outs))
    return _comm(kernel, outs, scratch, collective_id, specs)(rows, weights, out_weight, *smalls)


def column_sum(x, collective_id):
    def kernel(x_ref, o_ref, buf, send, recv):
        u, z = lax.axis_index("uly"), lax.axis_index("blk")
        here = (u, z)
        column = _column_peers(u, z)
        _greet(u, z, (), others=[to for to, c, k in column])
        for i, (to, c, k) in enumerate(column):
            _send(x_ref, buf.at[i], send.at[i], recv.at[i], to)
        total = x_ref[...]
        for i in range(7):
            _expect(buf.at[i], recv.at[i], here)
            total = total + buf[i]
        o_ref[...] = total
        for i in range(7):
            _sent(x_ref, send.at[i], here)

    scratch = [pltpu.VMEM((7,) + x.shape, F32), DMA((7,)), DMA((7,))]
    out = jax.ShapeDtypeStruct(x.shape, F32)
    return _comm(kernel, out, scratch, collective_id, ([IN_VMEM], IN_VMEM))(x)


def plane_pair(first, second, rows, collective_id):
    def kernel(a_ref, b_ref, x_ref, a_out, b_out, x_out, *sems):
        u, z = lax.axis_index("uly"), lax.axis_index("blk")
        _greet(u, z, (2, 4), line=True)
        own, outs = (a_ref, b_ref), (a_out, b_out)
        _run(
            _plane_part(u, z, lambda h: own[h], lambda h, v: outs[h].at[v // 2], sems[:3]),
            _line_part(u, z, x_ref, lambda c, level: x_out.at[u * DEPTH + level], sems[3:], share=False),
        )

    outs = [jax.ShapeDtypeStruct((4,) + x.shape, x.dtype) for x in (first, second)]
    outs += [jax.ShapeDtypeStruct((32,) + rows.shape, rows.dtype)]
    specs = ([IN_VMEM] * 2 + [ANY_SPACE], [ANY_SPACE] * 3)
    return _comm(kernel, outs, PLANE_SEMS + LINE_SEMS, collective_id, specs)(first, second, rows)


def column_gather(rows, x, collective_id):
    T, D = rows.shape

    def kernel(r_ref, x_ref, r_out, x_out, *refs):
        u, z = lax.axis_index("uly"), lax.axis_index("blk")
        _greet(u, z, (1, 2, 4), line=True)
        order = _line_order(z)

        def keep(i, work):
            x_out[order[i]] = work[i, 0]

        _run(
            _line_part(u, z, r_ref, lambda c, level: r_out.at[c, level], refs[-5:]),
            _tree_sum_part(u, z, lambda who, level: x_ref.at[who * DEPTH + level], order, T, refs[:-5], keep),
        )

    outs = [jax.ShapeDtypeStruct((2, 4, T, D), BF16), jax.ShapeDtypeStruct((4, T, D), BF16)]
    specs = ([IN_VMEM, ANY_SPACE], [ANY_SPACE, IN_VMEM])
    scratch = _tree_sum_scratch(T, D) + LINE_SEMS
    return _comm(kernel, outs, scratch, collective_id, specs)(rows, x.reshape(32, T, D))


def _line_sum_scratch(T, D):
    return [pltpu.VMEM((4, T, D), BF16), pltpu.VMEM((4, T, D), BF16), pltpu.VMEM((2, 4, T, D), BF16)]


def column_scatter(x, rows, collective_id):
    T, D = x.shape[2:]

    def kernel(x_ref, g_ref, o_ref, g_out, work, c_buf, z_buf, *sems):
        u, z = lax.axis_index("uly"), lax.axis_index("blk")
        _greet(u, z, (1, 2, 4), line=True)

        def finish():
            o_ref[...] = work[3]

        _run(
            _line_sum_part(u, z, lambda c, level: x_ref.at[c, level], work, (c_buf, z_buf), sems[:5], T, finish),
            _plane_share_part(u, z, lambda who, i: g_out.at[who * DEPTH + i], T // 2, sems[5:]),
        )

    outs = [jax.ShapeDtypeStruct((T, D), BF16), jax.ShapeDtypeStruct((32, T, D), BF16)]
    scratch = _line_sum_scratch(T, D) + LINE_SUM_SEMS + PLANE_SHARE_SEMS
    specs = ([ANY_SPACE] * 2, [IN_VMEM, ANY_SPACE])
    out, gathered = _comm(kernel, outs, scratch, collective_id, specs, aliases={1: 1})(x, rows)
    return out, gathered.reshape(32 * T, D)


def _plane_sum_scratch(rows, cols):
    return [pltpu.VMEM((2, 2, rows, cols), BF16), pltpu.VMEM((2, 2, rows, cols), BF16), pltpu.VMEM((2, rows, cols), BF16)]


def key_value_sums(dk, dv, out_part, x, collective_id):
    T = x.shape[1]
    L, C = dk.shape[1:]
    R, D = out_part.shape[1:]
    half = R // 2

    def kernel(
        k_ref, v_ref, w_ref, x_ref, k_out, v_out, w_out, x_out, work, p_buf, q_buf, o_work, op_buf, oq_buf, x_work, z_buf, *sems
    ):
        u, z = lax.axis_index("uly"), lax.axis_index("blk")
        here, core, chip = (u, z), u % 2, u // 2
        turned = (2 * z + core, chip)
        away = chip != z
        _greet(u, z, (2, 4), line=True, maybe=(turned, away))
        t_send, t_recv, load, z_send, z_recv = sems[10:15]
        order = tuple(reversed(_line_order(z)))

        def finish():
            k_out[...] = work[0, 0]
            v_out[...] = work[1, 0]

        def turn():
            for h in range(2):
                rows = pl.ds(h * half, half)

                @pl.when(away)
                def _(h=h, rows=rows):
                    _send(o_work.at[h, 0], w_out.at[rows], t_send.at[h], t_recv.at[h], turned)

                @pl.when(jnp.logical_not(away))
                def _(h=h, rows=rows):
                    w_out[rows, :] = o_work[h, 0]

        def line():
            copies = [pltpu.make_async_copy(x_ref.at[order[i]], x_work.at[i], load.at[i]) for i in range(4)]
            for copy in copies:
                copy.start()
            for copy in copies:
                copy.wait()
            for i in range(4):
                _line_end(u, z, order[i], i, x_work.at[i], z_buf, (z_send, z_recv), T)
                yield
            x_out[...] = x_work[3]
            for i in range(3):
                _sent(x_work.at[i], z_send.at[i], here)

        _run(
            _plane_sum_part(
                u,
                z,
                lambda h, v: w_ref.at[v // 2, pl.ds(h * half, half)],
                o_work,
                (op_buf, oq_buf),
                sems[5:10],
                half,
                turn,
            ),
            _plane_sum_part(
                u, z, lambda h, v: (k_ref, v_ref)[h].at[v // 2], work, (p_buf, q_buf), sems[:5], L, finish
            ),
            line(),
        )

        @pl.when(away)
        def _():
            for h in range(2):
                rows = pl.ds(h * half, half)
                _expect(w_out.at[rows], t_recv.at[h], here)
                _sent(o_work.at[h, 0], t_send.at[h], here)

    outs = [jax.ShapeDtypeStruct((L, C), BF16)] * 2 + [jax.ShapeDtypeStruct((R, D), BF16), jax.ShapeDtypeStruct((T, D), BF16)]
    scratch = _plane_sum_scratch(L, C) + _plane_sum_scratch(half, D)
    scratch += [pltpu.VMEM((4, T, D), BF16), pltpu.VMEM((2, 4, T, D), BF16)] + PLANE_SUM_SEMS * 2
    scratch += [DMA((2,)), DMA((2,)), DMA((4,)), DMA((4,)), DMA((2, 4))]
    specs = ([ANY_SPACE] * 4, [IN_VMEM] * 4)
    return _comm(kernel, outs, scratch, collective_id, specs)(dk, dv, out_part, x)


def leave(x, weights, smalls, collective_id):
    n = len(smalls)
    T, D = x.shape[2:]
    rows, W = weights.shape[2:]
    R = rows // 4

    def kernel(x_ref, w_ref, *refs):
        small_in, (o_ref, w_out), small_out = refs[:n], refs[n : n + 2], refs[n + 2 : 2 * n + 2]
        work, c_buf, z_buf, w_work, wp_buf, wq_buf = refs[2 * n + 2 : 2 * n + 8]
        sems = refs[2 * n + 8 :]
        u, z = lax.axis_index("uly"), lax.axis_index("blk")
        here, core, chip = (u, z), u % 2, u // 2
        column = _column_peers(u, z)
        _greet(u, z, range(1, 8), others=[to for to, c, k in column if k])
        t_send, t_recv = sems[10:12]
        group = 2 * z + core

        def finish():
            o_ref[...] = work[3]

        def cut(c, level):
            return w_work.at[c, 0, pl.ds(pl.multiple_of(level * R, R), R)]

        def deal():
            for i, (to, c, k) in enumerate(column):
                _send(cut(core ^ c, z ^ k), w_out.at[group], t_send.at[i], t_recv.at[i], to)
            w_out[group] = cut(core, z)[...]

        _run(
            _plane_sum_part(u, z, lambda h, v: w_ref.at[v // 2, h], w_work, (wp_buf, wq_buf), sems[5:10], rows, deal),
            _line_sum_part(u, z, lambda c, level: x_ref.at[c, level], work, (c_buf, z_buf), sems[:5], T, finish),
            _small_part(u, z, small_in, small_out, sems[12:]),
        )
        for i, (to, c, k) in enumerate(column):
            _expect(w_out.at[2 * (z ^ k) + (core ^ c)], t_recv.at[i], here)
            _sent(cut(core ^ c, z ^ k), t_send.at[i], here)

    outs = [jax.ShapeDtypeStruct((T, D), BF16), jax.ShapeDtypeStruct((8, R, W), BF16)]
    outs += [jax.ShapeDtypeStruct((8, 4) + x.shape, x.dtype) for x in smalls]
    scratch = _line_sum_scratch(T, D) + _plane_sum_scratch(rows, W) + LINE_SUM_SEMS + PLANE_SUM_SEMS
    scratch += [DMA((7,)), DMA((7,))] + _small_sems(n)
    specs = ([ANY_SPACE] * 2 + [IN_VMEM] * n, [IN_VMEM] * 2 + [ANY_SPACE] * n)
    return _comm(kernel, outs, scratch, collective_id, specs)(x, weights, *smalls)


def _gather_all_kernel(x_ref, o_ref, own_sem, z_send, z_recv, p_send, p_recv, c_send, c_recv):
    u, z = lax.axis_index("uly"), lax.axis_index("blk")
    depth = DEPTH
    half = x_ref.shape[0] // 2
    halves = (pl.ds(0, half), pl.ds(half, half))
    here = (u, z)
    _greet(u, z, (1, 2, 4), line=True)
    own = pltpu.make_async_copy(x_ref, o_ref.at[u * depth + z], own_sem)
    own.start()
    order = _line_order(z)

    def block(who, level):
        return o_ref.at[who * depth + level]

    def part(who, level, h):
        return o_ref.at[who * depth + level, halves[h]]

    first, then = (2, 4), (4, 2)

    def along(level, source, step):
        @pl.when((z > 0) & (level >= z))
        def _():
            step(source, 0, level, (u, z - 1))

        @pl.when((z < depth - 1) & (level <= z))
        def _():
            step(source, 1, level, (u, z + 1))

    def go(source, way, level, to):
        _send(source, block(u, level), z_send.at[way, level], z_recv.at[level], to)

    def gone(source, way, level, to):
        _sent(source, z_send.at[way, level], here)

    def across(level, source):
        for h in range(2):
            _send(
                source.at[halves[h]], part(u, level, h), p_send.at[level, h, 0], p_recv.at[level, h, 0], (u ^ first[h], z)
            )
        _send(source, block(u, level), c_send.at[level, 0], c_recv.at[level, 0], (u ^ 1, z))

    def onward(level, source):
        for h in range(2):
            _expect(part(u ^ first[h], level, h), p_recv.at[level, h, 0], here)
            to = (u ^ then[h], z)
            _send(source.at[halves[h]], part(u, level, h), p_send.at[level, h, 1], p_recv.at[level, h, 1], to)
            _send(
                part(u ^ first[h], level, h),
                part(u ^ first[h], level, h),
                p_send.at[level, h, 2],
                p_recv.at[level, h, 2],
                to,
            )

    def share(level):
        for h in range(2):
            _expect(part(u ^ then[h], level, h), p_recv.at[level, h, 1], here)
            _expect(part(u ^ 6, level, h), p_recv.at[level, h, 2], here)
        for i, bit in enumerate((2, 4, 6)):
            _send(block(u ^ bit, level), block(u ^ bit, level), c_send.at[level, i + 1], c_recv.at[level, i + 1], (u ^ 1, z))

    sources = [x_ref] + [block(u, order[i]) for i in range(1, 4)]
    along(z, x_ref, go)
    across(z, x_ref)
    for i in range(1, 4):
        _expect(block(u, order[i]), z_recv.at[order[i]], here)
        along(order[i], sources[i], go)
        across(order[i], sources[i])
        onward(order[i - 1], sources[i - 1])
        if i >= 2:
            share(order[i - 2])
    onward(order[3], sources[3])
    share(order[2])
    share(order[3])
    for i in range(4):
        level = order[i]
        along(level, sources[i], gone)
        for h in range(2):
            for k in range(3):
                _sent(part(u, level, h), p_send.at[level, h, k], here)
        for k, bit in enumerate((0, 2, 4, 6)):
            _sent(block(u, level), c_send.at[level, k], here)
            _expect(block(u ^ 1 ^ bit, level), c_recv.at[level, k], here)
    own.wait()


def gather_all(x, collective_id):
    T, D = x.shape
    scratch = [DMA, DMA((2, 4)), DMA((4,)), DMA((4, 2, 3)), DMA((4, 2, 3)), DMA((4, 4)), DMA((4, 4))]
    out = jax.ShapeDtypeStruct((32, T, D), x.dtype)
    return _comm(_gather_all_kernel, out, scratch, collective_id, ([IN_VMEM], ANY_SPACE))(x).reshape(32 * T, D)


def _tree_sum_part(u, z, source, order, T, refs, level_done):
    work, c_buf, p_buf, q_buf, load_sem, c_send, c_recv, p_send, p_recv, q_send, q_recv = refs
    here = (u, z)
    half = T // 2
    halves = (pl.ds(0, half), pl.ds(half, half))

    def load(i, k, bit):
        return pltpu.make_async_copy(source(u ^ bit, order[i]), work.at[i, k], load_sem.at[i, k])

    for i in range(4):
        for k, bit in enumerate(CHIPS):
            _send(source(u ^ bit ^ 1, order[i]), c_buf.at[i, k], c_send.at[i, k], c_recv.at[i, k], (u ^ 1, z))
            load(i, k, bit).start()

    def add_core(i):
        for k in (3, 2, 1, 0):
            load(i, k, CHIPS[k]).wait()
            _expect(c_buf.at[i, k], c_recv.at[i, k], here)
            _accumulate(work.at[i, k], c_buf.at[i, k], T)
        for h in range(2):
            for j, bit in enumerate((THEN[h], 6)):
                k = CHIPS.index(bit)
                part = work.at[i, k, halves[h]]
                _send(part, p_buf.at[i, h, j], p_send.at[i, h, j], p_recv.at[i, h, j], (u ^ THEN[h], z))

    def add_first(i):
        for h in range(2):
            k = CHIPS.index(FIRST[h])
            _expect(p_buf.at[i, h, 1], p_recv.at[i, h, 1], here)
            _accumulate(work.at[i, k, halves[h]], p_buf.at[i, h, 1], half)
            _send(work.at[i, k, halves[h]], q_buf.at[i, h], q_send.at[i, h], q_recv.at[i, h], (u ^ FIRST[h], z))
            _expect(p_buf.at[i, h, 0], p_recv.at[i, h, 0], here)
            _accumulate(work.at[i, 0, halves[h]], p_buf.at[i, h, 0], half)

    def add_then(i):
        for h in range(2):
            _expect(q_buf.at[i, h], q_recv.at[i, h], here)
            _accumulate(work.at[i, 0, halves[h]], q_buf.at[i, h], half)
        level_done(i, work)

    for i in range(6):
        yield
        if i < 4:
            add_core(i)
        if 1 <= i < 5:
            add_first(i - 1)
        if i >= 2:
            add_then(i - 2)
    yield
    for i in range(4):
        for k in range(4):
            _sent(c_buf.at[i, k], c_send.at[i, k], here)
        for h in range(2):
            for j in range(2):
                _sent(p_buf.at[i, h, j], p_send.at[i, h, j], here)
            _sent(q_buf.at[i, h], q_send.at[i, h], here)


def _tree_sum_scratch(T, D):
    half = T // 2
    return [
        pltpu.VMEM((4, 4, T, D), BF16),
        pltpu.VMEM((4, 4, T, D), BF16),
        pltpu.VMEM((4, 2, 2, half, D), BF16),
        pltpu.VMEM((4, 2, half, D), BF16),
        DMA((4, 4)),
        DMA((4, 4)),
        DMA((4, 4)),
        DMA((4, 2, 2)),
        DMA((4, 2, 2)),
        DMA((4, 2)),
        DMA((4, 2)),
    ]


def _line_end(u, z, level, i, part, z_buf, sems, rows):
    z_send, z_recv = sems
    here = (u, z)

    @pl.when((level >= z) & (z > 0))
    def _():
        _expect(z_buf.at[0, level], z_recv.at[0, level], here)
        _accumulate(part, z_buf.at[0, level], rows)

    @pl.when((level <= z) & (z < DEPTH - 1))
    def _():
        _expect(z_buf.at[1, level], z_recv.at[1, level], here)
        _accumulate(part, z_buf.at[1, level], rows)

    if i < 3:

        @pl.when(level > z)
        def _():
            _send(part, z_buf.at[0, level], z_send.at[i], z_recv.at[0, level], (u, z + 1))

        @pl.when(level < z)
        def _():
            _send(part, z_buf.at[1, level], z_send.at[i], z_recv.at[1, level], (u, z - 1))


def scatter_all(x, collective_id):
    N, D = x.shape
    T = N // 32

    def kernel(x_ref, o_ref, z_buf, z_send, z_recv, *refs):
        u, z = lax.axis_index("uly"), lax.axis_index("blk")
        _greet(u, z, (1, 2, 4), line=True)
        order = tuple(reversed(_line_order(z)))
        work = refs[0]

        def done(i, work):
            _line_end(u, z, order[i], i, work.at[i, 0], z_buf, (z_send, z_recv), T)

        _run(_tree_sum_part(u, z, lambda who, level: x_ref.at[who * DEPTH + level], order, T, refs, done))
        o_ref[...] = work[3, 0]
        for i in range(3):
            _sent(work.at[i, 0], z_send.at[i], (u, z))

    scratch = [pltpu.VMEM((2, 4, T, D), BF16), DMA((4,)), DMA((2, 4))] + _tree_sum_scratch(T, D)
    out = jax.ShapeDtypeStruct((T, D), x.dtype)
    return _comm(kernel, out, scratch, collective_id, ([ANY_SPACE], IN_VMEM))(x.reshape(32, T, D))


class Slice:
    def __init__(self, U, Z, T, D):
        self.U, self.Z, self.T, self.D = U, Z, T, D
        self.u, self.z = lax.axis_index("uly"), lax.axis_index("blk")
        self.C = D // 8
        self.L = 8 * T
        self.group = 2 * self.z + self.u % 2
        self.first_block, self.block_step = 8 * (self.u // 2), 1

    def enter(self, rows, scaled, out_weight, pack, routes):
        R = scaled.shape[0]
        cut = scaled.reshape(R, 3, 4, 2, self.C).transpose(3, 2, 0, 1, 4).reshape(2, 4, R, 3 * self.C)
        rows, weights, outs, packs, routes = enter(rows, cut, out_weight, [pack, routes], 1)
        return (
            rows.reshape(self.L, self.D),
            weights.reshape(self.D, 3 * self.C),
            outs.reshape(self.C, self.D),
            packs.reshape(self.D, -1),
            routes,
        )

    def head_sum(self, x):
        return column_sum(x, 2)

    def head_sum_again(self, x):
        return column_sum(x, 3)

    def sequence(self, key, value, upstream):
        keys, values, self.upstream_line = plane_pair(key, value, upstream, 4)
        return keys.reshape(-1, self.C), values.reshape(-1, self.C)

    def heads_to_rows(self, x):
        return column_scatter(x.reshape(2, 4, self.T, self.D), self.upstream_line, 5)

    def rows_to_heads(self, x, out_part):
        rows, self.out_line = column_gather(x, out_part, 6)
        return rows.reshape(self.L, self.D)

    def gather(self, x):
        return gather_all(x, 7)

    def scatter_wide(self, x):
        return scatter_all(x, 8)

    def sequence_sums(self, dk, dv, out_part):
        cut = (4, self.L, self.C)
        return key_value_sums(dk.reshape(cut), dv.reshape(cut), out_part.reshape(4, -1, self.D), self.out_line, 10)

    def leave(self, first_part, weight_part, logit_grad, ffn_part, head_parts):
        T, R = self.T, self.D // 32
        thin = jnp.concatenate([ffn_part.reshape(-1, 128), head_parts.reshape(-1, 128)], axis=0)
        wide = self.D // 128
        used = thin.shape[0]
        thin = jnp.pad(thin, ((0, -used % 8), (0, 0)))
        first, weights, logit_all, thin = leave(
            first_part.reshape(2, 4, T, self.D),
            weight_part.reshape(4, 2, 4 * R, 3 * self.C),
            [logit_grad.reshape(T // 2, 2 * EXPERTS), thin],
            11,
        )
        weights = weights.reshape(8, R, 3, self.C).transpose(1, 2, 0, 3).reshape(R, 3, self.D)
        ffn = lax.dynamic_slice_in_dim(
            jnp.sum(thin[:, :, :wide], axis=(0, 1)).reshape(self.D), (self.u * 4 + self.z) * R, R, 0
        )
        mine = lax.dynamic_index_in_dim(thin.reshape(4, 2, 4, -1, 128), self.u % 2, 1, False)
        mine = lax.dynamic_index_in_dim(mine, self.u // 2, 1, False)
        heads = jnp.sum(mine[:, wide:used], axis=0).reshape(2, self.C)
        heads = lax.dynamic_slice_in_dim(heads, self.z * R, R, 1)
        return first, weights, logit_all.reshape(32 * T, EXPERTS), ffn, heads


class General:
    def __init__(self, U, Z, T, D):
        self.U, self.Z, self.T, self.D = U, Z, T, D
        self.u, self.z = lax.axis_index("uly"), lax.axis_index("blk")
        self.C = D // U
        self.L = U * T
        self.group = self.u
        self.first_block, self.block_step = self.z, Z

    def gather(self, x):
        return lax.all_gather(x, ALL, axis=0, tiled=True)

    def scatter_wide(self, x):
        return lax.psum_scatter(x, ALL, scatter_dimension=0, tiled=True)

    def enter(self, rows, scaled, out_weight, pack, routes):
        U, R = self.U, scaled.shape[0]
        swapped = lax.all_to_all(scaled.reshape(R, 3, U, self.C), "uly", split_axis=2, concat_axis=0, tiled=True)
        weights = lax.all_gather(swapped.reshape(U, R, 3 * self.C), "blk", axis=1, tiled=True)
        return (
            self.rows_all(rows),
            weights.reshape(self.D, 3 * self.C),
            lax.all_gather(out_weight, "blk", axis=0, tiled=True),
            self.gather(pack),
            self.gather(routes[None]).reshape((U, self.Z) + routes.shape),
        )

    def head_sum(self, x):
        return lax.psum(x, "uly")

    head_sum_again = head_sum

    def sequence(self, key, value, upstream):
        self.upstream = upstream
        pair = jnp.stack([key, value]).reshape(2, self.U, self.T, self.C)
        pair = lax.all_gather(pair, "blk", axis=2, tiled=False).reshape(2, -1, self.C)
        return pair[0], pair[1]

    def heads_to_rows(self, x):
        return self.rows_sum(x), self.gather(self.upstream)

    def rows_sum(self, x):
        return lax.psum_scatter(x, "uly", scatter_dimension=0, tiled=True)

    def rows_all(self, x):
        return lax.all_gather(x, "uly", axis=0, tiled=True)

    def rows_to_heads(self, x, out_part):
        self.out_sum = self.scatter_wide(out_part)
        return self.rows_all(x)

    def sequence_sums(self, dk, dv, out_part):
        pair = jnp.stack([dk, dv]).reshape(2, self.U, self.Z, self.T, self.C)
        pair = lax.psum_scatter(pair, "blk", scatter_dimension=2, tiled=True).reshape(2, self.L, self.C)
        return pair[0], pair[1], lax.psum_scatter(out_part, "blk", scatter_dimension=0, tiled=True), self.out_sum

    def leave(self, first_part, weight_part, logit_grad, ffn_part, head_parts):
        U, R = self.U, self.D // (self.U * self.Z)
        part = weight_part.reshape(U, self.Z * R, 3 * self.C)
        part = lax.psum_scatter(part, "blk", scatter_dimension=1, tiled=True)
        part = lax.all_to_all(part, "uly", split_axis=0, concat_axis=0, tiled=True)
        weights = part.reshape(U, R, 3, self.C).transpose(1, 2, 0, 3).reshape(R, 3, self.D)
        heads = lax.psum_scatter(head_parts, "blk", scatter_dimension=1, tiled=True)
        return self.rows_sum(first_part), weights, self.gather(logit_grad), self.scatter_wide(ffn_part), heads


def _row_limits(doc_ref, first, rows):
    position = first + lax.broadcasted_iota(jnp.int32, (rows, 1), 0)
    start = jnp.zeros_like(position)
    lowest = jnp.int32(0)
    for d in range(doc_ref.shape[0]):
        begin = doc_ref[d]
        start = jnp.where(begin <= position, jnp.maximum(start, begin), start)
        lowest = jnp.where(begin <= first, jnp.maximum(lowest, begin), lowest)
    return position, start, lowest


def _scores(query, key, position, start, key_first, scaling):
    raw = dot(query, key, LAST_DIM) * scaling
    key_position = key_first + lax.broadcasted_iota(jnp.int32, raw.shape, 1)
    return jnp.where((key_position <= position) & (key_position >= start), raw, NEG)


def _attend_kernel(index_ref, doc_ref, q_ref, k_ref, v_ref, o_ref, log_ref, *, chunk, scaling):
    rows = q_ref.shape[0]
    heads = q_ref.shape[1] // HEAD_DIM
    first = (pl.program_id(0) * index_ref[1] + index_ref[0]) * rows
    position, start, lowest = _row_limits(doc_ref, first, rows)

    def step(i, state):
        at = pl.multiple_of(i * chunk, chunk)
        new = []
        for h in range(heads):
            cols = pl.ds(h * HEAD_DIM, HEAD_DIM)
            top, total, out = state[h]
            scores = _scores(q_ref[:, cols], k_ref[pl.ds(at, chunk), cols], position, start, at, scaling)
            now = jnp.maximum(top, jnp.max(scores, axis=1, keepdims=True))
            weights = jnp.exp(scores - now)
            fade = jnp.exp(top - now)
            total = total * fade + jnp.sum(weights, axis=1, keepdims=True)
            out = out * fade + dot(weights.astype(BF16), v_ref[pl.ds(at, chunk), cols])
            new.append((now, total, out))
        return tuple(new)

    zero = (
        jnp.full((rows, 1), NEG, F32),
        jnp.zeros((rows, 1), F32),
        jnp.zeros((rows, HEAD_DIM), F32),
    )
    last = first + rows
    state = lax.fori_loop(lowest // chunk, (last + chunk - 1) // chunk, step, (zero,) * heads)
    for h in range(heads):
        cols = pl.ds(h * HEAD_DIM, HEAD_DIM)
        top, total, out = state[h]
        o_ref[:, cols] = out / total
        log_ref[:, cols] = jnp.broadcast_to(top + jnp.log(total), (rows, HEAD_DIM))


def _attend_back_kernel(
    index_ref, doc_ref, q_ref, g_ref, o_ref, log_ref, k_ref, v_ref, dq_ref, dk_ref, dv_ref, dk_sum, dv_sum, *, chunk, scaling
):
    rows = q_ref.shape[0]
    heads = q_ref.shape[1] // HEAD_DIM
    first = (pl.program_id(0) * index_ref[1] + index_ref[0]) * rows
    position, start, lowest = _row_limits(doc_ref, first, rows)

    @pl.when(pl.program_id(0) == 0)
    def _():
        dk_sum[...] = jnp.zeros_like(dk_sum)
        dv_sum[...] = jnp.zeros_like(dv_sum)

    deltas, logs = [], []
    for h in range(heads):
        cols = pl.ds(h * HEAD_DIM, HEAD_DIM)
        deltas.append(jnp.sum(g_ref[:, cols].astype(F32) * o_ref[:, cols], axis=1, keepdims=True))
        logs.append(log_ref[:, cols][:, :1])

    def step(i, state):
        at = pl.multiple_of(i * chunk, chunk)
        new = []
        for h in range(heads):
            cols = pl.ds(h * HEAD_DIM, HEAD_DIM)
            query, grad = q_ref[:, cols], g_ref[:, cols]
            key = k_ref[pl.ds(at, chunk), cols]
            scores = _scores(query, key, position, start, at, scaling)
            weights = jnp.exp(scores - logs[h])
            weight_grad = dot(grad, v_ref[pl.ds(at, chunk), cols], LAST_DIM)
            score_grad = (weights * (weight_grad - deltas[h])).astype(BF16)
            dv_sum[pl.ds(at, chunk), cols] += dot(weights.astype(BF16), grad, FIRST_DIM)
            dk_sum[pl.ds(at, chunk), cols] += dot(score_grad, query, FIRST_DIM)
            new.append(state[h] + dot(score_grad, key))
        return tuple(new)

    last = first + rows
    state = lax.fori_loop(
        lowest // chunk, (last + chunk - 1) // chunk, step, (jnp.zeros((rows, HEAD_DIM), F32),) * heads
    )
    for h in range(heads):
        dq_ref[:, pl.ds(h * HEAD_DIM, HEAD_DIM)] = (state[h] * scaling).astype(BF16)

    @pl.when(pl.program_id(0) == pl.num_programs(0) - 1)
    def _():
        dk_ref[...] = (dk_sum[...] * scaling).astype(BF16)
        dv_ref[...] = dv_sum[...].astype(BF16)


def _attention_specs(L, N, C, rows):
    block = pl.BlockSpec((rows, C), lambda i, *_: (i, 0))
    whole = pl.BlockSpec((N, C), lambda i, *_: (0, 0), pipeline_mode=pl.Buffered(1))
    return block, whole


def attention_forward(index, docs, query, key_all, value_all, rows, chunk):
    (L, C), N = query.shape, key_all.shape[0]
    block, whole = _attention_specs(L, N, C, rows)
    return pl.pallas_call(
        functools.partial(_attend_kernel, chunk=chunk, scaling=HEAD_DIM ** (-0.5)),
        out_shape=[jax.ShapeDtypeStruct((L, C), F32)] * 2,
        grid_spec=pltpu.PrefetchScalarGridSpec(
            num_scalar_prefetch=2, grid=(L // rows,), in_specs=[block, whole, whole], out_specs=[block, block]
        ),
        compiler_params=pltpu.CompilerParams(vmem_limit_bytes=VMEM_BYTES),
        cost_estimate=pl.CostEstimate(flops=4 * L * C * 1024, bytes_accessed=4 * N * C, transcendentals=L * 1024),
    )(index, docs, query, key_all, value_all)


def attention_backward(index, docs, query, grad, attended, logs, key_all, value_all, rows, chunk):
    (L, C), N = query.shape, key_all.shape[0]
    block, whole = _attention_specs(L, N, C, rows)
    return pl.pallas_call(
        functools.partial(_attend_back_kernel, chunk=chunk, scaling=HEAD_DIM ** (-0.5)),
        out_shape=[jax.ShapeDtypeStruct((L, C), BF16)] + [jax.ShapeDtypeStruct((N, C), BF16)] * 2,
        grid_spec=pltpu.PrefetchScalarGridSpec(
            num_scalar_prefetch=2,
            grid=(L // rows,),
            in_specs=[block, block, block, block, whole, whole],
            out_specs=[block, whole, whole],
            scratch_shapes=[pltpu.VMEM((N, C), F32)] * 2,
        ),
        compiler_params=pltpu.CompilerParams(vmem_limit_bytes=VMEM_BYTES),
        cost_estimate=pl.CostEstimate(flops=10 * L * C * 1024, bytes_accessed=8 * N * C, transcendentals=L * 1024),
    )(index, docs, query, grad, attended, logs, key_all, value_all)


def _pick_kernel(slot_ref, router_ref, x_ref, g_ref, xr_ref, gr_ref, gate_ref, *, slots, width):
    experts, group = slot_ref.shape
    logits = lax.dot_general(router_ref[...], x_ref[...], (((0,), (1,)), ((), ())), preferred_element_type=F32)
    powers = jnp.exp(logits - jnp.max(logits, axis=0, keepdims=True))
    chances = powers / jnp.sum(powers, axis=0, keepdims=True)
    row = lax.broadcasted_iota(jnp.int32, (slots, group), 0)
    picks = []
    for e in range(experts):
        hit = slot_ref[e : e + 1, :] == row
        gate = jnp.sum(jnp.where(hit, chances[e : e + 1, :], 0.0), axis=1, keepdims=True)
        gate_ref[e, 0] = jnp.broadcast_to(gate, (slots, 128))
        picks.append(jnp.where(hit, 1.0, 0.0).astype(BF16))
    pick = jnp.concatenate(picks, axis=0)
    for source, target in ((x_ref, xr_ref), (g_ref, gr_ref)):

        def step(i, _, source=source, target=target):
            cols = pl.ds(pl.multiple_of(i * width, width), width)
            rows = dot(pick, source[:, cols]).astype(BF16)
            for e in range(experts):
                target[e, 0, :, cols] = rows[e * slots : (e + 1) * slots]
            return 0

        lax.fori_loop(0, source.shape[1] // width, step, 0)


def pick_rows(slot, router, x, g, group, slots):
    EL, N = slot.shape
    D = x.shape[1]
    groups = N // group
    tokens = pl.BlockSpec((group, D), lambda i: (i, 0))
    picked = pl.BlockSpec((EL, 1, slots, D), lambda i: (0, i, 0, 0))
    rows = jax.ShapeDtypeStruct((EL, groups, slots, D), BF16)
    return pl.pallas_call(
        functools.partial(_pick_kernel, slots=slots, width=512),
        out_shape=[rows, rows, jax.ShapeDtypeStruct((EL, groups, slots, 128), F32)],
        grid=(groups,),
        in_specs=[
            pl.BlockSpec((EL, group), lambda i: (0, i)),
            pl.BlockSpec(router.shape, lambda i: (0, 0)),
            tokens,
            tokens,
        ],
        out_specs=[picked, picked, pl.BlockSpec((EL, 1, slots, 128), lambda i: (0, i, 0, 0))],
        compiler_params=pltpu.CompilerParams(vmem_limit_bytes=VMEM_BYTES),
        cost_estimate=pl.CostEstimate(
            flops=4 * EL * slots * N * D, bytes_accessed=8 * N * D, transcendentals=N * EXPERTS
        ),
    )(slot, router, x, g)


def _expert_kernel(x_ref, g_ref, gate_ref, w_ref, out_ref, entry_ref, dw_ref, gg_ref, *, width):
    x, g = x_ref[0], g_ref[0]
    gate = gate_ref[0][:, :1]
    gate_pre = dot(x, w_ref[0, 0])
    up = dot(x, w_ref[0, 1])
    back = dot(g, w_ref[0, 2])
    sig = jax.nn.sigmoid(gate_pre)
    act = gate_pre * sig
    inner = act * up
    gg_ref[0] = jnp.broadcast_to(jnp.sum(inner * back, axis=1, keepdims=True), gg_ref.shape[1:])
    inner_grad = back * gate
    gate_pre_grad = (inner_grad * up * sig * (1.0 + gate_pre * (1.0 - sig))).astype(BF16)
    up_grad = (inner_grad * act).astype(BF16)
    gated = (inner * gate).astype(BF16)
    first = pl.program_id(1) == 0

    def step(i, _):
        at = pl.ds(pl.multiple_of(i * width, width), width)
        out_ref[0, :, at] = dot(gated, w_ref[0, 2, at, :], LAST_DIM).astype(BF16)
        entry = dot(gate_pre_grad, w_ref[0, 0, at, :], LAST_DIM) + dot(up_grad, w_ref[0, 1, at, :], LAST_DIM)
        entry_ref[0, :, at] = entry.astype(BF16)
        parts = (
            dot(x_ref[0, :, at], gate_pre_grad, FIRST_DIM),
            dot(x_ref[0, :, at], up_grad, FIRST_DIM),
            dot(g_ref[0, :, at], gated, FIRST_DIM),
        )
        for k in range(3):

            @pl.when(first)
            def _(k=k):
                dw_ref[0, k, at, :] = parts[k]

            @pl.when(jnp.logical_not(first))
            def _(k=k):
                dw_ref[0, k, at, :] += parts[k]

        return 0

    lax.fori_loop(0, x_ref.shape[2] // width, step, 0)


def run_experts(x, g, gate, weights, chunk):
    EL, rows, D = x.shape
    FL = weights.shape[3]
    row_block = pl.BlockSpec((1, chunk, D), lambda e, c: (e, c, 0))
    thin = pl.BlockSpec((1, chunk, 128), lambda e, c: (e, c, 0))
    matrices = pl.BlockSpec((1, 3, D, FL), lambda e, c: (e, 0, 0, 0))
    return pl.pallas_call(
        functools.partial(_expert_kernel, width=512),
        out_shape=[
            jax.ShapeDtypeStruct(x.shape, BF16),
            jax.ShapeDtypeStruct(x.shape, BF16),
            jax.ShapeDtypeStruct(weights.shape, F32),
            jax.ShapeDtypeStruct((EL, rows, 128), F32),
        ],
        grid=(EL, rows // chunk),
        in_specs=[row_block, row_block, thin, matrices],
        out_specs=[row_block, row_block, matrices, thin],
        compiler_params=pltpu.CompilerParams(vmem_limit_bytes=VMEM_BYTES),
        cost_estimate=pl.CostEstimate(
            flops=18 * EL * rows * D * FL, bytes_accessed=8 * EL * rows * D + 18 * EL * D * FL, transcendentals=EL * rows * FL
        ),
    )(x, g, gate, weights)


def _spread_kernel(own_ref, slot_ref, gg_ref, out_ref, entry_ref, o_ref, e_ref, *, width):
    group, experts = slot_ref.shape
    slots = out_ref.shape[2]
    total = experts * slots
    D = out_ref.shape[3]
    lane = lax.broadcasted_iota(jnp.int32, (experts, total), 1)
    which = lax.broadcasted_iota(jnp.int32, (experts, total), 0)
    choose = jnp.where((lane >= which * slots) & (lane < (which + 1) * slots), 1.0, 0.0).astype(BF16)
    offset = lane[:1] - jnp.sum(jnp.where(lane >= (which + 1) * slots, slots, 0), axis=0, keepdims=True)
    mine = dot(slot_ref[...].astype(BF16), choose)
    pick = jnp.where(mine == offset.astype(F32), 1.0, 0.0).astype(BF16)
    column = lax.broadcasted_iota(jnp.int32, (slots, 128), 1)
    grads = [jnp.where(column == own_ref[0] + e, gg_ref[e, 0], 0.0).astype(BF16) for e in range(experts)]
    e_ref[:, pl.ds(D, 128)] = dot(pick, jnp.concatenate(grads, axis=0)).astype(BF16)

    def step(i, _):
        cols = pl.ds(pl.multiple_of(i * width, width), width)
        for source, target in ((out_ref, o_ref), (entry_ref, e_ref)):
            rows = jnp.concatenate([source[e, 0, :, cols] for e in range(experts)], axis=0)
            target[:, cols] = dot(pick, rows).astype(BF16)
        return 0

    lax.fori_loop(0, D // width, step, 0)


def spread_rows(own, slot, gate_grads, out_rows, entry_rows, group):
    N, EL = slot.shape
    _, groups, slots, D = out_rows.shape
    picked = pl.BlockSpec((EL, 1, slots, D), lambda i, *_: (0, i, 0, 0))
    return pl.pallas_call(
        functools.partial(_spread_kernel, width=512),
        out_shape=[jax.ShapeDtypeStruct((N, D), BF16), jax.ShapeDtypeStruct((N, D + 128), BF16)],
        grid_spec=pltpu.PrefetchScalarGridSpec(
            num_scalar_prefetch=1,
            grid=(groups,),
            in_specs=[
                pl.BlockSpec((group, EL), lambda i, *_: (i, 0)),
                pl.BlockSpec((EL, 1, slots, 128), lambda i, *_: (0, i, 0, 0)),
                picked,
                picked,
            ],
            out_specs=[
                pl.BlockSpec((group, D), lambda i, *_: (i, 0)),
                pl.BlockSpec((group, D + 128), lambda i, *_: (i, 0)),
            ],
        ),
        compiler_params=pltpu.CompilerParams(vmem_limit_bytes=VMEM_BYTES),
        cost_estimate=pl.CostEstimate(flops=4 * EL * slots * N * D, bytes_accessed=8 * N * D, transcendentals=0),
    )(own, slot, gate_grads, out_rows, entry_rows)


def body(
    hidden_in,
    out_grad,
    attn_gain,
    query_weight,
    key_weight,
    value_weight,
    out_weight,
    query_gain,
    key_gain,
    ffn_gain,
    router_weight,
    expert_weights,
    routes,
    doc_starts,
):
    U = lax.axis_size("uly")
    Z = lax.axis_size("blk")
    u = lax.axis_index("uly")
    z = lax.axis_index("blk")
    T, D = hidden_in.shape
    EL = expert_weights.shape[0]
    N = U * Z * T
    RW = query_weight.shape[0]
    move = (Slice if (U, Z, T, D) == (8, 4, 128, 2048) else General)(U, Z, T, D)
    C, L = move.C, move.L

    gain_rows = attn_gain.astype(F32)[:, None]
    own_weights = jnp.stack([query_weight, key_weight, value_weight], axis=1).astype(F32)
    scaled_rows = (own_weights * gain_rows[:, :, None]).astype(BF16)
    pack = jnp.concatenate([router_weight] + [g[:, None] for g in (ffn_gain, query_gain, key_gain)], axis=1)
    pack = jnp.pad(pack, ((0, 0), (0, 128 - pack.shape[1])))
    hidden = hidden_in.astype(F32)
    first_scale = norm_scale(hidden)
    first_rows, qkv_weight, out_rows, packed, routes_all = move.enter(
        (hidden * first_scale).astype(BF16), scaled_rows, out_weight, pack, routes.T
    )
    routes_all = routes_all.transpose(0, 1, 3, 2).reshape(N, -1)
    weight_router = packed[:, :EXPERTS]
    gain_ffn = packed[:, EXPERTS].astype(F32)
    head_gains = lax.dynamic_slice_in_dim(packed[:, EXPERTS + 1 : EXPERTS + 3], move.group * C, C, 0).astype(F32)
    gain_query, gain_key = head_gains[:, 0], head_gains[:, 1]
    qkv_pre = dot(first_rows, qkv_weight)
    query_pre, key_pre, value_pre = qkv_pre[:, :C], qkv_pre[:, C : 2 * C], qkv_pre[:, 2 * C :]
    squares = jnp.stack([jnp.sum(query_pre * query_pre, axis=1), jnp.sum(key_pre * key_pre, axis=1)])
    scales = lax.rsqrt(move.head_sum(squares.reshape(-1, 128)).reshape(2, L) / D + EPS)
    query_scale, key_scale = scales[0][:, None], scales[1][:, None]
    local = jnp.arange(L, dtype=jnp.int32)
    position = (local // T * move.block_step + move.first_block) * T + local % T
    cosine, sine = rotary_tables(position)
    cosine, sine = cosine[:, None, :], sine[:, None, :]

    def rotated(pre, scale, gain):
        split = (pre * scale * gain).reshape(L, C // HEAD_DIM, HEAD_DIM)
        return rotate_forward(split, cosine, sine).reshape(L, C).astype(BF16)

    query_rot = rotated(query_pre, query_scale, gain_query)
    key_all, value_all = move.sequence(
        rotated(key_pre, key_scale, gain_key), value_pre.astype(BF16), out_grad
    )
    index = jnp.stack([move.first_block, jnp.int32(move.block_step)]).astype(jnp.int32)
    chunk = min(512, N)
    attended, logs = attention_forward(index, doc_starts, query_rot, key_all, value_all, T, chunk)
    attended_low = attended.astype(BF16)
    mixed, upstream_all = move.heads_to_rows(dot(attended_low, out_rows).astype(BF16))
    residual = hidden + mixed.astype(F32)

    second_scale = norm_scale(residual)
    second_low = (residual * second_scale * gain_ffn).astype(BF16)
    probabilities = jax.nn.softmax(dot(second_low, weight_router), axis=-1)
    second_all = move.gather(second_low)

    group = min(512, N)
    groups = N // group
    slots = -(-(group // T * CAP) // 16) * 16
    rows = groups * slots
    own_first = u * EL
    own_experts = own_first + jnp.arange(EL, dtype=jnp.int32)
    chosen = jnp.any(routes_all[None] == own_experts[:, None, None], axis=2).reshape(EL, groups, group)
    before = jnp.arange(group)[:, None] < jnp.arange(group)[None, :]
    earlier = jnp.einsum("egs,st->egt", chosen.astype(BF16), before.astype(BF16), preferred_element_type=F32)
    slot = jnp.where(chosen, earlier.astype(jnp.int32), -1).reshape(EL, N)
    own_router = jnp.roll(weight_router, -own_first, axis=1)
    entry_in, upstream_in, gate_rows = pick_rows(slot, own_router, second_all, upstream_all, group, slots)
    out_rows_e, entry_rows, expert_grads, gate_grads = run_experts(
        entry_in.reshape(EL, rows, D),
        upstream_in.reshape(EL, rows, D),
        gate_rows.reshape(EL, rows, 128),
        expert_weights,
        min(8, groups) * slots,
    )
    split = (EL, groups, slots, D)
    out_part, entry_part = spread_rows(
        own_first.astype(jnp.int32)[None],
        slot.T,
        gate_grads.reshape(EL, groups, slots, 128),
        out_rows_e.reshape(split),
        entry_rows.reshape(split),
        group,
    )
    entry_sum = move.scatter_wide(entry_part).astype(F32)

    second_grad, prob_grad = entry_sum[:, :D], entry_sum[:, D : D + EXPERTS]
    logit_grad = (
        probabilities * (prob_grad - jnp.sum(probabilities * prob_grad, axis=1, keepdims=True))
    ).astype(BF16)
    second_grad = second_grad + dot(logit_grad, weight_router, LAST_DIM)
    upstream = out_grad.astype(F32)
    weighted = second_grad * gain_ffn
    inner_mean = jnp.mean(weighted * residual, axis=-1, keepdims=True)
    residual_grad = upstream + second_scale * weighted - residual * (second_scale**3) * inner_mean
    ffn_gain_part = jnp.sum(second_grad * residual * second_scale, axis=0)

    residual_rows = move.rows_to_heads(residual_grad.astype(BF16), out_part)
    out_weight_part = dot(attended_low, residual_rows, FIRST_DIM).astype(BF16)
    attended_grad = dot(residual_rows, out_rows, LAST_DIM).astype(BF16)
    dq, dk_part, dv_part = attention_backward(
        index, doc_starts, query_rot, attended_grad, attended, logs, key_all, value_all, T, chunk
    )
    dk, dv, out_weight_grad, out_sum = move.sequence_sums(dk_part, dv_part, out_weight_part)
    output = (residual + out_sum.astype(F32)).astype(BF16)

    def rotated_back(grad):
        return rotate_backward(grad.astype(F32).reshape(L, C // HEAD_DIM, HEAD_DIM), cosine, sine).reshape(L, C)

    query_up, key_up = rotated_back(dq), rotated_back(dk)
    inner_sums = jnp.stack(
        [jnp.sum(query_up * gain_query * query_pre, axis=1), jnp.sum(key_up * gain_key * key_pre, axis=1)]
    )
    inner_sums = move.head_sum_again(inner_sums.reshape(-1, 128)).reshape(2, L) / D

    def pre_grad(up, gain, pre, scale, mean):
        return (scale * (up * gain) - pre * (scale**3) * mean[:, None]).astype(BF16)

    pre_grads = jnp.concatenate(
        [
            pre_grad(query_up, gain_query, query_pre, query_scale, inner_sums[0]),
            pre_grad(key_up, gain_key, key_pre, key_scale, inner_sums[1]),
            dv,
        ],
        axis=1,
    )
    gain_parts = jnp.stack(
        [jnp.sum(query_up * query_pre * query_scale, axis=0), jnp.sum(key_up * key_pre * key_scale, axis=0)]
    )
    weight_part = dot(first_rows, pre_grads, FIRST_DIM).astype(BF16)
    first_part = dot(pre_grads, qkv_weight, LAST_DIM).astype(BF16)
    first_weighted, weight_sum, logit_grad_all, ffn_gain_grad, head_gain_grads = move.leave(
        first_part, weight_part, logit_grad, ffn_gain_part, gain_parts
    )
    own_columns = lax.dynamic_slice_in_dim(second_all, (u * Z + z) * RW, RW, 1)
    router_grad = dot(own_columns, logit_grad_all, FIRST_DIM)
    weight_sum = weight_sum.astype(F32)
    attn_gain_grad = jnp.sum(own_weights * weight_sum, axis=(1, 2))
    weight_grads = weight_sum * gain_rows[:, :, None]
    first_weighted = first_weighted.astype(F32)
    first_mean = jnp.mean(first_weighted * hidden, axis=-1, keepdims=True)
    hidden_grad = residual_grad + first_scale * first_weighted - hidden * (first_scale**3) * first_mean
    return (
        output,
        hidden_grad,
        attn_gain_grad,
        weight_grads[:, 0],
        weight_grads[:, 1],
        weight_grads[:, 2],
        out_weight_grad.astype(F32),
        head_gain_grads[0],
        head_gain_grads[1],
        ffn_gain_grad,
        router_grad,
        expert_grads,
    )


def solution(mesh):
    rows = P(ALL, None)
    flat = P(ALL)
    experts = P("uly", None, None, "blk")
    return jax.shard_map(
        body,
        mesh=mesh,
        in_specs=(rows, rows, flat, rows, rows, rows, rows, flat, flat, flat, rows, experts, rows, P()),
        out_specs=(rows, rows, flat, rows, rows, rows, rows, flat, flat, flat, rows, experts),
        check_vma=False,
    )
```

time: 1400 us -> 975 us (0.70)
  Pallas kernels: 368 us -> 834 us
  waiting for transfers between devices: 395 us -> 0 us
  matrix products: 294 us -> 33.8 us
  blocking collectives: 84.5 us -> 0 us
  local copies, waits for them, and re-layouts: 108 us -> 39.7 us
  other arithmetic: 116 us -> 59 us
  between operations: 16.8 us -> 1.6 us
    pallas_call x5 -> x13, Pallas kernels: 332 us -> 796 us  [the longest x1 88.2 us: scatter_all(): _comm(kernel, out, scratch, collective_id, ([ANY_SPACE], IN_VMEM))]
    dot_general x16 -> x1, matrix products: 249 us -> 0.21 us  [body(): jnp.einsum('egs,st->egt', chosen.astype(BF16), before.astype(BF16), prefe...]
    all_gather x6 -> x0, waiting for transfers between devices: 217 us -> none  [the longest x1 78.7 us: body(): lax.all_gather(jnp.stack([key_rot, value_pre.astype(BF16)]).reshape(2, U,...]
    unnamed x14 -> x0, waiting for transfers between devices: 147 us -> none
    another operation x6 -> x1, other arithmetic: 48.5 us -> 0.59 us  [body(): jnp.stack([move.first_block, jnp.int32(move.block_step)]).astype(jnp.int32)]
    unnamed x161 -> x89, local copies, waits for them, and re-layouts: 46.4 us -> 1.9 us
    unnamed x1 -> x0, blocking collectives: 39.7 us -> none
    convert_element_type x7 -> x2, local copies, waits for them, and re-layouts: 38 us -> 6.12 us  [body(): weight_sum = weight_sum.astype(F32)]
  transfers between devices with their start and end apart: 13 -> 0, of which waited for: 8 -> 0; matrix products, arithmetic and copies ran while one was open for 22% -> 0% of each run, Pallas kernels for 18% -> 0%
where the time goes in v2:
time: 975 us; the launch traced here: 968 us
  Pallas kernels  834 us (86%)
  other arithmetic  59 us (6%)
  local copies, waits for them, and re-layouts  39.7 us (4%)
  matrix products  33.8 us (3%)
    pallas_call x1, Pallas kernels, scatter_all(): _comm(kernel, out, scratch, collective_id, ([ANY_SPACE], IN_VMEM))  88.2 us
    pallas_call x1, Pallas kernels, gather_all(): _comm(_gather_all_kernel, out, scratch, collective_id, ([IN_VMEM], ANY_SP...  84.6 us
    pallas_call x1, Pallas kernels, column_gather(): _comm(kernel, outs, scratch, collective_id, specs)  83.2 us
    pallas_call x1, Pallas kernels, leave(): _comm(kernel, outs, scratch, collective_id, specs)(x, weights, *smalls)  81.6 us
    pallas_call x1, Pallas kernels, column_scatter(): _comm(kernel, outs, scratch, collective_id, specs, aliases={1: 1})(x, rows)  79.6 us
    pallas_call x1, Pallas kernels, enter(): _comm(kernel, outs, scratch, collective_id, specs)  77.8 us
    pallas_call x1, Pallas kernels, run_experts(): pl.pallas_call(functools.partial(_expert_kernel, width=512), out_shape=[j...  70 us
    pallas_call x1, Pallas kernels, key_value_sums(): _comm(kernel, outs, scratch, collective_id, specs)(dk, dv, out_part, x)  56.2 us

profile of v2, /device:TPU:13, one launch (start us, length us, event | category | flops | bytes accessed | tf_op | source)
XLA Modules:
  0.0 968.1 jit_solution(5104231912135599042)
XLA Ops:
  0.7 1.3 fusion.3
  2.5 2.0 fusion.4.refs_0_
  5.1 1.1 stack.55
  6.7 1.1 stack.56
  8.9 1.9 fusion.7
  10.8 1.7 reshape.316.refs_1_
  13.6 77.8 %shard_map.229 = (bf16[2,4,128,2048]{3,2,1,0:T(8,128)(2,1)}, bf16[4,2,4,64,768]{4,3,2,1,0:T(8,128)(2,1)}, bf16[4,64,2048]{2,1,0:T(8,128)(2,1)}, bf16[8,4,64,128]{3,2,1,0:T(8,128)(2,1)}, s32[8,4,8,128]{3,2,1,0:T(8,128)}) custom-call(bf16[128,2048]{1,0:T(8,128)(2,1)} %fusion.4.refs_0_, bf16[2,4,64,768]{3,2,1,0:T(8,128)(2,1)} %reshape.316.refs_1_, ...), custom_call_target="tpu_custom_call" | custom-call | bytes 100000000 | tf_op jit(solution)/shard_map/pallas_call | solution.py:438
  91.4 1.2 slice.124
  92.9 6.1 fusion.48
  100.3 16.2 %shard_map.230 = f32[16,128]{1,0:T(8,128)} custom-call(f32[16,128]{1,0:T(8,128)} %reshape.319.x_ref), custom_call_target="tpu_custom_call" | custom-call | bytes 100000000 | tf_op jit(solution)/shard_map/pallas_call | solution.py:459
  117.8 1.7 multiply_multiply_fusion
  119.5 2.8 reshape.321
  122.3 2.7 reshape.322
  125.0 6.4 slice_negate_fusion.2
  131.4 1.9 multiply_cosine_fusion
  133.7 3.6 maximum_multiply_fusion.1
  137.7 1.4 fusion.8
  140.0 49.5 %shard_map.231 = (bf16[4,1024,256]{2,1,0:T(8,128)(2,1)}, bf16[4,1024,256]{2,1,0:T(8,128)(2,1)}, bf16[32,128,2048]{2,1,0:T(8,128)(2,1)}) custom-call(bf16[1024,256]{1,0:T(8,128)(2,1)} %get-tuple-element.109.a_ref, bf16[1024,256]{1,0:T(8,128)(2,1)} %slice.187.b_ref, bf16[128,2048]{1,0:T(8,128)(2,1)} %x_ref.1), custom_call_target="tpu_custom_call" | custom-call | bytes 100000000 | tf_op jit(solution)/shard_map/pallas_call | solution.py:475
  190.1 16.2 %shard_map.232 = (f32[1024,256]{1,0:T(8,128)}, f32[1024,256]{1,0:T(8,128)}) custom-call(s32[2]{0:T(128)} %pad_add_fusion.index_ref, s32[5]{0:T(128)} %doc_ref.3, bf16[1024,256]{1,0:T(8,128)(2,1)} %get-tuple-element.110.q_ref, bf16[4096,256]{1,0:T(8,128)(2,1)} %bitcast.167, bf16[4096,256]{1,0:T(8,128)(2,1)} %bitcast.169), custom_call_target="tpu_custom_call" | custom-call | flops 1073741824 | bytes 4194304 | tf_op jit(solution)/shard_map/pallas_call | solution.py:1115
  206.3 4.5 convolution_convert_fusion
  210.8 79.6 %shard_map.233 = (bf16[128,2048]{1,0:T(8,128)(2,1)}, bf16[32,128,2048]{2,1,0:T(8,128)(2,1)}) custom-call(bf16[2,4,128,2048]{3,2,1,0:T(8,128)(2,1)} %bitcast.144, bf16[32,128,2048]{2,1,0:T(8,128)(2,1)} %get-tuple-element.53.g_ref), custom_call_target="tpu_custom_call", output_to_operand_aliasing={{1}: (1, {})} | custom-call | bytes 100000000 | tf_op jit(solution)/shard_map/pallas_call | solution.py:522
  290.4 1.3 multiply_reduce_fusion.7
  292.1 2.0 multiply_convert_fusion.1.x_ref
  294.2 84.6 %shard_map.234 = bf16[32,128,2048]{2,1,0:T(8,128)(2,1)} custom-call(bf16[128,2048]{1,0:T(8,128)(2,1)} %multiply_convert_fusion.1.x_ref), custom_call_target="tpu_custom_call" | custom-call | bytes 100000000 | tf_op jit(solution)/shard_map/pallas_call | solution.py:743
  378.9 1.4 dynamic-slice_maximum_fusion.router_ref
  380.8 1.9 copy.79
  382.8 2.8 copy.80.slot_ref
  385.6 47.3 %shard_map.235 = (bf16[8,8,80,2048]{3,2,1,0:T(8,128)(2,1)}, bf16[8,8,80,2048]{3,2,1,0:T(8,128)(2,1)}, f32[8,8,80,128]{3,2,1,0:T(8,128)}) custom-call(s32[8,4096]{1,0:T(8,128)} %copy.80.slot_ref, bf16[2048,64]{1,0:T(8,128)(2,1)} %dynamic-slice_maximum_fusion.router_ref, bf16[4096,2048]{1,0:T(8,128)(2,1)} %bitcast.145, bf16[4096,2048]{1,0:T(8,128)(2,1)} %bitcast.148), custom_call_target="tpu_custom_call" | custom-call | flops 21474836480 | bytes 67108864 | tf_op jit(solution)/shard_map/pallas_call | solution.py:1176
  432.9 70.0 %shard_map.236 = (bf16[8,640,2048]{2,1,0:T(8,128)(2,1)}, bf16[8,640,2048]{2,1,0:T(8,128)(2,1)}, f32[8,3,2048,256]{3,2,1,0:T(8,128)}, f32[8,640,128]{2,1,0:T(8,128)}) custom-call(bf16[8,640,2048]{2,1,0:T(8,128)(2,1)} %bitcast.203, bf16[8,640,2048]{2,1,0:T(8,128)(2,1)} %bitcast.204, f32[8,640,128]{2,1,0:T(8,128)} %bitcast.206, bf16[8,3,2048,256]{3,2,1,0:T(8,128)(2,1)} %w_ref.1), custom_call_target="tpu_custom_call" | custom-call | flops 48318382080 | bytes 159383552 | tf_op jit(solution)/shard_map/pallas_call | solution.py:1241
  502.9 41.1 %shard_map.237 = (bf16[4096,2048]{1,0:T(8,128)(2,1)}, bf16[4096,2176]{1,0:T(8,128)(2,1)}) custom-call(s32[1]{0:T(128)} %bitcast.17.own_ref, s32[4096,8]{1,0:T(8,128)} %bitcast.158, f32[8,8,80,128]{3,2,1,0:T(8,128)} %bitcast.205, bf16[8,8,80,2048]{3,2,1,0:T(8,128)(2,1)} %bitcast.201, bf16[8,8,80,2048]{3,2,1,0:T(8,128)(2,1)} %bitcast.202), custom_call_target="tpu_custom_call" | custom-call | flops 21474836480 | bytes 67108864 | tf_op jit(solution)/shard_map/pallas_call | solution.py:1288
  544.0 88.2 %shard_map.238 = bf16[128,2176]{1,0:T(8,128)(2,1)} custom-call(bf16[32,128,2176]{2,1,0:T(8,128)(2,1)} %bitcast.147), custom_call_target="tpu_custom_call" | custom-call | bytes 100000000 | tf_op jit(solution)/shard_map/pallas_call | solution.py:866
  632.2 2.2 convert_element_type.158
  635.1 1.0 multiply_reduce_fusion.10
  636.1 1.0 multiply_convert_fusion.2
  637.1 1.8 multiply_reduce_fusion.3
  638.9 1.2 fusion.44.r_ref
  640.1 83.2 %shard_map.239 = (bf16[2,4,128,2048]{3,2,1,0:T(8,128)(2,1)}, bf16[4,128,2048]{2,1,0:T(8,128)(2,1)}) custom-call(bf16[128,2048]{1,0:T(8,128)(2,1)} %fusion.44.r_ref, bf16[32,128,2048]{2,1,0:T(8,128)(2,1)} %bitcast.149), custom_call_target="tpu_custom_call" | custom-call | bytes 100000000 | tf_op jit(solution)/shard_map/pallas_call | solution.py:497
  723.4 4.6 convolution_convert_fusion.3
  728.0 2.1 convolution_convert_fusion.4.g_ref
  730.1 21.7 %shard_map.240 = (bf16[1024,256]{1,0:T(8,128)(2,1)}, bf16[4096,256]{1,0:T(8,128)(2,1)}, bf16[4096,256]{1,0:T(8,128)(2,1)}) custom-call(s32[2]{0:T(128)} %pad_add_fusion.index_ref, s32[5]{0:T(128)} %doc_ref.3, bf16[1024,256]{1,0:T(8,128)(2,1)} %get-tuple-element.110.q_ref, bf16[1024,256]{1,0:T(8,128)(2,1)} %convolution_convert_fusion.4.g_ref, ...), custom_call_target="tpu_custom_call" | custom-call | flops 2684354560 | bytes 8388608 | tf_op jit(solution)/shard_map/pallas_call | solution.py:1129
  751.7 56.2 %shard_map.241 = (bf16[1024,256]{1,0:T(8,128)(2,1)}, bf16[1024,256]{1,0:T(8,128)(2,1)}, bf16[64,2048]{1,0:T(8,128)(2,1)}, bf16[128,2048]{1,0:T(8,128)(2,1)}) custom-call(bf16[4,1024,256]{2,1,0:T(8,128)(2,1)} %bitcast.165, bf16[4,1024,256]{2,1,0:T(8,128)(2,1)} %bitcast.166, bf16[4,64,2048]{2,1,0:T(8,128)(2,1)} %bitcast.173, ...), custom_call_target="tpu_custom_call" | custom-call | bytes 100000000 | tf_op jit(solution)/shard_map/pallas_call | solution.py:605
  808.0 2.6 reshape.344
  810.5 2.5 reshape.343
  813.1 2.4 broadcast_multiply_fusion.1
  815.5 1.5 fusion.45
  817.1 1.1 pad_maximum_fusion.2
  818.3 1.5 fusion.46
  819.8 1.1 pad_maximum_fusion.1
  821.0 2.0 multiply_reduce_fusion.2
  824.2 20.8 %shard_map.242 = f32[16,128]{1,0:T(8,128)} custom-call(f32[16,128]{1,0:T(8,128)} %reshape.345.x_ref), custom_call_target="tpu_custom_call" | custom-call | bytes 100000000 | tf_op jit(solution)/shard_map/pallas_call | solution.py:459
  845.8 2.9 subtract_convert_fusion.1
  848.7 6.1 convolution_convert_fusion.2
  854.8 5.0 convolution_convert_fusion.1
  860.5 81.6 %shard_map.243 = (bf16[128,2048]{1,0:T(8,128)(2,1)}, bf16[8,64,768]{2,1,0:T(8,128)(2,1)}, bf16[8,4,64,128]{3,2,1,0:T(8,128)(2,1)}, f32[8,4,24,128]{3,2,1,0:T(8,128)}) custom-call(bf16[2,4,128,2048]{3,2,1,0:T(8,128)(2,1)} %bitcast.159, bf16[4,2,256,768]{3,2,1,0:T(8,128)(2,1)} %bitcast.164, bf16[64,128]{1,0:T(8,128)(2,1)} %reshape.348.refs_0_, ...), custom_call_target="tpu_custom_call" | custom-call | bytes 100000000 | tf_op jit(solution)/shard_map/pallas_call | solution.py:650
  942.1 2.4 reshape.354
  944.6 3.0 fusion.10
  947.5 3.6 reshape.357
  951.2 1.0 copy.92
  952.2 4.2 multiply_reduce_fusion
  956.4 2.6 reshape.356
  959.0 1.7 broadcast_multiply_fusion
  960.7 1.2 slice_bitcast_fusion
  962.2 1.9 fusion.2
  965.6 1.0 slice_reduce_fusion
  (138 shorter events, 16.3 us)
Async XLA Ops:
  0.6 7.7 copy-start.24
  2.5 2.0 copy-start.31
  5.1 5.7 copy-start.33
  7.8 4.7 copy-start.35
  7.8 4.8 copy-start.36
  7.9 4.9 copy-start.37
  7.9 5.0 copy-start.30
  99.0 40.1 %copy-start.1 = (f32[1024,768]{1,0:T(8,128)}, f32[1024,768]{1,0:T(8,128)S(1)}, u32[]{:S(2)}) copy-start(f32[1024,768]{1,0:T(8,128)S(1)} %fusion.48) | copy-start | bytes 9437188
  117.2 0.6 copy-start.28
  131.4 2.3 copy-start.13
  131.4 2.3 copy-start.14
  131.4 2.3 copy-start.15
  133.7 3.7 copy-start.11
  133.7 4.0 copy-start.5
  133.7 4.0 copy-start.6
  137.7 1.4 copy-start.7
  140.0 66.3 %copy-start.20 = (bf16[4,64,2048]{2,1,0:T(8,128)(2,1)S(1)}, bf16[4,64,2048]{2,1,0:T(8,128)(2,1)}, u32[]{:S(2)}) copy-start(bf16[4,64,2048]{2,1,0:T(8,128)(2,1)} %get-tuple-element.52) | copy-start | bytes 3145732
  210.8 79.6 %copy-start = (bf16[128,2048]{1,0:T(8,128)(2,1)S(1)}, bf16[128,2048]{1,0:T(8,128)(2,1)}, u32[]{:S(2)}) copy-start(bf16[128,2048]{1,0:T(8,128)(2,1)} %param.14) | copy-start | bytes 1572868
  210.8 81.0 %copy-start.4 = (bf16[8,4,64,128]{3,2,1,0:T(8,128)(2,1)S(1)}, bf16[8,4,64,128]{3,2,1,0:T(8,128)(2,1)}, u32[]{:S(2)}) copy-start(bf16[8,4,64,128]{3,2,1,0:T(8,128)(2,1)} %get-tuple-element.48) | copy-start | bytes 1572868
  294.2 86.0 %copy-start.27 = (s32[8,4,8,128]{3,2,1,0:T(8,128)S(1)}, s32[8,4,8,128]{3,2,1,0:T(8,128)}, u32[]{:S(2)}) copy-start(s32[8,4,8,128]{3,2,1,0:T(8,128)} %get-tuple-element.55) | copy-start | bytes 393220
  544.0 90.4 %copy-start.9 = (bf16[128,2048]{1,0:T(8,128)(2,1)S(1)}, bf16[128,2048]{1,0:T(8,128)(2,1)}, u32[]{:S(2)}) copy-start(bf16[128,2048]{1,0:T(8,128)(2,1)} %multiply_convert_fusion.1.x_ref) | copy-start | bytes 1572868
  632.2 4.9 copy-start.3
  632.2 6.7 copy-start.10
  640.1 83.2 %copy-start.16 = (f32[1024,256]{1,0:T(8,128)S(1)}, f32[1024,256]{1,0:T(8,128)}, u32[]{:S(2)}) copy-start(f32[1024,256]{1,0:T(8,128)} %get-tuple-element.51.o_ref) | copy-start | bytes 3145732
  723.4 4.6 copy-start.21
  723.4 4.6 copy-start.40
  808.0 5.1 copy-start.12
  818.2 2.7 copy-start.2
  818.2 2.7 copy-start.8
  818.2 2.7 copy-start.18
  818.2 2.7 copy-start.19
  821.0 24.8 %copy-start.29 = (f32[16,128]{1,0:T(8,128)S(1)}, f32[16,128]{1,0:T(8,128)}, u32[]{:S(2)}) copy-start(f32[16,128]{1,0:T(8,128)} %copy-done.28) | copy-start | bytes 24580
  824.2 24.4 %copy-start.39 = (bf16[2,4,128,2048]{3,2,1,0:T(8,128)(2,1)S(1)}, bf16[2,4,128,2048]{3,2,1,0:T(8,128)(2,1)}, u32[]{:S(2)}) copy-start(bf16[2,4,128,2048]{3,2,1,0:T(8,128)(2,1)} %get-tuple-element.46) | copy-start | bytes 12582916
  848.7 6.1 copy-start.41
  848.7 6.1 copy-start.42
  942.1 8.9 copy-start.22
  944.6 6.6 copy-start.23
  952.2 6.8 copy-start.34
  959.0 2.9 copy-start.17
  959.0 3.2 copy-start.25
  959.0 3.2 copy-start.32
  959.0 3.2 copy-start.38
  961.9 5.2 copy-start.26

commit v3 on v2

--- a/solution.py
+++ b/solution.py
@@ -21,6 +21,8 @@
 F32 = jnp.float32
 BF16 = jnp.bfloat16
 VMEM_BYTES = 56 * 1024 * 1024
+PICK_WIDTH = 512
+SPREAD_WIDTH = 2048
 
 
 def dot(a, b, dims=(((1,), (0,)), ((), ()))):
@@ -80,7 +82,7 @@
     ).wait_send()
 
 
-def _greet(u, z, planes, line=False, others=(), maybe=None):
+def _greet(u, z, planes, line=False, others=()):
     barrier = pltpu.get_barrier_semaphore()
     for bit in planes:
         pl.semaphore_signal(barrier, inc=1, device_id=(u ^ bit, z), device_id_type=MESH)
@@ -98,14 +100,6 @@
             pl.semaphore_signal(barrier, inc=1, device_id=(u, z + 1), device_id_type=MESH)
 
         count = count + jnp.where((z == 0) | (z == DEPTH - 1), 1, 2)
-    if maybe is not None:
-        to, real = maybe
-
-        @pl.when(real)
-        def _():
-            pl.semaphore_signal(barrier, inc=1, device_id=to, device_id_type=MESH)
-
-        count = count + jnp.where(real, 1, 0)
     pl.semaphore_wait(barrier, count)
 
 
@@ -127,7 +121,9 @@
     lax.fori_loop(0, rows // strip, step, 0)
 
 
-def _run(*parts):
+def _run(*parts, order=()):
+    for i in order:
+        next(parts[i])
     live = list(parts)
     while live:
         for part in list(live):
@@ -183,17 +179,16 @@
 def _plane_part(u, z, own, block, sems):
     p_send, p_recv, o_sem = sems
     here = (u, z)
-    for h in range(2):
-        _send(own(h), block(h, u), p_send.at[h, 0], p_recv.at[h, 0], (u ^ FIRST[h], z))
+    for way, bits in enumerate((FIRST, THEN)):
+        for h in range(2):
+            _send(own(h), block(h, u), p_send.at[h, way], p_recv.at[h, way], (u ^ bits[h], z))
     for h in range(2):
         pltpu.make_async_copy(own(h), block(h, u), o_sem.at[h]).start()
     for h in range(2):
         yield
         _expect(block(h, u ^ FIRST[h]), p_recv.at[h, 0], here)
-        to = (u ^ THEN[h], z)
-        _send(own(h), block(h, u), p_send.at[h, 1], p_recv.at[h, 1], to)
         near = block(h, u ^ FIRST[h])
-        _send(near, near, p_send.at[h, 2], p_recv.at[h, 2], to)
+        _send(near, near, p_send.at[h, 2], p_recv.at[h, 2], (u ^ THEN[h], z))
     yield
     for h in range(2):
         _expect(block(h, u ^ THEN[h]), p_recv.at[h, 1], here)
@@ -214,9 +209,10 @@
         return block(u, i)
 
     for i in range(4):
-        for h in range(2):
-            at = halves[h]
-            _send(source(i).at[at], block(u, i).at[at], p_send.at[i, h, 0], p_recv.at[i, h, 0], (u ^ FIRST[h], z))
+        for way, bits in enumerate((FIRST, THEN)):
+            for h in range(2):
+                at = block(u, i).at[halves[h]]
+                _send(at, at, p_send.at[i, h, way], p_recv.at[i, h, way], (u ^ bits[h], z))
         _send(source(i), block(u, i), c_send.at[i, 0], c_recv.at[i, 0], (u ^ 1, z))
 
     def share(i):
@@ -233,9 +229,7 @@
             at = halves[h]
             near = block(u ^ FIRST[h], i).at[at]
             _expect(near, p_recv.at[i, h, 0], here)
-            to = (u ^ THEN[h], z)
-            _send(source(i).at[at], block(u, i).at[at], p_send.at[i, h, 1], p_recv.at[i, h, 1], to)
-            _send(near, near, p_send.at[i, h, 2], p_recv.at[i, h, 2], to)
+            _send(near, near, p_send.at[i, h, 2], p_recv.at[i, h, 2], (u ^ THEN[h], z))
         if i > 0:
             share(i - 1)
     yield
@@ -257,9 +251,11 @@
     p_buf, q_buf = bufs
     load, p_send, p_recv, q_send, q_recv = sems
     here = (u, z)
+    for j in (1, 0):
+        for h in range(2):
+            bit = (THEN[h], 6)[j]
+            _send(source(h, u ^ bit), p_buf.at[h, j], p_send.at[h, j], p_recv.at[h, j], (u ^ THEN[h], z))
     for h in range(2):
-        for j, bit in enumerate((THEN[h], 6)):
-            _send(source(h, u ^ bit), p_buf.at[h, j], p_send.at[h, j], p_recv.at[h, j], (u ^ THEN[h], z))
         for j, bit in enumerate((0, FIRST[h])):
             pltpu.make_async_copy(source(h, u ^ bit), work.at[h, j], load.at[h, j]).start()
     for h in range(2):
@@ -269,9 +265,10 @@
         _expect(p_buf.at[h, 1], p_recv.at[h, 1], here)
         _accumulate(work.at[h, 1], p_buf.at[h, 1], rows)
         _send(work.at[h, 1], q_buf.at[h], q_send.at[h], q_recv.at[h], (u ^ FIRST[h], z))
+    yield
+    for h in range(2):
         _expect(p_buf.at[h, 0], p_recv.at[h, 0], here)
         _accumulate(work.at[h, 0], p_buf.at[h, 0], rows)
-    yield
     for h in range(2):
         _expect(q_buf.at[h], q_recv.at[h], here)
         _accumulate(work.at[h, 0], q_buf.at[h], rows)
@@ -326,6 +323,8 @@
     )
 
 
+ENTER_ORDER = (0, 2, 1, 0, 2, 1, 0, 2, 0, 2)
+LEAVE_ORDER = (0, 1, 2, 1, 2, 1, 0, 0, 1, 0, 1, 1)
 LINE_SEMS = [DMA((2, 4)), DMA((4,)), DMA((4,)), DMA((4,)), DMA]
 PLANE_SEMS = [DMA((2, 3)), DMA((2, 3)), DMA((2,))]
 PLANE_SUM_SEMS = [DMA((2, 2)), DMA((2, 2)), DMA((2, 2)), DMA((2,)), DMA((2,))]
@@ -360,82 +359,58 @@
     return [DMA((n,)), DMA((n, 4)), DMA((n, 4)), DMA((n, 8)), DMA((n, 8))]
 
 
-def enter(rows, weights, out_weight, smalls, collective_id):
+def enter(rows, weights, smalls, collective_id):
+    R, C = weights.shape[1], weights.shape[2] // 8
+    held = (2, 4, R, 3 * C)
     n = len(smalls)
 
     def kernel(*refs):
-        x_ref, w_ref, o_ref = refs[:3]
-        small_in = refs[3 : 3 + n]
-        x_out, w_out, o_out = refs[3 + n : 6 + n]
-        small_out = refs[6 + n : 6 + 2 * n]
-        w_buf, o_buf = refs[6 + 2 * n : 8 + 2 * n]
-        sems = refs[8 + 2 * n :]
-        line, plane_w, plane_o, (w_own, w_send, w_recv, o_own, o_send, o_recv) = sems[:5], sems[5:8], sems[8:11], sems[11:17]
-        small_sems = sems[17:]
+        x_ref, w_ref = refs[:2]
+        small_in = refs[2 : 2 + n]
+        x_out, w_out = refs[2 + n : 4 + n]
+        small_out = refs[4 + n : 4 + 2 * n]
+        w_buf, w_send, w_recv = refs[4 + 2 * n : 7 + 2 * n]
+        sems = refs[7 + 2 * n :]
         u, z = lax.axis_index("uly"), lax.axis_index("blk")
         here, core, chip = (u, z), u % 2, u // 2
-        turned = (2 * z + core, chip)
-        away = chip != z
         column = _column_peers(u, z)
-        _greet(u, z, range(1, 8), others=[to for to, c, k in column if k], maybe=(turned, away))
+        _greet(u, z, range(1, 8), others=[to for to, c, k in column if k])
 
         def weight_part():
-            own = pltpu.make_async_copy(w_ref.at[core, z], w_buf.at[core, z], w_own)
-            own.start()
+            def cut(j, c, level):
+                return w_ref.at[j, :, pl.ds(pl.multiple_of((2 * level + c) * C, C), C)]
+
+            def slot(j, c, level):
+                return w_buf.at[c, level, :, pl.ds(j * C, C)]
+
             for i, (to, c, k) in enumerate(column):
-                _send(w_ref.at[core ^ c, z ^ k], w_buf.at[core, z], w_send.at[i], w_recv.at[i], to)
+                for j in range(3):
+                    _send(cut(j, core ^ c, z ^ k), slot(j, core, z), w_send.at[i, j], w_recv.at[i, j], to)
+            for j in range(3):
+                slot(j, core, z)[...] = cut(j, core, z)[...]
             yield
-            own.wait()
             for i, (to, c, k) in enumerate(column):
-                _expect(w_buf.at[core ^ c, z ^ k], w_recv.at[i], here)
-            yield from _plane_part(u, z, lambda h: w_buf.at[h], lambda h, v: w_out.at[v // 2, h], plane_w)
+                for j in range(3):
+                    _expect(slot(j, core ^ c, z ^ k), w_recv.at[i, j], here)
+            yield from _plane_part(u, z, lambda h: w_buf.at[h], lambda h, v: w_out.at[v // 2, h], sems[:3])
             for i, (to, c, k) in enumerate(column):
-                _sent(w_ref.at[core ^ c, z ^ k], w_send.at[i], here)
-
-        def out_part():
-            @pl.when(away)
-            def _():
-                _send(o_ref, o_buf, o_send, o_recv, turned)
-
-            @pl.when(jnp.logical_not(away))
-            def _():
-                pltpu.make_async_copy(o_ref, o_buf, o_own).start()
-
-            yield
-            yield
-
-            @pl.when(away)
-            def _():
-                _expect(o_buf, o_recv, here)
-
-            @pl.when(jnp.logical_not(away))
-            def _():
-                pltpu.make_async_copy(o_ref, o_buf, o_own).wait()
-
-            half = out_weight.shape[0] // 2
-            cut = [pl.ds(h * half, half) for h in range(2)]
-            yield from _plane_part(u, z, lambda h: o_buf.at[cut[h]], lambda h, v: o_out.at[v // 2, cut[h]], plane_o)
-
-            @pl.when(away)
-            def _():
-                _sent(o_ref, o_send, here)
+                for j in range(3):
+                    _sent(cut(j, core ^ c, z ^ k), w_send.at[i, j], here)
 
         _run(
             weight_part(),
-            _small_part(u, z, small_in, small_out, small_sems),
-            _line_part(u, z, x_ref, lambda c, level: x_out.at[c, level], line),
-            out_part(),
+            _small_part(u, z, small_in, small_out, sems[8:]),
+            _line_part(u, z, x_ref, lambda c, level: x_out.at[c, level], sems[3:8]),
+            order=ENTER_ORDER,
         )
 
     outs = [
         jax.ShapeDtypeStruct((2, 4) + rows.shape, rows.dtype),
-        jax.ShapeDtypeStruct((4,) + weights.shape, weights.dtype),
-        jax.ShapeDtypeStruct((4,) + out_weight.shape, out_weight.dtype),
+        jax.ShapeDtypeStruct((4,) + held, weights.dtype),
     ] + [jax.ShapeDtypeStruct((8, 4) + x.shape, x.dtype) for x in smalls]
-    scratch = [pltpu.VMEM(weights.shape, BF16), pltpu.VMEM(out_weight.shape, BF16)]
-    scratch += LINE_SEMS + PLANE_SEMS * 2 + [DMA, DMA((7,)), DMA((7,)), DMA, DMA, DMA] + _small_sems(n)
-    specs = ([IN_VMEM, IN_VMEM, ANY_SPACE] + [IN_VMEM] * n, [ANY_SPACE] * len(outs))
-    return _comm(kernel, outs, scratch, collective_id, specs)(rows, weights, out_weight, *smalls)
+    scratch = [pltpu.VMEM(held, BF16), DMA((7, 3)), DMA((7, 3))] + PLANE_SEMS + LINE_SEMS + _small_sems(n)
+    specs = ([IN_VMEM, IN_VMEM] + [IN_VMEM] * n, [ANY_SPACE] * len(outs))
+    return _comm(kernel, outs, scratch, collective_id, specs)(rows, weights, *smalls)
 
 
 def column_sum(x, collective_id):
@@ -475,26 +450,27 @@
     return _comm(kernel, outs, PLANE_SEMS + LINE_SEMS, collective_id, specs)(first, second, rows)
 
 
-def column_gather(rows, x, collective_id):
+def column_gather(rows, slot, out_rows, collective_id):
     T, D = rows.shape
-
-    def kernel(r_ref, x_ref, r_out, x_out, *refs):
+    EL, _, slots, _ = out_rows.shape
+
+    def kernel(r_ref, slot_ref, rows_ref, r_out, x_out, *refs):
         u, z = lax.axis_index("uly"), lax.axis_index("blk")
         _greet(u, z, (1, 2, 4), line=True)
         order = _line_order(z)
 
-        def keep(i, work):
-            x_out[order[i]] = work[i, 0]
+        def keep(i, part):
+            x_out[order[i]] = part[...]
 
         _run(
             _line_part(u, z, r_ref, lambda c, level: r_out.at[c, level], refs[-5:]),
-            _tree_sum_part(u, z, lambda who, level: x_ref.at[who * DEPTH + level], order, T, refs[:-5], keep),
+            _spread_part(u, z, slot_ref, rows_ref, None, order, refs[:-5], keep),
         )
 
     outs = [jax.ShapeDtypeStruct((2, 4, T, D), BF16), jax.ShapeDtypeStruct((4, T, D), BF16)]
-    specs = ([IN_VMEM, ANY_SPACE], [ANY_SPACE, IN_VMEM])
-    scratch = _tree_sum_scratch(T, D) + LINE_SEMS
-    return _comm(kernel, outs, scratch, collective_id, specs)(rows, x.reshape(32, T, D))
+    specs = ([IN_VMEM, IN_VMEM, ANY_SPACE], [ANY_SPACE, IN_VMEM])
+    scratch = _spread_scratch(T, D, (EL, slots, D)) + LINE_SEMS
+    return _comm(kernel, outs, scratch, collective_id, specs)(rows, slot, out_rows)
 
 
 def _line_sum_scratch(T, D):
@@ -527,38 +503,19 @@
     return [pltpu.VMEM((2, 2, rows, cols), BF16), pltpu.VMEM((2, 2, rows, cols), BF16), pltpu.VMEM((2, rows, cols), BF16)]
 
 
-def key_value_sums(dk, dv, out_part, x, collective_id):
-    T = x.shape[1]
+def key_value_sums(dk, dv, x, collective_id):
+    T, D = x.shape[1:]
     L, C = dk.shape[1:]
-    R, D = out_part.shape[1:]
-    half = R // 2
-
-    def kernel(
-        k_ref, v_ref, w_ref, x_ref, k_out, v_out, w_out, x_out, work, p_buf, q_buf, o_work, op_buf, oq_buf, x_work, z_buf, *sems
-    ):
+
+    def kernel(k_ref, v_ref, x_ref, k_out, v_out, x_out, work, p_buf, q_buf, x_work, z_buf, *sems):
         u, z = lax.axis_index("uly"), lax.axis_index("blk")
-        here, core, chip = (u, z), u % 2, u // 2
-        turned = (2 * z + core, chip)
-        away = chip != z
-        _greet(u, z, (2, 4), line=True, maybe=(turned, away))
-        t_send, t_recv, load, z_send, z_recv = sems[10:15]
+        _greet(u, z, (2, 4), line=True)
+        load, z_send, z_recv = sems[5:]
         order = tuple(reversed(_line_order(z)))
 
         def finish():
             k_out[...] = work[0, 0]
             v_out[...] = work[1, 0]
-
-        def turn():
-            for h in range(2):
-                rows = pl.ds(h * half, half)
-
-                @pl.when(away)
-                def _(h=h, rows=rows):
-                    _send(o_work.at[h, 0], w_out.at[rows], t_send.at[h], t_recv.at[h], turned)
-
-                @pl.when(jnp.logical_not(away))
-                def _(h=h, rows=rows):
-                    w_out[rows, :] = o_work[h, 0]
 
         def line():
             copies = [pltpu.make_async_copy(x_ref.at[order[i]], x_work.at[i], load.at[i]) for i in range(4)]
@@ -571,45 +528,28 @@
                 yield
             x_out[...] = x_work[3]
             for i in range(3):
-                _sent(x_work.at[i], z_send.at[i], here)
+                _sent(x_work.at[i], z_send.at[i], (u, z))
 
         _run(
-            _plane_sum_part(
-                u,
-                z,
-                lambda h, v: w_ref.at[v // 2, pl.ds(h * half, half)],
-                o_work,
-                (op_buf, oq_buf),
-                sems[5:10],
-                half,
-                turn,
-            ),
             _plane_sum_part(
                 u, z, lambda h, v: (k_ref, v_ref)[h].at[v // 2], work, (p_buf, q_buf), sems[:5], L, finish
             ),
             line(),
+            order=(0, 1, 0, 0),
         )
 
-        @pl.when(away)
-        def _():
-            for h in range(2):
-                rows = pl.ds(h * half, half)
-                _expect(w_out.at[rows], t_recv.at[h], here)
-                _sent(o_work.at[h, 0], t_send.at[h], here)
-
-    outs = [jax.ShapeDtypeStruct((L, C), BF16)] * 2 + [jax.ShapeDtypeStruct((R, D), BF16), jax.ShapeDtypeStruct((T, D), BF16)]
-    scratch = _plane_sum_scratch(L, C) + _plane_sum_scratch(half, D)
-    scratch += [pltpu.VMEM((4, T, D), BF16), pltpu.VMEM((2, 4, T, D), BF16)] + PLANE_SUM_SEMS * 2
-    scratch += [DMA((2,)), DMA((2,)), DMA((4,)), DMA((4,)), DMA((2, 4))]
-    specs = ([ANY_SPACE] * 4, [IN_VMEM] * 4)
-    return _comm(kernel, outs, scratch, collective_id, specs)(dk, dv, out_part, x)
+    outs = [jax.ShapeDtypeStruct((L, C), BF16)] * 2 + [jax.ShapeDtypeStruct((T, D), BF16)]
+    scratch = _plane_sum_scratch(L, C) + [pltpu.VMEM((4, T, D), BF16), pltpu.VMEM((2, 4, T, D), BF16)]
+    scratch += PLANE_SUM_SEMS + [DMA((4,)), DMA((4,)), DMA((2, 4))]
+    specs = ([ANY_SPACE] * 3, [IN_VMEM] * 3)
+    return _comm(kernel, outs, scratch, collective_id, specs)(dk, dv, x)
 
 
 def leave(x, weights, smalls, collective_id):
     n = len(smalls)
     T, D = x.shape[2:]
     rows, W = weights.shape[2:]
-    R = rows // 4
+    R, C = rows // 4, W // 3
 
     def kernel(x_ref, w_ref, *refs):
         small_in, (o_ref, w_out), small_out = refs[:n], refs[n : n + 2], refs[n + 2 : 2 * n + 2]
@@ -625,56 +565,141 @@
         def finish():
             o_ref[...] = work[3]
 
-        def cut(c, level):
-            return w_work.at[c, 0, pl.ds(pl.multiple_of(level * R, R), R)]
+        def cut(j, c, level):
+            return w_work.at[c, 0, pl.ds(pl.multiple_of(level * R, R), R), pl.ds(j * C, C)]
+
+        def slot(j, g):
+            return w_out.at[j, :, pl.ds(pl.multiple_of(g * C, C), C)]
 
         def deal():
             for i, (to, c, k) in enumerate(column):
-                _send(cut(core ^ c, z ^ k), w_out.at[group], t_send.at[i], t_recv.at[i], to)
-            w_out[group] = cut(core, z)[...]
+                for j in range(3):
+                    _send(cut(j, core ^ c, z ^ k), slot(j, group), t_send.at[i, j], t_recv.at[i, j], to)
+            for j in range(3):
+                slot(j, group)[...] = cut(j, core, z)[...]
 
         _run(
             _plane_sum_part(u, z, lambda h, v: w_ref.at[v // 2, h], w_work, (wp_buf, wq_buf), sems[5:10], rows, deal),
             _line_sum_part(u, z, lambda c, level: x_ref.at[c, level], work, (c_buf, z_buf), sems[:5], T, finish),
             _small_part(u, z, small_in, small_out, sems[12:]),
+            order=LEAVE_ORDER,
         )
         for i, (to, c, k) in enumerate(column):
-            _expect(w_out.at[2 * (z ^ k) + (core ^ c)], t_recv.at[i], here)
-            _sent(cut(core ^ c, z ^ k), t_send.at[i], here)
-
-    outs = [jax.ShapeDtypeStruct((T, D), BF16), jax.ShapeDtypeStruct((8, R, W), BF16)]
+            for j in range(3):
+                _expect(slot(j, 2 * (z ^ k) + (core ^ c)), t_recv.at[i, j], here)
+                _sent(cut(j, core ^ c, z ^ k), t_send.at[i, j], here)
+
+    outs = [jax.ShapeDtypeStruct((T, D), BF16), jax.ShapeDtypeStruct((3, R, 8 * C), BF16)]
     outs += [jax.ShapeDtypeStruct((8, 4) + x.shape, x.dtype) for x in smalls]
     scratch = _line_sum_scratch(T, D) + _plane_sum_scratch(rows, W) + LINE_SUM_SEMS + PLANE_SUM_SEMS
-    scratch += [DMA((7,)), DMA((7,))] + _small_sems(n)
+    scratch += [DMA((7, 3)), DMA((7, 3))] + _small_sems(n)
     specs = ([ANY_SPACE] * 2 + [IN_VMEM] * n, [IN_VMEM] * 2 + [ANY_SPACE] * n)
     return _comm(kernel, outs, scratch, collective_id, specs)(x, weights, *smalls)
 
 
-def _gather_all_kernel(x_ref, o_ref, own_sem, z_send, z_recv, p_send, p_recv, c_send, c_recv):
+class _Jobs:
+    def __init__(self, load, compute):
+        self.load, self.compute = load, compute
+        self.queue, self.count, self.ready = [], 0, None
+
+    def add(self, *jobs):
+        self.queue += jobs
+
+    def _next(self):
+        if not self.queue:
+            return None
+        job = (self.count, self.queue.pop(0))
+        self.count += 1
+        self.load(*job, True)
+        return job
+
+    def run(self, number=1):
+        for _ in range(number):
+            now = self.ready or self._next()
+            if now is None:
+                return
+            self.ready = self._next()
+            self.load(*now, False)
+            self.compute(*now)
+
+
+def _gather_pick_kernel(
+    x_ref, g_ref, slot_ref, router_ref, o_ref, xr_ref, gr_ref, gate_ref, pick, in_buf, out_buf, in_sem, out_sem, *sems, width
+):
+    own_sem, z_send, z_recv, p_send, p_recv, c_send, c_recv = sems
     u, z = lax.axis_index("uly"), lax.axis_index("blk")
-    depth = DEPTH
-    half = x_ref.shape[0] // 2
+    core = u % 2
+    T, D = x_ref.shape
+    experts, group = slot_ref.shape[1:]
+    slots = out_buf.shape[2]
+    half = T // 2
     halves = (pl.ds(0, half), pl.ds(half, half))
     here = (u, z)
     _greet(u, z, (1, 2, 4), line=True)
-    own = pltpu.make_async_copy(x_ref, o_ref.at[u * depth + z], own_sem)
+    own = pltpu.make_async_copy(x_ref, o_ref.at[u * DEPTH + z], own_sem)
     own.start()
     order = _line_order(z)
 
     def block(who, level):
-        return o_ref.at[who * depth + level]
+        return o_ref.at[who * DEPTH + level]
 
     def part(who, level, h):
-        return o_ref.at[who * depth + level, halves[h]]
-
-    first, then = (2, 4), (4, 2)
+        return o_ref.at[who * DEPTH + level, halves[h]]
+
+    def load(n, job, start):
+        source, level, which = job[:3]
+        ref = g_ref if source == "g" else o_ref
+        for p in range(4):
+            copy = pltpu.make_async_copy(
+                ref.at[(2 * p + which) * DEPTH + level], in_buf.at[n % 2, pl.ds(p * T, T)], in_sem.at[n % 2, p]
+            )
+            copy.start() if start else copy.wait()
+
+    def out_copy(n, target, at):
+        return pltpu.make_async_copy(out_buf.at[n % 2], target.at[:, at], out_sem.at[n % 2])
+
+    sent = {}
+
+    def compute(n, job):
+        source, level, which = job
+        at = 2 * level + which
+        rows_in, rows_out = in_buf.at[n % 2], out_buf.at[n % 2]
+        row = lax.broadcasted_iota(jnp.int32, (slots, group), 0)
+        if source == "g":
+            picks = [jnp.where(slot_ref[at, e : e + 1, :] == row, 1.0, 0.0).astype(BF16) for e in range(experts)]
+            pick[at] = jnp.concatenate(picks, axis=0)
+        else:
+            logits = lax.dot_general(
+                router_ref[...], rows_in[...], (((0,), (1,)), ((), ())), preferred_element_type=F32
+            )
+            powers = jnp.exp(logits - jnp.max(logits, axis=0, keepdims=True))
+            chances = powers / jnp.sum(powers, axis=0, keepdims=True)
+            for e in range(experts):
+                gates = jnp.where(slot_ref[at, e : e + 1, :] == row, chances[e : e + 1, :], 0.0)
+                gate_ref[e, at] = jnp.broadcast_to(jnp.sum(gates, axis=1, keepdims=True), (slots, 128))
+        if n >= 2:
+            sent.pop(n - 2).wait()
+
+        def step(i, _):
+            cols = pl.ds(pl.multiple_of(i * width, width), width)
+            rows = dot(pick[at], rows_in[:, cols]).astype(BF16)
+            for e in range(experts):
+                rows_out[e, :, cols] = rows[e * slots : (e + 1) * slots]
+            return 0
+
+        lax.fori_loop(0, D // width, step, 0)
+        sent[n] = out_copy(n, gr_ref if source == "g" else xr_ref, at)
+        sent[n].start()
+
+    jobs = _Jobs(load, compute)
+    jobs.add(*[("g", level, c) for level in range(4) for c in range(2)])
 
     def along(level, source, step):
         @pl.when((z > 0) & (level >= z))
         def _():
             step(source, 0, level, (u, z - 1))
 
-        @pl.when((z < depth - 1) & (level <= z))
+        @pl.when((z < DEPTH - 1) & (level <= z))
         def _():
             step(source, 1, level, (u, z + 1))
 
@@ -684,131 +709,288 @@
     def gone(source, way, level, to):
         _sent(source, z_send.at[way, level], here)
 
-    def across(level, source):
+    sources = [x_ref] + [block(u, order[i]) for i in range(1, 4)]
+
+    def arrive(i):
+        level = order[i]
+        if i:
+            _expect(block(u, level), z_recv.at[level], here)
+        along(level, sources[i], go)
+        for way, bits in enumerate((FIRST, THEN)):
+            for h in range(2):
+                cut = sources[i].at[halves[h]]
+                _send(cut, part(u, level, h), p_send.at[level, h, way], p_recv.at[level, h, way], (u ^ bits[h], z))
+        _send(sources[i], block(u, level), c_send.at[level, 0], c_recv.at[level, 0], (u ^ 1, z))
+
+    def onward(i):
+        level = order[i]
         for h in range(2):
-            _send(
-                source.at[halves[h]], part(u, level, h), p_send.at[level, h, 0], p_recv.at[level, h, 0], (u ^ first[h], z)
-            )
-        _send(source, block(u, level), c_send.at[level, 0], c_recv.at[level, 0], (u ^ 1, z))
-
-    def onward(level, source):
+            near = part(u ^ FIRST[h], level, h)
+            _expect(near, p_recv.at[level, h, 0], here)
+            _send(near, near, p_send.at[level, h, 2], p_recv.at[level, h, 2], (u ^ THEN[h], z))
+
+    def share(i):
+        level = order[i]
         for h in range(2):
-            _expect(part(u ^ first[h], level, h), p_recv.at[level, h, 0], here)
-            to = (u ^ then[h], z)
-            _send(source.at[halves[h]], part(u, level, h), p_send.at[level, h, 1], p_recv.at[level, h, 1], to)
-            _send(
-                part(u ^ first[h], level, h),
-                part(u ^ first[h], level, h),
-                p_send.at[level, h, 2],
-                p_recv.at[level, h, 2],
-                to,
-            )
-
-    def share(level):
-        for h in range(2):
-            _expect(part(u ^ then[h], level, h), p_recv.at[level, h, 1], here)
+            _expect(part(u ^ THEN[h], level, h), p_recv.at[level, h, 1], here)
             _expect(part(u ^ 6, level, h), p_recv.at[level, h, 2], here)
-        for i, bit in enumerate((2, 4, 6)):
-            _send(block(u ^ bit, level), block(u ^ bit, level), c_send.at[level, i + 1], c_recv.at[level, i + 1], (u ^ 1, z))
-
-    sources = [x_ref] + [block(u, order[i]) for i in range(1, 4)]
-    along(z, x_ref, go)
-    across(z, x_ref)
-    for i in range(1, 4):
-        _expect(block(u, order[i]), z_recv.at[order[i]], here)
-        along(order[i], sources[i], go)
-        across(order[i], sources[i])
-        onward(order[i - 1], sources[i - 1])
-        if i >= 2:
-            share(order[i - 2])
-    onward(order[3], sources[3])
-    share(order[2])
-    share(order[3])
+        for k, bit in enumerate((2, 4, 6)):
+            ref = block(u ^ bit, level)
+            _send(ref, ref, c_send.at[level, k + 1], c_recv.at[level, k + 1], (u ^ 1, z))
+        jobs.add(("x", level, core))
+
+    def received(i):
+        level = order[i]
+        for k, bit in enumerate((0, 2, 4, 6)):
+            _expect(block(u ^ 1 ^ bit, level), c_recv.at[level, k], here)
+        jobs.add(("x", level, 1 - core))
+
+    arrive(0)
+    jobs.run(2)
+    onward(0)
+    jobs.run(1)
+    arrive(1)
+    jobs.run(2)
+    own.wait()
+    share(0)
+    jobs.run(2)
+    onward(1)
+    arrive(2)
+    received(0)
+    jobs.run(2)
+    arrive(3)
+    share(1)
+    received(1)
+    jobs.run(1)
+    onward(2)
+    jobs.run(2)
+    share(2)
+    received(2)
+    jobs.run(1)
+    onward(3)
+    jobs.run(2)
+    share(3)
+    received(3)
+    jobs.run(16)
     for i in range(4):
         level = order[i]
         along(level, sources[i], gone)
         for h in range(2):
             for k in range(3):
                 _sent(part(u, level, h), p_send.at[level, h, k], here)
-        for k, bit in enumerate((0, 2, 4, 6)):
+        for k in range(4):
             _sent(block(u, level), c_send.at[level, k], here)
-            _expect(block(u ^ 1 ^ bit, level), c_recv.at[level, k], here)
-    own.wait()
-
-
-def gather_all(x, collective_id):
+    for copy in sent.values():
+        copy.wait()
+
+
+def gather_pick(x, g_all, slot, router, slots, collective_id):
     T, D = x.shape
-    scratch = [DMA, DMA((2, 4)), DMA((4,)), DMA((4, 2, 3)), DMA((4, 2, 3)), DMA((4, 4)), DMA((4, 4))]
-    out = jax.ShapeDtypeStruct((32, T, D), x.dtype)
-    return _comm(_gather_all_kernel, out, scratch, collective_id, ([IN_VMEM], ANY_SPACE))(x).reshape(32 * T, D)
-
-
-def _tree_sum_part(u, z, source, order, T, refs, level_done):
-    work, c_buf, p_buf, q_buf, load_sem, c_send, c_recv, p_send, p_recv, q_send, q_recv = refs
+    groups, EL, group = slot.shape
+    picked = jax.ShapeDtypeStruct((EL, groups, slots, D), BF16)
+    outs = [
+        jax.ShapeDtypeStruct((32, T, D), BF16),
+        picked,
+        picked,
+        jax.ShapeDtypeStruct((EL, groups, slots, 128), F32),
+    ]
+    scratch = [
+        pltpu.VMEM((groups, EL * slots, group), BF16),
+        pltpu.VMEM((2, group, D), BF16),
+        pltpu.VMEM((2, EL, slots, D), BF16),
+        DMA((2, 4)),
+        DMA((2,)),
+        DMA,
+        DMA((2, 4)),
+        DMA((4,)),
+        DMA((4, 2, 3)),
+        DMA((4, 2, 3)),
+        DMA((4, 4)),
+        DMA((4, 4)),
+    ]
+    specs = ([IN_VMEM, ANY_SPACE, IN_VMEM, IN_VMEM], [ANY_SPACE] * 3 + [IN_VMEM])
+    kernel = functools.partial(_gather_pick_kernel, width=PICK_WIDTH)
+    out, xr, gr, gates = _comm(kernel, outs, scratch, collective_id, specs)(x, g_all.reshape(32, T, D), slot, router)
+    return out.reshape(32 * T, D), xr, gr, gates
+
+
+def _tree_sum_steps(u, z, own, bufs, sems, T):
+    c_buf, p_buf, q_buf = bufs
+    c_send, c_recv, p_send, p_recv, q_send, q_recv = sems
     here = (u, z)
     half = T // 2
     halves = (pl.ds(0, half), pl.ds(half, half))
 
-    def load(i, k, bit):
-        return pltpu.make_async_copy(source(u ^ bit, order[i]), work.at[i, k], load_sem.at[i, k])
-
-    for i in range(4):
-        for k, bit in enumerate(CHIPS):
-            _send(source(u ^ bit ^ 1, order[i]), c_buf.at[i, k], c_send.at[i, k], c_recv.at[i, k], (u ^ 1, z))
-            load(i, k, bit).start()
+    def to_sibling(i, k, ref):
+        _send(ref, c_buf.at[i, k], c_send.at[i, k], c_recv.at[i, k], (u ^ 1, z))
 
     def add_core(i):
         for k in (3, 2, 1, 0):
-            load(i, k, CHIPS[k]).wait()
             _expect(c_buf.at[i, k], c_recv.at[i, k], here)
-            _accumulate(work.at[i, k], c_buf.at[i, k], T)
+            _accumulate(own(i, k), c_buf.at[i, k], T)
+            for h in range(2):
+                if k and (k == 3 or CHIPS[k] == THEN[h]):
+                    j = 1 if k == 3 else 0
+                    part = own(i, k).at[halves[h]]
+                    _send(part, p_buf.at[i, h, j], p_send.at[i, h, j], p_recv.at[i, h, j], (u ^ THEN[h], z))
+
+    def add_far(i):
         for h in range(2):
-            for j, bit in enumerate((THEN[h], 6)):
-                k = CHIPS.index(bit)
-                part = work.at[i, k, halves[h]]
-                _send(part, p_buf.at[i, h, j], p_send.at[i, h, j], p_recv.at[i, h, j], (u ^ THEN[h], z))
-
-    def add_first(i):
+            part = own(i, CHIPS.index(FIRST[h])).at[halves[h]]
+            _expect(p_buf.at[i, h, 1], p_recv.at[i, h, 1], here)
+            _accumulate(part, p_buf.at[i, h, 1], half)
+            _send(part, q_buf.at[i, h], q_send.at[i, h], q_recv.at[i, h], (u ^ FIRST[h], z))
+
+    def add_near(i):
         for h in range(2):
-            k = CHIPS.index(FIRST[h])
-            _expect(p_buf.at[i, h, 1], p_recv.at[i, h, 1], here)
-            _accumulate(work.at[i, k, halves[h]], p_buf.at[i, h, 1], half)
-            _send(work.at[i, k, halves[h]], q_buf.at[i, h], q_send.at[i, h], q_recv.at[i, h], (u ^ FIRST[h], z))
             _expect(p_buf.at[i, h, 0], p_recv.at[i, h, 0], here)
-            _accumulate(work.at[i, 0, halves[h]], p_buf.at[i, h, 0], half)
+            _accumulate(own(i, 0).at[halves[h]], p_buf.at[i, h, 0], half)
 
     def add_then(i):
         for h in range(2):
             _expect(q_buf.at[i, h], q_recv.at[i, h], here)
-            _accumulate(work.at[i, 0, halves[h]], q_buf.at[i, h], half)
-        level_done(i, work)
-
-    for i in range(6):
-        yield
-        if i < 4:
-            add_core(i)
-        if 1 <= i < 5:
-            add_first(i - 1)
-        if i >= 2:
-            add_then(i - 2)
-    yield
+            _accumulate(own(i, 0).at[halves[h]], q_buf.at[i, h], half)
+
+    def finish():
+        for i in range(4):
+            for k in range(4):
+                _sent(c_buf.at[i, k], c_send.at[i, k], here)
+            for h in range(2):
+                for j in range(2):
+                    _sent(p_buf.at[i, h, j], p_send.at[i, h, j], here)
+                _sent(q_buf.at[i, h], q_send.at[i, h], here)
+
+    return to_sibling, add_core, add_far, add_near, add_then, finish
+
+
+def _line_end(u, z, level, i, part, z_buf, sems, rows):
+    z_send, z_recv = sems
+    here = (u, z)
+
+    @pl.when((level >= z) & (z > 0))
+    def _():
+        _expect(z_buf.at[0, level], z_recv.at[0, level], here)
+        _accumulate(part, z_buf.at[0, level], rows)
+
+    @pl.when((level <= z) & (z < DEPTH - 1))
+    def _():
+        _expect(z_buf.at[1, level], z_recv.at[1, level], here)
+        _accumulate(part, z_buf.at[1, level], rows)
+
+    if i < 3:
+
+        @pl.when(level > z)
+        def _():
+            _send(part, z_buf.at[0, level], z_send.at[i], z_recv.at[0, level], (u, z + 1))
+
+        @pl.when(level < z)
+        def _():
+            _send(part, z_buf.at[1, level], z_send.at[i], z_recv.at[1, level], (u, z - 1))
+
+
+def _spread_part(u, z, slot_ref, source, gg_ref, order, refs, level_done, later=lambda i: None):
+    work, c_buf, p_buf, q_buf, side, in_buf, in_sem = refs[:7]
+    core, chip = u % 2, u // 2
+    other = 1 - core
+    _, group, experts = slot_ref.shape
+    slots, D = source.shape[2:]
+    total = experts * slots
+    T = group // 4
+
+    def place(k):
+        return pl.ds(pl.multiple_of((chip ^ (CHIPS[k] // 2)) * T, T), T)
+
+    def own(i, k):
+        return work.at[i, place(k)]
+
+    to_sibling, add_core, add_far, add_near, add_then, finish = _tree_sum_steps(
+        u, z, own, (c_buf, p_buf, q_buf), refs[7:], T
+    )
+    lane = lax.broadcasted_iota(jnp.int32, (experts, total), 1)
+    which = lax.broadcasted_iota(jnp.int32, (experts, total), 0)
+    choose = jnp.where((lane >= which * slots) & (lane < (which + 1) * slots), 1.0, 0.0).astype(BF16)
+    offset = lane[:1] - jnp.sum(jnp.where(lane >= (which + 1) * slots, slots, 0), axis=0, keepdims=True)
+    offset = offset.astype(F32)
+    column = lax.broadcasted_iota(jnp.int32, (slots, 128), 1)
+
+    def load(n, job, start):
+        i, c = job
+        copy = pltpu.make_async_copy(source.at[:, 2 * order[i] + c], in_buf.at[n % 2], in_sem.at[n % 2])
+        copy.start() if start else copy.wait()
+
+    def compute(n, job):
+        i, c = job
+        at = 2 * order[i] + c
+        mine = dot(slot_ref[at].astype(BF16), choose)
+        pick = jnp.where(mine == offset, 1.0, 0.0).astype(BF16)
+        rows_in = in_buf.at[n % 2]
+        target = work.at[i] if c is core else side.at[i]
+        if gg_ref is not None:
+            grads = [jnp.where(column == u * experts + e, gg_ref[e, at], 0.0).astype(BF16) for e in range(experts)]
+            target[:, pl.ds(D, 128)] = dot(pick, jnp.concatenate(grads, axis=0)).astype(BF16)
+
+        def step(j, _):
+            cols = pl.ds(pl.multiple_of(j * SPREAD_WIDTH, SPREAD_WIDTH), SPREAD_WIDTH)
+            rows = jnp.concatenate([rows_in[e, :, cols] for e in range(experts)], axis=0)
+            target[:, cols] = dot(pick, rows).astype(BF16)
+            return 0
+
+        lax.fori_loop(0, D // SPREAD_WIDTH, step, 0)
+        if c is not core:
+            for k in (3, 2, 1, 0):
+                to_sibling(i, k, side.at[i, place(k)])
+
+    def end(i):
+        add_then(i)
+        level_done(i, own(i, 0))
+
+    jobs = _Jobs(load, compute)
     for i in range(4):
-        for k in range(4):
-            _sent(c_buf.at[i, k], c_send.at[i, k], here)
-        for h in range(2):
-            for j in range(2):
-                _sent(p_buf.at[i, h, j], p_send.at[i, h, j], here)
-            _sent(q_buf.at[i, h], q_send.at[i, h], here)
-
-
-def _tree_sum_scratch(T, D):
+        jobs.add((i, other), (i, core))
+    jobs.run(2)
+    add_core(0)
+    yield
+    jobs.run(2)
+    add_far(0)
+    add_core(1)
+    yield
+    add_near(0)
+    jobs.run(2)
+    add_far(1)
+    add_core(2)
+    yield
+    end(0)
+    later(0)
+    add_near(1)
+    jobs.run(2)
+    add_far(2)
+    add_core(3)
+    yield
+    end(1)
+    later(1)
+    add_near(2)
+    add_far(3)
+    yield
+    end(2)
+    later(2)
+    add_near(3)
+    yield
+    end(3)
+    later(3)
+    yield
+    finish()
+
+
+def _spread_scratch(T, W, rows_shape):
     half = T // 2
     return [
-        pltpu.VMEM((4, 4, T, D), BF16),
-        pltpu.VMEM((4, 4, T, D), BF16),
-        pltpu.VMEM((4, 2, 2, half, D), BF16),
-        pltpu.VMEM((4, 2, half, D), BF16),
-        DMA((4, 4)),
+        pltpu.VMEM((4, 4 * T, W), BF16),
+        pltpu.VMEM((4, 4, T, W), BF16),
+        pltpu.VMEM((4, 2, 2, half, W), BF16),
+        pltpu.VMEM((4, 2, half, W), BF16),
+        pltpu.VMEM((4, 4 * T, W), BF16),
+        pltpu.VMEM((2,) + rows_shape, BF16),
+        DMA((2,)),
         DMA((4, 4)),
         DMA((4, 4)),
         DMA((4, 2, 2)),
@@ -818,52 +1000,39 @@
     ]
 
 
-def _line_end(u, z, level, i, part, z_buf, sems, rows):
-    z_send, z_recv = sems
-    here = (u, z)
-
-    @pl.when((level >= z) & (z > 0))
-    def _():
-        _expect(z_buf.at[0, level], z_recv.at[0, level], here)
-        _accumulate(part, z_buf.at[0, level], rows)
-
-    @pl.when((level <= z) & (z < DEPTH - 1))
-    def _():
-        _expect(z_buf.at[1, level], z_recv.at[1, level], here)
-        _accumulate(part, z_buf.at[1, level], rows)
-
-    if i < 3:
-
-        @pl.when(level > z)
-        def _():
-            _send(part, z_buf.at[0, level], z_send.at[i], z_recv.at[0, level], (u, z + 1))
-
-        @pl.when(level < z)
-        def _():
-            _send(part, z_buf.at[1, level], z_send.at[i], z_recv.at[1, level], (u, z - 1))
-
-
-def scatter_all(x, collective_id):
-    N, D = x.shape
-    T = N // 32
-
-    def kernel(x_ref, o_ref, z_buf, z_send, z_recv, *refs):
+def spread_scatter(slot, gate_grads, entry_rows, collective_id):
+    groups, group, EL = slot.shape
+    slots, D = entry_rows.shape[2:]
+    T, W = group // 4, D + 128
+
+    def kernel(slot_ref, gg_ref, entry_ref, o_ref, z_buf, z_send, z_recv, *refs):
         u, z = lax.axis_index("uly"), lax.axis_index("blk")
+        order = tuple(reversed(_line_order(z)))
+        parts = []
+
+        def done(i, part):
+            parts.append(part)
+
+        def line(i):
+            _line_end(u, z, order[i], i, parts[i], z_buf, (z_send, z_recv), T)
+
         _greet(u, z, (1, 2, 4), line=True)
-        order = tuple(reversed(_line_order(z)))
-        work = refs[0]
-
-        def done(i, work):
-            _line_end(u, z, order[i], i, work.at[i, 0], z_buf, (z_send, z_recv), T)
-
-        _run(_tree_sum_part(u, z, lambda who, level: x_ref.at[who * DEPTH + level], order, T, refs, done))
-        o_ref[...] = work[3, 0]
+        _run(_spread_part(u, z, slot_ref, entry_ref, gg_ref, order, refs, done, line))
+        o_ref[...] = parts[3][...]
         for i in range(3):
-            _sent(work.at[i, 0], z_send.at[i], (u, z))
-
-    scratch = [pltpu.VMEM((2, 4, T, D), BF16), DMA((4,)), DMA((2, 4))] + _tree_sum_scratch(T, D)
-    out = jax.ShapeDtypeStruct((T, D), x.dtype)
-    return _comm(kernel, out, scratch, collective_id, ([ANY_SPACE], IN_VMEM))(x.reshape(32, T, D))
+            _sent(parts[i], z_send.at[i], (u, z))
+
+    scratch = [pltpu.VMEM((2, 4, T, W), BF16), DMA((4,)), DMA((2, 4))] + _spread_scratch(T, W, (EL, slots, D))
+    specs = ([IN_VMEM, IN_VMEM, ANY_SPACE], IN_VMEM)
+    out = jax.ShapeDtypeStruct((T, W), BF16)
+    return _comm(kernel, out, scratch, collective_id, specs)(slot, gate_grads, entry_rows)
+
+
+def slots_of(chosen):
+    count = chosen.shape[-1]
+    before = (jnp.arange(count)[:, None] < jnp.arange(count)[None, :]).astype(BF16)
+    earlier = jnp.einsum("abs,st->abt", chosen.astype(BF16), before, preferred_element_type=F32)
+    return jnp.where(chosen, earlier.astype(jnp.int32), -1)
 
 
 class Slice:
@@ -876,9 +1045,13 @@
         self.first_block, self.block_step = 8 * (self.u // 2), 1
 
     def enter(self, rows, scaled, out_weight, pack, routes):
-        R = scaled.shape[0]
-        cut = scaled.reshape(R, 3, 4, 2, self.C).transpose(3, 2, 0, 1, 4).reshape(2, 4, R, 3 * self.C)
-        rows, weights, outs, packs, routes = enter(rows, cut, out_weight, [pack, routes], 1)
+        rows, weights, packs, routes = enter(rows, scaled, [pack, routes], 1)
+        there = [((2 * ((z + u // 2) % 4) + u % 2), u // 2) for u in range(8) for z in range(4)]
+        self.forth = [(i, 4 * u + z) for i, (u, z) in enumerate(there)]
+        mine = self.permute(out_weight, self.forth)
+        outs = jnp.stack([mine] + [self.permute(mine, self.across(bit)) for bit in (2, 4, 6)])
+        part = jnp.arange(4, dtype=jnp.int32)
+        outs = outs[(self.u // 2) ^ ((part + self.z) % 4)]
         return (
             rows.reshape(self.L, self.D),
             weights.reshape(self.D, 3 * self.C),
@@ -887,6 +1060,12 @@
             routes,
         )
 
+    def permute(self, x, pairs):
+        return lax.ppermute(x, ALL, pairs)
+
+    def across(self, bit):
+        return [(i, i ^ (4 * bit)) for i in range(32)]
+
     def head_sum(self, x):
         return column_sum(x, 2)
 
@@ -900,19 +1079,38 @@
     def heads_to_rows(self, x):
         return column_scatter(x.reshape(2, 4, self.T, self.D), self.upstream_line, 5)
 
-    def rows_to_heads(self, x, out_part):
-        rows, self.out_line = column_gather(x, out_part, 6)
-        return rows.reshape(self.L, self.D)
-
-    def gather(self, x):
-        return gather_all(x, 7)
-
-    def scatter_wide(self, x):
-        return scatter_all(x, 8)
+    def experts(self, second_low, upstream_all, routes, weights, router):
+        EL, T, D = weights.shape[0], self.T, self.D
+        slots = -(-4 * CAP // 16) * 16
+        chosen = jnp.any(routes[None] == (self.u * EL + jnp.arange(EL, dtype=jnp.int32))[:, None, None, None, None], axis=3)
+        chosen = chosen.reshape(EL, 4, 2, 4, T).transpose(3, 2, 0, 1, 4).reshape(8, EL, 4 * T)
+        slot = slots_of(chosen)
+        second_all, xr, gr, gates = gather_pick(second_low, upstream_all, slot, router, slots, 7)
+        flat, cut = (EL, 8 * slots, -1), (EL, 8, slots, -1)
+        out_rows, entry_rows, self.expert_grads, gate_grads = run_experts(
+            xr.reshape(flat), gr.reshape(flat), gates.reshape(flat), weights, 8 * slots
+        )
+        self.slot, self.out_rows = slot.transpose(0, 2, 1), out_rows.reshape(cut)
+        return second_all, spread_scatter(self.slot, gate_grads.reshape(cut), entry_rows.reshape(cut), 8)
+
+    def rows_to_heads(self, x):
+        rows, self.out_line = column_gather(x, self.slot, self.out_rows, 6)
+        return rows.reshape(self.L, self.D), self.expert_grads
 
     def sequence_sums(self, dk, dv, out_part):
         cut = (4, self.L, self.C)
-        return key_value_sums(dk.reshape(cut), dv.reshape(cut), out_part.reshape(4, -1, self.D), self.out_line, 10)
+        dk, dv, out_sum = key_value_sums(dk.reshape(cut), dv.reshape(cut), self.out_line, 10)
+        parts = out_part.reshape(4, -1, self.D)
+        chip = self.u // 2
+
+        def part(bit):
+            return lax.dynamic_index_in_dim(parts, ((chip ^ (bit // 2)) - self.z) % 4, 0, False)
+
+        total = part(0).astype(F32)
+        for bit in (2, 4, 6):
+            total = total + self.permute(part(bit), self.across(bit)).astype(F32)
+        out_grad = self.permute(total.astype(BF16), [(b, a) for a, b in self.forth])
+        return dk, dv, out_grad, out_sum
 
     def leave(self, first_part, weight_part, logit_grad, ffn_part, head_parts):
         T, R = self.T, self.D // 32
@@ -926,7 +1124,6 @@
             [logit_grad.reshape(T // 2, 2 * EXPERTS), thin],
             11,
         )
-        weights = weights.reshape(8, R, 3, self.C).transpose(1, 2, 0, 3).reshape(R, 3, self.D)
         ffn = lax.dynamic_slice_in_dim(
             jnp.sum(thin[:, :, :wide], axis=(0, 1)).reshape(self.D), (self.u * 4 + self.z) * R, R, 0
         )
@@ -953,8 +1150,8 @@
         return lax.psum_scatter(x, ALL, scatter_dimension=0, tiled=True)
 
     def enter(self, rows, scaled, out_weight, pack, routes):
-        U, R = self.U, scaled.shape[0]
-        swapped = lax.all_to_all(scaled.reshape(R, 3, U, self.C), "uly", split_axis=2, concat_axis=0, tiled=True)
+        U, R = self.U, scaled.shape[1]
+        swapped = lax.all_to_all(scaled.transpose(1, 0, 2).reshape(R, 3, U, self.C), "uly", split_axis=2, concat_axis=0, tiled=True)
         weights = lax.all_gather(swapped.reshape(U, R, 3 * self.C), "blk", axis=1, tiled=True)
         return (
             self.rows_all(rows),
@@ -984,9 +1181,35 @@
     def rows_all(self, x):
         return lax.all_gather(x, "uly", axis=0, tiled=True)
 
-    def rows_to_heads(self, x, out_part):
+    def experts(self, second_low, upstream_all, routes, weights, router):
+        EL, D = weights.shape[0], self.D
+        N = upstream_all.shape[0]
+        second_all = self.gather(second_low)
+        group = min(512, N)
+        groups = N // group
+        slots = -(-(group // self.T * CAP) // 16) * 16
+        rows = groups * slots
+        own_first = self.u * EL
+        chosen = jnp.any(routes[None] == (own_first + jnp.arange(EL, dtype=jnp.int32))[:, None, None, None, None], axis=3)
+        slot = slots_of(chosen.reshape(EL, groups, group)).reshape(EL, N)
+        entry_in, upstream_in, gates = pick_rows(slot, router, second_all, upstream_all, group, slots)
+        flat, split = (EL, rows, -1), (EL, groups, slots, -1)
+        out_rows, entry_rows, self.expert_grads, gate_grads = run_experts(
+            entry_in.reshape(flat), upstream_in.reshape(flat), gates.reshape(flat), weights, min(8, groups) * slots
+        )
+        out_part, entry_part = spread_rows(
+            own_first.astype(jnp.int32)[None],
+            slot.T,
+            gate_grads.reshape(split),
+            out_rows.reshape(split),
+            entry_rows.reshape(split),
+            group,
+        )
         self.out_sum = self.scatter_wide(out_part)
-        return self.rows_all(x)
+        return second_all, self.scatter_wide(entry_part)
+
+    def rows_to_heads(self, x):
+        return self.rows_all(x), self.expert_grads
 
     def sequence_sums(self, dk, dv, out_part):
         pair = jnp.stack([dk, dv]).reshape(2, self.U, self.Z, self.T, self.C)
@@ -998,7 +1221,7 @@
         part = weight_part.reshape(U, self.Z * R, 3 * self.C)
         part = lax.psum_scatter(part, "blk", scatter_dimension=1, tiled=True)
         part = lax.all_to_all(part, "uly", split_axis=0, concat_axis=0, tiled=True)
-        weights = part.reshape(U, R, 3, self.C).transpose(1, 2, 0, 3).reshape(R, 3, self.D)
+        weights = part.reshape(U, R, 3, self.C).transpose(2, 1, 0, 3).reshape(3, R, self.D)
         heads = lax.psum_scatter(head_parts, "blk", scatter_dimension=1, tiled=True)
         return self.rows_sum(first_part), weights, self.gather(logit_grad), self.scatter_wide(ffn_part), heads
 
@@ -1191,7 +1414,7 @@
     )(slot, router, x, g)
 
 
-def _expert_kernel(x_ref, g_ref, gate_ref, w_ref, out_ref, entry_ref, dw_ref, gg_ref, *, width):
+def _expert_kernel(x_ref, g_ref, gate_ref, w_ref, out_ref, entry_ref, dw_ref, gg_ref):
     x, g = x_ref[0], g_ref[0]
     gate = gate_ref[0][:, :1]
     gate_pre = dot(x, w_ref[0, 0])
@@ -1205,31 +1428,22 @@
     gate_pre_grad = (inner_grad * up * sig * (1.0 + gate_pre * (1.0 - sig))).astype(BF16)
     up_grad = (inner_grad * act).astype(BF16)
     gated = (inner * gate).astype(BF16)
+    both = jnp.concatenate([gate_pre_grad, up_grad], axis=1)
+    out_ref[0] = dot(gated, w_ref[0, 2], LAST_DIM).astype(BF16)
+    entry_ref[0] = dot(both, jnp.concatenate([w_ref[0, 0], w_ref[0, 1]], axis=1), LAST_DIM).astype(BF16)
+    FL = w_ref.shape[3]
+    pair = dot(x, both, FIRST_DIM)
+    parts = (pair[:, :FL], pair[:, FL:], dot(g, gated, FIRST_DIM))
     first = pl.program_id(1) == 0
-
-    def step(i, _):
-        at = pl.ds(pl.multiple_of(i * width, width), width)
-        out_ref[0, :, at] = dot(gated, w_ref[0, 2, at, :], LAST_DIM).astype(BF16)
-        entry = dot(gate_pre_grad, w_ref[0, 0, at, :], LAST_DIM) + dot(up_grad, w_ref[0, 1, at, :], LAST_DIM)
-        entry_ref[0, :, at] = entry.astype(BF16)
-        parts = (
-            dot(x_ref[0, :, at], gate_pre_grad, FIRST_DIM),
-            dot(x_ref[0, :, at], up_grad, FIRST_DIM),
-            dot(g_ref[0, :, at], gated, FIRST_DIM),
-        )
-        for k in range(3):
-
-            @pl.when(first)
-            def _(k=k):
-                dw_ref[0, k, at, :] = parts[k]
-
-            @pl.when(jnp.logical_not(first))
-            def _(k=k):
-                dw_ref[0, k, at, :] += parts[k]
-
-        return 0
-
-    lax.fori_loop(0, x_ref.shape[2] // width, step, 0)
+    for k in range(3):
+
+        @pl.when(first)
+        def _(k=k):
+            dw_ref[0, k] = parts[k]
+
+        @pl.when(jnp.logical_not(first))
+        def _(k=k):
+            dw_ref[0, k] += parts[k]
 
 
 def run_experts(x, g, gate, weights, chunk):
@@ -1239,7 +1453,7 @@
     thin = pl.BlockSpec((1, chunk, 128), lambda e, c: (e, c, 0))
     matrices = pl.BlockSpec((1, 3, D, FL), lambda e, c: (e, 0, 0, 0))
     return pl.pallas_call(
-        functools.partial(_expert_kernel, width=512),
+        _expert_kernel,
         out_shape=[
             jax.ShapeDtypeStruct(x.shape, BF16),
             jax.ShapeDtypeStruct(x.shape, BF16),
@@ -1335,8 +1549,8 @@
     C, L = move.C, move.L
 
     gain_rows = attn_gain.astype(F32)[:, None]
-    own_weights = jnp.stack([query_weight, key_weight, value_weight], axis=1).astype(F32)
-    scaled_rows = (own_weights * gain_rows[:, :, None]).astype(BF16)
+    own_weights = [w.astype(F32) for w in (query_weight, key_weight, value_weight)]
+    scaled_rows = jnp.stack([(w * gain_rows).astype(BF16) for w in own_weights])
     pack = jnp.concatenate([router_weight] + [g[:, None] for g in (ffn_gain, query_gain, key_gain)], axis=1)
     pack = jnp.pad(pack, ((0, 0), (0, 128 - pack.shape[1])))
     hidden = hidden_in.astype(F32)
@@ -1344,7 +1558,6 @@
     first_rows, qkv_weight, out_rows, packed, routes_all = move.enter(
         (hidden * first_scale).astype(BF16), scaled_rows, out_weight, pack, routes.T
     )
-    routes_all = routes_all.transpose(0, 1, 3, 2).reshape(N, -1)
     weight_router = packed[:, :EXPERTS]
     gain_ffn = packed[:, EXPERTS].astype(F32)
     head_gains = lax.dynamic_slice_in_dim(packed[:, EXPERTS + 1 : EXPERTS + 3], move.group * C, C, 0).astype(F32)
@@ -1377,37 +1590,9 @@
     second_scale = norm_scale(residual)
     second_low = (residual * second_scale * gain_ffn).astype(BF16)
     probabilities = jax.nn.softmax(dot(second_low, weight_router), axis=-1)
-    second_all = move.gather(second_low)
-
-    group = min(512, N)
-    groups = N // group
-    slots = -(-(group // T * CAP) // 16) * 16
-    rows = groups * slots
-    own_first = u * EL
-    own_experts = own_first + jnp.arange(EL, dtype=jnp.int32)
-    chosen = jnp.any(routes_all[None] == own_experts[:, None, None], axis=2).reshape(EL, groups, group)
-    before = jnp.arange(group)[:, None] < jnp.arange(group)[None, :]
-    earlier = jnp.einsum("egs,st->egt", chosen.astype(BF16), before.astype(BF16), preferred_element_type=F32)
-    slot = jnp.where(chosen, earlier.astype(jnp.int32), -1).reshape(EL, N)
-    own_router = jnp.roll(weight_router, -own_first, axis=1)
-    entry_in, upstream_in, gate_rows = pick_rows(slot, own_router, second_all, upstream_all, group, slots)
-    out_rows_e, entry_rows, expert_grads, gate_grads = run_experts(
-        entry_in.reshape(EL, rows, D),
-        upstream_in.reshape(EL, rows, D),
-        gate_rows.reshape(EL, rows, 128),
-        expert_weights,
-        min(8, groups) * slots,
-    )
-    split = (EL, groups, slots, D)
-    out_part, entry_part = spread_rows(
-        own_first.astype(jnp.int32)[None],
-        slot.T,
-        gate_grads.reshape(EL, groups, slots, 128),
-        out_rows_e.reshape(split),
-        entry_rows.reshape(split),
-        group,
-    )
-    entry_sum = move.scatter_wide(entry_part).astype(F32)
+    own_router = jnp.roll(weight_router, -u * EL, axis=1)
+    second_all, entry_sum = move.experts(second_low, upstream_all, routes_all, expert_weights, own_router)
+    entry_sum = entry_sum.astype(F32)
 
     second_grad, prob_grad = entry_sum[:, :D], entry_sum[:, D : D + EXPERTS]
     logit_grad = (
@@ -1420,7 +1605,7 @@
     residual_grad = upstream + second_scale * weighted - residual * (second_scale**3) * inner_mean
     ffn_gain_part = jnp.sum(second_grad * residual * second_scale, axis=0)
 
-    residual_rows = move.rows_to_heads(residual_grad.astype(BF16), out_part)
+    residual_rows, expert_grads = move.rows_to_heads(residual_grad.astype(BF16))
     out_weight_part = dot(attended_low, residual_rows, FIRST_DIM).astype(BF16)
     attended_grad = dot(residual_rows, out_rows, LAST_DIM).astype(BF16)
     dq, dk_part, dv_part = attention_backward(
@@ -1460,8 +1645,8 @@
     own_columns = lax.dynamic_slice_in_dim(second_all, (u * Z + z) * RW, RW, 1)
     router_grad = dot(own_columns, logit_grad_all, FIRST_DIM)
     weight_sum = weight_sum.astype(F32)
-    attn_gain_grad = jnp.sum(own_weights * weight_sum, axis=(1, 2))
-    weight_grads = weight_sum * gain_rows[:, :, None]
+    attn_gain_grad = sum(jnp.sum(w * g, axis=1) for w, g in zip(own_weights, weight_sum))
+    weight_grads = [g * gain_rows for g in weight_sum]
     first_weighted = first_weighted.astype(F32)
     first_mean = jnp.mean(first_weighted * hidden, axis=-1, keepdims=True)
     hidden_grad = residual_grad + first_scale * first_weighted - hidden * (first_scale**3) * first_mean
@@ -1469,9 +1654,9 @@
         output,
         hidden_grad,
         attn_gain_grad,
-        weight_grads[:, 0],
-        weight_grads[:, 1],
-        weight_grads[:, 2],
+        weight_grads[0],
+        weight_grads[1],
+        weight_grads[2],
         out_weight_grad.astype(F32),
         head_gain_grads[0],
         head_gain_grads[1],

time: 975 us -> 850 us (0.87)
  Pallas kernels: 834 us -> 706 us
  local copies, waits for them, and re-layouts: 39.7 us -> 25.3 us
  starting transfers between devices: 0 us -> 13 us
    pallas_call x8 -> x6, Pallas kernels: 548 us -> 453 us  [the longest x1 98.3 us: gather_pick(): _comm(kernel, outs, scratch, collective_id, specs)]
    pallas_call x2, Pallas kernels: 37 us -> 20 us  [column_sum(): return _comm(kernel, out, scratch, collective_id, ([IN_VMEM], IN_VMEM))(x)]
    pallas_call x1, Pallas kernels: 81.6 us -> 67.6 us  [leave(): _comm(kernel, outs, scratch, collective_id, specs)(x, weights, *smalls)]
    ppermute x0 -> x8, starting transfers between devices: none -> 13 us  [permute(): return lax.ppermute(x, ALL, pairs)]
  transfers between devices with their start and end apart: 0 -> 8, of which waited for: 0 -> 1; matrix products, arithmetic and copies ran while one was open for 0% -> 7% of each run, Pallas kernels for 0% -> 24%
where the time goes in v3:
time: 850 us; the launch traced here: 839 us
  Pallas kernels  706 us (83%)
  other arithmetic  55.8 us (7%)
  matrix products  32.1 us (4%)
  local copies, waits for them, and re-layouts  25.3 us (3%)
  starting transfers between devices  13 us (2%)
    pallas_call x1, Pallas kernels, gather_pick(): _comm(kernel, outs, scratch, collective_id, specs)  98.3 us
    pallas_call x1, Pallas kernels, spread_scatter(): _comm(kernel, out, scratch, collective_id, specs)  86.4 us
    pallas_call x1, Pallas kernels, column_gather(): _comm(kernel, outs, scratch, collective_id, specs)(rows, slot, out_rows)  81.4 us
    pallas_call x1, Pallas kernels, column_scatter(): _comm(kernel, outs, scratch, collective_id, specs, aliases={1: 1})(x, rows)  78.7 us
    pallas_call x1, Pallas kernels, leave(): _comm(kernel, outs, scratch, collective_id, specs)(x, weights, *smalls)  67.6 us
    pallas_call x1, Pallas kernels, run_experts(): pl.pallas_call(_expert_kernel, out_shape=[jax.ShapeDtypeStruct(x.shape, B...  64.9 us
    pallas_call x1, Pallas kernels, key_value_sums(): return _comm(kernel, outs, scratch, collective_id, specs)(dk, dv, x)  62.9 us
    pallas_call x1, Pallas kernels, enter(): _comm(kernel, outs, scratch, collective_id, specs)(rows, weights, *smalls)  58.8 us
  transfers between devices with their start and end apart: 8, of which 1 were waited for; matrix products, arithmetic and copies ran while one was open for 7% of the time, Pallas kernels for 24%

profile of v3, /device:TPU:13, one launch (start us, length us, event | category | flops | bytes accessed | tf_op | source)
XLA Modules:
  0.0 839.4 jit_solution(16151738119703893179)
XLA Ops:
  0.7 4.1 collective-permute-start
  6.5 1.2 fusion.2
  10.6 2.0 fusion.3.refs_0_
  12.6 1.3 fusion.26
  13.9 1.0 pad_maximum_fusion.4.refs_1_
  15.5 58.8 %shard_map.229 = (bf16[2,4,128,2048]{3,2,1,0:T(8,128)(2,1)}, bf16[4,2,4,64,768]{4,3,2,1,0:T(8,128)(2,1)}, bf16[8,4,64,128]{3,2,1,0:T(8,128)(2,1)}, s32[8,4,8,128]{3,2,1,0:T(8,128)}) custom-call(bf16[128,2048]{1,0:T(8,128)(2,1)} %fusion.3.refs_0_, bf16[3,64,2048]{2,1,0:T(8,128)(2,1)} %pad_maximum_fusion.4.refs_1_, bf16[64,128]{1,0:T(8,128)(2,1)} %fusion.37.refs_2_, ...), custom_call_target="tpu_custom_call" | custom-call | bytes 100000000 | tf_op jit(solution)/shard_map/pallas_call | solution.py:413
  74.3 1.4 convert_reduce_fusion
  75.8 2.0 slice.114
  77.8 6.3 fusion.62
  85.4 11.3 %shard_map.230 = f32[16,128]{1,0:T(8,128)} custom-call(f32[16,128]{1,0:T(8,128)} %reshape.339.x_ref), custom_call_target="tpu_custom_call" | custom-call | bytes 100000000 | tf_op jit(solution)/shard_map/pallas_call | solution.py:434
  98.9 1.2 pad_clamp_fusion
  101.1 1.4 copy.55
  103.6 1.7 multiply_multiply_fusion
  105.3 1.8 reshape.342
  107.1 1.7 reshape.341
  109.4 1.9 multiply_cosine_fusion
  111.7 2.3 slice_negate_fusion.2
  114.0 2.3 maximum_multiply_fusion.1
  116.8 1.3 fusion.6
  118.1 48.9 %shard_map.231 = (bf16[4,1024,256]{2,1,0:T(8,128)(2,1)}, bf16[4,1024,256]{2,1,0:T(8,128)(2,1)}, bf16[32,128,2048]{2,1,0:T(8,128)(2,1)}) custom-call(bf16[1024,256]{1,0:T(8,128)(2,1)} %get-tuple-element.110.a_ref, bf16[1024,256]{1,0:T(8,128)(2,1)} %slice.171.b_ref, bf16[128,2048]{1,0:T(8,128)(2,1)} %x_ref.1), custom_call_target="tpu_custom_call" | custom-call | bytes 100000000 | tf_op jit(solution)/shard_map/pallas_call | solution.py:450
  167.9 1.3 collective-permute-start.3
  169.3 1.3 collective-permute-start.1
  170.6 16.3 %shard_map.232 = (f32[1024,256]{1,0:T(8,128)}, f32[1024,256]{1,0:T(8,128)}) custom-call(s32[2]{0:T(128)} %pad_add_fusion.index_ref, s32[5]{0:T(128)} %doc_ref.3, bf16[1024,256]{1,0:T(8,128)(2,1)} %get-tuple-element.111.q_ref, bf16[4096,256]{1,0:T(8,128)(2,1)} %bitcast.171, bf16[4096,256]{1,0:T(8,128)(2,1)} %bitcast.173), custom_call_target="tpu_custom_call" | custom-call | flops 1073741824 | bytes 4194304 | tf_op jit(solution)/shard_map/pallas_call | solution.py:1338
  186.9 1.2 copy.58.slot_ref
  188.2 1.3 dynamic-slice_maximum_fusion.router_ref
  189.5 1.1 pad_maximum_fusion.1
  191.4 4.9 convolution_convert_fusion
  196.2 78.7 %shard_map.233 = (bf16[128,2048]{1,0:T(8,128)(2,1)}, bf16[32,128,2048]{2,1,0:T(8,128)(2,1)}) custom-call(bf16[2,4,128,2048]{3,2,1,0:T(8,128)(2,1)} %bitcast.148, bf16[32,128,2048]{2,1,0:T(8,128)(2,1)} %get-tuple-element.49.g_ref), custom_call_target="tpu_custom_call", output_to_operand_aliasing={{1}: (1, {})} | custom-call | bytes 100000000 | tf_op jit(solution)/shard_map/pallas_call | solution.py:498
  275.0 1.3 multiply_reduce_fusion.6
  276.3 1.3 multiply_convert_fusion.x_ref
  278.3 98.3 %shard_map.234 = (bf16[32,128,2048]{2,1,0:T(8,128)(2,1)}, bf16[8,8,80,2048]{3,2,1,0:T(8,128)(2,1)}, bf16[8,8,80,2048]{3,2,1,0:T(8,128)(2,1)}, f32[8,8,80,128]{3,2,1,0:T(8,128)}) custom-call(bf16[128,2048]{1,0:T(8,128)(2,1)} %copy-done.10, bf16[32,128,2048]{2,1,0:T(8,128)(2,1)} %get-tuple-element.52.g_ref, s32[8,8,512]{2,1,0:T(8,128)} %copy.58.slot_ref, ...), custom_call_target="tpu_custom_call" | custom-call | bytes 100000000 | tf_op jit(solution)/shard_map/pallas_call | solution.py:813
  376.6 64.9 %shard_map.235 = (bf16[8,640,2048]{2,1,0:T(8,128)(2,1)}, bf16[8,640,2048]{2,1,0:T(8,128)(2,1)}, f32[8,3,2048,256]{3,2,1,0:T(8,128)}, f32[8,640,128]{2,1,0:T(8,128)}) custom-call(bf16[8,640,2048]{2,1,0:T(8,128)(2,1)} %bitcast.196, bf16[8,640,2048]{2,1,0:T(8,128)(2,1)} %bitcast.197, f32[8,640,128]{2,1,0:T(8,128)} %bitcast.204, bf16[8,3,2048,256]{3,2,1,0:T(8,128)(2,1)} %w_ref.1), custom_call_target="tpu_custom_call" | custom-call | flops 48318382080 | bytes 159383552 | tf_op jit(solution)/shard_map/pallas_call | solution.py:1455
  441.5 86.4 %shard_map.236 = bf16[128,2176]{1,0:T(8,128)(2,1)} custom-call(s32[8,512,8]{2,1,0:T(8,128)} %bitcast.151, f32[8,8,80,128]{3,2,1,0:T(8,128)} %bitcast.168, bf16[8,8,80,2048]{3,2,1,0:T(8,128)(2,1)} %bitcast.150), custom_call_target="tpu_custom_call" | custom-call | bytes 100000000 | tf_op jit(solution)/shard_map/pallas_call | solution.py:1028
  527.9 1.2 convert_element_type.173
  530.9 1.2 fusion.58.r_ref
  532.1 81.4 %shard_map.237 = (bf16[2,4,128,2048]{3,2,1,0:T(8,128)(2,1)}, bf16[4,128,2048]{2,1,0:T(8,128)(2,1)}) custom-call(bf16[128,2048]{1,0:T(8,128)(2,1)} %fusion.58.r_ref, s32[8,512,8]{2,1,0:T(8,128)} %bitcast.152, bf16[8,8,80,2048]{3,2,1,0:T(8,128)(2,1)} %bitcast.149), custom_call_target="tpu_custom_call" | custom-call | bytes 100000000 | tf_op jit(solution)/shard_map/pallas_call | solution.py:473
  613.6 4.4 convolution_convert_fusion.4.g_ref
  618.0 2.2 convolution_convert_fusion.3
  620.2 21.6 %shard_map.238 = (bf16[1024,256]{1,0:T(8,128)(2,1)}, bf16[4096,256]{1,0:T(8,128)(2,1)}, bf16[4096,256]{1,0:T(8,128)(2,1)}) custom-call(s32[2]{0:T(128)} %pad_add_fusion.index_ref, s32[5]{0:T(128)} %doc_ref.3, bf16[1024,256]{1,0:T(8,128)(2,1)} %get-tuple-element.111.q_ref, bf16[1024,256]{1,0:T(8,128)(2,1)} %convolution_convert_fusion.4.g_ref, ...), custom_call_target="tpu_custom_call" | custom-call | flops 2684354560 | bytes 8388608 | tf_op jit(solution)/shard_map/pallas_call | solution.py:1352
  641.9 62.9 %shard_map.239 = (bf16[1024,256]{1,0:T(8,128)(2,1)}, bf16[1024,256]{1,0:T(8,128)(2,1)}, bf16[128,2048]{1,0:T(8,128)(2,1)}) custom-call(bf16[4,1024,256]{2,1,0:T(8,128)(2,1)} %bitcast.169, bf16[4,1024,256]{2,1,0:T(8,128)(2,1)} %bitcast.170, bf16[4,128,2048]{2,1,0:T(8,128)(2,1)} %get-tuple-element.63.x_ref), custom_call_target="tpu_custom_call" | custom-call | bytes 100000000 | tf_op jit(solution)/shard_map/pallas_call | solution.py:545
  704.8 2.6 reshape.359
  707.3 2.5 reshape.358
  709.9 2.4 broadcast_multiply_fusion
  712.3 1.5 fusion.59
  713.9 1.5 fusion.60
  715.4 1.1 pad_maximum_fusion.3
  716.6 1.1 pad_maximum_fusion.2
  717.8 2.0 multiply_reduce_fusion.1
  720.5 8.8 %shard_map.240 = f32[16,128]{1,0:T(8,128)} custom-call(f32[16,128]{1,0:T(8,128)} %reshape.360.x_ref), custom_call_target="tpu_custom_call" | custom-call | bytes 100000000 | tf_op jit(solution)/shard_map/pallas_call | solution.py:434
  729.9 2.9 subtract_convert_fusion.1
  732.9 5.0 convolution_convert_fusion.2
  737.8 5.0 convolution_convert_fusion.1
  743.7 1.9 collective-permute-start.4
  745.6 1.2 collective-permute-start.6
  747.4 67.6 %shard_map.241 = (bf16[128,2048]{1,0:T(8,128)(2,1)}, bf16[3,64,2048]{2,1,0:T(8,128)(2,1)}, bf16[8,4,64,128]{3,2,1,0:T(8,128)(2,1)}, f32[8,4,24,128]{3,2,1,0:T(8,128)}) custom-call(bf16[2,4,128,2048]{3,2,1,0:T(8,128)(2,1)} %bitcast.162, bf16[4,2,256,768]{3,2,1,0:T(8,128)(2,1)} %bitcast.167, bf16[64,128]{1,0:T(8,128)(2,1)} %reshape.363.refs_0_, ...), custom_call_target="tpu_custom_call" | custom-call | bytes 100000000 | tf_op jit(solution)/shard_map/pallas_call | solution.py:597
  815.1 1.3 fusion.5
  817.3 1.4 convert_element_type.186
  818.8 1.4 fusion.23
  820.3 2.0 fusion.1
  823.3 1.3 fusion.20
  824.6 3.1 collective-permute-start.7
  827.8 1.6 reshape.371
  830.0 2.6 fusion.8
  832.6 5.8 collective-permute-done.7
  (146 shorter events, 23.0 us)
Async XLA Ops:
  0.6 14.2 %copy-start.31 = (bf16[64,64]{1,0:T(8,128)(2,1)S(1)}, bf16[64,64]{1,0:T(8,128)(2,1)}, u32[]{:S(2)}) copy-start(bf16[64,64]{1,0:T(8,128)(2,1)} %param.24) | copy-start | bytes 24580
  0.7 167.2 %collective-permute-start = (bf16[64,2048]{1,0:T(8,128)(2,1)}, bf16[64,2048]{1,0:T(8,128)(2,1)S(1)}, u32[]{:S(2)}, u32[]{:S(2)}) collective-permute-start(bf16[64,2048]{1,0:T(8,128)(2,1)} %param.20), channel_id=1, source_target_pairs={{0,0},{1,8},{2,16},{3,24},{4,4},{5,12},{6,20},{7,28},{8,9},{9,17},... | collective-permute-start | bytes 786440 | tf_op jit(solution)/shard_map/ppermute | solution.py:1064
  6.5 69.2 %copy-start.32 = (f32[64]{0:T(128)}, f32[64]{0:T(128)S(1)}, u32[]{:S(2)}) copy-start(f32[64]{0:T(128)S(1)} %convert_element_type.154) | copy-start | bytes 772
  8.3 69.5 %copy-start.34 = (f32[128]{0:T(128)}, f32[128]{0:T(128)S(1)}, u32[]{:S(2)}) copy-start(f32[128]{0:T(128)S(1)} %get-tuple-element.131) | copy-start | bytes 1540
  84.1 21.2 %copy-start.1 = (f32[1024,768]{1,0:T(8,128)}, f32[1024,768]{1,0:T(8,128)S(1)}, u32[]{:S(2)}) copy-start(f32[1024,768]{1,0:T(8,128)S(1)} %fusion.62) | copy-start | bytes 9437188
  84.1 16.6 %copy-start.27 = (s32[8,4,8,128]{3,2,1,0:T(8,128)S(1)}, s32[8,4,8,128]{3,2,1,0:T(8,128)}, u32[]{:S(2)}) copy-start(s32[8,4,8,128]{3,2,1,0:T(8,128)} %get-tuple-element.51) | copy-start | bytes 393220
  105.3 4.1 copy-start.28
  105.3 4.1 copy-start.36
  111.7 2.3 copy-start.12
  114.0 2.8 copy-start.6
  114.0 2.8 copy-start.7
  116.7 1.4 copy-start.8
  116.7 50.3 %copy-start.24 = (pred[4,2,8,4,128]{2,4,3,1,0:T(8,128)(4,1)S(1)}, pred[4,2,8,4,128]{2,4,3,1,0:T(8,128)(4,1)}, u32[]{:S(2)}) copy-start(pred[4,2,8,4,128]{2,4,3,1,0:T(8,128)(4,1)} %copy.55) | copy-start | bytes 98308
  167.9 20.3 %copy-start.3 = (s32[8,8,512]{1,2,0:T(8,128)}, s32[8,8,512]{1,2,0:T(8,128)S(1)}, u32[]{:S(2)}) copy-start(s32[8,8,512]{1,2,0:T(8,128)S(1)} %convert_select_fusion) | copy-start | bytes 393220
  167.9 21.6 %collective-permute-start.3 = (bf16[64,2048]{1,0:T(8,128)(2,1)S(1)}, bf16[64,2048]{1,0:T(8,128)(2,1)S(1)}, u32[]{:S(2)}, u32[]{:S(2)}) collective-permute-start(bf16[64,2048]{1,0:T(8,128)(2,1)S(1)} %collective-permute-done), channel_id=1, source_target_pairs={{0,24},{1,25},{2,26},{3,27},{4,28},{5,29},{6,30},{7,31},{8,16},{9,... | collective-permute-start | bytes 786440 | tf_op jit(solution)/shard_map/ppermute | solution.py:1064
  169.1 20.4 %collective-permute-start.2 = (bf16[64,2048]{1,0:T(8,128)(2,1)S(1)}, bf16[64,2048]{1,0:T(8,128)(2,1)S(1)}, u32[]{:S(2)}, u32[]{:S(2)}) collective-permute-start(bf16[64,2048]{1,0:T(8,128)(2,1)S(1)} %collective-permute-done), channel_id=1, source_target_pairs={{0,16},{1,17},{2,18},{3,19},{4,20},{5,21},{6,22},{7,23},{8,24},{9,... | collective-permute-start | bytes 786440 | tf_op jit(solution)/shard_map/ppermute | solution.py:1064
  169.3 20.2 %collective-permute-start.1 = (bf16[64,2048]{1,0:T(8,128)(2,1)S(1)}, bf16[64,2048]{1,0:T(8,128)(2,1)}, u32[]{:S(2)}, u32[]{:S(2)}) collective-permute-start(bf16[64,2048]{1,0:T(8,128)(2,1)S(1)} %collective-permute-done), channel_id=1, source_target_pairs={{0,8},{1,9},{2,10},{3,11},{4,12},{5,13},{6,14},{7,15},{8,0},{9,1},... | collective-permute-start | bytes 786440 | tf_op jit(solution)/shard_map/ppermute | solution.py:1064
  170.6 17.6 %copy-start.4 = (bf16[8,4,64,128]{3,2,1,0:T(8,128)(2,1)S(1)}, bf16[8,4,64,128]{3,2,1,0:T(8,128)(2,1)}, u32[]{:S(2)}) copy-start(bf16[8,4,64,128]{3,2,1,0:T(8,128)(2,1)} %get-tuple-element.45) | copy-start | bytes 1572868
  191.3 4.9 copy-start.14
  196.2 78.7 %copy-start = (bf16[128,2048]{1,0:T(8,128)(2,1)S(1)}, bf16[128,2048]{1,0:T(8,128)(2,1)}, u32[]{:S(2)}) copy-start(bf16[128,2048]{1,0:T(8,128)(2,1)} %param.14) | copy-start | bytes 1572868
  277.5 0.8 copy-start.10
  441.5 88.1 %copy-start.5 = (bf16[128,2048]{1,0:T(8,128)(2,1)S(1)}, bf16[128,2048]{1,0:T(8,128)(2,1)}, u32[]{:S(2)}) copy-start(bf16[128,2048]{1,0:T(8,128)(2,1)} %get-tuple-element.50) | copy-start | bytes 1572868
  527.9 3.0 copy-start.11
  532.1 81.4 %copy-start.15 = (bf16[4,64,2048]{2,1,0:T(8,128)(2,1)S(1)}, bf16[4,64,2048]{2,1,0:T(8,128)(2,1)}, u32[]{:S(2)}) copy-start(bf16[4,64,2048]{2,1,0:T(8,128)(2,1)} %copy-done.14) | copy-start | bytes 3145732
  613.5 4.4 copy-start.16
  613.6 4.4 copy-start.39
  704.8 5.1 copy-start.13
  715.4 2.3 copy-start.2
  715.4 2.3 copy-start.9
  715.4 2.3 copy-start.18
  715.4 2.4 copy-start.19
  717.8 12.1 %copy-start.29 = (f32[1024]{0:T(1024)S(1)}, f32[1024]{0:T(1024)}, u32[]{:S(2)}) copy-start(f32[1024]{0:T(1024)} %get-tuple-element.120) | copy-start | bytes 12292
  717.8 12.1 %copy-start.30 = (f32[1024]{0:T(1024)S(1)}, f32[1024]{0:T(1024)}, u32[]{:S(2)}) copy-start(f32[1024]{0:T(1024)} %get-tuple-element.121) | copy-start | bytes 12292
  719.8 13.0 %copy-start.41 = (bf16[1024,256]{1,0:T(8,128)(2,1)S(1)}, bf16[1024,256]{1,0:T(8,128)(2,1)}, u32[]{:S(2)}) copy-start(bf16[1024,256]{1,0:T(8,128)(2,1)} %get-tuple-element.67) | copy-start | bytes 1572868
  720.4 12.4 %copy-start.38 = (bf16[2,4,128,2048]{3,2,1,0:T(8,128)(2,1)S(1)}, bf16[2,4,128,2048]{3,2,1,0:T(8,128)(2,1)}, u32[]{:S(2)}) copy-start(bf16[2,4,128,2048]{3,2,1,0:T(8,128)(2,1)} %get-tuple-element.43) | copy-start | bytes 12582916
  732.9 5.0 copy-start.40
  737.8 5.0 copy-start.20
  743.7 79.5 %collective-permute-start.4 = (bf16[64,2048]{1,0:T(8,128)(2,1)}, bf16[64,2048]{1,0:T(8,128)(2,1)}, u32[]{:S(2)}, u32[]{:S(2)}) collective-permute-start(bf16[64,2048]{1,0:T(8,128)(2,1)} %get-tuple-element.101), channel_id=1, source_target_pairs={{0,8},{1,9},{2,10},{3,11},{4,12},{5,13},{6,14},{7,15},{8,0},{9,1},... | collective-permute-start | bytes 786440 | tf_op jit(solution)/shard_map/ppermute | solution.py:1064
  745.6 77.7 %collective-permute-start.6 = (bf16[64,2048]{1,0:T(8,128)(2,1)}, bf16[64,2048]{1,0:T(8,128)(2,1)}, u32[]{:S(2)}, u32[]{:S(2)}) collective-permute-start(bf16[64,2048]{1,0:T(8,128)(2,1)} %get-tuple-element.102), channel_id=1, source_target_pairs={{0,24},{1,25},{2,26},{3,27},{4,28},{5,29},{6,30},{7,31},{8,16},{9,... | collective-permute-start | bytes 786440 | tf_op jit(solution)/shard_map/ppermute | solution.py:1064
  746.8 76.5 %collective-permute-start.5 = (bf16[64,2048]{1,0:T(8,128)(2,1)}, bf16[64,2048]{1,0:T(8,128)(2,1)}, u32[]{:S(2)}, u32[]{:S(2)}) collective-permute-start(bf16[64,2048]{1,0:T(8,128)(2,1)} %get-tuple-element.103), channel_id=1, source_target_pairs={{0,16},{1,17},{2,18},{3,19},{4,20},{5,21},{6,22},{7,23},{8,24},{9,... | collective-permute-start | bytes 786440 | tf_op jit(solution)/shard_map/ppermute | solution.py:1064
  815.1 3.6 copy-start.21
  815.1 3.6 copy-start.22
  815.1 3.6 copy-start.23
  815.1 3.6 copy-start.33
  817.3 3.0 copy-start.17
  817.3 3.0 copy-start.25
  817.3 3.0 copy-start.35
  817.3 2.9 copy-start.37
  820.3 7.4 copy-start.26
  824.6 13.8 %collective-permute-start.7 = (bf16[64,2048]{1,0:T(8,128)(2,1)S(1)}, bf16[64,2048]{1,0:T(8,128)(2,1)S(1)}, u32[]{:S(2)}, u32[]{:S(2)}) collective-permute-start(bf16[64,2048]{1,0:T(8,128)(2,1)S(1)} %fusion.20), channel_id=1, source_target_pairs={{0,0},{8,1},{16,2},{24,3},{4,4},{12,5},{20,6},{28,7},{9,8},{17,9},... | collective-permute-start | bytes 786440 | tf_op jit(solution)/shard_map/ppermute | solution.py:1064

commit v4 on v3

--- a/solution.py
+++ b/solution.py
@@ -22,6 +22,7 @@
 BF16 = jnp.bfloat16
 VMEM_BYTES = 56 * 1024 * 1024
 PICK_WIDTH = 512
+ATTEND_CHUNK = 512
 SPREAD_WIDTH = 2048
 
 
@@ -33,22 +34,8 @@
     halfway = HEAD_DIM // 2
     frequency = THETA ** (-(jnp.arange(halfway).astype(F32) * 2.0 / HEAD_DIM))
     angles = position.astype(F32)[:, None] * frequency[None, :]
-    cosine = jnp.concatenate([jnp.cos(angles), jnp.cos(angles)], axis=1)
-    sine = jnp.concatenate([jnp.sin(angles), jnp.sin(angles)], axis=1)
-    return cosine, sine
-
-
-def rotate_forward(values, cosine, sine):
-    halfway = values.shape[-1] // 2
-    turned = jnp.concatenate([-values[..., halfway:], values[..., :halfway]], axis=-1)
-    return values * cosine + turned * sine
-
-
-def rotate_backward(upstream, cosine, sine):
-    halfway = upstream.shape[-1] // 2
-    moved = upstream * sine
-    turned = jnp.concatenate([moved[..., halfway:], -moved[..., :halfway]], axis=-1)
-    return upstream * cosine + turned
+    cosine, sine = jnp.cos(angles), jnp.sin(angles)
+    return jnp.concatenate([cosine, cosine], axis=1), jnp.concatenate([-sine, sine], axis=1)
 
 
 def norm_scale(values):
@@ -82,7 +69,7 @@
     ).wait_send()
 
 
-def _greet(u, z, planes, line=False, others=()):
+def _greet(u, z, planes, line=False, others=(), meanwhile=lambda: None):
     barrier = pltpu.get_barrier_semaphore()
     for bit in planes:
         pl.semaphore_signal(barrier, inc=1, device_id=(u ^ bit, z), device_id_type=MESH)
@@ -100,6 +87,7 @@
             pl.semaphore_signal(barrier, inc=1, device_id=(u, z + 1), device_id_type=MESH)
 
         count = count + jnp.where((z == 0) | (z == DEPTH - 1), 1, 2)
+    meanwhile()
     pl.semaphore_wait(barrier, count)
 
 
@@ -198,53 +186,6 @@
         for k in range(3):
             _sent(block(h, u), p_send.at[h, k], here)
         pltpu.make_async_copy(own(h), block(h, u), o_sem.at[h]).wait()
-
-
-def _plane_share_part(u, z, block, half, sems):
-    p_send, p_recv, c_send, c_recv = sems
-    here = (u, z)
-    halves = (pl.ds(0, half), pl.ds(half, half))
-
-    def source(i):
-        return block(u, i)
-
-    for i in range(4):
-        for way, bits in enumerate((FIRST, THEN)):
-            for h in range(2):
-                at = block(u, i).at[halves[h]]
-                _send(at, at, p_send.at[i, h, way], p_recv.at[i, h, way], (u ^ bits[h], z))
-        _send(source(i), block(u, i), c_send.at[i, 0], c_recv.at[i, 0], (u ^ 1, z))
-
-    def share(i):
-        for h in range(2):
-            _expect(block(u ^ THEN[h], i).at[halves[h]], p_recv.at[i, h, 1], here)
-            _expect(block(u ^ 6, i).at[halves[h]], p_recv.at[i, h, 2], here)
-        for k, bit in enumerate((2, 4, 6)):
-            ref = block(u ^ bit, i)
-            _send(ref, ref, c_send.at[i, k + 1], c_recv.at[i, k + 1], (u ^ 1, z))
-
-    for i in range(4):
-        yield
-        for h in range(2):
-            at = halves[h]
-            near = block(u ^ FIRST[h], i).at[at]
-            _expect(near, p_recv.at[i, h, 0], here)
-            _send(near, near, p_send.at[i, h, 2], p_recv.at[i, h, 2], (u ^ THEN[h], z))
-        if i > 0:
-            share(i - 1)
-    yield
-    share(3)
-    yield
-    for i in range(4):
-        for h in range(2):
-            for k in range(3):
-                _sent(block(u, i).at[halves[h]], p_send.at[i, h, k], here)
-        for k, bit in enumerate((0, 2, 4, 6)):
-            _sent(block(u, i), c_send.at[i, k], here)
-            _expect(block(u ^ 1 ^ bit, i), c_recv.at[i, k], here)
-
-
-PLANE_SHARE_SEMS = [DMA((4, 2, 3)), DMA((4, 2, 3)), DMA((4, 4)), DMA((4, 4))]
 
 
 def _plane_sum_part(u, z, source, work, bufs, sems, rows, then_do):
@@ -308,14 +249,13 @@
     return [((u ^ c, z ^ k), c, k) for c in range(2) for k in range(4) if c or k]
 
 
-def _comm(kernel, outs, scratch, collective_id, specs, flops=0, moved=100_000_000, aliases={}):
+def _comm(kernel, outs, scratch, collective_id, specs, flops=0, moved=100_000_000):
     return pl.pallas_call(
         kernel,
         out_shape=outs,
         in_specs=specs[0],
         out_specs=specs[1],
         scratch_shapes=scratch,
-        input_output_aliases=aliases,
         compiler_params=pltpu.CompilerParams(
             collective_id=collective_id, has_side_effects=True, vmem_limit_bytes=VMEM_BYTES
         ),
@@ -324,6 +264,8 @@
 
 
 ENTER_ORDER = (0, 2, 1, 0, 2, 1, 0, 2, 0, 2)
+KV_ORDER = (2, 0, 1, 0, 0, 1, 2, 1, 0, 1)
+PAIR_ORDER = (2, 0, 1, 0, 0, 1, 2, 1, 0, 1)
 LEAVE_ORDER = (0, 1, 2, 1, 2, 1, 0, 0, 1, 0, 1, 1)
 LINE_SEMS = [DMA((2, 4)), DMA((4,)), DMA((4,)), DMA((4,)), DMA]
 PLANE_SEMS = [DMA((2, 3)), DMA((2, 3)), DMA((2,))]
@@ -359,22 +301,26 @@
     return [DMA((n,)), DMA((n, 4)), DMA((n, 4)), DMA((n, 8)), DMA((n, 8))]
 
 
-def enter(rows, weights, smalls, collective_id):
-    R, C = weights.shape[1], weights.shape[2] // 8
+def _packed(router, gains):
+    lane = lax.broadcasted_iota(jnp.int32, (router.shape[0], 128 - EXPERTS), 1)
+    tail = jnp.zeros(lane.shape, F32)
+    for j in range(1, 4):
+        tail = jnp.where(lane == j - 1, gains[:, j : j + 1], tail)
+    return router, tail.astype(BF16)
+
+
+def enter(hidden, weights, gains, router, routes, collective_id):
+    T, D = hidden.shape
+    R, C = weights[0].shape[0], weights[0].shape[1] // 8
     held = (2, 4, R, 3 * C)
-    n = len(smalls)
-
-    def kernel(*refs):
-        x_ref, w_ref = refs[:2]
-        small_in = refs[2 : 2 + n]
-        x_out, w_out = refs[2 + n : 4 + n]
-        small_out = refs[4 + n : 4 + 2 * n]
-        w_buf, w_send, w_recv = refs[4 + 2 * n : 7 + 2 * n]
-        sems = refs[7 + 2 * n :]
+    strip = 16
+
+    def kernel(h_ref, wq_ref, wk_ref, wv_ref, gain_ref, router_ref, route_ref, x_out, w_out, p_out, r_out, *refs):
+        x_ref, w_ref, pack_ref, w_buf, w_send, w_recv = refs[:6]
+        sems = refs[6:]
         u, z = lax.axis_index("uly"), lax.axis_index("blk")
         here, core, chip = (u, z), u % 2, u // 2
         column = _column_peers(u, z)
-        _greet(u, z, range(1, 8), others=[to for to, c, k in column if k])
 
         def weight_part():
             def cut(j, c, level):
@@ -397,57 +343,90 @@
                 for j in range(3):
                     _sent(cut(j, core ^ c, z ^ k), w_send.at[i, j], here)
 
+        def prepare():
+            gains = gain_ref[...].astype(F32)
+            for j, ref in enumerate((wq_ref, wk_ref, wv_ref)):
+                w_ref[j] = (ref[...].astype(F32) * gains[:, :1]).astype(BF16)
+
+            def norm(i, _):
+                at = pl.ds(pl.multiple_of(i * strip, strip), strip)
+                value = h_ref[at, :].astype(F32)
+                x_ref[at, :] = (value * norm_scale(value)).astype(BF16)
+                return 0
+
+            lax.fori_loop(0, T // strip, norm, 0)
+            pack_ref[:, pl.ds(0, EXPERTS)], pack_ref[:, pl.ds(EXPERTS, 128 - EXPERTS)] = _packed(router_ref[...], gains)
+
+        _greet(u, z, range(1, 8), others=[to for to, c, k in column if k], meanwhile=prepare)
         _run(
             weight_part(),
-            _small_part(u, z, small_in, small_out, sems[8:]),
+            _small_part(u, z, (pack_ref, route_ref), (p_out, r_out), sems[8:]),
             _line_part(u, z, x_ref, lambda c, level: x_out.at[c, level], sems[3:8]),
             order=ENTER_ORDER,
         )
 
     outs = [
-        jax.ShapeDtypeStruct((2, 4) + rows.shape, rows.dtype),
-        jax.ShapeDtypeStruct((4,) + held, weights.dtype),
-    ] + [jax.ShapeDtypeStruct((8, 4) + x.shape, x.dtype) for x in smalls]
-    scratch = [pltpu.VMEM(held, BF16), DMA((7, 3)), DMA((7, 3))] + PLANE_SEMS + LINE_SEMS + _small_sems(n)
-    specs = ([IN_VMEM, IN_VMEM] + [IN_VMEM] * n, [ANY_SPACE] * len(outs))
-    return _comm(kernel, outs, scratch, collective_id, specs)(rows, weights, *smalls)
-
-
-def column_sum(x, collective_id):
-    def kernel(x_ref, o_ref, buf, send, recv):
+        jax.ShapeDtypeStruct((2, 4, T, D), BF16),
+        jax.ShapeDtypeStruct((4,) + held, BF16),
+        jax.ShapeDtypeStruct((8, 4, R, 128), BF16),
+        jax.ShapeDtypeStruct((8, 4) + routes.shape, routes.dtype),
+    ]
+    scratch = [pltpu.VMEM((T, D), BF16), pltpu.VMEM((3, R, D), BF16), pltpu.VMEM((R, 128), BF16)]
+    scratch += [pltpu.VMEM(held, BF16), DMA((7, 3)), DMA((7, 3))] + PLANE_SEMS + LINE_SEMS + _small_sems(2)
+    specs = ([IN_VMEM] * 7, [ANY_SPACE] * 4)
+    return _comm(kernel, outs, scratch, collective_id, specs)(hidden, *weights, gains, router, routes)
+
+
+def _column_sum_part(u, z, x_ref, total, buf, sems, then_do):
+    send, recv = sems
+    here = (u, z)
+    column = _column_peers(u, z)
+    for i, (to, c, k) in enumerate(column):
+        _send(x_ref, buf.at[i], send.at[i], recv.at[i], to)
+    yield
+    value = x_ref[...]
+    for i in range(7):
+        _expect(buf.at[i], recv.at[i], here)
+        value = value + buf[i]
+    total[...] = value
+    then_do()
+    yield
+    for i in range(7):
+        _sent(x_ref, send.at[i], here)
+
+
+def plane_pair(first, second, rows, squares, collective_id):
+    R = squares.shape[0] // 2
+
+    def kernel(a_ref, b_ref, x_ref, s_ref, a_out, b_out, x_out, s_out, k_out, buf, *sems):
         u, z = lax.axis_index("uly"), lax.axis_index("blk")
-        here = (u, z)
-        column = _column_peers(u, z)
-        _greet(u, z, (), others=[to for to, c, k in column])
-        for i, (to, c, k) in enumerate(column):
-            _send(x_ref, buf.at[i], send.at[i], recv.at[i], to)
-        total = x_ref[...]
-        for i in range(7):
-            _expect(buf.at[i], recv.at[i], here)
-            total = total + buf[i]
-        o_ref[...] = total
-        for i in range(7):
-            _sent(x_ref, send.at[i], here)
-
-    scratch = [pltpu.VMEM((7,) + x.shape, F32), DMA((7,)), DMA((7,))]
-    out = jax.ShapeDtypeStruct(x.shape, F32)
-    return _comm(kernel, out, scratch, collective_id, ([IN_VMEM], IN_VMEM))(x)
-
-
-def plane_pair(first, second, rows, collective_id):
-    def kernel(a_ref, b_ref, x_ref, a_out, b_out, x_out, *sems):
-        u, z = lax.axis_index("uly"), lax.axis_index("blk")
-        _greet(u, z, (2, 4), line=True)
+        here, chip = (u, z), u // 2
+        k_send, k_recv = sems[10:]
+        _greet(u, z, (2, 4, 6), others=[to for to, c, k in _column_peers(u, z)])
         own, outs = (a_ref, b_ref), (a_out, b_out)
+        keys = s_out.at[pl.ds(R, R)]
+
+        def tell():
+            k_out[chip] = keys[...]
+            for i, bit in enumerate((2, 4, 6)):
+                _send(keys, k_out.at[chip], k_send.at[i], k_recv.at[i], (u ^ bit, z))
+
         _run(
             _plane_part(u, z, lambda h: own[h], lambda h, v: outs[h].at[v // 2], sems[:3]),
-            _line_part(u, z, x_ref, lambda c, level: x_out.at[u * DEPTH + level], sems[3:], share=False),
+            _line_part(u, z, x_ref, lambda c, level: x_out.at[level], sems[3:8], share=False),
+            _column_sum_part(u, z, s_ref, s_out, buf, sems[8:10], tell),
+            order=PAIR_ORDER,
         )
+        for i, bit in enumerate((2, 4, 6)):
+            _expect(k_out.at[(u ^ bit) // 2], k_recv.at[i], here)
+            _sent(keys, k_send.at[i], here)
 
     outs = [jax.ShapeDtypeStruct((4,) + x.shape, x.dtype) for x in (first, second)]
-    outs += [jax.ShapeDtypeStruct((32,) + rows.shape, rows.dtype)]
-    specs = ([IN_VMEM] * 2 + [ANY_SPACE], [ANY_SPACE] * 3)
-    return _comm(kernel, outs, PLANE_SEMS + LINE_SEMS, collective_id, specs)(first, second, rows)
+    outs += [jax.ShapeDtypeStruct((4,) + rows.shape, rows.dtype)]
+    outs += [jax.ShapeDtypeStruct(squares.shape, F32), jax.ShapeDtypeStruct((4, R, 128), F32)]
+    specs = ([IN_VMEM] * 2 + [ANY_SPACE, IN_VMEM], [ANY_SPACE] * 3 + [IN_VMEM] * 2)
+    scratch = [pltpu.VMEM((7,) + squares.shape, F32)] + PLANE_SEMS + LINE_SEMS + [DMA((7,)), DMA((7,)), DMA((3,)), DMA((3,))]
+    return _comm(kernel, outs, scratch, collective_id, specs)(first, second, rows, squares)
 
 
 def column_gather(rows, slot, out_rows, collective_id):
@@ -477,41 +456,46 @@
     return [pltpu.VMEM((4, T, D), BF16), pltpu.VMEM((4, T, D), BF16), pltpu.VMEM((2, 4, T, D), BF16)]
 
 
-def column_scatter(x, rows, collective_id):
+def column_scatter(x, collective_id):
     T, D = x.shape[2:]
 
-    def kernel(x_ref, g_ref, o_ref, g_out, work, c_buf, z_buf, *sems):
+    def kernel(x_ref, o_ref, work, c_buf, z_buf, *sems):
         u, z = lax.axis_index("uly"), lax.axis_index("blk")
-        _greet(u, z, (1, 2, 4), line=True)
+        _greet(u, z, (1,), line=True)
 
         def finish():
             o_ref[...] = work[3]
 
-        _run(
-            _line_sum_part(u, z, lambda c, level: x_ref.at[c, level], work, (c_buf, z_buf), sems[:5], T, finish),
-            _plane_share_part(u, z, lambda who, i: g_out.at[who * DEPTH + i], T // 2, sems[5:]),
-        )
-
-    outs = [jax.ShapeDtypeStruct((T, D), BF16), jax.ShapeDtypeStruct((32, T, D), BF16)]
-    scratch = _line_sum_scratch(T, D) + LINE_SUM_SEMS + PLANE_SHARE_SEMS
-    specs = ([ANY_SPACE] * 2, [IN_VMEM, ANY_SPACE])
-    out, gathered = _comm(kernel, outs, scratch, collective_id, specs, aliases={1: 1})(x, rows)
-    return out, gathered.reshape(32 * T, D)
+        _run(_line_sum_part(u, z, lambda c, level: x_ref.at[c, level], work, (c_buf, z_buf), sems, T, finish))
+
+    scratch = _line_sum_scratch(T, D) + LINE_SUM_SEMS
+    return _comm(kernel, jax.ShapeDtypeStruct((T, D), BF16), scratch, collective_id, ([ANY_SPACE], IN_VMEM))(x)
 
 
 def _plane_sum_scratch(rows, cols):
     return [pltpu.VMEM((2, 2, rows, cols), BF16), pltpu.VMEM((2, 2, rows, cols), BF16), pltpu.VMEM((2, rows, cols), BF16)]
 
 
-def key_value_sums(dk, dv, x, collective_id):
+def key_value_sums(dk, dv, x, inner, collective_id):
     T, D = x.shape[1:]
     L, C = dk.shape[1:]
-
-    def kernel(k_ref, v_ref, x_ref, k_out, v_out, x_out, work, p_buf, q_buf, x_work, z_buf, *sems):
+    R = inner.shape[0] // 5
+
+    def kernel(
+        k_ref, v_ref, x_ref, s_ref, k_out, v_out, x_out, s_out, work, p_buf, q_buf, x_work, z_buf, buf, total, k_buf, *sems
+    ):
         u, z = lax.axis_index("uly"), lax.axis_index("blk")
-        _greet(u, z, (2, 4), line=True)
-        load, z_send, z_recv = sems[5:]
+        here, chip = (u, z), u // 2
+        _greet(u, z, (2, 4, 6), others=[to for to, c, k in _column_peers(u, z)])
+        load, z_send, z_recv, k_send, k_recv = sems[7:]
         order = tuple(reversed(_line_order(z)))
+
+        def keys(v):
+            return total.at[pl.ds(pl.multiple_of((v // 2 + 1) * R, R), R)]
+
+        def tell():
+            for i, bit in enumerate((2, 4, 6)):
+                _send(keys(u ^ bit), k_buf.at[i], k_send.at[i], k_recv.at[i], (u ^ bit, z))
 
         def finish():
             k_out[...] = work[0, 0]
@@ -535,14 +519,24 @@
                 u, z, lambda h, v: (k_ref, v_ref)[h].at[v // 2], work, (p_buf, q_buf), sems[:5], L, finish
             ),
             line(),
-            order=(0, 1, 0, 0),
+            _column_sum_part(u, z, s_ref, total, buf, sems[5:7], tell),
+            order=KV_ORDER,
         )
+        value = keys(u)[...]
+        for i, bit in enumerate((2, 4, 6)):
+            _expect(k_buf.at[i], k_recv.at[i], here)
+            value = value + k_buf[i]
+            _sent(k_buf.at[i], k_send.at[i], here)
+        s_out[pl.ds(0, R), :] = total[pl.ds(0, R), :]
+        s_out[pl.ds(R, R), :] = value
 
     outs = [jax.ShapeDtypeStruct((L, C), BF16)] * 2 + [jax.ShapeDtypeStruct((T, D), BF16)]
+    outs += [jax.ShapeDtypeStruct((2 * R, 128), F32)]
     scratch = _plane_sum_scratch(L, C) + [pltpu.VMEM((4, T, D), BF16), pltpu.VMEM((2, 4, T, D), BF16)]
-    scratch += PLANE_SUM_SEMS + [DMA((4,)), DMA((4,)), DMA((2, 4))]
-    specs = ([ANY_SPACE] * 3, [IN_VMEM] * 3)
-    return _comm(kernel, outs, scratch, collective_id, specs)(dk, dv, x)
+    scratch += [pltpu.VMEM((7,) + inner.shape, F32), pltpu.VMEM(inner.shape, F32), pltpu.VMEM((3, R, 128), F32)]
+    scratch += PLANE_SUM_SEMS + [DMA((7,)), DMA((7,)), DMA((4,)), DMA((4,)), DMA((2, 4)), DMA((3,)), DMA((3,))]
+    specs = ([ANY_SPACE] * 3 + [IN_VMEM], [IN_VMEM] * 4)
+    return _comm(kernel, outs, scratch, collective_id, specs)(dk, dv, x, inner)
 
 
 def leave(x, weights, smalls, collective_id):
@@ -597,6 +591,51 @@
     return _comm(kernel, outs, scratch, collective_id, specs)(x, weights, *smalls)
 
 
+def _finish_kernel(
+    h_ref, r_ref, rg_ref, first_ref, sum_ref, wq_ref, wk_ref, wv_ref, dw_ref, do_ref, gain_ref, out_ref, hg_ref, ag_ref, *dws
+):
+    out_ref[...] = (r_ref[...] + sum_ref[...].astype(F32)).astype(BF16)
+    hidden, weighted = h_ref[...].astype(F32), first_ref[...].astype(F32)
+    scale = norm_scale(hidden)
+    mean = jnp.mean(weighted * hidden, axis=-1, keepdims=True)
+    hg_ref[...] = rg_ref[...] + scale * weighted - hidden * (scale * scale * scale) * mean
+    gain = gain_ref[...].astype(F32)[:, :1]
+    total = jnp.zeros(dws[0].shape, F32)
+    for j, ref in enumerate((wq_ref, wk_ref, wv_ref)):
+        grad = dw_ref[j].astype(F32)
+        total = total + grad * ref[...].astype(F32)
+        dws[j][...] = grad * gain
+    ag_ref[...] = jnp.sum(total, axis=1, keepdims=True)
+    dws[3][...] = do_ref[...].astype(F32)
+
+
+def finish(hidden, residual, residual_grad, first_weighted, out_sum, weights, weight_sum, out_weight_grad, gains):
+    T, D = hidden.shape
+    R = gains.shape[0]
+    steps = 4 if R % 64 == 0 else 1
+
+    def rows(count, width):
+        return pl.BlockSpec((count // steps, width), lambda i: (i, 0))
+
+    tokens, dense = rows(T, D), rows(R, D)
+    return pl.pallas_call(
+        _finish_kernel,
+        out_shape=[
+            jax.ShapeDtypeStruct((T, D), BF16),
+            jax.ShapeDtypeStruct((T, D), F32),
+            jax.ShapeDtypeStruct((R, 1), F32),
+        ]
+        + [jax.ShapeDtypeStruct((R, D), F32)] * 4,
+        grid=(steps,),
+        in_specs=[tokens] * 5
+        + [dense] * 3
+        + [pl.BlockSpec((3, R // steps, D), lambda i: (0, i, 0)), dense, rows(R, 4)],
+        out_specs=[tokens, tokens, rows(R, 1)] + [dense] * 4,
+        compiler_params=pltpu.CompilerParams(vmem_limit_bytes=VMEM_BYTES),
+        cost_estimate=pl.CostEstimate(flops=20 * T * D, bytes_accessed=24 * T * D, transcendentals=0),
+    )(hidden, residual, residual_grad, first_weighted, out_sum, *weights, weight_sum, out_weight_grad, gains)
+
+
 class _Jobs:
     def __init__(self, load, compute):
         self.load, self.compute = load, compute
@@ -624,11 +663,13 @@
 
 
 def _gather_pick_kernel(
-    x_ref, g_ref, slot_ref, router_ref, o_ref, xr_ref, gr_ref, gate_ref, pick, in_buf, out_buf, in_sem, out_sem, *sems, width
+    x_ref, g0, g1, g2, g3, slot_ref, router_ref, o_ref, xr_ref, gr_ref, gate_ref, other_g, pick, in_buf, out_buf, in_sem, out_sem, *sems, width
 ):
-    own_sem, z_send, z_recv, p_send, p_recv, c_send, c_recv = sems
+    own_sem, z_send, z_recv, p_send, p_recv, c_send, c_recv, g_send, g_recv = sems
+    own_g = (g0, g1, g2, g3)
     u, z = lax.axis_index("uly"), lax.axis_index("blk")
-    core = u % 2
+    core, chip = u % 2, u // 2
+    other = 1 - core
     T, D = x_ref.shape
     experts, group = slot_ref.shape[1:]
     slots = out_buf.shape[2]
@@ -647,12 +688,16 @@
         return o_ref.at[who * DEPTH + level, halves[h]]
 
     def load(n, job, start):
-        source, level, which = job[:3]
-        ref = g_ref if source == "g" else o_ref
-        for p in range(4):
-            copy = pltpu.make_async_copy(
-                ref.at[(2 * p + which) * DEPTH + level], in_buf.at[n % 2, pl.ds(p * T, T)], in_sem.at[n % 2, p]
-            )
+        source, level, which = job
+        steps = (0, jnp.where(which == 0, 1, 2), jnp.where(which == 0, 2, 1), 3)
+        for k in range(4):
+            p = chip ^ steps[k]
+            if source == "x":
+                ref = o_ref.at[(2 * p + which) * DEPTH + level]
+            else:
+                ref = (own_g[k] if which is core else other_g.at[k]).at[level]
+            rows = pl.ds(pl.multiple_of(p * T, T), T)
+            copy = pltpu.make_async_copy(ref, in_buf.at[n % 2, rows], in_sem.at[n % 2, k])
             copy.start() if start else copy.wait()
 
     def out_copy(n, target, at):
@@ -669,14 +714,17 @@
             picks = [jnp.where(slot_ref[at, e : e + 1, :] == row, 1.0, 0.0).astype(BF16) for e in range(experts)]
             pick[at] = jnp.concatenate(picks, axis=0)
         else:
-            logits = lax.dot_general(
-                router_ref[...], rows_in[...], (((0,), (1,)), ((), ())), preferred_element_type=F32
-            )
-            powers = jnp.exp(logits - jnp.max(logits, axis=0, keepdims=True))
-            chances = powers / jnp.sum(powers, axis=0, keepdims=True)
+            logits = dot(rows_in[...], router_ref[...])
+            powers = jnp.exp(logits - jnp.max(logits, axis=1, keepdims=True))
+            chances = powers / jnp.sum(powers, axis=1, keepdims=True)
+            high = chances.astype(BF16)
+            low = (chances - high.astype(F32)).astype(BF16)
+            gates = dot(pick[at], jnp.concatenate([high, low], axis=1))
+            lane = lax.broadcasted_iota(jnp.int32, (slots, 2 * EXPERTS), 1)
             for e in range(experts):
-                gates = jnp.where(slot_ref[at, e : e + 1, :] == row, chances[e : e + 1, :], 0.0)
-                gate_ref[e, at] = jnp.broadcast_to(jnp.sum(gates, axis=1, keepdims=True), (slots, 128))
+                part = gates[e * slots : (e + 1) * slots]
+                part = jnp.where((lane == e) | (lane == EXPERTS + e), part, 0.0)
+                gate_ref[e, at] = jnp.broadcast_to(jnp.sum(part, axis=1, keepdims=True), (slots, 128))
         if n >= 2:
             sent.pop(n - 2).wait()
 
@@ -692,7 +740,7 @@
         sent[n].start()
 
     jobs = _Jobs(load, compute)
-    jobs.add(*[("g", level, c) for level in range(4) for c in range(2)])
+    jobs.add(*[("g", level, core) for level in range(4)])
 
     def along(level, source, step):
         @pl.when((z > 0) & (level >= z))
@@ -743,13 +791,18 @@
         level = order[i]
         for k, bit in enumerate((0, 2, 4, 6)):
             _expect(block(u ^ 1 ^ bit, level), c_recv.at[level, k], here)
-        jobs.add(("x", level, 1 - core))
+        jobs.add(("x", level, other))
 
     arrive(0)
+    for k in range(4):
+        _send(own_g[k], other_g.at[k], g_send.at[k], g_recv.at[k], (u ^ 1, z))
     jobs.run(2)
     onward(0)
     jobs.run(1)
     arrive(1)
+    for k in range(4):
+        _expect(other_g.at[k], g_recv.at[k], here)
+    jobs.add(*[("g", level, other) for level in range(4)])
     jobs.run(2)
     own.wait()
     share(0)
@@ -780,11 +833,13 @@
                 _sent(part(u, level, h), p_send.at[level, h, k], here)
         for k in range(4):
             _sent(block(u, level), c_send.at[level, k], here)
+    for k in range(4):
+        _sent(other_g.at[k], g_send.at[k], here)
     for copy in sent.values():
         copy.wait()
 
 
-def gather_pick(x, g_all, slot, router, slots, collective_id):
+def gather_pick(x, g, slot, router, slots, collective_id):
     T, D = x.shape
     groups, EL, group = slot.shape
     picked = jax.ShapeDtypeStruct((EL, groups, slots, D), BF16)
@@ -793,6 +848,7 @@
         picked,
         picked,
         jax.ShapeDtypeStruct((EL, groups, slots, 128), F32),
+        jax.ShapeDtypeStruct((4, 4, T, D), BF16),
     ]
     scratch = [
         pltpu.VMEM((groups, EL * slots, group), BF16),
@@ -807,10 +863,12 @@
         DMA((4, 2, 3)),
         DMA((4, 4)),
         DMA((4, 4)),
+        DMA((4,)),
+        DMA((4,)),
     ]
-    specs = ([IN_VMEM, ANY_SPACE, IN_VMEM, IN_VMEM], [ANY_SPACE] * 3 + [IN_VMEM])
+    specs = ([IN_VMEM] + [ANY_SPACE] * 4 + [IN_VMEM] * 2, [ANY_SPACE] * 3 + [IN_VMEM, ANY_SPACE])
     kernel = functools.partial(_gather_pick_kernel, width=PICK_WIDTH)
-    out, xr, gr, gates = _comm(kernel, outs, scratch, collective_id, specs)(x, g_all.reshape(32, T, D), slot, router)
+    out, xr, gr, gates, _ = _comm(kernel, outs, scratch, collective_id, specs)(x, *g, slot, router)
     return out.reshape(32 * T, D), xr, gr, gates
 
 
@@ -1044,18 +1102,17 @@
         self.group = 2 * self.z + self.u % 2
         self.first_block, self.block_step = 8 * (self.u // 2), 1
 
-    def enter(self, rows, scaled, out_weight, pack, routes):
-        rows, weights, packs, routes = enter(rows, scaled, [pack, routes], 1)
+    def enter(self, hidden, weights, gains, out_weight, router, routes):
+        rows, weights, packs, routes = enter(hidden, weights, gains, router, routes, 1)
         there = [((2 * ((z + u // 2) % 4) + u % 2), u // 2) for u in range(8) for z in range(4)]
         self.forth = [(i, 4 * u + z) for i, (u, z) in enumerate(there)]
-        mine = self.permute(out_weight, self.forth)
-        outs = jnp.stack([mine] + [self.permute(mine, self.across(bit)) for bit in (2, 4, 6)])
-        part = jnp.arange(4, dtype=jnp.int32)
-        outs = outs[(self.u // 2) ^ ((part + self.z) % 4)]
+        rows, mine = lax.optimization_barrier((rows, self.permute(out_weight, self.forth)))
+        self.out_parts = [mine] + [self.permute(mine, self.across(bit)) for bit in (2, 4, 6)]
+        self.parts = [((self.u // 2) ^ k) - self.z + 4 for k in range(4)]
+        self.parts = [p % 4 for p in self.parts]
         return (
             rows.reshape(self.L, self.D),
             weights.reshape(self.D, 3 * self.C),
-            outs.reshape(self.C, self.D),
             packs.reshape(self.D, -1),
             routes,
         )
@@ -1066,26 +1123,26 @@
     def across(self, bit):
         return [(i, i ^ (4 * bit)) for i in range(32)]
 
-    def head_sum(self, x):
-        return column_sum(x, 2)
-
-    def head_sum_again(self, x):
-        return column_sum(x, 3)
-
-    def sequence(self, key, value, upstream):
-        keys, values, self.upstream_line = plane_pair(key, value, upstream, 4)
-        return keys.reshape(-1, self.C), values.reshape(-1, self.C)
+    def sequence(self, key, value, squares, upstream):
+        keys, values, own, stats, k_stat = plane_pair(key, value, upstream, squares.reshape(-1, 128), 4)
+        own, *self.out_parts = lax.optimization_barrier((own, *self.out_parts))
+        first = [(i, i ^ (8 if i // 4 % 2 == 0 else 16)) for i in range(32)]
+        self.then = [(i, i ^ (16 if i // 4 % 2 == 0 else 8)) for i in range(32)]
+        self.upstream = (own, self.permute(own, first))
+        return keys.reshape(-1, self.C), values.reshape(-1, self.C), stats.reshape(2, -1, 128), k_stat.reshape(-1, 128)
 
     def heads_to_rows(self, x):
-        return column_scatter(x.reshape(2, 4, self.T, self.D), self.upstream_line, 5)
-
-    def experts(self, second_low, upstream_all, routes, weights, router):
+        x, own, near = lax.optimization_barrier((x, *self.upstream))
+        self.upstream = (own, near, self.permute(own, self.then), self.permute(near, self.then))
+        return column_scatter(x.reshape(2, 4, self.T, self.D), 5)
+
+    def experts(self, second_low, routes, weights, router):
         EL, T, D = weights.shape[0], self.T, self.D
         slots = -(-4 * CAP // 16) * 16
         chosen = jnp.any(routes[None] == (self.u * EL + jnp.arange(EL, dtype=jnp.int32))[:, None, None, None, None], axis=3)
         chosen = chosen.reshape(EL, 4, 2, 4, T).transpose(3, 2, 0, 1, 4).reshape(8, EL, 4 * T)
         slot = slots_of(chosen)
-        second_all, xr, gr, gates = gather_pick(second_low, upstream_all, slot, router, slots, 7)
+        second_all, xr, gr, gates = gather_pick(second_low, self.upstream, slot, router, slots, 7)
         flat, cut = (EL, 8 * slots, -1), (EL, 8, slots, -1)
         out_rows, entry_rows, self.expert_grads, gate_grads = run_experts(
             xr.reshape(flat), gr.reshape(flat), gates.reshape(flat), weights, 8 * slots
@@ -1097,23 +1154,21 @@
         rows, self.out_line = column_gather(x, self.slot, self.out_rows, 6)
         return rows.reshape(self.L, self.D), self.expert_grads
 
-    def sequence_sums(self, dk, dv, out_part):
+    def sequence_sums(self, dk, dv, out_part, q_inner, k_inner):
         cut = (4, self.L, self.C)
-        dk, dv, out_sum = key_value_sums(dk.reshape(cut), dv.reshape(cut), self.out_line, 10)
+        inner = jnp.concatenate([q_inner, k_inner.reshape(-1, 128)], axis=0)
+        dk, dv, out_sum, inner = key_value_sums(dk.reshape(cut), dv.reshape(cut), self.out_line, inner, 10)
         parts = out_part.reshape(4, -1, self.D)
-        chip = self.u // 2
-
-        def part(bit):
-            return lax.dynamic_index_in_dim(parts, ((chip ^ (bit // 2)) - self.z) % 4, 0, False)
-
-        total = part(0).astype(F32)
-        for bit in (2, 4, 6):
-            total = total + self.permute(part(bit), self.across(bit)).astype(F32)
-        out_grad = self.permute(total.astype(BF16), [(b, a) for a, b in self.forth])
-        return dk, dv, out_grad, out_sum
+        mine, *others = [lax.dynamic_index_in_dim(parts, p, 0, False) for p in self.parts]
+        dk, *others = lax.optimization_barrier((dk, *others))
+        self.out_terms = [mine] + [self.permute(x, self.across(bit)) for x, bit in zip(others, (2, 4, 6))]
+        return dk, dv, out_sum, inner.reshape(2, -1, 128)
 
     def leave(self, first_part, weight_part, logit_grad, ffn_part, head_parts):
         T, R = self.T, self.D // 32
+        first_part, *terms = lax.optimization_barrier((first_part, *self.out_terms))
+        out_grad = sum(x.astype(F32) for x in terms).astype(BF16)
+        out_grad = self.permute(out_grad, [(b, a) for a, b in self.forth])
         thin = jnp.concatenate([ffn_part.reshape(-1, 128), head_parts.reshape(-1, 128)], axis=0)
         wide = self.D // 128
         used = thin.shape[0]
@@ -1131,7 +1186,7 @@
         mine = lax.dynamic_index_in_dim(mine, self.u // 2, 1, False)
         heads = jnp.sum(mine[:, wide:used], axis=0).reshape(2, self.C)
         heads = lax.dynamic_slice_in_dim(heads, self.z * R, R, 1)
-        return first, weights, logit_all.reshape(32 * T, EXPERTS), ffn, heads
+        return first, weights, out_grad, logit_all.reshape(32 * T, EXPERTS), ffn, heads
 
 
 class General:
@@ -1141,6 +1196,7 @@
         self.C = D // U
         self.L = U * T
         self.group = self.u
+        self.parts = range(4)
         self.first_block, self.block_step = self.z, Z
 
     def gather(self, x):
@@ -1149,31 +1205,32 @@
     def scatter_wide(self, x):
         return lax.psum_scatter(x, ALL, scatter_dimension=0, tiled=True)
 
-    def enter(self, rows, scaled, out_weight, pack, routes):
-        U, R = self.U, scaled.shape[1]
+    def enter(self, hidden, weights, gains, out_weight, router, routes):
+        U, R = self.U, router.shape[0]
+        gains, hidden = gains.astype(F32), hidden.astype(F32)
+        scaled = jnp.stack([(w.astype(F32) * gains[:, :1]).astype(BF16) for w in weights])
+        pack = jnp.concatenate(_packed(router, gains), axis=1)
+        rows = (hidden * norm_scale(hidden)).astype(BF16)
+        self.out_parts = jnp.split(lax.all_gather(out_weight, "blk", axis=0, tiled=True), 4)
         swapped = lax.all_to_all(scaled.transpose(1, 0, 2).reshape(R, 3, U, self.C), "uly", split_axis=2, concat_axis=0, tiled=True)
         weights = lax.all_gather(swapped.reshape(U, R, 3 * self.C), "blk", axis=1, tiled=True)
         return (
             self.rows_all(rows),
             weights.reshape(self.D, 3 * self.C),
-            lax.all_gather(out_weight, "blk", axis=0, tiled=True),
             self.gather(pack),
             self.gather(routes[None]).reshape((U, self.Z) + routes.shape),
         )
 
-    def head_sum(self, x):
-        return lax.psum(x, "uly")
-
-    head_sum_again = head_sum
-
-    def sequence(self, key, value, upstream):
+    def sequence(self, key, value, squares, upstream):
         self.upstream = upstream
         pair = jnp.stack([key, value]).reshape(2, self.U, self.T, self.C)
         pair = lax.all_gather(pair, "blk", axis=2, tiled=False).reshape(2, -1, self.C)
-        return pair[0], pair[1]
+        stats = lax.psum(squares, "uly")
+        k_stat = lax.all_gather(stats[1].reshape(self.U, -1, 128), "blk", axis=1, tiled=False).reshape(-1, 128)
+        return pair[0], pair[1], stats, k_stat
 
     def heads_to_rows(self, x):
-        return self.rows_sum(x), self.gather(self.upstream)
+        return self.rows_sum(x)
 
     def rows_sum(self, x):
         return lax.psum_scatter(x, "uly", scatter_dimension=0, tiled=True)
@@ -1181,10 +1238,10 @@
     def rows_all(self, x):
         return lax.all_gather(x, "uly", axis=0, tiled=True)
 
-    def experts(self, second_low, upstream_all, routes, weights, router):
+    def experts(self, second_low, routes, weights, router):
         EL, D = weights.shape[0], self.D
+        second_all, upstream_all = self.gather(second_low), self.gather(self.upstream)
         N = upstream_all.shape[0]
-        second_all = self.gather(second_low)
         group = min(512, N)
         groups = N // group
         slots = -(-(group // self.T * CAP) // 16) * 16
@@ -1211,10 +1268,15 @@
     def rows_to_heads(self, x):
         return self.rows_all(x), self.expert_grads
 
-    def sequence_sums(self, dk, dv, out_part):
+    def sequence_sums(self, dk, dv, out_part, q_inner, k_inner):
         pair = jnp.stack([dk, dv]).reshape(2, self.U, self.Z, self.T, self.C)
         pair = lax.psum_scatter(pair, "blk", scatter_dimension=2, tiled=True).reshape(2, self.L, self.C)
-        return pair[0], pair[1], lax.psum_scatter(out_part, "blk", scatter_dimension=0, tiled=True), self.out_sum
+        k_inner = lax.psum_scatter(
+            k_inner.reshape(self.U, self.Z, -1, 128), "blk", scatter_dimension=1, tiled=True
+        ).reshape(-1, 128)
+        inner = lax.psum(jnp.stack([q_inner, k_inner]), "uly")
+        self.out_grad = lax.psum_scatter(out_part, "blk", scatter_dimension=0, tiled=True)
+        return pair[0], pair[1], self.out_sum, inner
 
     def leave(self, first_part, weight_part, logit_grad, ffn_part, head_parts):
         U, R = self.U, self.D // (self.U * self.Z)
@@ -1223,7 +1285,8 @@
         part = lax.all_to_all(part, "uly", split_axis=0, concat_axis=0, tiled=True)
         weights = part.reshape(U, R, 3, self.C).transpose(2, 1, 0, 3).reshape(3, R, self.D)
         heads = lax.psum_scatter(head_parts, "blk", scatter_dimension=1, tiled=True)
-        return self.rows_sum(first_part), weights, self.gather(logit_grad), self.scatter_wide(ffn_part), heads
+        first = self.rows_sum(first_part)
+        return first, weights, self.out_grad, self.gather(logit_grad), self.scatter_wide(ffn_part), heads
 
 
 def _row_limits(doc_ref, first, rows):
@@ -1237,30 +1300,67 @@
     return position, start, lowest
 
 
-def _scores(query, key, position, start, key_first, scaling):
-    raw = dot(query, key, LAST_DIM) * scaling
+def _norm_row(squares, width):
+    return lax.rsqrt(squares * (1.0 / width) + EPS)
+
+
+def _as_column(row):
+    return jnp.broadcast_to(row, (128, 128)).T
+
+
+def _row_sums(values):
+    ones = jnp.ones((8, values.shape[1]), F32)
+    return lax.dot_general(ones, values, LAST_DIM, precision=lax.Precision.HIGHEST, preferred_element_type=F32)[:1]
+
+
+def _key_scales(stat_ref, at, chunk, width):
+    rows = stat_ref[pl.ds(pl.multiple_of(at // 128, chunk // 128), chunk // 128), :]
+    return _norm_row(jnp.concatenate([rows[r : r + 1] for r in range(chunk // 128)], axis=1), width)
+
+
+def _scores(query, key, factor, position, start, key_first):
+    raw = dot(query, key, LAST_DIM) * factor
     key_position = key_first + lax.broadcasted_iota(jnp.int32, raw.shape, 1)
     return jnp.where((key_position <= position) & (key_position >= start), raw, NEG)
 
 
-def _attend_kernel(index_ref, doc_ref, q_ref, k_ref, v_ref, o_ref, log_ref, *, chunk, scaling):
+def _scaled_query(q_ref, stat_ref, width):
+    heads = q_ref.shape[1] // HEAD_DIM
+    scale = _as_column(_norm_row(stat_ref[pl.ds(pl.program_id(0), 1), :], width))
+    cols = [pl.ds(h * HEAD_DIM, HEAD_DIM) for h in range(heads)]
+    return [(q_ref[:, at].astype(F32) * scale).astype(BF16) for at in cols], cols
+
+
+def _lay_parts(index_ref, parts, whole):
+    @pl.when(pl.program_id(0) == 0)
+    def _():
+        for i, part in enumerate(parts):
+            height = part.shape[0]
+            whole[pl.ds(pl.multiple_of(index_ref[2 + i] * height, height), height), :] = part[...]
+
+
+def _attend_kernel(
+    index_ref, doc_ref, q_stat, k_stat, q_ref, k_ref, v_ref, w0, w1, w2, w3, o_ref, log_ref, mix_ref, whole, *, chunk, scaling, width
+):
     rows = q_ref.shape[0]
+    _lay_parts(index_ref, (w0, w1, w2, w3), whole)
     heads = q_ref.shape[1] // HEAD_DIM
     first = (pl.program_id(0) * index_ref[1] + index_ref[0]) * rows
     position, start, lowest = _row_limits(doc_ref, first, rows)
+    queries, cols = _scaled_query(q_ref, q_stat, width)
 
     def step(i, state):
         at = pl.multiple_of(i * chunk, chunk)
+        factor = _key_scales(k_stat, at, chunk, width) * scaling
         new = []
         for h in range(heads):
-            cols = pl.ds(h * HEAD_DIM, HEAD_DIM)
             top, total, out = state[h]
-            scores = _scores(q_ref[:, cols], k_ref[pl.ds(at, chunk), cols], position, start, at, scaling)
+            scores = _scores(queries[h], k_ref[pl.ds(at, chunk), cols[h]], factor, position, start, at)
             now = jnp.maximum(top, jnp.max(scores, axis=1, keepdims=True))
             weights = jnp.exp(scores - now)
             fade = jnp.exp(top - now)
             total = total * fade + jnp.sum(weights, axis=1, keepdims=True)
-            out = out * fade + dot(weights.astype(BF16), v_ref[pl.ds(at, chunk), cols])
+            out = out * fade + dot(weights.astype(BF16), v_ref[pl.ds(at, chunk), cols[h]])
             new.append((now, total, out))
         return tuple(new)
 
@@ -1272,96 +1372,260 @@
     last = first + rows
     state = lax.fori_loop(lowest // chunk, (last + chunk - 1) // chunk, step, (zero,) * heads)
     for h in range(heads):
-        cols = pl.ds(h * HEAD_DIM, HEAD_DIM)
         top, total, out = state[h]
-        o_ref[:, cols] = out / total
-        log_ref[:, cols] = jnp.broadcast_to(top + jnp.log(total), (rows, HEAD_DIM))
+        o_ref[:, cols[h]] = out / total
+        log_ref[:, cols[h]] = jnp.broadcast_to(top + jnp.log(total), (rows, HEAD_DIM))
+    mix_ref[...] = dot(o_ref[...].astype(BF16), whole[...]).astype(BF16)
 
 
 def _attend_back_kernel(
-    index_ref, doc_ref, q_ref, g_ref, o_ref, log_ref, k_ref, v_ref, dq_ref, dk_ref, dv_ref, dk_sum, dv_sum, *, chunk, scaling
+    index_ref,
+    doc_ref,
+    q_stat,
+    k_stat,
+    q_ref,
+    r_ref,
+    o_ref,
+    log_ref,
+    k_ref,
+    v_ref,
+    w0,
+    w1,
+    w2,
+    w3,
+    dq_ref,
+    dk_ref,
+    dv_ref,
+    dw_ref,
+    mq_ref,
+    mk_ref,
+    dk_sum,
+    dv_sum,
+    dw_sum,
+    whole,
+    *,
+    chunk,
+    scaling,
+    width,
 ):
     rows = q_ref.shape[0]
+    _lay_parts(index_ref, (w0, w1, w2, w3), whole)
     heads = q_ref.shape[1] // HEAD_DIM
     first = (pl.program_id(0) * index_ref[1] + index_ref[0]) * rows
     position, start, lowest = _row_limits(doc_ref, first, rows)
+    queries, cols = _scaled_query(q_ref, q_stat, width)
 
     @pl.when(pl.program_id(0) == 0)
     def _():
         dk_sum[...] = jnp.zeros_like(dk_sum)
         dv_sum[...] = jnp.zeros_like(dv_sum)
-
-    deltas, logs = [], []
-    for h in range(heads):
-        cols = pl.ds(h * HEAD_DIM, HEAD_DIM)
-        deltas.append(jnp.sum(g_ref[:, cols].astype(F32) * o_ref[:, cols], axis=1, keepdims=True))
-        logs.append(log_ref[:, cols][:, :1])
+        dw_sum[...] = jnp.zeros_like(dw_sum)
+        mk_ref[...] = jnp.zeros_like(mk_ref)
+
+    upstream = r_ref[...]
+    dw_sum[...] += dot(o_ref[...].astype(BF16), upstream, FIRST_DIM)
+    all_grads = dot(upstream, whole[...], LAST_DIM).astype(BF16)
+    grads = [all_grads[:, h * HEAD_DIM : (h + 1) * HEAD_DIM] for h in range(heads)]
+    deltas = [jnp.sum(grads[h].astype(F32) * o_ref[:, cols[h]], axis=1, keepdims=True) for h in range(heads)]
+    logs = [log_ref[:, at][:, :1] for at in cols]
 
     def step(i, state):
         at = pl.multiple_of(i * chunk, chunk)
+        scale = _key_scales(k_stat, at, chunk, width)
         new = []
+        key_inner = jnp.zeros((1, chunk), F32)
+        query_inner = state[-1]
         for h in range(heads):
-            cols = pl.ds(h * HEAD_DIM, HEAD_DIM)
-            query, grad = q_ref[:, cols], g_ref[:, cols]
-            key = k_ref[pl.ds(at, chunk), cols]
-            scores = _scores(query, key, position, start, at, scaling)
+            grad = grads[h]
+            key = k_ref[pl.ds(at, chunk), cols[h]]
+            scores = _scores(queries[h], key, scale * scaling, position, start, at)
             weights = jnp.exp(scores - logs[h])
-            weight_grad = dot(grad, v_ref[pl.ds(at, chunk), cols], LAST_DIM)
-            score_grad = (weights * (weight_grad - deltas[h])).astype(BF16)
-            dv_sum[pl.ds(at, chunk), cols] += dot(weights.astype(BF16), grad, FIRST_DIM)
-            dk_sum[pl.ds(at, chunk), cols] += dot(score_grad, query, FIRST_DIM)
-            new.append(state[h] + dot(score_grad, key))
-        return tuple(new)
+            weight_grad = dot(grad, v_ref[pl.ds(at, chunk), cols[h]], LAST_DIM)
+            score_grad = weights * (weight_grad - deltas[h])
+            inner = score_grad * scores
+            key_inner = key_inner + jnp.sum(inner, axis=0, keepdims=True)
+            query_inner = query_inner + jnp.sum(inner, axis=1, keepdims=True)
+            dv_sum[pl.ds(at, chunk), cols[h]] += dot(weights.astype(BF16), grad, FIRST_DIM)
+            dk_sum[pl.ds(at, chunk), cols[h]] += dot(score_grad.astype(BF16), queries[h], FIRST_DIM)
+            new.append(state[h] + dot((score_grad * scale).astype(BF16), key))
+        mk_ref[pl.ds(i, 1), :] += key_inner
+        return tuple(new) + (query_inner,)
 
     last = first + rows
-    state = lax.fori_loop(
-        lowest // chunk, (last + chunk - 1) // chunk, step, (jnp.zeros((rows, HEAD_DIM), F32),) * heads
-    )
+    zeros = (jnp.zeros((rows, HEAD_DIM), F32),) * heads + (jnp.zeros((rows, 1), F32),)
+    state = lax.fori_loop(lowest // chunk, (last + chunk - 1) // chunk, step, zeros)
     for h in range(heads):
-        dq_ref[:, pl.ds(h * HEAD_DIM, HEAD_DIM)] = (state[h] * scaling).astype(BF16)
+        dq_ref[:, cols[h]] = (state[h] * scaling).astype(BF16)
+    mq_ref[pl.ds(pl.program_id(0), 1), :] = jnp.broadcast_to(state[-1], (rows, 128)).T[:1]
 
     @pl.when(pl.program_id(0) == pl.num_programs(0) - 1)
     def _():
         dk_ref[...] = (dk_sum[...] * scaling).astype(BF16)
         dv_ref[...] = dv_sum[...].astype(BF16)
-
-
-def _attention_specs(L, N, C, rows):
+        dw_ref[...] = dw_sum[...].astype(BF16)
+
+
+def _resident(*shape):
+    return pl.BlockSpec(shape, lambda i, *_: (0,) * len(shape), pipeline_mode=pl.Buffered(1))
+
+
+def attention_forward(index, docs, q_stat, k_stat, query, key_all, value_all, out_parts, rows, chunk):
+    (L, C), N = query.shape, key_all.shape[0]
+    D = out_parts[0].shape[1]
     block = pl.BlockSpec((rows, C), lambda i, *_: (i, 0))
-    whole = pl.BlockSpec((N, C), lambda i, *_: (0, 0), pipeline_mode=pl.Buffered(1))
-    return block, whole
-
-
-def attention_forward(index, docs, query, key_all, value_all, rows, chunk):
-    (L, C), N = query.shape, key_all.shape[0]
-    block, whole = _attention_specs(L, N, C, rows)
+    stats = [_resident(*q_stat.shape), _resident(*k_stat.shape)]
     return pl.pallas_call(
-        functools.partial(_attend_kernel, chunk=chunk, scaling=HEAD_DIM ** (-0.5)),
-        out_shape=[jax.ShapeDtypeStruct((L, C), F32)] * 2,
+        functools.partial(_attend_kernel, chunk=chunk, scaling=HEAD_DIM ** (-0.5), width=HEADS * HEAD_DIM),
+        out_shape=[jax.ShapeDtypeStruct((L, C), F32)] * 2 + [jax.ShapeDtypeStruct((L, D), BF16)],
         grid_spec=pltpu.PrefetchScalarGridSpec(
-            num_scalar_prefetch=2, grid=(L // rows,), in_specs=[block, whole, whole], out_specs=[block, block]
+            num_scalar_prefetch=2,
+            grid=(L // rows,),
+            in_specs=stats + [block, _resident(N, C), _resident(N, C)] + [_resident(C // 4, D)] * 4,
+            out_specs=[block, block, pl.BlockSpec((rows, D), lambda i, *_: (i, 0))],
+            scratch_shapes=[pltpu.VMEM((C, D), BF16)],
         ),
         compiler_params=pltpu.CompilerParams(vmem_limit_bytes=VMEM_BYTES),
         cost_estimate=pl.CostEstimate(flops=4 * L * C * 1024, bytes_accessed=4 * N * C, transcendentals=L * 1024),
-    )(index, docs, query, key_all, value_all)
-
-
-def attention_backward(index, docs, query, grad, attended, logs, key_all, value_all, rows, chunk):
+    )(index, docs, q_stat, k_stat, query, key_all, value_all, *out_parts)
+
+
+def attention_backward(
+    index, docs, q_stat, k_stat, query, residual_grad, attended, logs, key_all, value_all, out_parts, rows, chunk
+):
     (L, C), N = query.shape, key_all.shape[0]
-    block, whole = _attention_specs(L, N, C, rows)
+    D = residual_grad.shape[1]
+    block = pl.BlockSpec((rows, C), lambda i, *_: (i, 0))
+    whole = _resident(N, C)
+    stats = [_resident(*q_stat.shape), _resident(*k_stat.shape)]
     return pl.pallas_call(
-        functools.partial(_attend_back_kernel, chunk=chunk, scaling=HEAD_DIM ** (-0.5)),
-        out_shape=[jax.ShapeDtypeStruct((L, C), BF16)] + [jax.ShapeDtypeStruct((N, C), BF16)] * 2,
+        functools.partial(_attend_back_kernel, chunk=chunk, scaling=HEAD_DIM ** (-0.5), width=HEADS * HEAD_DIM),
+        out_shape=[jax.ShapeDtypeStruct((L, C), BF16)]
+        + [jax.ShapeDtypeStruct((N, C), BF16)] * 2
+        + [jax.ShapeDtypeStruct((C, D), BF16)]
+        + [jax.ShapeDtypeStruct(q_stat.shape, F32), jax.ShapeDtypeStruct((N // chunk, chunk), F32)],
         grid_spec=pltpu.PrefetchScalarGridSpec(
             num_scalar_prefetch=2,
             grid=(L // rows,),
-            in_specs=[block, block, block, block, whole, whole],
-            out_specs=[block, whole, whole],
-            scratch_shapes=[pltpu.VMEM((N, C), F32)] * 2,
+            in_specs=stats
+            + [block, pl.BlockSpec((rows, D), lambda i, *_: (i, 0)), block, block, whole, whole]
+            + [_resident(C // 4, D)] * 4,
+            out_specs=[block, whole, whole, _resident(C, D), stats[0], _resident(N // chunk, chunk)],
+            scratch_shapes=[pltpu.VMEM((N, C), F32)] * 2 + [pltpu.VMEM((C, D), F32), pltpu.VMEM((C, D), BF16)],
         ),
         compiler_params=pltpu.CompilerParams(vmem_limit_bytes=VMEM_BYTES),
         cost_estimate=pl.CostEstimate(flops=10 * L * C * 1024, bytes_accessed=8 * N * C, transcendentals=L * 1024),
-    )(index, docs, query, grad, attended, logs, key_all, value_all)
+    )(index, docs, q_stat, k_stat, query, residual_grad, attended, logs, key_all, value_all, *out_parts)
+
+
+def _project_kernel(x_ref, w_ref, gain_ref, cos_ref, sin_ref, pre_ref, q_ref, k_ref, v_ref, stat_ref):
+    rows = x_ref.shape[0]
+    C = q_ref.shape[1]
+    pre = dot(x_ref[...], w_ref[...])
+    pre_ref[...] = pre[:, : 2 * C]
+    v_ref[...] = pre[:, 2 * C :].astype(BF16)
+    cosine, sine = cos_ref[...], sin_ref[...]
+    for j, out in enumerate((q_ref, k_ref)):
+        part = pre[:, j * C : (j + 1) * C]
+        sums = _row_sums(part * part)
+        for r in range(rows // 128):
+            stat_ref[j, pl.ds(pl.program_id(0) * (rows // 128) + r, 1), :] = sums[:, r * 128 : (r + 1) * 128]
+        scaled = part * gain_ref[j : j + 1, :]
+        for h in range(C // HEAD_DIM):
+            one = scaled[:, h * HEAD_DIM : (h + 1) * HEAD_DIM]
+            turned = pltpu.roll(one, HEAD_DIM // 2, 1)
+            out[:, pl.ds(h * HEAD_DIM, HEAD_DIM)] = (one * cosine + turned * sine).astype(BF16)
+
+
+def project(x, weights, gains, cosine, sine):
+    L, D = x.shape
+    C = weights.shape[1] // 3
+    rows = 256
+
+    def block(width):
+        return pl.BlockSpec((rows, width), lambda i: (i, 0))
+
+    return pl.pallas_call(
+        _project_kernel,
+        out_shape=[jax.ShapeDtypeStruct((L, 2 * C), F32)]
+        + [jax.ShapeDtypeStruct((L, C), BF16)] * 3
+        + [jax.ShapeDtypeStruct((2, L // 128, 128), F32)],
+        grid=(L // rows,),
+        in_specs=[block(D), _resident(D, 3 * C), _resident(8, C), block(HEAD_DIM), block(HEAD_DIM)],
+        out_specs=[block(2 * C), block(C), block(C), block(C), _resident(2, L // 128, 128)],
+        compiler_params=pltpu.CompilerParams(vmem_limit_bytes=VMEM_BYTES),
+        cost_estimate=pl.CostEstimate(flops=6 * L * D * C, bytes_accessed=2 * L * D + 6 * D * C, transcendentals=0),
+    )(x, weights, gains, cosine, sine)
+
+
+def _project_back_kernel(
+    dq_ref, dk_ref, dv_ref, pre_ref, stat_ref, inner_ref, gain_ref, cos_ref, sin_ref, x_ref, w_ref, dw_ref, first_ref, dg_ref, total, *, width
+):
+    rows, C = dq_ref.shape
+    cosine, sine = cos_ref[...], sin_ref[...]
+    start = pl.program_id(0) == 0
+
+    @pl.when(start)
+    def _():
+        dg_ref[...] = jnp.zeros_like(dg_ref)
+
+    grads = []
+    for j, ref in enumerate((dq_ref, dk_ref)):
+        scales, means = [], []
+        for r in range(rows // 128):
+            at = pl.ds(pl.program_id(0) * (rows // 128) + r, 1)
+            scale = _norm_row(stat_ref[j, at, :], width)
+            scales.append(_as_column(scale))
+            means.append(_as_column(inner_ref[j, at, :] * scale * scale * (1.0 / width)))
+        scale, mean = jnp.concatenate(scales, axis=0), jnp.concatenate(means, axis=0)
+        for h in range(C // HEAD_DIM):
+            at = pl.ds(h * HEAD_DIM, HEAD_DIM)
+            up = ref[:, at].astype(F32)
+            up = up * cosine + pltpu.roll(up * sine, HEAD_DIM // 2, 1)
+            pre = pre_ref[:, pl.ds(j * C + h * HEAD_DIM, HEAD_DIM)]
+            grads.append((scale * up * gain_ref[j : j + 1, at] - pre * mean).astype(BF16))
+            dg_ref[j : j + 1, at] += jnp.sum(up * pre * scale, axis=0, keepdims=True)
+    grads.append(dv_ref[...])
+    both = jnp.concatenate(grads, axis=1)
+    first_ref[...] = dot(both, w_ref[...], LAST_DIM).astype(BF16)
+    part = dot(x_ref[...], both, FIRST_DIM)
+
+    @pl.when(start)
+    def _():
+        total[...] = part
+
+    @pl.when(jnp.logical_not(start))
+    def _():
+        total[...] += part
+
+    @pl.when(pl.program_id(0) == pl.num_programs(0) - 1)
+    def _():
+        dw_ref[...] = total[...].astype(BF16)
+
+
+def project_back(dq, dk, dv, pre, stats, inner, gains, cosine, sine, x, weights):
+    L, D = x.shape
+    C = weights.shape[1] // 3
+    rows = min(512, L)
+
+    def block(width):
+        return pl.BlockSpec((rows, width), lambda i: (i, 0))
+
+    return pl.pallas_call(
+        functools.partial(_project_back_kernel, width=D),
+        out_shape=[
+            jax.ShapeDtypeStruct((D, 3 * C), BF16),
+            jax.ShapeDtypeStruct((L, D), BF16),
+            jax.ShapeDtypeStruct((8, C), F32),
+        ],
+        grid=(L // rows,),
+        in_specs=[block(C)] * 3
+        + [block(2 * C), _resident(*stats.shape), _resident(*inner.shape), _resident(8, C)]
+        + [block(HEAD_DIM), block(HEAD_DIM), block(D), _resident(D, 3 * C)],
+        out_specs=[_resident(D, 3 * C), block(D), _resident(8, C)],
+        scratch_shapes=[pltpu.VMEM((D, 3 * C), F32)],
+        compiler_params=pltpu.CompilerParams(vmem_limit_bytes=VMEM_BYTES),
+        cost_estimate=pl.CostEstimate(flops=12 * L * D * C, bytes_accessed=4 * L * D + 12 * D * C, transcendentals=0),
+    )(dq, dk, dv, pre, stats, inner, gains, cosine, sine, x, weights)
 
 
 def _pick_kernel(slot_ref, router_ref, x_ref, g_ref, xr_ref, gr_ref, gate_ref, *, slots, width):
@@ -1548,50 +1812,32 @@
     move = (Slice if (U, Z, T, D) == (8, 4, 128, 2048) else General)(U, Z, T, D)
     C, L = move.C, move.L
 
-    gain_rows = attn_gain.astype(F32)[:, None]
-    own_weights = [w.astype(F32) for w in (query_weight, key_weight, value_weight)]
-    scaled_rows = jnp.stack([(w * gain_rows).astype(BF16) for w in own_weights])
-    pack = jnp.concatenate([router_weight] + [g[:, None] for g in (ffn_gain, query_gain, key_gain)], axis=1)
-    pack = jnp.pad(pack, ((0, 0), (0, 128 - pack.shape[1])))
+    own_weights = (query_weight, key_weight, value_weight)
+    gains = jnp.stack([attn_gain, ffn_gain, query_gain, key_gain], axis=1)
+    first_rows, qkv_weight, packed, routes_all = move.enter(
+        hidden_in, own_weights, gains, out_weight, router_weight, routes.T
+    )
     hidden = hidden_in.astype(F32)
-    first_scale = norm_scale(hidden)
-    first_rows, qkv_weight, out_rows, packed, routes_all = move.enter(
-        (hidden * first_scale).astype(BF16), scaled_rows, out_weight, pack, routes.T
-    )
     weight_router = packed[:, :EXPERTS]
     gain_ffn = packed[:, EXPERTS].astype(F32)
     head_gains = lax.dynamic_slice_in_dim(packed[:, EXPERTS + 1 : EXPERTS + 3], move.group * C, C, 0).astype(F32)
-    gain_query, gain_key = head_gains[:, 0], head_gains[:, 1]
-    qkv_pre = dot(first_rows, qkv_weight)
-    query_pre, key_pre, value_pre = qkv_pre[:, :C], qkv_pre[:, C : 2 * C], qkv_pre[:, 2 * C :]
-    squares = jnp.stack([jnp.sum(query_pre * query_pre, axis=1), jnp.sum(key_pre * key_pre, axis=1)])
-    scales = lax.rsqrt(move.head_sum(squares.reshape(-1, 128)).reshape(2, L) / D + EPS)
-    query_scale, key_scale = scales[0][:, None], scales[1][:, None]
+    head_gains = jnp.pad(head_gains.T, ((0, 6), (0, 0)))
     local = jnp.arange(L, dtype=jnp.int32)
-    position = (local // T * move.block_step + move.first_block) * T + local % T
-    cosine, sine = rotary_tables(position)
-    cosine, sine = cosine[:, None, :], sine[:, None, :]
-
-    def rotated(pre, scale, gain):
-        split = (pre * scale * gain).reshape(L, C // HEAD_DIM, HEAD_DIM)
-        return rotate_forward(split, cosine, sine).reshape(L, C).astype(BF16)
-
-    query_rot = rotated(query_pre, query_scale, gain_query)
-    key_all, value_all = move.sequence(
-        rotated(key_pre, key_scale, gain_key), value_pre.astype(BF16), out_grad
+    cosine, sine = rotary_tables((local // T * move.block_step + move.first_block) * T + local % T)
+    pre, query_rot, key_rot, value, squares = project(first_rows, qkv_weight, head_gains, cosine, sine)
+    key_all, value_all, stats, k_stat = move.sequence(key_rot, value, squares, out_grad)
+    index = jnp.stack([jnp.int32(i) for i in (move.first_block, move.block_step, *move.parts)])
+    chunk = min(ATTEND_CHUNK, N)
+    attended, logs, mixed = attention_forward(
+        index, doc_starts, stats[0], k_stat, query_rot, key_all, value_all, move.out_parts, T, chunk
     )
-    index = jnp.stack([move.first_block, jnp.int32(move.block_step)]).astype(jnp.int32)
-    chunk = min(512, N)
-    attended, logs = attention_forward(index, doc_starts, query_rot, key_all, value_all, T, chunk)
-    attended_low = attended.astype(BF16)
-    mixed, upstream_all = move.heads_to_rows(dot(attended_low, out_rows).astype(BF16))
-    residual = hidden + mixed.astype(F32)
+    residual = hidden + move.heads_to_rows(mixed).astype(F32)
 
     second_scale = norm_scale(residual)
     second_low = (residual * second_scale * gain_ffn).astype(BF16)
     probabilities = jax.nn.softmax(dot(second_low, weight_router), axis=-1)
     own_router = jnp.roll(weight_router, -u * EL, axis=1)
-    second_all, entry_sum = move.experts(second_low, upstream_all, routes_all, expert_weights, own_router)
+    second_all, entry_sum = move.experts(second_low, routes_all, expert_weights, own_router)
     entry_sum = entry_sum.astype(F32)
 
     second_grad, prob_grad = entry_sum[:, :D], entry_sum[:, D : D + EXPERTS]
@@ -1606,58 +1852,42 @@
     ffn_gain_part = jnp.sum(second_grad * residual * second_scale, axis=0)
 
     residual_rows, expert_grads = move.rows_to_heads(residual_grad.astype(BF16))
-    out_weight_part = dot(attended_low, residual_rows, FIRST_DIM).astype(BF16)
-    attended_grad = dot(residual_rows, out_rows, LAST_DIM).astype(BF16)
-    dq, dk_part, dv_part = attention_backward(
-        index, doc_starts, query_rot, attended_grad, attended, logs, key_all, value_all, T, chunk
+    dq, dk_part, dv_part, out_weight_part, q_inner, k_inner = attention_backward(
+        index,
+        doc_starts,
+        stats[0],
+        k_stat,
+        query_rot,
+        residual_rows,
+        attended,
+        logs,
+        key_all,
+        value_all,
+        move.out_parts,
+        T,
+        chunk,
     )
-    dk, dv, out_weight_grad, out_sum = move.sequence_sums(dk_part, dv_part, out_weight_part)
-    output = (residual + out_sum.astype(F32)).astype(BF16)
-
-    def rotated_back(grad):
-        return rotate_backward(grad.astype(F32).reshape(L, C // HEAD_DIM, HEAD_DIM), cosine, sine).reshape(L, C)
-
-    query_up, key_up = rotated_back(dq), rotated_back(dk)
-    inner_sums = jnp.stack(
-        [jnp.sum(query_up * gain_query * query_pre, axis=1), jnp.sum(key_up * gain_key * key_pre, axis=1)]
+    dk, dv, out_sum, inner = move.sequence_sums(dk_part, dv_part, out_weight_part, q_inner, k_inner)
+    weight_part, first_part, gain_parts = project_back(
+        dq, dk, dv, pre, stats, inner, head_gains, cosine, sine, first_rows, qkv_weight
     )
-    inner_sums = move.head_sum_again(inner_sums.reshape(-1, 128)).reshape(2, L) / D
-
-    def pre_grad(up, gain, pre, scale, mean):
-        return (scale * (up * gain) - pre * (scale**3) * mean[:, None]).astype(BF16)
-
-    pre_grads = jnp.concatenate(
-        [
-            pre_grad(query_up, gain_query, query_pre, query_scale, inner_sums[0]),
-            pre_grad(key_up, gain_key, key_pre, key_scale, inner_sums[1]),
-            dv,
-        ],
-        axis=1,
-    )
-    gain_parts = jnp.stack(
-        [jnp.sum(query_up * query_pre * query_scale, axis=0), jnp.sum(key_up * key_pre * key_scale, axis=0)]
-    )
-    weight_part = dot(first_rows, pre_grads, FIRST_DIM).astype(BF16)
-    first_part = dot(pre_grads, qkv_weight, LAST_DIM).astype(BF16)
-    first_weighted, weight_sum, logit_grad_all, ffn_gain_grad, head_gain_grads = move.leave(
+    gain_parts = gain_parts[:2]
+    first_weighted, weight_sum, out_weight_grad, logit_grad_all, ffn_gain_grad, head_gain_grads = move.leave(
         first_part, weight_part, logit_grad, ffn_gain_part, gain_parts
     )
     own_columns = lax.dynamic_slice_in_dim(second_all, (u * Z + z) * RW, RW, 1)
     router_grad = dot(own_columns, logit_grad_all, FIRST_DIM)
-    weight_sum = weight_sum.astype(F32)
-    attn_gain_grad = sum(jnp.sum(w * g, axis=1) for w, g in zip(own_weights, weight_sum))
-    weight_grads = [g * gain_rows for g in weight_sum]
-    first_weighted = first_weighted.astype(F32)
-    first_mean = jnp.mean(first_weighted * hidden, axis=-1, keepdims=True)
-    hidden_grad = residual_grad + first_scale * first_weighted - hidden * (first_scale**3) * first_mean
+    output, hidden_grad, attn_gain_grad, *weight_grads = finish(
+        hidden_in, residual, residual_grad, first_weighted, out_sum, own_weights, weight_sum, out_weight_grad, gains
+    )
     return (
         output,
         hidden_grad,
-        attn_gain_grad,
+        attn_gain_grad[:, 0],
         weight_grads[0],
         weight_grads[1],
         weight_grads[2],
-        out_weight_grad.astype(F32),
+        weight_grads[3],
         head_gain_grads[0],
         head_gain_grads[1],
         ffn_gain_grad,

time: 850 us -> 759 us (0.89)
  other arithmetic: 55.8 us -> 17.3 us
  matrix products: 32.1 us -> 4.36 us
  Pallas kernels: 706 us -> 688 us
  local copies, waits for them, and re-layouts: 25.3 us -> 13.2 us
    pallas_call x7 -> x8, Pallas kernels: 367 us -> 335 us  [the longest x1 97.1 us: gather_pick(): _comm(kernel, outs, scratch, collective_id, specs)(x, *g, slot, router)]
    dot_general x9 -> x3, matrix products: 31.3 us -> 3.52 us  [dot(): return lax.dot_general(a, b, dims, preferred_element_type=F32)]
    convert_element_type x8 -> x1, other arithmetic: 11.3 us -> 0.13 us  [leave(): out_grad = sum((x.astype(F32) for x in terms)).astype(BF16)]
    reshape x7 -> x2, local copies, waits for them, and re-layouts: 11.8 us -> 2.37 us  [the longest x1 1.64 us: leave(): logit_all.reshape(32 * T, EXPERTS)]
    pallas_call x1, Pallas kernels: 21.6 us -> 30.3 us  [attention_backward(): pl.pallas_call(functools.partial(_attend_back_kernel, chunk=chunk, scalin...]
    ppermute x8 -> x11, starting transfers between devices: 13 us -> 17.3 us  [permute(): return lax.ppermute(x, ALL, pairs)]
  transfers between devices with their start and end apart: 8 -> 11, of which waited for: 1 -> 2; matrix products, arithmetic and copies ran while one was open for 7% -> 3% of each run, Pallas kernels for 24% -> 28%
where the time goes in v4:
time: 759 us; the launch traced here: 750 us
  Pallas kernels  688 us (91%)
  starting transfers between devices  17.3 us (2%)
  other arithmetic  17.3 us (2%)
  local copies, waits for them, and re-layouts  13.2 us (2%)
  waiting for transfers between devices  8.59 us (1%)
    pallas_call x1, Pallas kernels, gather_pick(): _comm(kernel, outs, scratch, collective_id, specs)(x, *g, slot, router)  97.1 us
    pallas_call x1, Pallas kernels, spread_scatter(): _comm(kernel, out, scratch, collective_id, specs)  90.4 us
    pallas_call x1, Pallas kernels, column_gather(): _comm(kernel, outs, scratch, collective_id, specs)(rows, slot, out_rows)  81.6 us
    pallas_call x1, Pallas kernels, enter(): _comm(kernel, outs, scratch, collective_id, specs)  66.6 us
    pallas_call x1, Pallas kernels, leave(): _comm(kernel, outs, scratch, collective_id, specs)(x, weights, *smalls)  65.8 us
    pallas_call x1, Pallas kernels, run_experts(): pl.pallas_call(_expert_kernel, out_shape=[jax.ShapeDtypeStruct(x.shape, B...  64.7 us
    pallas_call x1, Pallas kernels, plane_pair(): _comm(kernel, outs, scratch, collective_id, specs)  54.1 us
    pallas_call x1, Pallas kernels, key_value_sums(): return _comm(kernel, outs, scratch, collective_id, specs)(dk, dv, x, inner)  44.7 us
  transfers between devices with their start and end apart: 11, of which 2 were waited for; matrix products, arithmetic and copies ran while one was open for 3% of the time, Pallas kernels for 28%

profile of v4, /device:TPU:13, one launch (start us, length us, event | category | flops | bytes accessed | tf_op | source)
XLA Modules:
  0.0 750.0 jit_solution(6895862810753332393)
XLA Ops:
  0.6 4.1 collective-permute-start
  4.9 0.7 pad_maximum_fusion.3
  5.6 0.7 copy.64.gain_ref
  6.3 66.6 %shard_map.229 = (bf16[2,4,128,2048]{3,2,1,0:T(8,128)(2,1)}, bf16[4,2,4,64,768]{4,3,2,1,0:T(8,128)(2,1)}, bf16[8,4,64,128]{3,2,1,0:T(8,128)(2,1)}, s32[8,4,8,128]{3,2,1,0:T(8,128)}) custom-call(bf16[128,2048]{1,0:T(8,128)(2,1)} %h_ref.3, bf16[64,2048]{1,0:T(8,128)(2,1)} %wq_ref.3, bf16[64,2048]{1,0:T(8,128)(2,1)} %wk_ref.3, bf16[64,2048]{1,0:T(8,128)(2,1)} %wv_ref.3, ...), custom_call_target="tpu_custom_call" | custom-call | bytes 100000000 | tf_op jit(solution)/shard_map/pallas_call | solution.py:377
  72.9 1.2 slice.46
  74.2 1.9 fusion.4
  76.1 0.1 copy.76
  76.2 0.6 pad_convert_fusion.gain_ref
  76.8 1.3 pad_maximum_fusion
  78.2 2.6 collective-permute-start.1
  80.8 9.2 %shard_map.230 = (f32[1024,512]{1,0:T(8,128)}, bf16[1024,256]{1,0:T(8,128)(2,1)}, bf16[1024,256]{1,0:T(8,128)(2,1)}, bf16[1024,256]{1,0:T(8,128)(2,1)}, f32[2,8,128]{2,1,0:T(8,128)}) custom-call(bf16[1024,2048]{1,0:T(8,128)(2,1)} %bitcast.105, bf16[2048,768]{1,0:T(8,128)(2,1)} %bitcast.107, f32[8,256]{1,0:T(8,128)} %pad_convert_fusion.gain_ref, ...), custom_call_target="tpu_custom_call" | custom-call | flops 3221225472 | bytes 7340032 | tf_op jit(solution)/shard_map/pallas_call | solution.py:1547
  90.0 54.1 %shard_map.231 = (bf16[4,1024,256]{2,1,0:T(8,128)(2,1)}, bf16[4,1024,256]{2,1,0:T(8,128)(2,1)}, bf16[4,128,2048]{2,1,0:T(8,128)(2,1)}, f32[16,128]{1,0:T(8,128)}, f32[4,8,128]{2,1,0:T(8,128)}) custom-call(bf16[1024,256]{1,0:T(8,128)(2,1)} %get-tuple-element.86.a_ref, bf16[1024,256]{1,0:T(8,128)(2,1)} %get-tuple-element.87.b_ref, bf16[128,2048]{1,0:T(8,128)(2,1)} %x_ref.1, ...), custom_call_target="tpu_custom_call" | custom-call | bytes 100000000 | tf_op jit(solution)/shard_map/pallas_call | solution.py:429
  144.1 1.8 collective-permute-start.4
  146.0 0.7 stack.38.index_ref
  146.7 1.3 slice.36.q_stat
  148.0 20.2 %shard_map.232 = (f32[1024,256]{1,0:T(8,128)}, f32[1024,256]{1,0:T(8,128)}, bf16[1024,2048]{1,0:T(8,128)(2,1)}) custom-call(s32[6]{0:T(128)} %stack.38.index_ref, s32[5]{0:T(128)} %doc_ref.3, f32[8,128]{1,0:T(8,128)} %slice.36.q_stat, f32[32,128]{1,0:T(8,128)} %bitcast.90, bf16[1024,256]{1,0:T(8,128)(2,1)} %get-tuple-element.91.q_ref, ...), custom_call_target="tpu_custom_call" | custom-call | flops 1073741824 | bytes 4194304 | tf_op jit(solution)/shard_map/pallas_call | solution.py:1477
  168.1 1.9 collective-permute-done.4.g1
  170.0 1.4 collective-permute-start.5
  171.5 0.4 compare_reduce_fusion
  171.9 0.8 copy.67
  172.8 0.8 convert_select_fusion
  173.6 1.3 copy.70.slot_ref
  175.1 0.4 convert_reduce_fusion
  175.4 1.4 dynamic-slice_maximum_fusion.router_ref
  176.8 42.6 %shard_map.233 = bf16[128,2048]{1,0:T(8,128)(2,1)} custom-call(bf16[2,4,128,2048]{3,2,1,0:T(8,128)(2,1)} %bitcast.80), custom_call_target="tpu_custom_call" | custom-call | bytes 100000000 | tf_op jit(solution)/shard_map/pallas_call | solution.py:472
  219.4 1.3 multiply_reduce_fusion.2
  220.7 1.3 multiply_convert_fusion.x_ref
  222.0 0.4 fusion.23
  222.4 0.1 copy.71
  222.5 0.2 fusion.6
  222.7 0.1 copy-done.4
  222.8 97.1 %shard_map.234 = (bf16[32,128,2048]{2,1,0:T(8,128)(2,1)}, bf16[8,8,80,2048]{3,2,1,0:T(8,128)(2,1)}, bf16[8,8,80,2048]{3,2,1,0:T(8,128)(2,1)}, f32[8,8,80,128]{3,2,1,0:T(8,128)}, bf16[4,4,128,2048]{3,2,1,0:T(8,128)(2,1)}) custom-call(bf16[128,2048]{1,0:T(8,128)(2,1)} %copy-done.4, bf16[4,128,2048]{2,1,0:T(8,128)(2,1)} %get-tuple-element.104.g0, ...), custom_call_target="tpu_custom_call" | custom-call | bytes 100000000 | tf_op jit(solution)/shard_map/pallas_call | solution.py:871
  319.9 64.7 %shard_map.235 = (bf16[8,640,2048]{2,1,0:T(8,128)(2,1)}, bf16[8,640,2048]{2,1,0:T(8,128)(2,1)}, f32[8,3,2048,256]{3,2,1,0:T(8,128)}, f32[8,640,128]{2,1,0:T(8,128)}) custom-call(bf16[8,640,2048]{2,1,0:T(8,128)(2,1)} %bitcast.103, bf16[8,640,2048]{2,1,0:T(8,128)(2,1)} %bitcast.104, f32[8,640,128]{2,1,0:T(8,128)} %bitcast.109, bf16[8,3,2048,256]{3,2,1,0:T(8,128)(2,1)} %w_ref.1), custom_call_target="tpu_custom_call" | custom-call | flops 48318382080 | bytes 159383552 | tf_op jit(solution)/shard_map/pallas_call | solution.py:1719
  384.6 90.4 %shard_map.236 = bf16[128,2176]{1,0:T(8,128)(2,1)} custom-call(s32[8,512,8]{2,1,0:T(8,128)} %bitcast.68, f32[8,8,80,128]{3,2,1,0:T(8,128)} %bitcast.83, bf16[8,8,80,2048]{3,2,1,0:T(8,128)(2,1)} %bitcast.67), custom_call_target="tpu_custom_call" | custom-call | bytes 100000000 | tf_op jit(solution)/shard_map/pallas_call | solution.py:1086
  475.0 1.2 convert_element_type.79
  476.2 0.2 multiply_reduce_fusion.3
  476.4 0.1 multiply_convert_fusion.1
  476.5 0.6 multiply_reduce_fusion
  477.1 0.1 copy-done.5
  477.2 1.9 fusion.22
  479.1 81.6 %shard_map.237 = (bf16[2,4,128,2048]{3,2,1,0:T(8,128)(2,1)}, bf16[4,128,2048]{2,1,0:T(8,128)(2,1)}) custom-call(bf16[128,2048]{1,0:T(8,128)(2,1)} %get-tuple-element.154.r_ref, s32[8,512,8]{2,1,0:T(8,128)} %bitcast.69, bf16[8,8,80,2048]{3,2,1,0:T(8,128)(2,1)} %bitcast.66), custom_call_target="tpu_custom_call" | custom-call | bytes 100000000 | tf_op jit(solution)/shard_map/pallas_call | solution.py:452
  560.7 30.3 %shard_map.238 = (bf16[1024,256]{1,0:T(8,128)(2,1)}, bf16[4096,256]{1,0:T(8,128)(2,1)}, bf16[4096,256]{1,0:T(8,128)(2,1)}, bf16[256,2048]{1,0:T(8,128)(2,1)}, f32[8,128]{1,0:T(8,128)}, /*index=5*/f32[8,512]{1,0:T(8,128)}) custom-call(s32[6]{0:T(128)} %stack.38.index_ref, s32[5]{0:T(128)} %doc_ref.3, f32[8,128]{1,0:T(8,128)} %slice.36.q_stat, ...), custom_call_target="tpu_custom_call" | custom-call | flops 2684354560 | bytes 8388608 | tf_op jit(solution)/shard_map/pallas_call | solution.py:1500
  591.0 0.7 reshape.210
  591.8 1.3 pad_maximum_fusion.2.s_ref
  593.1 44.7 %shard_map.239 = (bf16[1024,256]{1,0:T(8,128)(2,1)}, bf16[1024,256]{1,0:T(8,128)(2,1)}, bf16[128,2048]{1,0:T(8,128)(2,1)}, f32[16,128]{1,0:T(8,128)}) custom-call(bf16[4,1024,256]{2,1,0:T(8,128)(2,1)} %bitcast.84, bf16[4,1024,256]{2,1,0:T(8,128)(2,1)} %bitcast.85, bf16[4,128,2048]{2,1,0:T(8,128)(2,1)} %get-tuple-element.118.x_ref, ...), custom_call_target="tpu_custom_call" | custom-call | bytes 100000000 | tf_op jit(solution)/shard_map/pallas_call | solution.py:539
  637.8 2.8 collective-permute-start.7
  640.7 1.3 collective-permute-start.9
  641.9 15.4 %shard_map.240 = (bf16[2048,768]{1,0:T(8,128)(2,1)}, bf16[1024,2048]{1,0:T(8,128)(2,1)}, f32[8,256]{1,0:T(8,128)}) custom-call(bf16[1024,256]{1,0:T(8,128)(2,1)} %get-tuple-element.115.dq_ref, bf16[1024,256]{1,0:T(8,128)(2,1)} %get-tuple-element.123.dk_ref, bf16[1024,256]{1,0:T(8,128)(2,1)} %get-tuple-element.124.dv_ref, ...), custom_call_target="tpu_custom_call" | custom-call | flops 6442450944 | bytes 14680064 | tf_op jit(solution)/shard_map/pallas_call | solution.py:1613
  657.4 0.7 reshape.216.refs_0_
  658.1 0.7 slice.41
  658.8 0.6 select_maximum_fusion.refs_1_
  659.4 65.8 %shard_map.241 = (bf16[128,2048]{1,0:T(8,128)(2,1)}, bf16[3,64,2048]{2,1,0:T(8,128)(2,1)}, bf16[8,4,64,128]{3,2,1,0:T(8,128)(2,1)}, f32[8,4,24,128]{3,2,1,0:T(8,128)}) custom-call(bf16[2,4,128,2048]{3,2,1,0:T(8,128)(2,1)} %bitcast.81, bf16[4,2,256,768]{3,2,1,0:T(8,128)(2,1)} %bitcast.82, bf16[64,128]{1,0:T(8,128)(2,1)} %reshape.216.refs_0_, ...), custom_call_target="tpu_custom_call" | custom-call | bytes 100000000 | tf_op jit(solution)/shard_map/pallas_call | solution.py:591
  725.2 0.8 dynamic-slice_bitcast_fusion.4
  726.1 0.5 slice_bitcast_fusion
  726.6 0.1 add_convert_fusion
  726.8 3.2 collective-permute-start.10
  730.0 1.0 slice_reduce_fusion
  731.0 1.6 reshape.223
  732.6 0.6 dynamic_slice.43
  733.2 2.6 fusion
  735.8 6.7 collective-permute-done.10.do_ref
  742.5 0.7 copy-done.11
  743.2 5.1 shard_map.242
  748.2 1.4 reduce.1
  (48 shorter events, 0.5 us)
Async XLA Ops:
  0.6 77.5 %collective-permute-start = (bf16[64,2048]{1,0:T(8,128)(2,1)}, bf16[64,2048]{1,0:T(8,128)(2,1)S(1)}, u32[]{:S(2)}, u32[]{:S(2)}) collective-permute-start(bf16[64,2048]{1,0:T(8,128)(2,1)} %param.20), channel_id=1, source_target_pairs={{0,0},{1,8},{2,16},{3,24},{4,4},{5,12},{6,20},{7,28},{8,9},{9,17},... | collective-permute-start | bytes 786440 | tf_op jit(solution)/shard_map/ppermute | solution.py:1121
  78.1 11.8 %copy-start.6 = (bf16[64,2048]{1,0:T(8,128)(2,1)}, bf16[64,2048]{1,0:T(8,128)(2,1)S(1)}, u32[]{:S(2)}) copy-start(bf16[64,2048]{1,0:T(8,128)(2,1)S(1)} %collective-permute-done.w0) | copy-start | bytes 786436
  78.1 66.0 %collective-permute-start.3 = (bf16[64,2048]{1,0:T(8,128)(2,1)S(1)}, bf16[64,2048]{1,0:T(8,128)(2,1)S(1)}, u32[]{:S(2)}, u32[]{:S(2)}) collective-permute-start(bf16[64,2048]{1,0:T(8,128)(2,1)S(1)} %collective-permute-done.w0), channel_id=1, source_target_pairs={{0,24},{1,25},{2,26},{3,27},{4,28},{5,29},{6,30},{7,31},{8,16},{9,... | collective-permute-start | bytes 786440 | tf_op jit(solution)/shard_map/ppermute | solution.py:1121
  78.1 66.0 %collective-permute-start.2 = (bf16[64,2048]{1,0:T(8,128)(2,1)S(1)}, bf16[64,2048]{1,0:T(8,128)(2,1)S(1)}, u32[]{:S(2)}, u32[]{:S(2)}) collective-permute-start(bf16[64,2048]{1,0:T(8,128)(2,1)S(1)} %collective-permute-done.w0), channel_id=1, source_target_pairs={{0,16},{1,17},{2,18},{3,19},{4,20},{5,21},{6,22},{7,23},{8,24},{9,... | collective-permute-start | bytes 786440 | tf_op jit(solution)/shard_map/ppermute | solution.py:1121
  78.2 65.9 %collective-permute-start.1 = (bf16[64,2048]{1,0:T(8,128)(2,1)S(1)}, bf16[64,2048]{1,0:T(8,128)(2,1)S(1)}, u32[]{:S(2)}, u32[]{:S(2)}) collective-permute-start(bf16[64,2048]{1,0:T(8,128)(2,1)S(1)} %collective-permute-done.w0), channel_id=1, source_target_pairs={{0,8},{1,9},{2,10},{3,11},{4,12},{5,13},{6,14},{7,15},{8,0},{9,1},... | collective-permute-start | bytes 786440 | tf_op jit(solution)/shard_map/ppermute | solution.py:1121
  144.1 3.8 copy-start.7
  144.1 3.8 copy-start.8
  144.1 3.8 copy-start.9
  144.1 25.9 %collective-permute-start.4 = (bf16[4,128,2048]{2,1,0:T(8,128)(2,1)}, bf16[4,128,2048]{2,1,0:T(8,128)(2,1)}, u32[]{:S(2)}, u32[]{:S(2)}) collective-permute-start(bf16[4,128,2048]{2,1,0:T(8,128)(2,1)} %get-tuple-element.104.g0), channel_id=1, source_target_pairs={{0,8},{1,9},{2,10},{3,11},{4,20},{5,21},{6,22},{7,23},{8,0},{9,1},... | collective-permute-start | bytes 6291464 | tf_op jit(solution)/shard_map/ppermute | solution.py:1121
  148.0 23.6 %copy-start.12 = (s32[8,4,8,128]{3,2,1,0:T(8,128)S(1)}, s32[8,4,8,128]{3,2,1,0:T(8,128)}, u32[]{:S(2)}) copy-start(s32[8,4,8,128]{3,2,1,0:T(8,128)} %get-tuple-element.103) | copy-start | bytes 393220
  170.0 52.6 %collective-permute-start.5 = (bf16[4,128,2048]{2,1,0:T(8,128)(2,1)}, bf16[4,128,2048]{2,1,0:T(8,128)(2,1)}, u32[]{:S(2)}, u32[]{:S(2)}) collective-permute-start(bf16[4,128,2048]{2,1,0:T(8,128)(2,1)} %get-tuple-element.104.g0), channel_id=1, source_target_pairs={{0,16},{1,17},{2,18},{3,19},{4,12},{5,13},{6,14},{7,15},{8,24},{9,... | collective-permute-start | bytes 6291464 | tf_op jit(solution)/shard_map/ppermute | solution.py:1121
  171.4 51.2 %collective-permute-start.6 = (bf16[4,128,2048]{2,1,0:T(8,128)(2,1)}, bf16[4,128,2048]{2,1,0:T(8,128)(2,1)}, u32[]{:S(2)}, u32[]{:S(2)}) collective-permute-start(bf16[4,128,2048]{2,1,0:T(8,128)(2,1)} %collective-permute-done.4.g1), channel_id=1, source_target_pairs={{0,16},{1,17},{2,18},{3,19},{4,12},{5,13},{6,14},{7,15},{8,24},{9,... | collective-permute-start | bytes 6291464 | tf_op jit(solution)/shard_map/ppermute | solution.py:1121
  173.6 45.8 %copy-start = (s32[8,8,512]{1,2,0:T(8,128)}, s32[8,8,512]{1,2,0:T(8,128)S(1)}, u32[]{:S(2)}) copy-start(s32[8,8,512]{1,2,0:T(8,128)S(1)} %convert_select_fusion) | copy-start | bytes 393220
  173.6 1.4 copy-start.3
  176.8 42.6 %copy-start.1 = (bf16[128,2048]{1,0:T(8,128)(2,1)S(1)}, bf16[128,2048]{1,0:T(8,128)(2,1)}, u32[]{:S(2)}) copy-start(bf16[128,2048]{1,0:T(8,128)(2,1)} %h_ref.3) | copy-start | bytes 1572868
  222.0 0.8 copy-start.4
  475.0 1.5 copy-start.2
  476.2 1.0 copy-start.5
  593.1 44.7 %copy-start.10 = (bf16[256,2048]{1,0:T(8,128)(2,1)S(1)}, bf16[256,2048]{1,0:T(8,128)(2,1)}, u32[]{:S(2)}) copy-start(bf16[256,2048]{1,0:T(8,128)(2,1)} %get-tuple-element.122) | copy-start | bytes 3145732
  637.8 21.5 %collective-permute-start.7 = (bf16[64,2048]{1,0:T(8,128)(2,1)S(1)}, bf16[64,2048]{1,0:T(8,128)(2,1)S(1)}, u32[]{:S(2)}, u32[]{:S(2)}) collective-permute-start(bf16[64,2048]{1,0:T(8,128)(2,1)S(1)} %get-tuple-element.128), channel_id=1, source_target_pairs={{0,8},{1,9},{2,10},{3,11},{4,12},{5,13},{6,14},{7,15},{8,0},{9,1},... | collective-permute-start | bytes 786440 | tf_op jit(solution)/shard_map/ppermute | solution.py:1121
  640.6 18.7 %collective-permute-start.8 = (bf16[64,2048]{1,0:T(8,128)(2,1)S(1)}, bf16[64,2048]{1,0:T(8,128)(2,1)S(1)}, u32[]{:S(2)}, u32[]{:S(2)}) collective-permute-start(bf16[64,2048]{1,0:T(8,128)(2,1)S(1)} %get-tuple-element.129), channel_id=1, source_target_pairs={{0,16},{1,17},{2,18},{3,19},{4,20},{5,21},{6,22},{7,23},{8,24},{9,... | collective-permute-start | bytes 786440 | tf_op jit(solution)/shard_map/ppermute | solution.py:1121
  640.7 18.7 %collective-permute-start.9 = (bf16[64,2048]{1,0:T(8,128)(2,1)S(1)}, bf16[64,2048]{1,0:T(8,128)(2,1)S(1)}, u32[]{:S(2)}, u32[]{:S(2)}) collective-permute-start(bf16[64,2048]{1,0:T(8,128)(2,1)S(1)} %get-tuple-element.130), channel_id=1, source_target_pairs={{0,24},{1,25},{2,26},{3,27},{4,28},{5,29},{6,30},{7,31},{8,16},{9,... | collective-permute-start | bytes 786440 | tf_op jit(solution)/shard_map/ppermute | solution.py:1121
  726.8 15.7 %collective-permute-start.10 = (bf16[64,2048]{1,0:T(8,128)(2,1)S(1)}, bf16[64,2048]{1,0:T(8,128)(2,1)S(1)}, u32[]{:S(2)}, u32[]{:S(2)}) collective-permute-start(bf16[64,2048]{1,0:T(8,128)(2,1)S(1)} %add_convert_fusion), channel_id=1, source_target_pairs={{0,0},{8,1},{16,2},{24,3},{4,4},{12,5},{20,6},{28,7},{9,8},{17,9},... | collective-permute-start | bytes 786440 | tf_op jit(solution)/shard_map/ppermute | solution.py:1121
  742.5 0.7 copy-start.11

commit v5 on v4

--- a/solution.py
+++ b/solution.py
@@ -23,6 +23,8 @@
 VMEM_BYTES = 56 * 1024 * 1024
 PICK_WIDTH = 512
 ATTEND_CHUNK = 512
+ATTEND_ROWS = 512
+BACK_ROWS = 1024
 SPREAD_WIDTH = 2048
 
 
@@ -265,7 +267,7 @@
 
 ENTER_ORDER = (0, 2, 1, 0, 2, 1, 0, 2, 0, 2)
 KV_ORDER = (2, 0, 1, 0, 0, 1, 2, 1, 0, 1)
-PAIR_ORDER = (2, 0, 1, 0, 0, 1, 2, 1, 0, 1)
+PAIR_ORDER = (1, 0, 2, 1, 0, 0, 1, 2, 1, 0)
 LEAVE_ORDER = (0, 1, 2, 1, 2, 1, 0, 0, 1, 0, 1, 1)
 LINE_SEMS = [DMA((2, 4)), DMA((4,)), DMA((4,)), DMA((4,)), DMA]
 PLANE_SEMS = [DMA((2, 3)), DMA((2, 3)), DMA((2,))]
@@ -1101,6 +1103,7 @@
         self.L = 8 * T
         self.group = 2 * self.z + self.u % 2
         self.first_block, self.block_step = 8 * (self.u // 2), 1
+        self.rows = ATTEND_ROWS
 
     def enter(self, hidden, weights, gains, out_weight, router, routes):
         rows, weights, packs, routes = enter(hidden, weights, gains, router, routes, 1)
@@ -1198,6 +1201,7 @@
         self.group = self.u
         self.parts = range(4)
         self.first_block, self.block_step = self.z, Z
+        self.rows = T
 
     def gather(self, x):
         return lax.all_gather(x, ALL, axis=0, tiled=True)
@@ -1325,8 +1329,10 @@
 
 
 def _scaled_query(q_ref, stat_ref, width):
-    heads = q_ref.shape[1] // HEAD_DIM
-    scale = _as_column(_norm_row(stat_ref[pl.ds(pl.program_id(0), 1), :], width))
+    heads, units = q_ref.shape[1] // HEAD_DIM, q_ref.shape[0] // 128
+    scale = jnp.concatenate(
+        [_as_column(_norm_row(stat_ref[pl.ds(pl.program_id(0) * units + r, 1), :], width)) for r in range(units)], axis=0
+    )
     cols = [pl.ds(h * HEAD_DIM, HEAD_DIM) for h in range(heads)]
     return [(q_ref[:, at].astype(F32) * scale).astype(BF16) for at in cols], cols
 
@@ -1456,7 +1462,9 @@
     state = lax.fori_loop(lowest // chunk, (last + chunk - 1) // chunk, step, zeros)
     for h in range(heads):
         dq_ref[:, cols[h]] = (state[h] * scaling).astype(BF16)
-    mq_ref[pl.ds(pl.program_id(0), 1), :] = jnp.broadcast_to(state[-1], (rows, 128)).T[:1]
+    for r in range(rows // 128):
+        inner = jnp.broadcast_to(state[-1][r * 128 : (r + 1) * 128], (128, 128)).T[:1]
+        mq_ref[pl.ds(pl.program_id(0) * (rows // 128) + r, 1), :] = inner
 
     @pl.when(pl.program_id(0) == pl.num_programs(0) - 1)
     def _():
@@ -1605,7 +1613,7 @@
 def project_back(dq, dk, dv, pre, stats, inner, gains, cosine, sine, x, weights):
     L, D = x.shape
     C = weights.shape[1] // 3
-    rows = min(512, L)
+    rows = min(BACK_ROWS, L)
 
     def block(width):
         return pl.BlockSpec((rows, width), lambda i: (i, 0))
@@ -1826,10 +1834,10 @@
     cosine, sine = rotary_tables((local // T * move.block_step + move.first_block) * T + local % T)
     pre, query_rot, key_rot, value, squares = project(first_rows, qkv_weight, head_gains, cosine, sine)
     key_all, value_all, stats, k_stat = move.sequence(key_rot, value, squares, out_grad)
-    index = jnp.stack([jnp.int32(i) for i in (move.first_block, move.block_step, *move.parts)])
+    index = jnp.stack([jnp.int32(i) for i in (move.first_block * T // move.rows, move.block_step, *move.parts)])
     chunk = min(ATTEND_CHUNK, N)
     attended, logs, mixed = attention_forward(
-        index, doc_starts, stats[0], k_stat, query_rot, key_all, value_all, move.out_parts, T, chunk
+        index, doc_starts, stats[0], k_stat, query_rot, key_all, value_all, move.out_parts, move.rows, chunk
     )
     residual = hidden + move.heads_to_rows(mixed).astype(F32)
 
@@ -1864,7 +1872,7 @@
         key_all,
         value_all,
         move.out_parts,
-        T,
+        move.rows,
         chunk,
     )
     dk, dv, out_sum, inner = move.sequence_sums(dk_part, dv_part, out_weight_part, q_inner, k_inner)

time: 759 us -> 741 us (0.976)
  Pallas kernels: 688 us -> 663 us
    pallas_call x1, Pallas kernels: 54.1 us -> 44.6 us  [plane_pair(): _comm(kernel, outs, scratch, collective_id, specs)]
    pallas_call x1, Pallas kernels: 30.3 us -> 21.7 us  [attention_backward(): pl.pallas_call(functools.partial(_attend_back_kernel, chunk=chunk, scalin...]
  transfers between devices with their start and end apart: 11 -> 11, of which waited for: 2 -> 2; matrix products, arithmetic and copies ran while one was open for 3% -> 3% of each run, Pallas kernels for 28% -> 26%
where the time goes in v5:
time: 741 us; the launch traced here: 731 us
  Pallas kernels  663 us (89%)
  other arithmetic  17.3 us (2%)
  waiting for transfers between devices  15.8 us (2%)
  starting transfers between devices  15.5 us (2%)
  local copies, waits for them, and re-layouts  13.2 us (2%)
    pallas_call x1, Pallas kernels, gather_pick(): _comm(kernel, outs, scratch, collective_id, specs)(x, *g, slot, router)  100 us
    pallas_call x1, Pallas kernels, spread_scatter(): _comm(kernel, out, scratch, collective_id, specs)  87 us
    pallas_call x1, Pallas kernels, column_gather(): _comm(kernel, outs, scratch, collective_id, specs)(rows, slot, out_rows)  81.6 us
    pallas_call x1, Pallas kernels, leave(): _comm(kernel, outs, scratch, collective_id, specs)(x, weights, *smalls)  66.8 us
    pallas_call x1, Pallas kernels, enter(): _comm(kernel, outs, scratch, collective_id, specs)  66.6 us
    pallas_call x1, Pallas kernels, run_experts(): pl.pallas_call(_expert_kernel, out_shape=[jax.ShapeDtypeStruct(x.shape, B...  64.7 us
    pallas_call x1, Pallas kernels, key_value_sums(): return _comm(kernel, outs, scratch, collective_id, specs)(dk, dv, x, inner)  44.7 us
    pallas_call x1, Pallas kernels, plane_pair(): _comm(kernel, outs, scratch, collective_id, specs)  44.6 us
  transfers between devices with their start and end apart: 11, of which 2 were waited for; matrix products, arithmetic and copies ran while one was open for 3% of the time, Pallas kernels for 26%

profile of v5, /device:TPU:13, one launch (start us, length us, event | category | flops | bytes accessed | tf_op | source)
XLA Modules:
  0.0 730.9 jit_solution(1518605368828106343)
XLA Ops:
  0.6 4.1 collective-permute-start
  4.9 0.7 pad_maximum_fusion.3
  5.6 0.7 copy.64.gain_ref
  6.3 66.6 %shard_map.229 = (bf16[2,4,128,2048]{3,2,1,0:T(8,128)(2,1)}, bf16[4,2,4,64,768]{4,3,2,1,0:T(8,128)(2,1)}, bf16[8,4,64,128]{3,2,1,0:T(8,128)(2,1)}, s32[8,4,8,128]{3,2,1,0:T(8,128)}) custom-call(bf16[128,2048]{1,0:T(8,128)(2,1)} %h_ref.3, bf16[64,2048]{1,0:T(8,128)(2,1)} %wq_ref.3, bf16[64,2048]{1,0:T(8,128)(2,1)} %wk_ref.3, bf16[64,2048]{1,0:T(8,128)(2,1)} %wv_ref.3, ...), custom_call_target="tpu_custom_call" | custom-call | bytes 100000000 | tf_op jit(solution)/shard_map/pallas_call | solution.py:379
  72.9 1.2 slice.46
  74.2 1.9 fusion.4
  76.2 0.6 pad_convert_fusion.gain_ref
  76.8 1.3 pad_maximum_fusion
  78.2 2.6 collective-permute-start.1
  80.8 9.2 %shard_map.230 = (f32[1024,512]{1,0:T(8,128)}, bf16[1024,256]{1,0:T(8,128)(2,1)}, bf16[1024,256]{1,0:T(8,128)(2,1)}, bf16[1024,256]{1,0:T(8,128)(2,1)}, f32[2,8,128]{2,1,0:T(8,128)}) custom-call(bf16[1024,2048]{1,0:T(8,128)(2,1)} %bitcast.105, bf16[2048,768]{1,0:T(8,128)(2,1)} %bitcast.107, f32[8,256]{1,0:T(8,128)} %pad_convert_fusion.gain_ref, ...), custom_call_target="tpu_custom_call" | custom-call | flops 3221225472 | bytes 7340032 | tf_op jit(solution)/shard_map/pallas_call | solution.py:1555
  89.9 44.6 %shard_map.231 = (bf16[4,1024,256]{2,1,0:T(8,128)(2,1)}, bf16[4,1024,256]{2,1,0:T(8,128)(2,1)}, bf16[4,128,2048]{2,1,0:T(8,128)(2,1)}, f32[16,128]{1,0:T(8,128)}, f32[4,8,128]{2,1,0:T(8,128)}) custom-call(bf16[1024,256]{1,0:T(8,128)(2,1)} %get-tuple-element.86.a_ref, bf16[1024,256]{1,0:T(8,128)(2,1)} %get-tuple-element.87.b_ref, bf16[128,2048]{1,0:T(8,128)(2,1)} %x_ref.1, ...), custom_call_target="tpu_custom_call" | custom-call | bytes 100000000 | tf_op jit(solution)/shard_map/pallas_call | solution.py:431
  134.6 0.5 collective-permute-start.4
  135.2 0.7 stack.38.index_ref
  135.8 1.3 slice.36.q_stat
  137.1 13.3 %shard_map.232 = (f32[1024,256]{1,0:T(8,128)}, f32[1024,256]{1,0:T(8,128)}, bf16[1024,2048]{1,0:T(8,128)(2,1)}) custom-call(s32[6]{0:T(128)} %stack.38.index_ref, s32[5]{0:T(128)} %doc_ref.3, f32[8,128]{1,0:T(8,128)} %slice.36.q_stat, f32[32,128]{1,0:T(8,128)} %bitcast.90, bf16[1024,256]{1,0:T(8,128)(2,1)} %get-tuple-element.91.q_ref, ...), custom_call_target="tpu_custom_call" | custom-call | flops 1073741824 | bytes 4194304 | tf_op jit(solution)/shard_map/pallas_call | solution.py:1485
  150.5 9.7 %collective-permute-done.4.g1 = bf16[4,128,2048]{2,1,0:T(8,128)(2,1)} collective-permute-done((bf16[4,128,2048]{2,1,0:T(8,128)(2,1)}, bf16[4,128,2048]{2,1,0:T(8,128)(2,1)}, u32[]{:S(2)}, u32[]{:S(2)}) %collective-permute-start.4) | collective-permute-done | bytes 2097184 | tf_op jit(solution)/shard_map/ppermute | solution.py:1124
  160.2 0.4 collective-permute-start.5
  160.6 1.1 collective-permute-start.6
  161.7 0.4 compare_reduce_fusion
  162.1 0.8 copy.67
  162.9 0.8 convert_select_fusion
  163.8 1.3 copy.70.slot_ref
  165.2 0.4 convert_reduce_fusion
  165.6 1.4 dynamic-slice_maximum_fusion.router_ref
  167.0 44.1 %shard_map.233 = bf16[128,2048]{1,0:T(8,128)(2,1)} custom-call(bf16[2,4,128,2048]{3,2,1,0:T(8,128)(2,1)} %bitcast.80), custom_call_target="tpu_custom_call" | custom-call | bytes 100000000 | tf_op jit(solution)/shard_map/pallas_call | solution.py:474
  211.1 1.3 multiply_reduce_fusion.2
  212.4 1.3 multiply_convert_fusion.x_ref
  213.7 0.4 fusion.23
  214.1 0.1 copy.71
  214.2 0.2 fusion.6
  214.4 0.1 copy-done.4
  214.5 100.1 %shard_map.234 = (bf16[32,128,2048]{2,1,0:T(8,128)(2,1)}, bf16[8,8,80,2048]{3,2,1,0:T(8,128)(2,1)}, bf16[8,8,80,2048]{3,2,1,0:T(8,128)(2,1)}, f32[8,8,80,128]{3,2,1,0:T(8,128)}, bf16[4,4,128,2048]{3,2,1,0:T(8,128)(2,1)}) custom-call(bf16[128,2048]{1,0:T(8,128)(2,1)} %copy-done.4, bf16[4,128,2048]{2,1,0:T(8,128)(2,1)} %get-tuple-element.104.g0, ...), custom_call_target="tpu_custom_call" | custom-call | bytes 100000000 | tf_op jit(solution)/shard_map/pallas_call | solution.py:873
  314.6 64.7 %shard_map.235 = (bf16[8,640,2048]{2,1,0:T(8,128)(2,1)}, bf16[8,640,2048]{2,1,0:T(8,128)(2,1)}, f32[8,3,2048,256]{3,2,1,0:T(8,128)}, f32[8,640,128]{2,1,0:T(8,128)}) custom-call(bf16[8,640,2048]{2,1,0:T(8,128)(2,1)} %bitcast.103, bf16[8,640,2048]{2,1,0:T(8,128)(2,1)} %bitcast.104, f32[8,640,128]{2,1,0:T(8,128)} %bitcast.109, bf16[8,3,2048,256]{3,2,1,0:T(8,128)(2,1)} %w_ref.1), custom_call_target="tpu_custom_call" | custom-call | flops 48318382080 | bytes 159383552 | tf_op jit(solution)/shard_map/pallas_call | solution.py:1727
  379.3 87.0 %shard_map.236 = bf16[128,2176]{1,0:T(8,128)(2,1)} custom-call(s32[8,512,8]{2,1,0:T(8,128)} %bitcast.68, f32[8,8,80,128]{3,2,1,0:T(8,128)} %bitcast.83, bf16[8,8,80,2048]{3,2,1,0:T(8,128)(2,1)} %bitcast.67), custom_call_target="tpu_custom_call" | custom-call | bytes 100000000 | tf_op jit(solution)/shard_map/pallas_call | solution.py:1088
  466.3 1.2 convert_element_type.79
  467.5 0.2 multiply_reduce_fusion.3
  467.7 0.1 multiply_convert_fusion.1
  467.8 0.6 multiply_reduce_fusion
  468.4 0.1 copy-done.5
  468.5 1.9 fusion.22
  470.4 81.6 %shard_map.237 = (bf16[2,4,128,2048]{3,2,1,0:T(8,128)(2,1)}, bf16[4,128,2048]{2,1,0:T(8,128)(2,1)}) custom-call(bf16[128,2048]{1,0:T(8,128)(2,1)} %get-tuple-element.154.r_ref, s32[8,512,8]{2,1,0:T(8,128)} %bitcast.69, bf16[8,8,80,2048]{3,2,1,0:T(8,128)(2,1)} %bitcast.66), custom_call_target="tpu_custom_call" | custom-call | bytes 100000000 | tf_op jit(solution)/shard_map/pallas_call | solution.py:454
  552.1 21.7 %shard_map.238 = (bf16[1024,256]{1,0:T(8,128)(2,1)}, bf16[4096,256]{1,0:T(8,128)(2,1)}, bf16[4096,256]{1,0:T(8,128)(2,1)}, bf16[256,2048]{1,0:T(8,128)(2,1)}, f32[8,128]{1,0:T(8,128)}, /*index=5*/f32[8,512]{1,0:T(8,128)}) custom-call(s32[6]{0:T(128)} %stack.38.index_ref, s32[5]{0:T(128)} %doc_ref.3, f32[8,128]{1,0:T(8,128)} %slice.36.q_stat, ...), custom_call_target="tpu_custom_call" | custom-call | flops 2684354560 | bytes 8388608 | tf_op jit(solution)/shard_map/pallas_call | solution.py:1508
  573.8 0.7 reshape.210
  574.5 1.3 pad_maximum_fusion.2.s_ref
  575.8 44.7 %shard_map.239 = (bf16[1024,256]{1,0:T(8,128)(2,1)}, bf16[1024,256]{1,0:T(8,128)(2,1)}, bf16[128,2048]{1,0:T(8,128)(2,1)}, f32[16,128]{1,0:T(8,128)}) custom-call(bf16[4,1024,256]{2,1,0:T(8,128)(2,1)} %bitcast.84, bf16[4,1024,256]{2,1,0:T(8,128)(2,1)} %bitcast.85, bf16[4,128,2048]{2,1,0:T(8,128)(2,1)} %get-tuple-element.118.x_ref, ...), custom_call_target="tpu_custom_call" | custom-call | bytes 100000000 | tf_op jit(solution)/shard_map/pallas_call | solution.py:541
  620.6 0.7 collective-permute-start.7
  621.3 3.0 collective-permute-start.8
  624.3 13.9 %shard_map.240 = (bf16[2048,768]{1,0:T(8,128)(2,1)}, bf16[1024,2048]{1,0:T(8,128)(2,1)}, f32[8,256]{1,0:T(8,128)}) custom-call(bf16[1024,256]{1,0:T(8,128)(2,1)} %get-tuple-element.115.dq_ref, bf16[1024,256]{1,0:T(8,128)(2,1)} %get-tuple-element.123.dk_ref, bf16[1024,256]{1,0:T(8,128)(2,1)} %get-tuple-element.124.dv_ref, ...), custom_call_target="tpu_custom_call" | custom-call | flops 6442450944 | bytes 14680064 | tf_op jit(solution)/shard_map/pallas_call | solution.py:1621
  638.2 0.7 reshape.216.refs_0_
  638.9 0.7 slice.41
  639.6 0.6 select_maximum_fusion.refs_1_
  640.2 66.8 %shard_map.241 = (bf16[128,2048]{1,0:T(8,128)(2,1)}, bf16[3,64,2048]{2,1,0:T(8,128)(2,1)}, bf16[8,4,64,128]{3,2,1,0:T(8,128)(2,1)}, f32[8,4,24,128]{3,2,1,0:T(8,128)}) custom-call(bf16[2,4,128,2048]{3,2,1,0:T(8,128)(2,1)} %bitcast.81, bf16[4,2,256,768]{3,2,1,0:T(8,128)(2,1)} %bitcast.82, bf16[64,128]{1,0:T(8,128)(2,1)} %reshape.216.refs_0_, ...), custom_call_target="tpu_custom_call" | custom-call | bytes 100000000 | tf_op jit(solution)/shard_map/pallas_call | solution.py:593
  707.0 0.8 dynamic-slice_bitcast_fusion.4
  707.9 0.5 slice_bitcast_fusion
  708.5 0.1 add_convert_fusion
  708.6 3.1 collective-permute-start.10
  711.7 1.0 slice_reduce_fusion
  712.7 1.6 reshape.223
  714.3 0.6 dynamic_slice.43
  714.9 2.6 fusion
  717.5 6.0 collective-permute-done.10.do_ref
  723.5 0.7 copy-done.11
  724.2 5.1 shard_map.242
  729.3 1.4 reduce.1
  (48 shorter events, 0.6 us)
Async XLA Ops:
  0.6 77.5 %collective-permute-start = (bf16[64,2048]{1,0:T(8,128)(2,1)}, bf16[64,2048]{1,0:T(8,128)(2,1)S(1)}, u32[]{:S(2)}, u32[]{:S(2)}) collective-permute-start(bf16[64,2048]{1,0:T(8,128)(2,1)} %param.20), channel_id=1, source_target_pairs={{0,0},{1,8},{2,16},{3,24},{4,4},{5,12},{6,20},{7,28},{8,9},{9,17},... | collective-permute-start | bytes 786440 | tf_op jit(solution)/shard_map/ppermute | solution.py:1124
  78.1 11.8 %copy-start.6 = (bf16[64,2048]{1,0:T(8,128)(2,1)}, bf16[64,2048]{1,0:T(8,128)(2,1)S(1)}, u32[]{:S(2)}) copy-start(bf16[64,2048]{1,0:T(8,128)(2,1)S(1)} %collective-permute-done.w0) | copy-start | bytes 786436
  78.1 56.5 %collective-permute-start.3 = (bf16[64,2048]{1,0:T(8,128)(2,1)S(1)}, bf16[64,2048]{1,0:T(8,128)(2,1)S(1)}, u32[]{:S(2)}, u32[]{:S(2)}) collective-permute-start(bf16[64,2048]{1,0:T(8,128)(2,1)S(1)} %collective-permute-done.w0), channel_id=1, source_target_pairs={{0,24},{1,25},{2,26},{3,27},{4,28},{5,29},{6,30},{7,31},{8,16},{9,... | collective-permute-start | bytes 786440 | tf_op jit(solution)/shard_map/ppermute | solution.py:1124
  78.1 56.5 %collective-permute-start.2 = (bf16[64,2048]{1,0:T(8,128)(2,1)S(1)}, bf16[64,2048]{1,0:T(8,128)(2,1)S(1)}, u32[]{:S(2)}, u32[]{:S(2)}) collective-permute-start(bf16[64,2048]{1,0:T(8,128)(2,1)S(1)} %collective-permute-done.w0), channel_id=1, source_target_pairs={{0,16},{1,17},{2,18},{3,19},{4,20},{5,21},{6,22},{7,23},{8,24},{9,... | collective-permute-start | bytes 786440 | tf_op jit(solution)/shard_map/ppermute | solution.py:1124
  78.2 56.4 %collective-permute-start.1 = (bf16[64,2048]{1,0:T(8,128)(2,1)S(1)}, bf16[64,2048]{1,0:T(8,128)(2,1)S(1)}, u32[]{:S(2)}, u32[]{:S(2)}) collective-permute-start(bf16[64,2048]{1,0:T(8,128)(2,1)S(1)} %collective-permute-done.w0), channel_id=1, source_target_pairs={{0,8},{1,9},{2,10},{3,11},{4,12},{5,13},{6,14},{7,15},{8,0},{9,1},... | collective-permute-start | bytes 786440 | tf_op jit(solution)/shard_map/ppermute | solution.py:1124
  134.6 2.5 copy-start.7
  134.6 2.5 copy-start.8
  134.6 2.5 copy-start.9
  134.6 25.6 %collective-permute-start.4 = (bf16[4,128,2048]{2,1,0:T(8,128)(2,1)}, bf16[4,128,2048]{2,1,0:T(8,128)(2,1)}, u32[]{:S(2)}, u32[]{:S(2)}) collective-permute-start(bf16[4,128,2048]{2,1,0:T(8,128)(2,1)} %get-tuple-element.104.g0), channel_id=1, source_target_pairs={{0,8},{1,9},{2,10},{3,11},{4,20},{5,21},{6,22},{7,23},{8,0},{9,1},... | collective-permute-start | bytes 6291464 | tf_op jit(solution)/shard_map/ppermute | solution.py:1124
  137.1 24.5 %copy-start.12 = (s32[8,4,8,128]{3,2,1,0:T(8,128)S(1)}, s32[8,4,8,128]{3,2,1,0:T(8,128)}, u32[]{:S(2)}) copy-start(s32[8,4,8,128]{3,2,1,0:T(8,128)} %get-tuple-element.103) | copy-start | bytes 393220
  160.2 54.2 %collective-permute-start.5 = (bf16[4,128,2048]{2,1,0:T(8,128)(2,1)}, bf16[4,128,2048]{2,1,0:T(8,128)(2,1)}, u32[]{:S(2)}, u32[]{:S(2)}) collective-permute-start(bf16[4,128,2048]{2,1,0:T(8,128)(2,1)} %get-tuple-element.104.g0), channel_id=1, source_target_pairs={{0,16},{1,17},{2,18},{3,19},{4,12},{5,13},{6,14},{7,15},{8,24},{9,... | collective-permute-start | bytes 6291464 | tf_op jit(solution)/shard_map/ppermute | solution.py:1124
  160.6 53.8 %collective-permute-start.6 = (bf16[4,128,2048]{2,1,0:T(8,128)(2,1)}, bf16[4,128,2048]{2,1,0:T(8,128)(2,1)}, u32[]{:S(2)}, u32[]{:S(2)}) collective-permute-start(bf16[4,128,2048]{2,1,0:T(8,128)(2,1)} %collective-permute-done.4.g1), channel_id=1, source_target_pairs={{0,16},{1,17},{2,18},{3,19},{4,12},{5,13},{6,14},{7,15},{8,24},{9,... | collective-permute-start | bytes 6291464 | tf_op jit(solution)/shard_map/ppermute | solution.py:1124
  163.8 47.3 %copy-start = (s32[8,8,512]{1,2,0:T(8,128)}, s32[8,8,512]{1,2,0:T(8,128)S(1)}, u32[]{:S(2)}) copy-start(s32[8,8,512]{1,2,0:T(8,128)S(1)} %convert_select_fusion) | copy-start | bytes 393220
  163.8 1.4 copy-start.3
  167.0 44.1 %copy-start.1 = (bf16[128,2048]{1,0:T(8,128)(2,1)S(1)}, bf16[128,2048]{1,0:T(8,128)(2,1)}, u32[]{:S(2)}) copy-start(bf16[128,2048]{1,0:T(8,128)(2,1)} %h_ref.3) | copy-start | bytes 1572868
  213.7 0.8 copy-start.4
  466.3 1.5 copy-start.2
  467.5 1.0 copy-start.5
  575.8 44.7 %copy-start.10 = (bf16[256,2048]{1,0:T(8,128)(2,1)S(1)}, bf16[256,2048]{1,0:T(8,128)(2,1)}, u32[]{:S(2)}) copy-start(bf16[256,2048]{1,0:T(8,128)(2,1)} %get-tuple-element.122) | copy-start | bytes 3145732
  620.6 19.6 %collective-permute-start.7 = (bf16[64,2048]{1,0:T(8,128)(2,1)S(1)}, bf16[64,2048]{1,0:T(8,128)(2,1)S(1)}, u32[]{:S(2)}, u32[]{:S(2)}) collective-permute-start(bf16[64,2048]{1,0:T(8,128)(2,1)S(1)} %get-tuple-element.128), channel_id=1, source_target_pairs={{0,8},{1,9},{2,10},{3,11},{4,12},{5,13},{6,14},{7,15},{8,0},{9,1},... | collective-permute-start | bytes 786440 | tf_op jit(solution)/shard_map/ppermute | solution.py:1124
  621.3 19.0 %collective-permute-start.8 = (bf16[64,2048]{1,0:T(8,128)(2,1)S(1)}, bf16[64,2048]{1,0:T(8,128)(2,1)S(1)}, u32[]{:S(2)}, u32[]{:S(2)}) collective-permute-start(bf16[64,2048]{1,0:T(8,128)(2,1)S(1)} %get-tuple-element.129), channel_id=1, source_target_pairs={{0,16},{1,17},{2,18},{3,19},{4,20},{5,21},{6,22},{7,23},{8,24},{9,... | collective-permute-start | bytes 786440 | tf_op jit(solution)/shard_map/ppermute | solution.py:1124
  624.3 15.9 %collective-permute-start.9 = (bf16[64,2048]{1,0:T(8,128)(2,1)S(1)}, bf16[64,2048]{1,0:T(8,128)(2,1)S(1)}, u32[]{:S(2)}, u32[]{:S(2)}) collective-permute-start(bf16[64,2048]{1,0:T(8,128)(2,1)S(1)} %get-tuple-element.130), channel_id=1, source_target_pairs={{0,24},{1,25},{2,26},{3,27},{4,28},{5,29},{6,30},{7,31},{8,16},{9,... | collective-permute-start | bytes 786440 | tf_op jit(solution)/shard_map/ppermute | solution.py:1124
  708.6 14.9 %collective-permute-start.10 = (bf16[64,2048]{1,0:T(8,128)(2,1)S(1)}, bf16[64,2048]{1,0:T(8,128)(2,1)S(1)}, u32[]{:S(2)}, u32[]{:S(2)}) collective-permute-start(bf16[64,2048]{1,0:T(8,128)(2,1)S(1)} %add_convert_fusion), channel_id=1, source_target_pairs={{0,0},{8,1},{16,2},{24,3},{4,4},{12,5},{20,6},{28,7},{9,8},{17,9},... | collective-permute-start | bytes 786440 | tf_op jit(solution)/shard_map/ppermute | solution.py:1124
  723.5 0.7 copy-start.11

commit v6 on v5

--- a/solution.py
+++ b/solution.py
@@ -25,6 +25,7 @@
 ATTEND_CHUNK = 512
 ATTEND_ROWS = 512
 BACK_ROWS = 1024
+PROJECT_ROWS = 256
 SPREAD_WIDTH = 2048
 
 
@@ -123,11 +124,16 @@
                 live.remove(part)
 
 
-def _line_part(u, z, source, block, sems, share=True):
+def _line_part(u, z, source, block, sems, share=True, place=None):
     z_send, z_recv, c_send, c_recv, own_sem = sems
     here, core = (u, z), u % 2
-    own = pltpu.make_async_copy(source, block(core, z), own_sem)
-    own.start()
+    if place is None:
+        own = pltpu.make_async_copy(source, block(core, z), own_sem)
+        own.start()
+    else:
+        def block(_, level):
+            return place(level, z)
+
     order = _line_order(z)
 
     def along(level, ref, step):
@@ -140,7 +146,8 @@
             step(ref, 1, level, (u, z + 1))
 
     def go(ref, way, level, to):
-        _send(ref, block(core, level), z_send.at[way, level], z_recv.at[level], to)
+        there = block(core, level) if place is None else place(level, to[1])
+        _send(ref, there, z_send.at[way, level], z_recv.at[level], to)
 
     def gone(ref, way, level, to):
         _sent(ref, z_send.at[way, level], here)
@@ -160,10 +167,11 @@
             _expect(block(1 - core, order[i]), c_recv.at[order[i]], here)
     yield
     for i in range(4):
-        along(order[i], block(core, order[i]), gone)
+        along(order[i], source, gone)
         if share:
-            _sent(block(core, order[i]), c_send.at[order[i]], here)
-    own.wait()
+            _sent(source, c_send.at[order[i]], here)
+    if place is None:
+        own.wait()
 
 
 def _plane_part(u, z, own, block, sems):
@@ -265,7 +273,7 @@
     )
 
 
-ENTER_ORDER = (0, 2, 1, 0, 2, 1, 0, 2, 0, 2)
+ENTER_ORDER = (0, 2, 3, 1, 3, 3, 0, 2, 1, 0, 2, 0, 2)
 KV_ORDER = (2, 0, 1, 0, 0, 1, 2, 1, 0, 1)
 PAIR_ORDER = (1, 0, 2, 1, 0, 0, 1, 2, 1, 0)
 LEAVE_ORDER = (0, 1, 2, 1, 2, 1, 0, 0, 1, 0, 1, 1)
@@ -311,14 +319,15 @@
     return router, tail.astype(BF16)
 
 
-def enter(hidden, weights, gains, router, routes, collective_id):
+def enter(hidden, weights, gains, router, routes, out_grad, collective_id):
     T, D = hidden.shape
     R, C = weights[0].shape[0], weights[0].shape[1] // 8
     held = (2, 4, R, 3 * C)
     strip = 16
 
-    def kernel(h_ref, wq_ref, wk_ref, wv_ref, gain_ref, router_ref, route_ref, x_out, w_out, p_out, r_out, *refs):
+    def kernel(h_ref, wq_ref, wk_ref, wv_ref, gain_ref, router_ref, route_ref, g_ref, x_out, w_out, p_out, r_out, g_out, *refs):
         x_ref, w_ref, pack_ref, w_buf, w_send, w_recv = refs[:6]
+        half = [pl.ds(h * (T // 2), T // 2) for h in range(2)]
         sems = refs[6:]
         u, z = lax.axis_index("uly"), lax.axis_index("blk")
         here, core, chip = (u, z), u % 2, u // 2
@@ -362,8 +371,9 @@
         _greet(u, z, range(1, 8), others=[to for to, c, k in column if k], meanwhile=prepare)
         _run(
             weight_part(),
-            _small_part(u, z, (pack_ref, route_ref), (p_out, r_out), sems[8:]),
+            _small_part(u, z, (pack_ref, route_ref), (p_out, r_out), sems[11:]),
             _line_part(u, z, x_ref, lambda c, level: x_out.at[c, level], sems[3:8]),
+            _plane_part(u, z, lambda h: g_ref.at[half[h]], lambda h, v: g_out.at[v // 2, half[h]], sems[8:11]),
             order=ENTER_ORDER,
         )
 
@@ -372,11 +382,12 @@
         jax.ShapeDtypeStruct((4,) + held, BF16),
         jax.ShapeDtypeStruct((8, 4, R, 128), BF16),
         jax.ShapeDtypeStruct((8, 4) + routes.shape, routes.dtype),
+        jax.ShapeDtypeStruct((4, T, D), BF16),
     ]
     scratch = [pltpu.VMEM((T, D), BF16), pltpu.VMEM((3, R, D), BF16), pltpu.VMEM((R, 128), BF16)]
-    scratch += [pltpu.VMEM(held, BF16), DMA((7, 3)), DMA((7, 3))] + PLANE_SEMS + LINE_SEMS + _small_sems(2)
-    specs = ([IN_VMEM] * 7, [ANY_SPACE] * 4)
-    return _comm(kernel, outs, scratch, collective_id, specs)(hidden, *weights, gains, router, routes)
+    scratch += [pltpu.VMEM(held, BF16), DMA((7, 3)), DMA((7, 3))] + PLANE_SEMS + LINE_SEMS + PLANE_SEMS + _small_sems(2)
+    specs = ([IN_VMEM] * 7 + [ANY_SPACE], [ANY_SPACE] * 5)
+    return _comm(kernel, outs, scratch, collective_id, specs)(hidden, *weights, gains, router, routes, out_grad)
 
 
 def _column_sum_part(u, z, x_ref, total, buf, sems, then_do):
@@ -415,7 +426,9 @@
 
         _run(
             _plane_part(u, z, lambda h: own[h], lambda h, v: outs[h].at[v // 2], sems[:3]),
-            _line_part(u, z, x_ref, lambda c, level: x_out.at[level], sems[3:8], share=False),
+            _line_part(
+                u, z, x_ref, None, sems[3:8], share=False, place=lambda level, at: x_out.at[(level - at + 3) % 4]
+            ),
             _column_sum_part(u, z, s_ref, s_out, buf, sems[8:10], tell),
             order=PAIR_ORDER,
         )
@@ -424,7 +437,7 @@
             _sent(keys, k_send.at[i], here)
 
     outs = [jax.ShapeDtypeStruct((4,) + x.shape, x.dtype) for x in (first, second)]
-    outs += [jax.ShapeDtypeStruct((4,) + rows.shape, rows.dtype)]
+    outs += [jax.ShapeDtypeStruct((3,) + rows.shape, rows.dtype)]
     outs += [jax.ShapeDtypeStruct(squares.shape, F32), jax.ShapeDtypeStruct((4, R, 128), F32)]
     specs = ([IN_VMEM] * 2 + [ANY_SPACE, IN_VMEM], [ANY_SPACE] * 3 + [IN_VMEM] * 2)
     scratch = [pltpu.VMEM((7,) + squares.shape, F32)] + PLANE_SEMS + LINE_SEMS + [DMA((7,)), DMA((7,)), DMA((3,)), DMA((3,))]
@@ -665,9 +678,9 @@
 
 
 def _gather_pick_kernel(
-    x_ref, g0, g1, g2, g3, slot_ref, router_ref, o_ref, xr_ref, gr_ref, gate_ref, other_g, pick, in_buf, out_buf, in_sem, out_sem, *sems, width
+    x_ref, here_g, g0, g1, g2, g3, slot_ref, router_ref, o_ref, xr_ref, gr_ref, gate_ref, other_here, other_g, pick, in_buf, out_buf, in_sem, out_sem, *sems, width
 ):
-    own_sem, z_send, z_recv, p_send, p_recv, c_send, c_recv, g_send, g_recv = sems
+    own_sem, z_send, z_recv, p_send, p_recv, c_send, c_recv, g_send, g_recv, h_send, h_recv = sems
     own_g = (g0, g1, g2, g3)
     u, z = lax.axis_index("uly"), lax.axis_index("blk")
     core, chip = u % 2, u // 2
@@ -696,8 +709,10 @@
             p = chip ^ steps[k]
             if source == "x":
                 ref = o_ref.at[(2 * p + which) * DEPTH + level]
+            elif source == 0:
+                ref = (here_g if which is core else other_here).at[p]
             else:
-                ref = (own_g[k] if which is core else other_g.at[k]).at[level]
+                ref = (own_g[k] if which is core else other_g.at[k]).at[source - 1]
             rows = pl.ds(pl.multiple_of(p * T, T), T)
             copy = pltpu.make_async_copy(ref, in_buf.at[n % 2, rows], in_sem.at[n % 2, k])
             copy.start() if start else copy.wait()
@@ -712,7 +727,7 @@
         at = 2 * level + which
         rows_in, rows_out = in_buf.at[n % 2], out_buf.at[n % 2]
         row = lax.broadcasted_iota(jnp.int32, (slots, group), 0)
-        if source == "g":
+        if source != "x":
             picks = [jnp.where(slot_ref[at, e : e + 1, :] == row, 1.0, 0.0).astype(BF16) for e in range(experts)]
             pick[at] = jnp.concatenate(picks, axis=0)
         else:
@@ -722,11 +737,8 @@
             high = chances.astype(BF16)
             low = (chances - high.astype(F32)).astype(BF16)
             gates = dot(pick[at], jnp.concatenate([high, low], axis=1))
-            lane = lax.broadcasted_iota(jnp.int32, (slots, 2 * EXPERTS), 1)
             for e in range(experts):
-                part = gates[e * slots : (e + 1) * slots]
-                part = jnp.where((lane == e) | (lane == EXPERTS + e), part, 0.0)
-                gate_ref[e, at] = jnp.broadcast_to(jnp.sum(part, axis=1, keepdims=True), (slots, 128))
+                gate_ref[e, at] = gates[e * slots : (e + 1) * slots]
         if n >= 2:
             sent.pop(n - 2).wait()
 
@@ -738,11 +750,11 @@
             return 0
 
         lax.fori_loop(0, D // width, step, 0)
-        sent[n] = out_copy(n, gr_ref if source == "g" else xr_ref, at)
+        sent[n] = out_copy(n, xr_ref if source == "x" else gr_ref, at)
         sent[n].start()
 
     jobs = _Jobs(load, compute)
-    jobs.add(*[("g", level, core) for level in range(4)])
+    jobs.add(*[(j, (z + j) % 4, core) for j in range(4)])
 
     def along(level, source, step):
         @pl.when((z > 0) & (level >= z))
@@ -796,15 +808,17 @@
         jobs.add(("x", level, other))
 
     arrive(0)
+    _send(here_g, other_here, h_send, h_recv, (u ^ 1, z))
     for k in range(4):
         _send(own_g[k], other_g.at[k], g_send.at[k], g_recv.at[k], (u ^ 1, z))
     jobs.run(2)
     onward(0)
     jobs.run(1)
     arrive(1)
+    _expect(other_here, h_recv, here)
     for k in range(4):
         _expect(other_g.at[k], g_recv.at[k], here)
-    jobs.add(*[("g", level, other) for level in range(4)])
+    jobs.add(*[(j, (z + j) % 4, other) for j in range(4)])
     jobs.run(2)
     own.wait()
     share(0)
@@ -835,13 +849,14 @@
                 _sent(part(u, level, h), p_send.at[level, h, k], here)
         for k in range(4):
             _sent(block(u, level), c_send.at[level, k], here)
+    _sent(other_here, h_send, here)
     for k in range(4):
         _sent(other_g.at[k], g_send.at[k], here)
     for copy in sent.values():
         copy.wait()
 
 
-def gather_pick(x, g, slot, router, slots, collective_id):
+def gather_pick(x, here_g, g, slot, router, slots, collective_id):
     T, D = x.shape
     groups, EL, group = slot.shape
     picked = jax.ShapeDtypeStruct((EL, groups, slots, D), BF16)
@@ -850,7 +865,8 @@
         picked,
         picked,
         jax.ShapeDtypeStruct((EL, groups, slots, 128), F32),
-        jax.ShapeDtypeStruct((4, 4, T, D), BF16),
+        jax.ShapeDtypeStruct((4, T, D), BF16),
+        jax.ShapeDtypeStruct((4, 3, T, D), BF16),
     ]
     scratch = [
         pltpu.VMEM((groups, EL * slots, group), BF16),
@@ -867,10 +883,12 @@
         DMA((4, 4)),
         DMA((4,)),
         DMA((4,)),
+        DMA,
+        DMA,
     ]
-    specs = ([IN_VMEM] + [ANY_SPACE] * 4 + [IN_VMEM] * 2, [ANY_SPACE] * 3 + [IN_VMEM, ANY_SPACE])
+    specs = ([IN_VMEM] + [ANY_SPACE] * 5 + [IN_VMEM] * 2, [ANY_SPACE] * 3 + [IN_VMEM] + [ANY_SPACE] * 2)
     kernel = functools.partial(_gather_pick_kernel, width=PICK_WIDTH)
-    out, xr, gr, gates, _ = _comm(kernel, outs, scratch, collective_id, specs)(x, *g, slot, router)
+    out, xr, gr, gates, *_ = _comm(kernel, outs, scratch, collective_id, specs)(x, here_g, *g, slot, router)
     return out.reshape(32 * T, D), xr, gr, gates
 
 
@@ -1105,8 +1123,8 @@
         self.first_block, self.block_step = 8 * (self.u // 2), 1
         self.rows = ATTEND_ROWS
 
-    def enter(self, hidden, weights, gains, out_weight, router, routes):
-        rows, weights, packs, routes = enter(hidden, weights, gains, router, routes, 1)
+    def enter(self, hidden, weights, gains, out_weight, router, routes, out_grad):
+        rows, weights, packs, routes, self.here = enter(hidden, weights, gains, router, routes, out_grad, 1)
         there = [((2 * ((z + u // 2) % 4) + u % 2), u // 2) for u in range(8) for z in range(4)]
         self.forth = [(i, 4 * u + z) for i, (u, z) in enumerate(there)]
         rows, mine = lax.optimization_barrier((rows, self.permute(out_weight, self.forth)))
@@ -1135,22 +1153,27 @@
         return keys.reshape(-1, self.C), values.reshape(-1, self.C), stats.reshape(2, -1, 128), k_stat.reshape(-1, 128)
 
     def heads_to_rows(self, x):
-        x, own, near = lax.optimization_barrier((x, *self.upstream))
+        x, own, near, *self.prepared = lax.optimization_barrier((x, *self.upstream, *self.prepared))
         self.upstream = (own, near, self.permute(own, self.then), self.permute(near, self.then))
         return column_scatter(x.reshape(2, 4, self.T, self.D), 5)
 
-    def experts(self, second_low, routes, weights, router):
-        EL, T, D = weights.shape[0], self.T, self.D
-        slots = -(-4 * CAP // 16) * 16
+    def prepare(self, routes, EL, router):
+        T = self.T
         chosen = jnp.any(routes[None] == (self.u * EL + jnp.arange(EL, dtype=jnp.int32))[:, None, None, None, None], axis=3)
         chosen = chosen.reshape(EL, 4, 2, 4, T).transpose(3, 2, 0, 1, 4).reshape(8, EL, 4 * T)
         slot = slots_of(chosen)
-        second_all, xr, gr, gates = gather_pick(second_low, self.upstream, slot, router, slots, 7)
+        self.prepared = (slot, slot.transpose(0, 2, 1), router)
+
+    def experts(self, second_low, weights):
+        EL, D = weights.shape[0], self.D
+        slots = -(-4 * CAP // 16) * 16
+        slot, self.slot, router = self.prepared
+        second_all, xr, gr, gates = gather_pick(second_low, self.here, self.upstream, slot, router, slots, 7)
         flat, cut = (EL, 8 * slots, -1), (EL, 8, slots, -1)
         out_rows, entry_rows, self.expert_grads, gate_grads = run_experts(
             xr.reshape(flat), gr.reshape(flat), gates.reshape(flat), weights, 8 * slots
         )
-        self.slot, self.out_rows = slot.transpose(0, 2, 1), out_rows.reshape(cut)
+        self.out_rows = out_rows.reshape(cut)
         return second_all, spread_scatter(self.slot, gate_grads.reshape(cut), entry_rows.reshape(cut), 8)
 
     def rows_to_heads(self, x):
@@ -1209,7 +1232,7 @@
     def scatter_wide(self, x):
         return lax.psum_scatter(x, ALL, scatter_dimension=0, tiled=True)
 
-    def enter(self, hidden, weights, gains, out_weight, router, routes):
+    def enter(self, hidden, weights, gains, out_weight, router, routes, out_grad):
         U, R = self.U, router.shape[0]
         gains, hidden = gains.astype(F32), hidden.astype(F32)
         scaled = jnp.stack([(w.astype(F32) * gains[:, :1]).astype(BF16) for w in weights])
@@ -1242,8 +1265,12 @@
     def rows_all(self, x):
         return lax.all_gather(x, "uly", axis=0, tiled=True)
 
-    def experts(self, second_low, routes, weights, router):
+    def prepare(self, routes, EL, router):
+        self.prepared = (routes, router)
+
+    def experts(self, second_low, weights):
         EL, D = weights.shape[0], self.D
+        routes, router = self.prepared
         second_all, upstream_all = self.gather(second_low), self.gather(self.upstream)
         N = upstream_all.shape[0]
         group = min(512, N)
@@ -1547,7 +1574,7 @@
 def project(x, weights, gains, cosine, sine):
     L, D = x.shape
     C = weights.shape[1] // 3
-    rows = 256
+    rows = min(PROJECT_ROWS, L)
 
     def block(width):
         return pl.BlockSpec((rows, width), lambda i: (i, 0))
@@ -1646,7 +1673,8 @@
     for e in range(experts):
         hit = slot_ref[e : e + 1, :] == row
         gate = jnp.sum(jnp.where(hit, chances[e : e + 1, :], 0.0), axis=1, keepdims=True)
-        gate_ref[e, 0] = jnp.broadcast_to(gate, (slots, 128))
+        lane = lax.broadcasted_iota(jnp.int32, (slots, 128), 1)
+        gate_ref[e, 0] = jnp.where(lane == e, gate, 0.0)
         picks.append(jnp.where(hit, 1.0, 0.0).astype(BF16))
     pick = jnp.concatenate(picks, axis=0)
     for source, target in ((x_ref, xr_ref), (g_ref, gr_ref)):
@@ -1688,7 +1716,9 @@
 
 def _expert_kernel(x_ref, g_ref, gate_ref, w_ref, out_ref, entry_ref, dw_ref, gg_ref):
     x, g = x_ref[0], g_ref[0]
-    gate = gate_ref[0][:, :1]
+    lane = lax.broadcasted_iota(jnp.int32, gate_ref.shape[1:], 1)
+    gate = jnp.where(lane % EXPERTS == pl.program_id(0), gate_ref[0], 0.0)
+    gate = jnp.sum(gate, axis=1, keepdims=True)
     gate_pre = dot(x, w_ref[0, 0])
     up = dot(x, w_ref[0, 1])
     back = dot(g, w_ref[0, 2])
@@ -1823,7 +1853,7 @@
     own_weights = (query_weight, key_weight, value_weight)
     gains = jnp.stack([attn_gain, ffn_gain, query_gain, key_gain], axis=1)
     first_rows, qkv_weight, packed, routes_all = move.enter(
-        hidden_in, own_weights, gains, out_weight, router_weight, routes.T
+        hidden_in, own_weights, gains, out_weight, router_weight, routes.T, out_grad
     )
     hidden = hidden_in.astype(F32)
     weight_router = packed[:, :EXPERTS]
@@ -1839,13 +1869,13 @@
     attended, logs, mixed = attention_forward(
         index, doc_starts, stats[0], k_stat, query_rot, key_all, value_all, move.out_parts, move.rows, chunk
     )
+    move.prepare(routes_all, EL, jnp.roll(weight_router, -u * EL, axis=1))
     residual = hidden + move.heads_to_rows(mixed).astype(F32)
 
     second_scale = norm_scale(residual)
     second_low = (residual * second_scale * gain_ffn).astype(BF16)
     probabilities = jax.nn.softmax(dot(second_low, weight_router), axis=-1)
-    own_router = jnp.roll(weight_router, -u * EL, axis=1)
-    second_all, entry_sum = move.experts(second_low, routes_all, expert_weights, own_router)
+    second_all, entry_sum = move.experts(second_low, expert_weights)
     entry_sum = entry_sum.astype(F32)
 
     second_grad, prob_grad = entry_sum[:, :D], entry_sum[:, D : D + EXPERTS]

time: 741 us -> 732 us (0.988)
  waiting for transfers between devices: 15.8 us -> 6.7 us
    ppermute x11, waiting for transfers between devices: 15.8 us -> 6.7 us  [permute(): return lax.ppermute(x, ALL, pairs)]
  transfers between devices with their start and end apart: 11 -> 11, of which waited for: 2 -> 1; matrix products, arithmetic and copies ran while one was open for 3% -> 3% of each run, Pallas kernels for 26% -> 26%
where the time goes in v6:
time: 732 us; the launch traced here: 722 us
  Pallas kernels  663 us (91%)
  starting transfers between devices  16.9 us (2%)
  other arithmetic  15.2 us (2%)
  local copies, waits for them, and re-layouts  13.5 us (2%)
    pallas_call x1, Pallas kernels, gather_pick(): _comm(kernel, outs, scratch, collective_id, specs)  98.3 us
    pallas_call x1, Pallas kernels, spread_scatter(): _comm(kernel, out, scratch, collective_id, specs)  89.3 us
    pallas_call x1, Pallas kernels, column_gather(): _comm(kernel, outs, scratch, collective_id, specs)(rows, slot, out_rows)  82.2 us
    pallas_call x1, Pallas kernels, enter(): _comm(kernel, outs, scratch, collective_id, specs)  66.8 us
    pallas_call x1, Pallas kernels, leave(): _comm(kernel, outs, scratch, collective_id, specs)(x, weights, *smalls)  65.8 us
    pallas_call x1, Pallas kernels, run_experts(): pl.pallas_call(_expert_kernel, out_shape=[jax.ShapeDtypeStruct(x.shape, B...  64.7 us
    pallas_call x1, Pallas kernels, key_value_sums(): return _comm(kernel, outs, scratch, collective_id, specs)(dk, dv, x, inner)  45 us
    pallas_call x1, Pallas kernels, plane_pair(): _comm(kernel, outs, scratch, collective_id, specs)  44.7 us
  transfers between devices with their start and end apart: 11, of which 1 were waited for; matrix products, arithmetic and copies ran while one was open for 3% of the time, Pallas kernels for 26%

profile of v6, /device:TPU:13, one launch (start us, length us, event | category | flops | bytes accessed | tf_op | source)
XLA Modules:
  0.0 721.9 jit_solution(18189377864036031699)
XLA Ops:
  0.6 4.1 collective-permute-start
  4.9 0.7 pad_maximum_fusion.3
  5.6 0.7 copy.64.gain_ref
  6.3 66.8 %shard_map.229 = (bf16[2,4,128,2048]{3,2,1,0:T(8,128)(2,1)}, bf16[4,2,4,64,768]{4,3,2,1,0:T(8,128)(2,1)}, bf16[8,4,64,128]{3,2,1,0:T(8,128)(2,1)}, s32[8,4,8,128]{3,2,1,0:T(8,128)}, bf16[4,128,2048]{2,1,0:T(8,128)(2,1)}) custom-call(bf16[128,2048]{1,0:T(8,128)(2,1)} %h_ref.3, bf16[64,2048]{1,0:T(8,128)(2,1)} %wq_ref.3, bf16[64,2048]{1,0:T(8,128)(2,1)} %wk_ref.3, ...), custom_call_target="tpu_custom_call" | custom-call | bytes 100000000 | tf_op jit(solution)/shard_map/pallas_call | solution.py:390
  73.1 1.2 slice.46
  74.3 1.9 fusion.4
  76.3 0.1 copy.76
  76.3 0.6 pad_convert_fusion.gain_ref
  77.0 1.3 pad_maximum_fusion
  78.4 2.6 collective-permute-start.1
  80.9 9.2 %shard_map.230 = (f32[1024,512]{1,0:T(8,128)}, bf16[1024,256]{1,0:T(8,128)(2,1)}, bf16[1024,256]{1,0:T(8,128)(2,1)}, bf16[1024,256]{1,0:T(8,128)(2,1)}, f32[2,8,128]{2,1,0:T(8,128)}) custom-call(bf16[1024,2048]{1,0:T(8,128)(2,1)} %bitcast.105, bf16[2048,768]{1,0:T(8,128)(2,1)} %bitcast.107, f32[8,256]{1,0:T(8,128)} %pad_convert_fusion.gain_ref, ...), custom_call_target="tpu_custom_call" | custom-call | flops 3221225472 | bytes 7340032 | tf_op jit(solution)/shard_map/pallas_call | solution.py:1582
  90.2 44.7 %shard_map.231 = (bf16[4,1024,256]{2,1,0:T(8,128)(2,1)}, bf16[4,1024,256]{2,1,0:T(8,128)(2,1)}, bf16[3,128,2048]{2,1,0:T(8,128)(2,1)}, f32[16,128]{1,0:T(8,128)}, f32[4,8,128]{2,1,0:T(8,128)}) custom-call(bf16[1024,256]{1,0:T(8,128)(2,1)} %get-tuple-element.90.a_ref, bf16[1024,256]{1,0:T(8,128)(2,1)} %get-tuple-element.91.b_ref, bf16[128,2048]{1,0:T(8,128)(2,1)} %x_ref.1, ...), custom_call_target="tpu_custom_call" | custom-call | bytes 100000000 | tf_op jit(solution)/shard_map/pallas_call | solution.py:444
  134.9 0.5 collective-permute-start.4
  135.4 0.4 compare_reduce_fusion
  135.9 1.4 copy.67
  137.3 0.6 stack.38.index_ref
  137.9 1.3 dynamic-slice_maximum_fusion.router_ref
  139.2 2.1 convert_select_fusion
  141.3 0.6 slice.36.q_stat
  142.0 13.2 %shard_map.232 = (f32[1024,256]{1,0:T(8,128)}, f32[1024,256]{1,0:T(8,128)}, bf16[1024,2048]{1,0:T(8,128)(2,1)}) custom-call(s32[6]{0:T(128)} %stack.38.index_ref, s32[5]{0:T(128)} %doc_ref.3, f32[8,128]{1,0:T(8,128)} %slice.36.q_stat, f32[32,128]{1,0:T(8,128)} %bitcast.90, bf16[1024,256]{1,0:T(8,128)(2,1)} %get-tuple-element.95.q_ref, ...), custom_call_target="tpu_custom_call" | custom-call | flops 1073741824 | bytes 4194304 | tf_op jit(solution)/shard_map/pallas_call | solution.py:1512
  155.2 2.2 collective-permute-start.5
  157.5 0.4 convert_reduce_fusion
  157.9 43.1 %shard_map.233 = bf16[128,2048]{1,0:T(8,128)(2,1)} custom-call(bf16[2,4,128,2048]{3,2,1,0:T(8,128)(2,1)} %bitcast.80), custom_call_target="tpu_custom_call" | custom-call | bytes 100000000 | tf_op jit(solution)/shard_map/pallas_call | solution.py:487
  201.0 1.2 copy.70.slot_ref
  202.2 0.3 multiply_reduce_fusion.2
  202.5 0.2 multiply_convert_fusion.x_ref
  202.7 0.5 copy-done.4
  203.3 0.4 fusion.23
  203.6 0.1 copy.71
  203.7 0.2 fusion.6
  203.9 0.1 copy-done.6
  204.1 98.3 %shard_map.234 = (bf16[32,128,2048]{2,1,0:T(8,128)(2,1)}, bf16[8,8,80,2048]{3,2,1,0:T(8,128)(2,1)}, bf16[8,8,80,2048]{3,2,1,0:T(8,128)(2,1)}, f32[8,8,80,128]{3,...) custom-call(bf16[128,2048]{1,0:T(8,128)(2,1)} %copy-done.6, ...), custom_call_target="tpu_custom_call" | custom-call | bytes 100000000 | tf_op jit(solution)/shard_map/pallas_call | solution.py:891
  302.4 64.7 %shard_map.235 = (bf16[8,640,2048]{2,1,0:T(8,128)(2,1)}, bf16[8,640,2048]{2,1,0:T(8,128)(2,1)}, f32[8,3,2048,256]{3,2,1,0:T(8,128)}, f32[8,640,128]{2,1,0:T(8,128)}) custom-call(bf16[8,640,2048]{2,1,0:T(8,128)(2,1)} %bitcast.103, bf16[8,640,2048]{2,1,0:T(8,128)(2,1)} %bitcast.104, f32[8,640,128]{2,1,0:T(8,128)} %bitcast.109, bf16[8,3,2048,256]{3,2,1,0:T(8,128)(2,1)} %w_ref.1), custom_call_target="tpu_custom_call" | custom-call | flops 48318382080 | bytes 159383552 | tf_op jit(solution)/shard_map/pallas_call | solution.py:1757
  367.1 89.3 %shard_map.236 = bf16[128,2176]{1,0:T(8,128)(2,1)} custom-call(s32[8,512,8]{2,1,0:T(8,128)} %bitcast.68, f32[8,8,80,128]{3,2,1,0:T(8,128)} %bitcast.83, bf16[8,8,80,2048]{3,2,1,0:T(8,128)(2,1)} %bitcast.67), custom_call_target="tpu_custom_call" | custom-call | bytes 100000000 | tf_op jit(solution)/shard_map/pallas_call | solution.py:1106
  456.4 1.1 convert_element_type.79
  457.6 0.2 multiply_reduce_fusion.3
  457.7 0.1 multiply_convert_fusion.1
  457.9 0.6 multiply_reduce_fusion
  458.5 0.1 copy-done.5
  458.6 1.9 fusion.22
  460.5 82.2 %shard_map.237 = (bf16[2,4,128,2048]{3,2,1,0:T(8,128)(2,1)}, bf16[4,128,2048]{2,1,0:T(8,128)(2,1)}) custom-call(bf16[128,2048]{1,0:T(8,128)(2,1)} %get-tuple-element.162.r_ref, s32[8,512,8]{2,1,0:T(8,128)} %bitcast.69, bf16[8,8,80,2048]{3,2,1,0:T(8,128)(2,1)} %bitcast.66), custom_call_target="tpu_custom_call" | custom-call | bytes 100000000 | tf_op jit(solution)/shard_map/pallas_call | solution.py:467
  542.7 21.6 %shard_map.238 = (bf16[1024,256]{1,0:T(8,128)(2,1)}, bf16[4096,256]{1,0:T(8,128)(2,1)}, bf16[4096,256]{1,0:T(8,128)(2,1)}, bf16[256,2048]{1,0:T(8,128)(2,1)}, f32[8,128]{1,0:T(8,128)}, /*index=5*/f32[8,512]{1,0:T(8,128)}) custom-call(s32[6]{0:T(128)} %stack.38.index_ref, s32[5]{0:T(128)} %doc_ref.3, f32[8,128]{1,0:T(8,128)} %slice.36.q_stat, ...), custom_call_target="tpu_custom_call" | custom-call | flops 2684354560 | bytes 8388608 | tf_op jit(solution)/shard_map/pallas_call | solution.py:1535
  564.4 0.7 reshape.210
  565.1 1.3 pad_maximum_fusion.2.s_ref
  566.4 45.0 %shard_map.239 = (bf16[1024,256]{1,0:T(8,128)(2,1)}, bf16[1024,256]{1,0:T(8,128)(2,1)}, bf16[128,2048]{1,0:T(8,128)(2,1)}, f32[16,128]{1,0:T(8,128)}) custom-call(bf16[4,1024,256]{2,1,0:T(8,128)(2,1)} %bitcast.84, bf16[4,1024,256]{2,1,0:T(8,128)(2,1)} %bitcast.85, bf16[4,128,2048]{2,1,0:T(8,128)(2,1)} %get-tuple-element.126.x_ref, ...), custom_call_target="tpu_custom_call" | custom-call | bytes 100000000 | tf_op jit(solution)/shard_map/pallas_call | solution.py:554
  611.5 2.8 collective-permute-start.7
  614.3 1.3 collective-permute-start.9
  615.6 13.9 %shard_map.240 = (bf16[2048,768]{1,0:T(8,128)(2,1)}, bf16[1024,2048]{1,0:T(8,128)(2,1)}, f32[8,256]{1,0:T(8,128)}) custom-call(bf16[1024,256]{1,0:T(8,128)(2,1)} %get-tuple-element.123.dq_ref, bf16[1024,256]{1,0:T(8,128)(2,1)} %get-tuple-element.131.dk_ref, bf16[1024,256]{1,0:T(8,128)(2,1)} %get-tuple-element.132.dv_ref, ...), custom_call_target="tpu_custom_call" | custom-call | flops 6442450944 | bytes 14680064 | tf_op jit(solution)/shard_map/pallas_call | solution.py:1648
  629.5 0.7 reshape.216.refs_0_
  630.2 0.7 slice.41
  630.9 0.6 select_maximum_fusion.refs_1_
  631.5 65.8 %shard_map.241 = (bf16[128,2048]{1,0:T(8,128)(2,1)}, bf16[3,64,2048]{2,1,0:T(8,128)(2,1)}, bf16[8,4,64,128]{3,2,1,0:T(8,128)(2,1)}, f32[8,4,24,128]{3,2,1,0:T(8,128)}) custom-call(bf16[2,4,128,2048]{3,2,1,0:T(8,128)(2,1)} %bitcast.81, bf16[4,2,256,768]{3,2,1,0:T(8,128)(2,1)} %bitcast.82, bf16[64,128]{1,0:T(8,128)(2,1)} %reshape.216.refs_0_, ...), custom_call_target="tpu_custom_call" | custom-call | bytes 100000000 | tf_op jit(solution)/shard_map/pallas_call | solution.py:606
  697.3 0.8 dynamic-slice_bitcast_fusion.4
  698.2 0.5 slice_bitcast_fusion
  698.8 0.1 add_convert_fusion
  698.9 3.2 collective-permute-start.10
  702.1 1.0 slice_reduce_fusion
  703.1 1.6 reshape.223
  704.8 0.6 dynamic_slice.43
  705.3 2.6 fusion
  707.9 6.7 collective-permute-done.10.do_ref
  714.6 0.7 copy-done.12
  715.3 5.1 shard_map.242
  720.4 1.4 reduce.1
  (52 shorter events, 0.5 us)
Async XLA Ops:
  0.6 77.6 %collective-permute-start = (bf16[64,2048]{1,0:T(8,128)(2,1)}, bf16[64,2048]{1,0:T(8,128)(2,1)S(1)}, u32[]{:S(2)}, u32[]{:S(2)}) collective-permute-start(bf16[64,2048]{1,0:T(8,128)(2,1)} %param.20), channel_id=1, source_target_pairs={{0,0},{1,8},{2,16},{3,24},{4,4},{5,12},{6,20},{7,28},{8,9},{9,17},... | collective-permute-start | bytes 786440 | tf_op jit(solution)/shard_map/ppermute | solution.py:1142
  78.3 11.9 %copy-start.7 = (bf16[64,2048]{1,0:T(8,128)(2,1)}, bf16[64,2048]{1,0:T(8,128)(2,1)S(1)}, u32[]{:S(2)}) copy-start(bf16[64,2048]{1,0:T(8,128)(2,1)S(1)} %collective-permute-done.w0) | copy-start | bytes 786436
  78.3 56.6 %collective-permute-start.3 = (bf16[64,2048]{1,0:T(8,128)(2,1)S(1)}, bf16[64,2048]{1,0:T(8,128)(2,1)S(1)}, u32[]{:S(2)}, u32[]{:S(2)}) collective-permute-start(bf16[64,2048]{1,0:T(8,128)(2,1)S(1)} %collective-permute-done.w0), channel_id=1, source_target_pairs={{0,24},{1,25},{2,26},{3,27},{4,28},{5,29},{6,30},{7,31},{8,16},{9,... | collective-permute-start | bytes 786440 | tf_op jit(solution)/shard_map/ppermute | solution.py:1142
  78.3 56.6 %collective-permute-start.2 = (bf16[64,2048]{1,0:T(8,128)(2,1)S(1)}, bf16[64,2048]{1,0:T(8,128)(2,1)S(1)}, u32[]{:S(2)}, u32[]{:S(2)}) collective-permute-start(bf16[64,2048]{1,0:T(8,128)(2,1)S(1)} %collective-permute-done.w0), channel_id=1, source_target_pairs={{0,16},{1,17},{2,18},{3,19},{4,20},{5,21},{6,22},{7,23},{8,24},{9,... | collective-permute-start | bytes 786440 | tf_op jit(solution)/shard_map/ppermute | solution.py:1142
  78.4 56.5 %collective-permute-start.1 = (bf16[64,2048]{1,0:T(8,128)(2,1)S(1)}, bf16[64,2048]{1,0:T(8,128)(2,1)S(1)}, u32[]{:S(2)}, u32[]{:S(2)}) collective-permute-start(bf16[64,2048]{1,0:T(8,128)(2,1)S(1)} %collective-permute-done.w0), channel_id=1, source_target_pairs={{0,8},{1,9},{2,10},{3,11},{4,12},{5,13},{6,14},{7,15},{8,0},{9,1},... | collective-permute-start | bytes 786440 | tf_op jit(solution)/shard_map/ppermute | solution.py:1142
  80.9 54.5 %copy-start.13 = (s32[8,4,8,128]{3,2,1,0:T(8,128)S(1)}, s32[8,4,8,128]{3,2,1,0:T(8,128)}, u32[]{:S(2)}) copy-start(s32[8,4,8,128]{3,2,1,0:T(8,128)} %get-tuple-element.106) | copy-start | bytes 393220
  90.1 47.7 %copy-start.3 = (bf16[8,4,64,128]{3,2,1,0:T(8,128)(2,1)S(1)}, bf16[8,4,64,128]{3,2,1,0:T(8,128)(2,1)}, u32[]{:S(2)}) copy-start(bf16[8,4,64,128]{3,2,1,0:T(8,128)(2,1)} %get-tuple-element.89) | copy-start | bytes 1572868
  134.8 6.4 copy-start.8
  134.9 6.4 copy-start.9
  134.9 4.3 copy-start.10
  134.9 20.3 %collective-permute-start.4 = (bf16[3,128,2048]{2,1,0:T(8,128)(2,1)}, bf16[3,128,2048]{2,1,0:T(8,128)(2,1)}, u32[]{:S(2)}, u32[]{:S(2)}) collective-permute-start(bf16[3,128,2048]{2,1,0:T(8,128)(2,1)} %get-tuple-element.110.g0), channel_id=1, source_target_pairs={{0,8},{1,9},{2,10},{3,11},{4,20},{5,21},{6,22},{7,23},{8,0},{9,1},... | collective-permute-start | bytes 4718600 | tf_op jit(solution)/shard_map/ppermute | solution.py:1142
  139.2 2.1 copy-start.14
  141.3 59.7 %copy-start = (s32[8,8,512]{1,2,0:T(8,128)}, s32[8,8,512]{1,2,0:T(8,128)S(1)}, u32[]{:S(2)}) copy-start(s32[8,8,512]{1,2,0:T(8,128)S(1)} %convert_select_fusion) | copy-start | bytes 393220
  155.2 48.7 %collective-permute-start.5 = (bf16[3,128,2048]{2,1,0:T(8,128)(2,1)}, bf16[3,128,2048]{2,1,0:T(8,128)(2,1)}, u32[]{:S(2)}, u32[]{:S(2)}) collective-permute-start(bf16[3,128,2048]{2,1,0:T(8,128)(2,1)} %get-tuple-element.110.g0), channel_id=1, source_target_pairs={{0,16},{1,17},{2,18},{3,19},{4,12},{5,13},{6,14},{7,15},{8,24},{9,... | collective-permute-start | bytes 4718600 | tf_op jit(solution)/shard_map/ppermute | solution.py:1142
  157.4 46.5 %collective-permute-start.6 = (bf16[3,128,2048]{2,1,0:T(8,128)(2,1)}, bf16[3,128,2048]{2,1,0:T(8,128)(2,1)}, u32[]{:S(2)}, u32[]{:S(2)}) collective-permute-start(bf16[3,128,2048]{2,1,0:T(8,128)(2,1)} %collective-permute-done.4.g1), channel_id=1, source_target_pairs={{0,16},{1,17},{2,18},{3,19},{4,12},{5,13},{6,14},{7,15},{8,24},{9,... | collective-permute-start | bytes 4718600 | tf_op jit(solution)/shard_map/ppermute | solution.py:1142
  201.0 1.3 copy-start.1
  201.0 1.2 copy-start.2
  202.2 1.0 copy-start.4
  203.3 0.8 copy-start.6
  457.5 1.0 copy-start.5
  566.4 45.0 %copy-start.11 = (bf16[256,2048]{1,0:T(8,128)(2,1)S(1)}, bf16[256,2048]{1,0:T(8,128)(2,1)}, u32[]{:S(2)}) copy-start(bf16[256,2048]{1,0:T(8,128)(2,1)} %get-tuple-element.130) | copy-start | bytes 3145732
  611.5 20.0 %collective-permute-start.7 = (bf16[64,2048]{1,0:T(8,128)(2,1)S(1)}, bf16[64,2048]{1,0:T(8,128)(2,1)S(1)}, u32[]{:S(2)}, u32[]{:S(2)}) collective-permute-start(bf16[64,2048]{1,0:T(8,128)(2,1)S(1)} %get-tuple-element.136), channel_id=1, source_target_pairs={{0,8},{1,9},{2,10},{3,11},{4,12},{5,13},{6,14},{7,15},{8,0},{9,1},... | collective-permute-start | bytes 786440 | tf_op jit(solution)/shard_map/ppermute | solution.py:1142
  614.3 17.2 %collective-permute-start.8 = (bf16[64,2048]{1,0:T(8,128)(2,1)S(1)}, bf16[64,2048]{1,0:T(8,128)(2,1)S(1)}, u32[]{:S(2)}, u32[]{:S(2)}) collective-permute-start(bf16[64,2048]{1,0:T(8,128)(2,1)S(1)} %get-tuple-element.137), channel_id=1, source_target_pairs={{0,16},{1,17},{2,18},{3,19},{4,20},{5,21},{6,22},{7,23},{8,24},{9,... | collective-permute-start | bytes 786440 | tf_op jit(solution)/shard_map/ppermute | solution.py:1142
  614.3 17.2 %collective-permute-start.9 = (bf16[64,2048]{1,0:T(8,128)(2,1)S(1)}, bf16[64,2048]{1,0:T(8,128)(2,1)S(1)}, u32[]{:S(2)}, u32[]{:S(2)}) collective-permute-start(bf16[64,2048]{1,0:T(8,128)(2,1)S(1)} %get-tuple-element.138), channel_id=1, source_target_pairs={{0,24},{1,25},{2,26},{3,27},{4,28},{5,29},{6,30},{7,31},{8,16},{9,... | collective-permute-start | bytes 786440 | tf_op jit(solution)/shard_map/ppermute | solution.py:1142
  698.9 15.7 %collective-permute-start.10 = (bf16[64,2048]{1,0:T(8,128)(2,1)S(1)}, bf16[64,2048]{1,0:T(8,128)(2,1)S(1)}, u32[]{:S(2)}, u32[]{:S(2)}) collective-permute-start(bf16[64,2048]{1,0:T(8,128)(2,1)S(1)} %add_convert_fusion), channel_id=1, source_target_pairs={{0,0},{8,1},{16,2},{24,3},{4,4},{12,5},{20,6},{28,7},{9,8},{17,9},... | collective-permute-start | bytes 786440 | tf_op jit(solution)/shard_map/ppermute | solution.py:1142
  714.6 0.7 copy-start.12

commit v7 on v6

--- a/solution.py
+++ b/solution.py
@@ -276,7 +276,7 @@
 ENTER_ORDER = (0, 2, 3, 1, 3, 3, 0, 2, 1, 0, 2, 0, 2)
 KV_ORDER = (2, 0, 1, 0, 0, 1, 2, 1, 0, 1)
 PAIR_ORDER = (1, 0, 2, 1, 0, 0, 1, 2, 1, 0)
-LEAVE_ORDER = (0, 1, 2, 1, 2, 1, 0, 0, 1, 0, 1, 1)
+LEAVE_ORDER = (0, 1, 2, 1, 2, 1, 0, 0, 1, 3, 3, 0, 1, 3, 3, 1)
 LINE_SEMS = [DMA((2, 4)), DMA((4,)), DMA((4,)), DMA((4,)), DMA]
 PLANE_SEMS = [DMA((2, 3)), DMA((2, 3)), DMA((2,))]
 PLANE_SUM_SEMS = [DMA((2, 2)), DMA((2, 2)), DMA((2, 2)), DMA((2,)), DMA((2,))]
@@ -448,22 +448,27 @@
     T, D = rows.shape
     EL, _, slots, _ = out_rows.shape
 
-    def kernel(r_ref, slot_ref, rows_ref, r_out, x_out, *refs):
+    def kernel(r_ref, slot_ref, rows_ref, r_out, x_out, part_out, stage, stage_sem, *refs):
         u, z = lax.axis_index("uly"), lax.axis_index("blk")
         _greet(u, z, (1, 2, 4), line=True)
-        order = _line_order(z)
+        order = _line_order(z)[1:]
 
         def keep(i, part):
-            x_out[order[i]] = part[...]
-
+            x_out[(order[i] - z + 3) % 4] = part[...]
+
+        extra = (stage, part_out, stage_sem)
         _run(
             _line_part(u, z, r_ref, lambda c, level: r_out.at[c, level], refs[-5:]),
-            _spread_part(u, z, slot_ref, rows_ref, None, order, refs[:-5], keep),
+            _spread_part(u, z, slot_ref, rows_ref, None, order, refs[:-5], keep, extra=extra),
         )
 
-    outs = [jax.ShapeDtypeStruct((2, 4, T, D), BF16), jax.ShapeDtypeStruct((4, T, D), BF16)]
-    specs = ([IN_VMEM, IN_VMEM, ANY_SPACE], [ANY_SPACE, IN_VMEM])
-    scratch = _spread_scratch(T, D, (EL, slots, D)) + LINE_SEMS
+    outs = [
+        jax.ShapeDtypeStruct((2, 4, T, D), BF16),
+        jax.ShapeDtypeStruct((3, T, D), BF16),
+        jax.ShapeDtypeStruct((2, 4 * T, D), BF16),
+    ]
+    specs = ([IN_VMEM, IN_VMEM, ANY_SPACE], [ANY_SPACE, IN_VMEM, ANY_SPACE])
+    scratch = [pltpu.VMEM((2, 4 * T, D), BF16), DMA((2,))] + _spread_scratch(T, D, (EL, slots, D), 3) + LINE_SEMS
     return _comm(kernel, outs, scratch, collective_id, specs)(rows, slot, out_rows)
 
 
@@ -517,9 +522,12 @@
             v_out[...] = work[1, 0]
 
         def line():
-            copies = [pltpu.make_async_copy(x_ref.at[order[i]], x_work.at[i], load.at[i]) for i in range(4)]
+            copies = [
+                pltpu.make_async_copy(x_ref.at[(order[i] - z + 3) % 4], x_work.at[i], load.at[i]) for i in range(3)
+            ]
             for copy in copies:
                 copy.start()
+            x_work[3] = jnp.zeros((T, D), BF16)
             for copy in copies:
                 copy.wait()
             for i in range(4):
@@ -554,16 +562,21 @@
     return _comm(kernel, outs, scratch, collective_id, specs)(dk, dv, x, inner)
 
 
-def leave(x, weights, smalls, collective_id):
+def leave(x, weights, smalls, ready, collective_id):
     n = len(smalls)
     T, D = x.shape[2:]
     rows, W = weights.shape[2:]
     R, C = rows // 4, W // 3
 
-    def kernel(x_ref, w_ref, *refs):
-        small_in, (o_ref, w_out), small_out = refs[:n], refs[n : n + 2], refs[n + 2 : 2 * n + 2]
-        work, c_buf, z_buf, w_work, wp_buf, wq_buf = refs[2 * n + 2 : 2 * n + 8]
-        sems = refs[2 * n + 8 :]
+    def kernel(x_ref, w_ref, ready_ref, *refs):
+        small_in, (o_ref, w_out, own_ref), small_out = refs[:n], refs[n : n + 3], refs[n + 3 : 2 * n + 3]
+        work, c_buf, z_buf, w_work, wp_buf, wq_buf = refs[2 * n + 3 : 2 * n + 9]
+        tree = refs[2 * n + 9 : 2 * n + 20]
+        sems = refs[2 * n + 20 :]
+
+        def keep(part):
+            own_ref[...] = part[...]
+
         u, z = lax.axis_index("uly"), lax.axis_index("blk")
         here, core, chip = (u, z), u % 2, u // 2
         column = _column_peers(u, z)
@@ -591,6 +604,7 @@
             _plane_sum_part(u, z, lambda h, v: w_ref.at[v // 2, h], w_work, (wp_buf, wq_buf), sems[5:10], rows, deal),
             _line_sum_part(u, z, lambda c, level: x_ref.at[c, level], work, (c_buf, z_buf), sems[:5], T, finish),
             _small_part(u, z, small_in, small_out, sems[12:]),
+            _tree_part(u, z, ready_ref, tree, T, keep),
             order=LEAVE_ORDER,
         )
         for i, (to, c, k) in enumerate(column):
@@ -598,18 +612,18 @@
                 _expect(slot(j, 2 * (z ^ k) + (core ^ c)), t_recv.at[i, j], here)
                 _sent(cut(j, core ^ c, z ^ k), t_send.at[i, j], here)
 
-    outs = [jax.ShapeDtypeStruct((T, D), BF16), jax.ShapeDtypeStruct((3, R, 8 * C), BF16)]
+    outs = [jax.ShapeDtypeStruct((T, D), BF16), jax.ShapeDtypeStruct((3, R, 8 * C), BF16), jax.ShapeDtypeStruct((T, D), BF16)]
     outs += [jax.ShapeDtypeStruct((8, 4) + x.shape, x.dtype) for x in smalls]
-    scratch = _line_sum_scratch(T, D) + _plane_sum_scratch(rows, W) + LINE_SUM_SEMS + PLANE_SUM_SEMS
+    scratch = _line_sum_scratch(T, D) + _plane_sum_scratch(rows, W) + _tree_scratch(T, D) + LINE_SUM_SEMS + PLANE_SUM_SEMS
     scratch += [DMA((7, 3)), DMA((7, 3))] + _small_sems(n)
-    specs = ([ANY_SPACE] * 2 + [IN_VMEM] * n, [IN_VMEM] * 2 + [ANY_SPACE] * n)
-    return _comm(kernel, outs, scratch, collective_id, specs)(x, weights, *smalls)
+    specs = ([ANY_SPACE] * 3 + [IN_VMEM] * n, [IN_VMEM] * 3 + [ANY_SPACE] * n)
+    return _comm(kernel, outs, scratch, collective_id, specs)(x, weights, ready, *smalls)
 
 
 def _finish_kernel(
-    h_ref, r_ref, rg_ref, first_ref, sum_ref, wq_ref, wk_ref, wv_ref, dw_ref, do_ref, gain_ref, out_ref, hg_ref, ag_ref, *dws
+    h_ref, r_ref, rg_ref, first_ref, sum_ref, own_ref, wq_ref, wk_ref, wv_ref, dw_ref, do_ref, gain_ref, out_ref, hg_ref, ag_ref, *dws
 ):
-    out_ref[...] = (r_ref[...] + sum_ref[...].astype(F32)).astype(BF16)
+    out_ref[...] = (r_ref[...] + (sum_ref[...].astype(F32) + own_ref[...].astype(F32))).astype(BF16)
     hidden, weighted = h_ref[...].astype(F32), first_ref[...].astype(F32)
     scale = norm_scale(hidden)
     mean = jnp.mean(weighted * hidden, axis=-1, keepdims=True)
@@ -624,7 +638,7 @@
     dws[3][...] = do_ref[...].astype(F32)
 
 
-def finish(hidden, residual, residual_grad, first_weighted, out_sum, weights, weight_sum, out_weight_grad, gains):
+def finish(hidden, residual, residual_grad, first_weighted, out_sum, out_own, weights, weight_sum, out_weight_grad, gains):
     T, D = hidden.shape
     R = gains.shape[0]
     steps = 4 if R % 64 == 0 else 1
@@ -642,13 +656,13 @@
         ]
         + [jax.ShapeDtypeStruct((R, D), F32)] * 4,
         grid=(steps,),
-        in_specs=[tokens] * 5
+        in_specs=[tokens] * 6
         + [dense] * 3
         + [pl.BlockSpec((3, R // steps, D), lambda i: (0, i, 0)), dense, rows(R, 4)],
         out_specs=[tokens, tokens, rows(R, 1)] + [dense] * 4,
         compiler_params=pltpu.CompilerParams(vmem_limit_bytes=VMEM_BYTES),
         cost_estimate=pl.CostEstimate(flops=20 * T * D, bytes_accessed=24 * T * D, transcendentals=0),
-    )(hidden, residual, residual_grad, first_weighted, out_sum, *weights, weight_sum, out_weight_grad, gains)
+    )(hidden, residual, residual_grad, first_weighted, out_sum, out_own, *weights, weight_sum, out_weight_grad, gains)
 
 
 class _Jobs:
@@ -892,7 +906,7 @@
     return out.reshape(32 * T, D), xr, gr, gates
 
 
-def _tree_sum_steps(u, z, own, bufs, sems, T):
+def _tree_sum_steps(u, z, own, bufs, sems, T, count):
     c_buf, p_buf, q_buf = bufs
     c_send, c_recv, p_send, p_recv, q_send, q_recv = sems
     here = (u, z)
@@ -930,7 +944,7 @@
             _accumulate(own(i, 0).at[halves[h]], q_buf.at[i, h], half)
 
     def finish():
-        for i in range(4):
+        for i in range(count):
             for k in range(4):
                 _sent(c_buf.at[i, k], c_send.at[i, k], here)
             for h in range(2):
@@ -966,7 +980,51 @@
             _send(part, z_buf.at[1, level], z_send.at[i], z_recv.at[1, level], (u, z - 1))
 
 
-def _spread_part(u, z, slot_ref, source, gg_ref, order, refs, level_done, later=lambda i: None):
+def _place(chip, k, T):
+    return pl.ds(pl.multiple_of((chip ^ (CHIPS[k] // 2)) * T, T), T)
+
+
+def _tree_part(u, z, ready, refs, T, then_do):
+    work, c_buf, p_buf, q_buf, sem = refs[:5]
+    core, chip = u % 2, u // 2
+    to_sibling, add_core, add_far, add_near, add_then, finish = _tree_sum_steps(
+        u, z, lambda i, k: work.at[_place(chip, k, T)], (c_buf, p_buf, q_buf), refs[5:], T, 1
+    )
+    for k in (3, 2, 1, 0):
+        to_sibling(0, k, ready.at[1 - core, _place(chip, k, T)])
+    copy = pltpu.make_async_copy(ready.at[core], work, sem)
+    copy.start()
+    yield
+    copy.wait()
+    add_core(0)
+    yield
+    add_far(0)
+    yield
+    add_near(0)
+    add_then(0)
+    then_do(work.at[_place(chip, 0, T)])
+    yield
+    finish()
+
+
+def _tree_scratch(T, D):
+    half = T // 2
+    return [
+        pltpu.VMEM((4 * T, D), BF16),
+        pltpu.VMEM((1, 4, T, D), BF16),
+        pltpu.VMEM((1, 2, 2, half, D), BF16),
+        pltpu.VMEM((1, 2, half, D), BF16),
+        DMA,
+        DMA((1, 4)),
+        DMA((1, 4)),
+        DMA((1, 2, 2)),
+        DMA((1, 2, 2)),
+        DMA((1, 2)),
+        DMA((1, 2)),
+    ]
+
+
+def _spread_part(u, z, slot_ref, source, gg_ref, order, refs, level_done, later=lambda i: None, extra=None):
     work, c_buf, p_buf, q_buf, side, in_buf, in_sem = refs[:7]
     core, chip = u % 2, u // 2
     other = 1 - core
@@ -974,15 +1032,16 @@
     slots, D = source.shape[2:]
     total = experts * slots
     T = group // 4
+    count = len(order)
 
     def place(k):
-        return pl.ds(pl.multiple_of((chip ^ (CHIPS[k] // 2)) * T, T), T)
+        return _place(chip, k, T)
 
     def own(i, k):
         return work.at[i, place(k)]
 
     to_sibling, add_core, add_far, add_near, add_then, finish = _tree_sum_steps(
-        u, z, own, (c_buf, p_buf, q_buf), refs[7:], T
+        u, z, own, (c_buf, p_buf, q_buf), refs[7:], T, count
     )
     lane = lax.broadcasted_iota(jnp.int32, (experts, total), 1)
     which = lax.broadcasted_iota(jnp.int32, (experts, total), 0)
@@ -993,16 +1052,20 @@
 
     def load(n, job, start):
         i, c = job
-        copy = pltpu.make_async_copy(source.at[:, 2 * order[i] + c], in_buf.at[n % 2], in_sem.at[n % 2])
+        level = z if i is None else order[i]
+        copy = pltpu.make_async_copy(source.at[:, 2 * level + c], in_buf.at[n % 2], in_sem.at[n % 2])
         copy.start() if start else copy.wait()
 
     def compute(n, job):
         i, c = job
-        at = 2 * order[i] + c
+        at = 2 * (z if i is None else order[i]) + c
         mine = dot(slot_ref[at].astype(BF16), choose)
         pick = jnp.where(mine == offset, 1.0, 0.0).astype(BF16)
         rows_in = in_buf.at[n % 2]
-        target = work.at[i] if c is core else side.at[i]
+        if i is None:
+            target = extra[0].at[c]
+        else:
+            target = work.at[i] if c is core else side.at[i]
         if gg_ref is not None:
             grads = [jnp.where(column == u * experts + e, gg_ref[e, at], 0.0).astype(BF16) for e in range(experts)]
             target[:, pl.ds(D, 128)] = dot(pick, jnp.concatenate(grads, axis=0)).astype(BF16)
@@ -1014,67 +1077,59 @@
             return 0
 
         lax.fori_loop(0, D // SPREAD_WIDTH, step, 0)
-        if c is not core:
+        if i is None:
+            extra_copy(c).start()
+        elif c is not core:
             for k in (3, 2, 1, 0):
                 to_sibling(i, k, side.at[i, place(k)])
+
+    def extra_copy(c):
+        return pltpu.make_async_copy(extra[0].at[c], extra[1].at[c], extra[2].at[c])
 
     def end(i):
         add_then(i)
         level_done(i, own(i, 0))
 
     jobs = _Jobs(load, compute)
-    for i in range(4):
+    for i in range(count):
         jobs.add((i, other), (i, core))
-    jobs.run(2)
-    add_core(0)
-    yield
-    jobs.run(2)
-    add_far(0)
-    add_core(1)
-    yield
-    add_near(0)
-    jobs.run(2)
-    add_far(1)
-    add_core(2)
-    yield
-    end(0)
-    later(0)
-    add_near(1)
-    jobs.run(2)
-    add_far(2)
-    add_core(3)
-    yield
-    end(1)
-    later(1)
-    add_near(2)
-    add_far(3)
-    yield
-    end(2)
-    later(2)
-    add_near(3)
-    yield
-    end(3)
-    later(3)
+    if extra is not None:
+        jobs.add((None, 0), (None, 1))
+    for step in range(count + 3):
+        if step >= 3:
+            end(step - 3)
+            later(step - 3)
+        if 0 <= step - 2 < count:
+            add_near(step - 2)
+        jobs.run(2 if step < count else 1)
+        if 0 <= step - 1 < count:
+            add_far(step - 1)
+        if step < count:
+            add_core(step)
+        yield
+    if extra is not None:
+        extra_copy(0).wait()
+        extra_copy(1).wait()
     yield
     finish()
 
 
-def _spread_scratch(T, W, rows_shape):
+def _spread_scratch(T, W, rows_shape, count=4):
     half = T // 2
     return [
-        pltpu.VMEM((4, 4 * T, W), BF16),
-        pltpu.VMEM((4, 4, T, W), BF16),
-        pltpu.VMEM((4, 2, 2, half, W), BF16),
-        pltpu.VMEM((4, 2, half, W), BF16),
-        pltpu.VMEM((4, 4 * T, W), BF16),
+        pltpu.VMEM((count, 4 * T, W), BF16),
+        pltpu.VMEM((count, 4, T, W), BF16),
+        pltpu.VMEM((count, 2, 2, half, W), BF16),
+        pltpu.VMEM((count, 2, half, W), BF16),
+        pltpu.VMEM((count, 4 * T, W), BF16),
         pltpu.VMEM((2,) + rows_shape, BF16),
         DMA((2,)),
-        DMA((4, 4)),
-        DMA((4, 4)),
-        DMA((4, 2, 2)),
-        DMA((4, 2, 2)),
-        DMA((4, 2)),
-        DMA((4, 2)),
+        DMA((count, 4)),
+        DMA((count, 4)),
+        DMA((count, 2, 2)),
+        DMA((count, 2, 2)),
+        DMA((count, 2)),
+        DMA((count, 2)),
     ]
 
 
@@ -1177,7 +1232,7 @@
         return second_all, spread_scatter(self.slot, gate_grads.reshape(cut), entry_rows.reshape(cut), 8)
 
     def rows_to_heads(self, x):
-        rows, self.out_line = column_gather(x, self.slot, self.out_rows, 6)
+        rows, self.out_line, self.out_here = column_gather(x, self.slot, self.out_rows, 6)
         return rows.reshape(self.L, self.D), self.expert_grads
 
     def sequence_sums(self, dk, dv, out_part, q_inner, k_inner):
@@ -1199,10 +1254,11 @@
         wide = self.D // 128
         used = thin.shape[0]
         thin = jnp.pad(thin, ((0, -used % 8), (0, 0)))
-        first, weights, logit_all, thin = leave(
+        first, weights, self.out_own, logit_all, thin = leave(
             first_part.reshape(2, 4, T, self.D),
             weight_part.reshape(4, 2, 4 * R, 3 * self.C),
             [logit_grad.reshape(T // 2, 2 * EXPERTS), thin],
+            self.out_here,
             11,
         )
         ffn = lax.dynamic_slice_in_dim(
@@ -1294,6 +1350,7 @@
             group,
         )
         self.out_sum = self.scatter_wide(out_part)
+        self.out_own = jnp.zeros_like(self.out_sum)
         return second_all, self.scatter_wide(entry_part)
 
     def rows_to_heads(self, x):
@@ -1916,7 +1973,7 @@
     own_columns = lax.dynamic_slice_in_dim(second_all, (u * Z + z) * RW, RW, 1)
     router_grad = dot(own_columns, logit_grad_all, FIRST_DIM)
     output, hidden_grad, attn_gain_grad, *weight_grads = finish(
-        hidden_in, residual, residual_grad, first_weighted, out_sum, own_weights, weight_sum, out_weight_grad, gains
+        hidden_in, residual, residual_grad, first_weighted, out_sum, move.out_own, own_weights, weight_sum, out_weight_grad, gains
     )
     return (
         output,

time: 732 us -> 715 us (0.977)
  Pallas kernels: 663 us -> 646 us
    pallas_call x1, Pallas kernels: 82.2 us -> 65 us  [column_gather(): _comm(kernel, outs, scratch, collective_id, specs)(rows, slot, out_rows)]
  transfers between devices with their start and end apart: 11 -> 11, of which waited for: 1 -> 1; matrix products, arithmetic and copies ran while one was open for 3% -> 3% of each run, Pallas kernels for 26% -> 27%
where the time goes in v7:
time: 715 us; the launch traced here: 705 us
  Pallas kernels  646 us (90%)
  starting transfers between devices  16.8 us (2%)
  other arithmetic  15.2 us (2%)
  local copies, waits for them, and re-layouts  13.4 us (2%)
    pallas_call x1, Pallas kernels, gather_pick(): _comm(kernel, outs, scratch, collective_id, specs)  98.3 us
    pallas_call x1, Pallas kernels, spread_scatter(): _comm(kernel, out, scratch, collective_id, specs)  89.3 us
    pallas_call x1, Pallas kernels, enter(): _comm(kernel, outs, scratch, collective_id, specs)  66.8 us
    pallas_call x1, Pallas kernels, leave(): _comm(kernel, outs, scratch, collective_id, specs)  66.2 us
    pallas_call x1, Pallas kernels, column_gather(): _comm(kernel, outs, scratch, collective_id, specs)(rows, slot, out_rows)  65 us
    pallas_call x1, Pallas kernels, run_experts(): pl.pallas_call(_expert_kernel, out_shape=[jax.ShapeDtypeStruct(x.shape, B...  64.7 us
    pallas_call x1, Pallas kernels, key_value_sums(): return _comm(kernel, outs, scratch, collective_id, specs)(dk, dv, x, inner)  45 us
    pallas_call x1, Pallas kernels, plane_pair(): _comm(kernel, outs, scratch, collective_id, specs)  44.7 us
  transfers between devices with their start and end apart: 11, of which 1 were waited for; matrix products, arithmetic and copies ran while one was open for 3% of the time, Pallas kernels for 27%

profile of v7, /device:TPU:13, one launch (start us, length us, event | category | flops | bytes accessed | tf_op | source)
XLA Modules:
  0.0 705.2 jit_solution(13532299416472490119)
XLA Ops:
  0.6 4.1 collective-permute-start
  4.9 0.7 pad_maximum_fusion.3
  5.6 0.7 copy.64.gain_ref
  6.3 66.8 %shard_map.229 = (bf16[2,4,128,2048]{3,2,1,0:T(8,128)(2,1)}, bf16[4,2,4,64,768]{4,3,2,1,0:T(8,128)(2,1)}, bf16[8,4,64,128]{3,2,1,0:T(8,128)(2,1)}, s32[8,4,8,128]{3,2,1,0:T(8,128)}, bf16[4,128,2048]{2,1,0:T(8,128)(2,1)}) custom-call(bf16[128,2048]{1,0:T(8,128)(2,1)} %h_ref.3, bf16[64,2048]{1,0:T(8,128)(2,1)} %wq_ref.3, bf16[64,2048]{1,0:T(8,128)(2,1)} %wk_ref.3, ...), custom_call_target="tpu_custom_call" | custom-call | bytes 100000000 | tf_op jit(solution)/shard_map/pallas_call | solution.py:390
  73.1 1.2 slice.46
  74.3 1.9 fusion.4
  76.3 0.1 copy.76
  76.3 0.6 pad_convert_fusion.gain_ref
  77.0 1.3 pad_maximum_fusion
  78.4 2.6 collective-permute-start.1
  80.9 9.2 %shard_map.230 = (f32[1024,512]{1,0:T(8,128)}, bf16[1024,256]{1,0:T(8,128)(2,1)}, bf16[1024,256]{1,0:T(8,128)(2,1)}, bf16[1024,256]{1,0:T(8,128)(2,1)}, f32[2,8,128]{2,1,0:T(8,128)}) custom-call(bf16[1024,2048]{1,0:T(8,128)(2,1)} %bitcast.105, bf16[2048,768]{1,0:T(8,128)(2,1)} %bitcast.107, f32[8,256]{1,0:T(8,128)} %pad_convert_fusion.gain_ref, ...), custom_call_target="tpu_custom_call" | custom-call | flops 3221225472 | bytes 7340032 | tf_op jit(solution)/shard_map/pallas_call | solution.py:1639
  90.2 44.7 %shard_map.231 = (bf16[4,1024,256]{2,1,0:T(8,128)(2,1)}, bf16[4,1024,256]{2,1,0:T(8,128)(2,1)}, bf16[3,128,2048]{2,1,0:T(8,128)(2,1)}, f32[16,128]{1,0:T(8,128)}, f32[4,8,128]{2,1,0:T(8,128)}) custom-call(bf16[1024,256]{1,0:T(8,128)(2,1)} %get-tuple-element.92.a_ref, bf16[1024,256]{1,0:T(8,128)(2,1)} %get-tuple-element.93.b_ref, bf16[128,2048]{1,0:T(8,128)(2,1)} %x_ref.1, ...), custom_call_target="tpu_custom_call" | custom-call | bytes 100000000 | tf_op jit(solution)/shard_map/pallas_call | solution.py:444
  134.9 0.5 collective-permute-start.4
  135.4 0.4 compare_reduce_fusion
  135.9 1.4 copy.67
  137.3 0.6 stack.38.index_ref
  137.9 1.3 dynamic-slice_maximum_fusion.router_ref
  139.2 2.1 convert_select_fusion
  141.3 0.6 slice.36.q_stat
  142.0 13.2 %shard_map.232 = (f32[1024,256]{1,0:T(8,128)}, f32[1024,256]{1,0:T(8,128)}, bf16[1024,2048]{1,0:T(8,128)(2,1)}) custom-call(s32[6]{0:T(128)} %stack.38.index_ref, s32[5]{0:T(128)} %doc_ref.3, f32[8,128]{1,0:T(8,128)} %slice.36.q_stat, f32[32,128]{1,0:T(8,128)} %bitcast.90, bf16[1024,256]{1,0:T(8,128)(2,1)} %get-tuple-element.97.q_ref, ...), custom_call_target="tpu_custom_call" | custom-call | flops 1073741824 | bytes 4194304 | tf_op jit(solution)/shard_map/pallas_call | solution.py:1569
  155.2 2.2 collective-permute-start.5
  157.5 0.4 convert_reduce_fusion
  157.9 43.1 %shard_map.233 = bf16[128,2048]{1,0:T(8,128)(2,1)} custom-call(bf16[2,4,128,2048]{3,2,1,0:T(8,128)(2,1)} %bitcast.80), custom_call_target="tpu_custom_call" | custom-call | bytes 100000000 | tf_op jit(solution)/shard_map/pallas_call | solution.py:492
  201.0 1.2 copy.70.slot_ref
  202.2 0.3 multiply_reduce_fusion.2
  202.5 0.2 multiply_convert_fusion.x_ref
  202.7 0.5 copy-done.4
  203.3 0.4 fusion.23
  203.6 0.1 copy.71
  203.7 0.2 fusion.6
  203.9 0.1 copy-done.6
  204.1 98.3 %shard_map.234 = (bf16[32,128,2048]{2,1,0:T(8,128)(2,1)}, bf16[8,8,80,2048]{3,2,1,0:T(8,128)(2,1)}, bf16[8,8,80,2048]{3,2,1,0:T(8,128)(2,1)}, f32[8,8,80,128]{3,...) custom-call(bf16[128,2048]{1,0:T(8,128)(2,1)} %copy-done.6, ...), custom_call_target="tpu_custom_call" | custom-call | bytes 100000000 | tf_op jit(solution)/shard_map/pallas_call | solution.py:905
  302.4 64.7 %shard_map.235 = (bf16[8,640,2048]{2,1,0:T(8,128)(2,1)}, bf16[8,640,2048]{2,1,0:T(8,128)(2,1)}, f32[8,3,2048,256]{3,2,1,0:T(8,128)}, f32[8,640,128]{2,1,0:T(8,128)}) custom-call(bf16[8,640,2048]{2,1,0:T(8,128)(2,1)} %bitcast.103, bf16[8,640,2048]{2,1,0:T(8,128)(2,1)} %bitcast.104, f32[8,640,128]{2,1,0:T(8,128)} %bitcast.109, bf16[8,3,2048,256]{3,2,1,0:T(8,128)(2,1)} %w_ref.1), custom_call_target="tpu_custom_call" | custom-call | flops 48318382080 | bytes 159383552 | tf_op jit(solution)/shard_map/pallas_call | solution.py:1814
  367.1 89.3 %shard_map.236 = bf16[128,2176]{1,0:T(8,128)(2,1)} custom-call(s32[8,512,8]{2,1,0:T(8,128)} %bitcast.68, f32[8,8,80,128]{3,2,1,0:T(8,128)} %bitcast.83, bf16[8,8,80,2048]{3,2,1,0:T(8,128)(2,1)} %bitcast.67), custom_call_target="tpu_custom_call" | custom-call | bytes 100000000 | tf_op jit(solution)/shard_map/pallas_call | solution.py:1161
  456.4 1.1 convert_element_type.79
  457.6 0.2 multiply_reduce_fusion.3
  457.7 0.1 multiply_convert_fusion.1
  457.9 0.6 multiply_reduce_fusion
  458.5 0.1 copy-done.5
  458.6 1.9 fusion.22
  460.5 65.0 %shard_map.237 = (bf16[2,4,128,2048]{3,2,1,0:T(8,128)(2,1)}, bf16[3,128,2048]{2,1,0:T(8,128)(2,1)}, bf16[2,512,2048]{2,1,0:T(8,128)(2,1)}) custom-call(bf16[128,2048]{1,0:T(8,128)(2,1)} %get-tuple-element.166.r_ref, s32[8,512,8]{2,1,0:T(8,128)} %bitcast.69, bf16[8,8,80,2048]{3,2,1,0:T(8,128)(2,1)} %bitcast.66), custom_call_target="tpu_custom_call" | custom-call | bytes 100000000 | tf_op jit(solution)/shard_map/pallas_call | solution.py:472
  525.5 21.6 %shard_map.238 = (bf16[1024,256]{1,0:T(8,128)(2,1)}, bf16[4096,256]{1,0:T(8,128)(2,1)}, bf16[4096,256]{1,0:T(8,128)(2,1)}, bf16[256,2048]{1,0:T(8,128)(2,1)}, f32[8,128]{1,0:T(8,128)}, /*index=5*/f32[8,512]{1,0:T(8,128)}) custom-call(s32[6]{0:T(128)} %stack.38.index_ref, s32[5]{0:T(128)} %doc_ref.3, f32[8,128]{1,0:T(8,128)} %slice.36.q_stat, ...), custom_call_target="tpu_custom_call" | custom-call | flops 2684354560 | bytes 8388608 | tf_op jit(solution)/shard_map/pallas_call | solution.py:1592
  547.2 0.7 reshape.210
  547.9 1.3 pad_maximum_fusion.2.s_ref
  549.2 45.0 %shard_map.239 = (bf16[1024,256]{1,0:T(8,128)(2,1)}, bf16[1024,256]{1,0:T(8,128)(2,1)}, bf16[128,2048]{1,0:T(8,128)(2,1)}, f32[16,128]{1,0:T(8,128)}) custom-call(bf16[4,1024,256]{2,1,0:T(8,128)(2,1)} %bitcast.84, bf16[4,1024,256]{2,1,0:T(8,128)(2,1)} %bitcast.85, bf16[3,128,2048]{2,1,0:T(8,128)(2,1)} %get-tuple-element.128.x_ref, ...), custom_call_target="tpu_custom_call" | custom-call | bytes 100000000 | tf_op jit(solution)/shard_map/pallas_call | solution.py:562
  594.3 2.8 collective-permute-start.7
  597.1 1.3 collective-permute-start.9
  598.3 13.9 %shard_map.240 = (bf16[2048,768]{1,0:T(8,128)(2,1)}, bf16[1024,2048]{1,0:T(8,128)(2,1)}, f32[8,256]{1,0:T(8,128)}) custom-call(bf16[1024,256]{1,0:T(8,128)(2,1)} %get-tuple-element.125.dq_ref, bf16[1024,256]{1,0:T(8,128)(2,1)} %get-tuple-element.133.dk_ref, bf16[1024,256]{1,0:T(8,128)(2,1)} %get-tuple-element.134.dv_ref, ...), custom_call_target="tpu_custom_call" | custom-call | flops 6442450944 | bytes 14680064 | tf_op jit(solution)/shard_map/pallas_call | solution.py:1705
  612.2 0.7 reshape.216.refs_0_
  612.9 0.7 slice.41
  613.6 0.6 select_maximum_fusion.refs_1_
  614.3 66.2 %shard_map.241 = (bf16[128,2048]{1,0:T(8,128)(2,1)}, bf16[3,64,2048]{2,1,0:T(8,128)(2,1)}, bf16[128,2048]{1,0:T(8,128)(2,1)}, bf16[8,4,64,128]{3,2,1,0:T(8,128)(2,1)}, f32[8,4,24,128]{3,2,1,0:T(8,128)}) custom-call(bf16[2,4,128,2048]{3,2,1,0:T(8,128)(2,1)} %bitcast.81, bf16[4,2,256,768]{3,2,1,0:T(8,128)(2,1)} %bitcast.82, ...), custom_call_target="tpu_custom_call" | custom-call | bytes 100000000 | tf_op jit(solution)/shard_map/pallas_call | solution.py:620
  680.5 0.8 dynamic-slice_bitcast_fusion.4
  681.4 0.5 slice_bitcast_fusion
  681.9 0.1 add_convert_fusion
  682.0 3.2 collective-permute-start.10
  685.2 1.0 slice_reduce_fusion
  686.2 1.6 reshape.223
  687.9 0.6 dynamic_slice.43
  688.4 2.6 fusion
  691.0 6.7 collective-permute-done.10.do_ref
  697.7 0.7 copy-done.12
  698.4 5.2 shard_map.242
  703.6 1.4 reduce.1
  (52 shorter events, 0.5 us)
Async XLA Ops:
  0.6 77.6 %collective-permute-start = (bf16[64,2048]{1,0:T(8,128)(2,1)}, bf16[64,2048]{1,0:T(8,128)(2,1)S(1)}, u32[]{:S(2)}, u32[]{:S(2)}) collective-permute-start(bf16[64,2048]{1,0:T(8,128)(2,1)} %param.20), channel_id=1, source_target_pairs={{0,0},{1,8},{2,16},{3,24},{4,4},{5,12},{6,20},{7,28},{8,9},{9,17},... | collective-permute-start | bytes 786440 | tf_op jit(solution)/shard_map/ppermute | solution.py:1197
  78.3 11.9 %copy-start.7 = (bf16[64,2048]{1,0:T(8,128)(2,1)}, bf16[64,2048]{1,0:T(8,128)(2,1)S(1)}, u32[]{:S(2)}) copy-start(bf16[64,2048]{1,0:T(8,128)(2,1)S(1)} %collective-permute-done.w0) | copy-start | bytes 786436
  78.3 56.6 %collective-permute-start.3 = (bf16[64,2048]{1,0:T(8,128)(2,1)S(1)}, bf16[64,2048]{1,0:T(8,128)(2,1)S(1)}, u32[]{:S(2)}, u32[]{:S(2)}) collective-permute-start(bf16[64,2048]{1,0:T(8,128)(2,1)S(1)} %collective-permute-done.w0), channel_id=1, source_target_pairs={{0,24},{1,25},{2,26},{3,27},{4,28},{5,29},{6,30},{7,31},{8,16},{9,... | collective-permute-start | bytes 786440 | tf_op jit(solution)/shard_map/ppermute | solution.py:1197
  78.3 56.6 %collective-permute-start.2 = (bf16[64,2048]{1,0:T(8,128)(2,1)S(1)}, bf16[64,2048]{1,0:T(8,128)(2,1)S(1)}, u32[]{:S(2)}, u32[]{:S(2)}) collective-permute-start(bf16[64,2048]{1,0:T(8,128)(2,1)S(1)} %collective-permute-done.w0), channel_id=1, source_target_pairs={{0,16},{1,17},{2,18},{3,19},{4,20},{5,21},{6,22},{7,23},{8,24},{9,... | collective-permute-start | bytes 786440 | tf_op jit(solution)/shard_map/ppermute | solution.py:1197
  78.4 56.5 %collective-permute-start.1 = (bf16[64,2048]{1,0:T(8,128)(2,1)S(1)}, bf16[64,2048]{1,0:T(8,128)(2,1)S(1)}, u32[]{:S(2)}, u32[]{:S(2)}) collective-permute-start(bf16[64,2048]{1,0:T(8,128)(2,1)S(1)} %collective-permute-done.w0), channel_id=1, source_target_pairs={{0,8},{1,9},{2,10},{3,11},{4,12},{5,13},{6,14},{7,15},{8,0},{9,1},... | collective-permute-start | bytes 786440 | tf_op jit(solution)/shard_map/ppermute | solution.py:1197
  80.9 54.5 %copy-start.13 = (s32[8,4,8,128]{3,2,1,0:T(8,128)S(1)}, s32[8,4,8,128]{3,2,1,0:T(8,128)}, u32[]{:S(2)}) copy-start(s32[8,4,8,128]{3,2,1,0:T(8,128)} %get-tuple-element.108) | copy-start | bytes 393220
  90.1 47.7 %copy-start.3 = (bf16[8,4,64,128]{3,2,1,0:T(8,128)(2,1)S(1)}, bf16[8,4,64,128]{3,2,1,0:T(8,128)(2,1)}, u32[]{:S(2)}) copy-start(bf16[8,4,64,128]{3,2,1,0:T(8,128)(2,1)} %get-tuple-element.91) | copy-start | bytes 1572868
  134.8 6.4 copy-start.8
  134.9 6.4 copy-start.9
  134.9 4.3 copy-start.10
  134.9 20.3 %collective-permute-start.4 = (bf16[3,128,2048]{2,1,0:T(8,128)(2,1)}, bf16[3,128,2048]{2,1,0:T(8,128)(2,1)}, u32[]{:S(2)}, u32[]{:S(2)}) collective-permute-start(bf16[3,128,2048]{2,1,0:T(8,128)(2,1)} %get-tuple-element.112.g0), channel_id=1, source_target_pairs={{0,8},{1,9},{2,10},{3,11},{4,20},{5,21},{6,22},{7,23},{8,0},{9,1},... | collective-permute-start | bytes 4718600 | tf_op jit(solution)/shard_map/ppermute | solution.py:1197
  139.2 2.1 copy-start.14
  141.3 59.7 %copy-start = (s32[8,8,512]{1,2,0:T(8,128)}, s32[8,8,512]{1,2,0:T(8,128)S(1)}, u32[]{:S(2)}) copy-start(s32[8,8,512]{1,2,0:T(8,128)S(1)} %convert_select_fusion) | copy-start | bytes 393220
  155.2 48.7 %collective-permute-start.5 = (bf16[3,128,2048]{2,1,0:T(8,128)(2,1)}, bf16[3,128,2048]{2,1,0:T(8,128)(2,1)}, u32[]{:S(2)}, u32[]{:S(2)}) collective-permute-start(bf16[3,128,2048]{2,1,0:T(8,128)(2,1)} %get-tuple-element.112.g0), channel_id=1, source_target_pairs={{0,16},{1,17},{2,18},{3,19},{4,12},{5,13},{6,14},{7,15},{8,24},{9,... | collective-permute-start | bytes 4718600 | tf_op jit(solution)/shard_map/ppermute | solution.py:1197
  157.4 46.5 %collective-permute-start.6 = (bf16[3,128,2048]{2,1,0:T(8,128)(2,1)}, bf16[3,128,2048]{2,1,0:T(8,128)(2,1)}, u32[]{:S(2)}, u32[]{:S(2)}) collective-permute-start(bf16[3,128,2048]{2,1,0:T(8,128)(2,1)} %collective-permute-done.4.g1), channel_id=1, source_target_pairs={{0,16},{1,17},{2,18},{3,19},{4,12},{5,13},{6,14},{7,15},{8,24},{9,... | collective-permute-start | bytes 4718600 | tf_op jit(solution)/shard_map/ppermute | solution.py:1197
  201.0 1.3 copy-start.1
  201.0 1.2 copy-start.2
  202.2 1.0 copy-start.4
  203.3 0.8 copy-start.6
  457.5 1.0 copy-start.5
  549.2 45.0 %copy-start.11 = (bf16[256,2048]{1,0:T(8,128)(2,1)S(1)}, bf16[256,2048]{1,0:T(8,128)(2,1)}, u32[]{:S(2)}) copy-start(bf16[256,2048]{1,0:T(8,128)(2,1)} %get-tuple-element.132) | copy-start | bytes 3145732
  594.3 20.0 %collective-permute-start.7 = (bf16[64,2048]{1,0:T(8,128)(2,1)S(1)}, bf16[64,2048]{1,0:T(8,128)(2,1)S(1)}, u32[]{:S(2)}, u32[]{:S(2)}) collective-permute-start(bf16[64,2048]{1,0:T(8,128)(2,1)S(1)} %get-tuple-element.138), channel_id=1, source_target_pairs={{0,8},{1,9},{2,10},{3,11},{4,12},{5,13},{6,14},{7,15},{8,0},{9,1},... | collective-permute-start | bytes 786440 | tf_op jit(solution)/shard_map/ppermute | solution.py:1197
  597.1 17.2 %collective-permute-start.8 = (bf16[64,2048]{1,0:T(8,128)(2,1)S(1)}, bf16[64,2048]{1,0:T(8,128)(2,1)S(1)}, u32[]{:S(2)}, u32[]{:S(2)}) collective-permute-start(bf16[64,2048]{1,0:T(8,128)(2,1)S(1)} %get-tuple-element.139), channel_id=1, source_target_pairs={{0,16},{1,17},{2,18},{3,19},{4,20},{5,21},{6,22},{7,23},{8,24},{9,... | collective-permute-start | bytes 786440 | tf_op jit(solution)/shard_map/ppermute | solution.py:1197
  597.1 17.2 %collective-permute-start.9 = (bf16[64,2048]{1,0:T(8,128)(2,1)S(1)}, bf16[64,2048]{1,0:T(8,128)(2,1)S(1)}, u32[]{:S(2)}, u32[]{:S(2)}) collective-permute-start(bf16[64,2048]{1,0:T(8,128)(2,1)S(1)} %get-tuple-element.140), channel_id=1, source_target_pairs={{0,24},{1,25},{2,26},{3,27},{4,28},{5,29},{6,30},{7,31},{8,16},{9,... | collective-permute-start | bytes 786440 | tf_op jit(solution)/shard_map/ppermute | solution.py:1197
  682.0 15.7 %collective-permute-start.10 = (bf16[64,2048]{1,0:T(8,128)(2,1)S(1)}, bf16[64,2048]{1,0:T(8,128)(2,1)S(1)}, u32[]{:S(2)}, u32[]{:S(2)}) collective-permute-start(bf16[64,2048]{1,0:T(8,128)(2,1)S(1)} %add_convert_fusion), channel_id=1, source_target_pairs={{0,0},{8,1},{16,2},{24,3},{4,4},{12,5},{20,6},{28,7},{9,8},{17,9},... | collective-permute-start | bytes 786440 | tf_op jit(solution)/shard_map/ppermute | solution.py:1197
  697.7 0.7 copy-start.12

commit v8 on v7

--- a/solution.py
+++ b/solution.py
@@ -25,7 +25,7 @@
 ATTEND_CHUNK = 512
 ATTEND_ROWS = 512
 BACK_ROWS = 1024
-PROJECT_ROWS = 256
+PROJECT_ROWS = 512
 SPREAD_WIDTH = 2048
 
 
@@ -744,7 +744,20 @@
         if source != "x":
             picks = [jnp.where(slot_ref[at, e : e + 1, :] == row, 1.0, 0.0).astype(BF16) for e in range(experts)]
             pick[at] = jnp.concatenate(picks, axis=0)
-        else:
+        if n >= 2:
+            sent.pop(n - 2).wait()
+
+        def step(i, _):
+            cols = pl.ds(pl.multiple_of(i * width, width), width)
+            rows = dot(pick[at], rows_in[:, cols]).astype(BF16)
+            for e in range(experts):
+                rows_out[e, :, cols] = rows[e * slots : (e + 1) * slots]
+            return 0
+
+        lax.fori_loop(0, D // width, step, 0)
+        sent[n] = out_copy(n, xr_ref if source == "x" else gr_ref, at)
+        sent[n].start()
+        if source == "x":
             logits = dot(rows_in[...], router_ref[...])
             powers = jnp.exp(logits - jnp.max(logits, axis=1, keepdims=True))
             chances = powers / jnp.sum(powers, axis=1, keepdims=True)
@@ -753,19 +766,6 @@
             gates = dot(pick[at], jnp.concatenate([high, low], axis=1))
             for e in range(experts):
                 gate_ref[e, at] = gates[e * slots : (e + 1) * slots]
-        if n >= 2:
-            sent.pop(n - 2).wait()
-
-        def step(i, _):
-            cols = pl.ds(pl.multiple_of(i * width, width), width)
-            rows = dot(pick[at], rows_in[:, cols]).astype(BF16)
-            for e in range(experts):
-                rows_out[e, :, cols] = rows[e * slots : (e + 1) * slots]
-            return 0
-
-        lax.fori_loop(0, D // width, step, 0)
-        sent[n] = out_copy(n, xr_ref if source == "x" else gr_ref, at)
-        sent[n].start()
 
     jobs = _Jobs(load, compute)
     jobs.add(*[(j, (z + j) % 4, core) for j in range(4)])

time: 715 us -> 714 us (level)
  no operation moved by 1% of the time
where the time goes in v8:
time: 714 us; the launch traced here: 704 us
  Pallas kernels  645 us (90%)
  starting transfers between devices  16.8 us (2%)
  other arithmetic  15.2 us (2%)
  local copies, waits for them, and re-layouts  13.4 us (2%)
    pallas_call x1, Pallas kernels, gather_pick(): _comm(kernel, outs, scratch, collective_id, specs)  97.3 us
    pallas_call x1, Pallas kernels, spread_scatter(): _comm(kernel, out, scratch, collective_id, specs)  89.9 us
    pallas_call x1, Pallas kernels, enter(): _comm(kernel, outs, scratch, collective_id, specs)  66.8 us
    pallas_call x1, Pallas kernels, leave(): _comm(kernel, outs, scratch, collective_id, specs)  66.2 us
    pallas_call x1, Pallas kernels, run_experts(): pl.pallas_call(_expert_kernel, out_shape=[jax.ShapeDtypeStruct(x.shape, B...  64.7 us
    pallas_call x1, Pallas kernels, column_gather(): _comm(kernel, outs, scratch, collective_id, specs)(rows, slot, out_rows)  64.7 us
    pallas_call x1, Pallas kernels, key_value_sums(): return _comm(kernel, outs, scratch, collective_id, specs)(dk, dv, x, inner)  45.3 us
    pallas_call x1, Pallas kernels, plane_pair(): _comm(kernel, outs, scratch, collective_id, specs)  44.7 us
  transfers between devices with their start and end apart: 11, of which 1 were waited for; matrix products, arithmetic and copies ran while one was open for 3% of the time, Pallas kernels for 27%

profile of v8, /device:TPU:13, one launch (start us, length us, event | category | flops | bytes accessed | tf_op | source)
XLA Modules:
  0.0 704.2 jit_solution(14868445854084320922)
XLA Ops:
  0.6 4.1 collective-permute-start
  4.9 0.7 pad_maximum_fusion.3
  5.6 0.7 copy.64.gain_ref
  6.3 66.8 %shard_map.229 = (bf16[2,4,128,2048]{3,2,1,0:T(8,128)(2,1)}, bf16[4,2,4,64,768]{4,3,2,1,0:T(8,128)(2,1)}, bf16[8,4,64,128]{3,2,1,0:T(8,128)(2,1)}, s32[8,4,8,128]{3,2,1,0:T(8,128)}, bf16[4,128,2048]{2,1,0:T(8,128)(2,1)}) custom-call(bf16[128,2048]{1,0:T(8,128)(2,1)} %h_ref.3, bf16[64,2048]{1,0:T(8,128)(2,1)} %wq_ref.3, bf16[64,2048]{1,0:T(8,128)(2,1)} %wk_ref.3, ...), custom_call_target="tpu_custom_call" | custom-call | bytes 100000000 | tf_op jit(solution)/shard_map/pallas_call | solution.py:390
  73.1 1.2 slice.46
  74.3 1.9 fusion.4
  76.3 0.1 copy.76
  76.3 0.6 pad_convert_fusion.gain_ref
  77.0 1.3 pad_maximum_fusion
  78.4 2.6 collective-permute-start.1
  80.9 8.6 %shard_map.230 = (f32[1024,512]{1,0:T(8,128)}, bf16[1024,256]{1,0:T(8,128)(2,1)}, bf16[1024,256]{1,0:T(8,128)(2,1)}, bf16[1024,256]{1,0:T(8,128)(2,1)}, f32[2,8,128]{2,1,0:T(8,128)}) custom-call(bf16[1024,2048]{1,0:T(8,128)(2,1)} %bitcast.105, bf16[2048,768]{1,0:T(8,128)(2,1)} %bitcast.107, f32[8,256]{1,0:T(8,128)} %pad_convert_fusion.gain_ref, ...), custom_call_target="tpu_custom_call" | custom-call | flops 3221225472 | bytes 7340032 | tf_op jit(solution)/shard_map/pallas_call | solution.py:1639
  89.5 44.7 %shard_map.231 = (bf16[4,1024,256]{2,1,0:T(8,128)(2,1)}, bf16[4,1024,256]{2,1,0:T(8,128)(2,1)}, bf16[3,128,2048]{2,1,0:T(8,128)(2,1)}, f32[16,128]{1,0:T(8,128)}, f32[4,8,128]{2,1,0:T(8,128)}) custom-call(bf16[1024,256]{1,0:T(8,128)(2,1)} %get-tuple-element.92.a_ref, bf16[1024,256]{1,0:T(8,128)(2,1)} %get-tuple-element.93.b_ref, bf16[128,2048]{1,0:T(8,128)(2,1)} %x_ref.1, ...), custom_call_target="tpu_custom_call" | custom-call | bytes 100000000 | tf_op jit(solution)/shard_map/pallas_call | solution.py:444
  134.3 0.5 collective-permute-start.4
  134.8 0.4 compare_reduce_fusion
  135.3 1.4 copy.67
  136.7 0.6 stack.38.index_ref
  137.2 1.3 dynamic-slice_maximum_fusion.router_ref
  138.6 2.1 convert_select_fusion
  140.7 0.6 slice.36.q_stat
  141.3 13.5 %shard_map.232 = (f32[1024,256]{1,0:T(8,128)}, f32[1024,256]{1,0:T(8,128)}, bf16[1024,2048]{1,0:T(8,128)(2,1)}) custom-call(s32[6]{0:T(128)} %stack.38.index_ref, s32[5]{0:T(128)} %doc_ref.3, f32[8,128]{1,0:T(8,128)} %slice.36.q_stat, f32[32,128]{1,0:T(8,128)} %bitcast.90, bf16[1024,256]{1,0:T(8,128)(2,1)} %get-tuple-element.97.q_ref, ...), custom_call_target="tpu_custom_call" | custom-call | flops 1073741824 | bytes 4194304 | tf_op jit(solution)/shard_map/pallas_call | solution.py:1569
  154.9 2.2 collective-permute-start.5
  157.2 0.4 convert_reduce_fusion
  157.6 42.5 %shard_map.233 = bf16[128,2048]{1,0:T(8,128)(2,1)} custom-call(bf16[2,4,128,2048]{3,2,1,0:T(8,128)(2,1)} %bitcast.80), custom_call_target="tpu_custom_call" | custom-call | bytes 100000000 | tf_op jit(solution)/shard_map/pallas_call | solution.py:492
  200.2 1.2 copy.70.slot_ref
  201.4 0.3 multiply_reduce_fusion.2
  201.7 0.2 multiply_convert_fusion.x_ref
  201.9 0.5 copy-done.4
  202.4 0.4 fusion.23
  202.8 0.1 copy.71
  202.9 0.2 fusion.6
  203.1 0.1 copy-done.6
  203.2 97.3 %shard_map.234 = (bf16[32,128,2048]{2,1,0:T(8,128)(2,1)}, bf16[8,8,80,2048]{3,2,1,0:T(8,128)(2,1)}, bf16[8,8,80,2048]{3,2,1,0:T(8,128)(2,1)}, f32[8,8,80,128]{3,...) custom-call(bf16[128,2048]{1,0:T(8,128)(2,1)} %copy-done.6, ...), custom_call_target="tpu_custom_call" | custom-call | bytes 100000000 | tf_op jit(solution)/shard_map/pallas_call | solution.py:905
  300.6 64.7 %shard_map.235 = (bf16[8,640,2048]{2,1,0:T(8,128)(2,1)}, bf16[8,640,2048]{2,1,0:T(8,128)(2,1)}, f32[8,3,2048,256]{3,2,1,0:T(8,128)}, f32[8,640,128]{2,1,0:T(8,128)}) custom-call(bf16[8,640,2048]{2,1,0:T(8,128)(2,1)} %bitcast.103, bf16[8,640,2048]{2,1,0:T(8,128)(2,1)} %bitcast.104, f32[8,640,128]{2,1,0:T(8,128)} %bitcast.109, bf16[8,3,2048,256]{3,2,1,0:T(8,128)(2,1)} %w_ref.1), custom_call_target="tpu_custom_call" | custom-call | flops 48318382080 | bytes 159383552 | tf_op jit(solution)/shard_map/pallas_call | solution.py:1814
  365.3 89.9 %shard_map.236 = bf16[128,2176]{1,0:T(8,128)(2,1)} custom-call(s32[8,512,8]{2,1,0:T(8,128)} %bitcast.68, f32[8,8,80,128]{3,2,1,0:T(8,128)} %bitcast.83, bf16[8,8,80,2048]{3,2,1,0:T(8,128)(2,1)} %bitcast.67), custom_call_target="tpu_custom_call" | custom-call | bytes 100000000 | tf_op jit(solution)/shard_map/pallas_call | solution.py:1161
  455.2 1.1 convert_element_type.79
  456.3 0.2 multiply_reduce_fusion.3
  456.5 0.1 multiply_convert_fusion.1
  456.6 0.6 multiply_reduce_fusion
  457.2 0.1 copy-done.5
  457.4 1.9 fusion.22
  459.3 64.7 %shard_map.237 = (bf16[2,4,128,2048]{3,2,1,0:T(8,128)(2,1)}, bf16[3,128,2048]{2,1,0:T(8,128)(2,1)}, bf16[2,512,2048]{2,1,0:T(8,128)(2,1)}) custom-call(bf16[128,2048]{1,0:T(8,128)(2,1)} %get-tuple-element.166.r_ref, s32[8,512,8]{2,1,0:T(8,128)} %bitcast.69, bf16[8,8,80,2048]{3,2,1,0:T(8,128)(2,1)} %bitcast.66), custom_call_target="tpu_custom_call" | custom-call | bytes 100000000 | tf_op jit(solution)/shard_map/pallas_call | solution.py:472
  524.0 21.7 %shard_map.238 = (bf16[1024,256]{1,0:T(8,128)(2,1)}, bf16[4096,256]{1,0:T(8,128)(2,1)}, bf16[4096,256]{1,0:T(8,128)(2,1)}, bf16[256,2048]{1,0:T(8,128)(2,1)}, f32[8,128]{1,0:T(8,128)}, /*index=5*/f32[8,512]{1,0:T(8,128)}) custom-call(s32[6]{0:T(128)} %stack.38.index_ref, s32[5]{0:T(128)} %doc_ref.3, f32[8,128]{1,0:T(8,128)} %slice.36.q_stat, ...), custom_call_target="tpu_custom_call" | custom-call | flops 2684354560 | bytes 8388608 | tf_op jit(solution)/shard_map/pallas_call | solution.py:1592
  545.6 0.7 reshape.210
  546.4 1.3 pad_maximum_fusion.2.s_ref
  547.7 45.3 %shard_map.239 = (bf16[1024,256]{1,0:T(8,128)(2,1)}, bf16[1024,256]{1,0:T(8,128)(2,1)}, bf16[128,2048]{1,0:T(8,128)(2,1)}, f32[16,128]{1,0:T(8,128)}) custom-call(bf16[4,1024,256]{2,1,0:T(8,128)(2,1)} %bitcast.84, bf16[4,1024,256]{2,1,0:T(8,128)(2,1)} %bitcast.85, bf16[3,128,2048]{2,1,0:T(8,128)(2,1)} %get-tuple-element.128.x_ref, ...), custom_call_target="tpu_custom_call" | custom-call | bytes 100000000 | tf_op jit(solution)/shard_map/pallas_call | solution.py:562
  593.1 2.8 collective-permute-start.7
  595.9 1.3 collective-permute-start.9
  597.1 13.9 %shard_map.240 = (bf16[2048,768]{1,0:T(8,128)(2,1)}, bf16[1024,2048]{1,0:T(8,128)(2,1)}, f32[8,256]{1,0:T(8,128)}) custom-call(bf16[1024,256]{1,0:T(8,128)(2,1)} %get-tuple-element.125.dq_ref, bf16[1024,256]{1,0:T(8,128)(2,1)} %get-tuple-element.133.dk_ref, bf16[1024,256]{1,0:T(8,128)(2,1)} %get-tuple-element.134.dv_ref, ...), custom_call_target="tpu_custom_call" | custom-call | flops 6442450944 | bytes 14680064 | tf_op jit(solution)/shard_map/pallas_call | solution.py:1705
  611.0 0.7 reshape.216.refs_0_
  611.7 0.7 slice.41
  612.4 0.6 select_maximum_fusion.refs_1_
  613.0 66.2 %shard_map.241 = (bf16[128,2048]{1,0:T(8,128)(2,1)}, bf16[3,64,2048]{2,1,0:T(8,128)(2,1)}, bf16[128,2048]{1,0:T(8,128)(2,1)}, bf16[8,4,64,128]{3,2,1,0:T(8,128)(2,1)}, f32[8,4,24,128]{3,2,1,0:T(8,128)}) custom-call(bf16[2,4,128,2048]{3,2,1,0:T(8,128)(2,1)} %bitcast.81, bf16[4,2,256,768]{3,2,1,0:T(8,128)(2,1)} %bitcast.82, ...), custom_call_target="tpu_custom_call" | custom-call | bytes 100000000 | tf_op jit(solution)/shard_map/pallas_call | solution.py:620
  679.3 0.8 dynamic-slice_bitcast_fusion.4
  680.2 0.5 slice_bitcast_fusion
  680.7 0.1 add_convert_fusion
  680.8 3.2 collective-permute-start.10
  684.0 1.0 slice_reduce_fusion
  685.0 1.6 reshape.223
  686.6 0.6 dynamic_slice.43
  687.2 2.6 fusion
  689.8 6.7 collective-permute-done.10.do_ref
  696.5 0.7 copy-done.12
  697.2 5.2 shard_map.242
  702.4 1.4 reduce.1
  (52 shorter events, 0.5 us)
Async XLA Ops:
  0.6 77.6 %collective-permute-start = (bf16[64,2048]{1,0:T(8,128)(2,1)}, bf16[64,2048]{1,0:T(8,128)(2,1)S(1)}, u32[]{:S(2)}, u32[]{:S(2)}) collective-permute-start(bf16[64,2048]{1,0:T(8,128)(2,1)} %param.20), channel_id=1, source_target_pairs={{0,0},{1,8},{2,16},{3,24},{4,4},{5,12},{6,20},{7,28},{8,9},{9,17},... | collective-permute-start | bytes 786440 | tf_op jit(solution)/shard_map/ppermute | solution.py:1197
  78.3 11.2 %copy-start.7 = (bf16[64,2048]{1,0:T(8,128)(2,1)}, bf16[64,2048]{1,0:T(8,128)(2,1)S(1)}, u32[]{:S(2)}) copy-start(bf16[64,2048]{1,0:T(8,128)(2,1)S(1)} %collective-permute-done.w0) | copy-start | bytes 786436
  78.3 55.9 %collective-permute-start.3 = (bf16[64,2048]{1,0:T(8,128)(2,1)S(1)}, bf16[64,2048]{1,0:T(8,128)(2,1)S(1)}, u32[]{:S(2)}, u32[]{:S(2)}) collective-permute-start(bf16[64,2048]{1,0:T(8,128)(2,1)S(1)} %collective-permute-done.w0), channel_id=1, source_target_pairs={{0,24},{1,25},{2,26},{3,27},{4,28},{5,29},{6,30},{7,31},{8,16},{9,... | collective-permute-start | bytes 786440 | tf_op jit(solution)/shard_map/ppermute | solution.py:1197
  78.3 56.0 %collective-permute-start.2 = (bf16[64,2048]{1,0:T(8,128)(2,1)S(1)}, bf16[64,2048]{1,0:T(8,128)(2,1)S(1)}, u32[]{:S(2)}, u32[]{:S(2)}) collective-permute-start(bf16[64,2048]{1,0:T(8,128)(2,1)S(1)} %collective-permute-done.w0), channel_id=1, source_target_pairs={{0,16},{1,17},{2,18},{3,19},{4,20},{5,21},{6,22},{7,23},{8,24},{9,... | collective-permute-start | bytes 786440 | tf_op jit(solution)/shard_map/ppermute | solution.py:1197
  78.4 55.9 %collective-permute-start.1 = (bf16[64,2048]{1,0:T(8,128)(2,1)S(1)}, bf16[64,2048]{1,0:T(8,128)(2,1)S(1)}, u32[]{:S(2)}, u32[]{:S(2)}) collective-permute-start(bf16[64,2048]{1,0:T(8,128)(2,1)S(1)} %collective-permute-done.w0), channel_id=1, source_target_pairs={{0,8},{1,9},{2,10},{3,11},{4,12},{5,13},{6,14},{7,15},{8,0},{9,1},... | collective-permute-start | bytes 786440 | tf_op jit(solution)/shard_map/ppermute | solution.py:1197
  80.9 53.9 %copy-start.13 = (s32[8,4,8,128]{3,2,1,0:T(8,128)S(1)}, s32[8,4,8,128]{3,2,1,0:T(8,128)}, u32[]{:S(2)}) copy-start(s32[8,4,8,128]{3,2,1,0:T(8,128)} %get-tuple-element.108) | copy-start | bytes 393220
  89.5 47.7 %copy-start.3 = (bf16[8,4,64,128]{3,2,1,0:T(8,128)(2,1)S(1)}, bf16[8,4,64,128]{3,2,1,0:T(8,128)(2,1)}, u32[]{:S(2)}) copy-start(bf16[8,4,64,128]{3,2,1,0:T(8,128)(2,1)} %get-tuple-element.91) | copy-start | bytes 1572868
  134.2 6.4 copy-start.8
  134.2 6.4 copy-start.9
  134.3 4.3 copy-start.10
  134.3 20.6 %collective-permute-start.4 = (bf16[3,128,2048]{2,1,0:T(8,128)(2,1)}, bf16[3,128,2048]{2,1,0:T(8,128)(2,1)}, u32[]{:S(2)}, u32[]{:S(2)}) collective-permute-start(bf16[3,128,2048]{2,1,0:T(8,128)(2,1)} %get-tuple-element.112.g0), channel_id=1, source_target_pairs={{0,8},{1,9},{2,10},{3,11},{4,20},{5,21},{6,22},{7,23},{8,0},{9,1},... | collective-permute-start | bytes 4718600 | tf_op jit(solution)/shard_map/ppermute | solution.py:1197
  138.6 2.1 copy-start.14
  140.7 59.4 %copy-start = (s32[8,8,512]{1,2,0:T(8,128)}, s32[8,8,512]{1,2,0:T(8,128)S(1)}, u32[]{:S(2)}) copy-start(s32[8,8,512]{1,2,0:T(8,128)S(1)} %convert_select_fusion) | copy-start | bytes 393220
  154.9 48.2 %collective-permute-start.5 = (bf16[3,128,2048]{2,1,0:T(8,128)(2,1)}, bf16[3,128,2048]{2,1,0:T(8,128)(2,1)}, u32[]{:S(2)}, u32[]{:S(2)}) collective-permute-start(bf16[3,128,2048]{2,1,0:T(8,128)(2,1)} %get-tuple-element.112.g0), channel_id=1, source_target_pairs={{0,16},{1,17},{2,18},{3,19},{4,12},{5,13},{6,14},{7,15},{8,24},{9,... | collective-permute-start | bytes 4718600 | tf_op jit(solution)/shard_map/ppermute | solution.py:1197
  157.1 46.0 %collective-permute-start.6 = (bf16[3,128,2048]{2,1,0:T(8,128)(2,1)}, bf16[3,128,2048]{2,1,0:T(8,128)(2,1)}, u32[]{:S(2)}, u32[]{:S(2)}) collective-permute-start(bf16[3,128,2048]{2,1,0:T(8,128)(2,1)} %collective-permute-done.4.g1), channel_id=1, source_target_pairs={{0,16},{1,17},{2,18},{3,19},{4,12},{5,13},{6,14},{7,15},{8,24},{9,... | collective-permute-start | bytes 4718600 | tf_op jit(solution)/shard_map/ppermute | solution.py:1197
  200.1 1.3 copy-start.1
  200.1 1.2 copy-start.2
  201.4 1.0 copy-start.4
  202.4 0.8 copy-start.6
  456.3 1.0 copy-start.5
  547.7 45.3 %copy-start.11 = (bf16[256,2048]{1,0:T(8,128)(2,1)S(1)}, bf16[256,2048]{1,0:T(8,128)(2,1)}, u32[]{:S(2)}) copy-start(bf16[256,2048]{1,0:T(8,128)(2,1)} %get-tuple-element.132) | copy-start | bytes 3145732
  593.1 20.0 %collective-permute-start.7 = (bf16[64,2048]{1,0:T(8,128)(2,1)S(1)}, bf16[64,2048]{1,0:T(8,128)(2,1)S(1)}, u32[]{:S(2)}, u32[]{:S(2)}) collective-permute-start(bf16[64,2048]{1,0:T(8,128)(2,1)S(1)} %get-tuple-element.138), channel_id=1, source_target_pairs={{0,8},{1,9},{2,10},{3,11},{4,12},{5,13},{6,14},{7,15},{8,0},{9,1},... | collective-permute-start | bytes 786440 | tf_op jit(solution)/shard_map/ppermute | solution.py:1197
  595.9 17.2 %collective-permute-start.8 = (bf16[64,2048]{1,0:T(8,128)(2,1)S(1)}, bf16[64,2048]{1,0:T(8,128)(2,1)S(1)}, u32[]{:S(2)}, u32[]{:S(2)}) collective-permute-start(bf16[64,2048]{1,0:T(8,128)(2,1)S(1)} %get-tuple-element.139), channel_id=1, source_target_pairs={{0,16},{1,17},{2,18},{3,19},{4,20},{5,21},{6,22},{7,23},{8,24},{9,... | collective-permute-start | bytes 786440 | tf_op jit(solution)/shard_map/ppermute | solution.py:1197
  595.9 17.2 %collective-permute-start.9 = (bf16[64,2048]{1,0:T(8,128)(2,1)S(1)}, bf16[64,2048]{1,0:T(8,128)(2,1)S(1)}, u32[]{:S(2)}, u32[]{:S(2)}) collective-permute-start(bf16[64,2048]{1,0:T(8,128)(2,1)S(1)} %get-tuple-element.140), channel_id=1, source_target_pairs={{0,24},{1,25},{2,26},{3,27},{4,28},{5,29},{6,30},{7,31},{8,16},{9,... | collective-permute-start | bytes 786440 | tf_op jit(solution)/shard_map/ppermute | solution.py:1197
  680.8 15.7 %collective-permute-start.10 = (bf16[64,2048]{1,0:T(8,128)(2,1)S(1)}, bf16[64,2048]{1,0:T(8,128)(2,1)S(1)}, u32[]{:S(2)}, u32[]{:S(2)}) collective-permute-start(bf16[64,2048]{1,0:T(8,128)(2,1)S(1)} %add_convert_fusion), channel_id=1, source_target_pairs={{0,0},{8,1},{16,2},{24,3},{4,4},{12,5},{20,6},{28,7},{9,8},{17,9},... | collective-permute-start | bytes 786440 | tf_op jit(solution)/shard_map/ppermute | solution.py:1197
  696.5 0.7 copy-start.12
